TPU v7x, 128 devices: a whole 4x4x4 slice. The times are simulated.
128 devices in a mesh: ctx: 32 (over z, x, core), exp: 4 (over y).
Axes of the slice: x: 4, y: 4, z: 4, core: 2. Of those that a mesh axis runs over, the one named last changes fastest.
Arguments:
- attn_query: bfloat16 [32768, 2048], P('ctx', 'exp'), may hold values from -224 to 224
- attn_key: bfloat16 [32768, 2048], P('ctx', 'exp'), may hold values from -56 to 56
- attn_value: bfloat16 [32768, 2048], P('ctx', 'exp'), may hold values from -56 to 56
- prefix_state: float32 [32, 16, 128, 128], P('ctx', 'exp'), may hold values from -163840 to 163840
- moe_in: bfloat16 [32768, 2048], P(('ctx', 'exp')), may hold values from -6 to 6
- grad_out: bfloat16 [32768, 2048], P(('ctx', 'exp')), may hold values from -6 to 6
- router_gates: bfloat16 [32768, 1], P(('ctx', 'exp')), may hold values from 0.099609375 to 1
- expert_ids: int32 [32768, 1], P(('ctx', 'exp')), may hold values from 0 to 3; in each aligned block of 256 rows (0 to 255, 256 to 511, ...) at most 96 rows name the same one
- w_gate_up: bfloat16 [4, 2048, 1024], P('exp'), may hold values from -0.125 to 0.125
- w_down: bfloat16 [4, 512, 2048], P('exp'), may hold values from -0.25 to 0.25
- w_out: bfloat16 [2048, 2048], P('exp'), may hold values from -0.125 to 0.125
Outputs:
- grad_query: bfloat16 [32768, 2048], P('ctx', 'exp')
- grad_key: bfloat16 [32768, 2048], P('ctx', 'exp')
- grad_value: bfloat16 [32768, 2048], P('ctx', 'exp')
- grad_resid: bfloat16 [32768, 2048], P(('ctx', 'exp'))
- grad_gates: bfloat16 [32768, 1], P(('ctx', 'exp'))
- grad_gate_up: float32 [4, 2048, 1024], P('exp', 'ctx')
- grad_down: float32 [4, 512, 2048], P('exp', 'ctx')
Inputs may be any that keep to these rules, and one draw needn't show every extreme that they name: `expert_ids`: among the 256 rows of one device (aligned blocks of rows) no expert is named more than 96 times, a bound that some block reaches.
All inputs are finite; a program needn't handle non-finite values.
Results may differ from a plain program's by a relative error of at most 0.0063.
Values may be sent and summed in bfloat16 or wider, within the bound.
No kernel may reach another device: no remote copies, remote signals or barrier semaphores. Data moves between devices by JAX's collectives and lax.ppermute only.
A program may use at most 192 MiB of HBM per device.

v0:
```python
import math

import jax
import jax.numpy as jnp
from jax import lax
from jax.sharding import PartitionSpec as P

highest = lax.Precision.HIGHEST


def in_one_piece(arrays, axis, split_dim, concat_dim, along):
    widths = [math.prod(a.shape[along:]) for a in arrays]
    both = jnp.concatenate(
        [a.reshape(*a.shape[:along], w) for a, w in zip(arrays, widths)], axis=along
    )
    filled = lax.all_to_all(both, axis, split_axis=split_dim, concat_axis=concat_dim, tiled=True)
    pieces = jnp.split(filled, [sum(widths[:k]) for k in range(1, len(widths))], axis=along)
    return tuple(
        (b.reshape(*filled.shape[:along], *a.shape[along:]) for a, b in zip(arrays, pieces))
    )


def in_blocks(value, dim, length):
    before, after = (value.shape[:dim], value.shape[dim + 1 :])
    return jnp.moveaxis(value.reshape(*before, length, -1, *after), dim, 0)


def one_scatter(arrays, axis, dims):
    length = lax.axis_size(axis)
    pieces = [in_blocks(a, dim, length) for a, dim in zip(arrays, dims)]
    lines = jnp.concatenate([b.reshape(length, -1) for b in pieces], axis=1)
    extent = max(16, -(-lines.shape[1] // 1024) * 8)
    lines = jnp.pad(lines, ((0, 0), (0, extent * 128 - lines.shape[1]))).reshape(-1, 128)
    vector, at, gathered = (lax.psum_scatter(lines, axis, tiled=True).reshape(-1), 0, [])
    for b in pieces:
        part = b[0]
        gathered.append(vector[at : at + part.size].reshape(part.shape))
        at += part.size
    return tuple(gathered)


def silu_slope(value):
    logistic = jax.nn.sigmoid(value)
    return logistic * (1.0 + value * (1.0 - logistic))


def contract_rows(left, right):
    return lax.dot_general(
        left, right, (((0,), (0,)), ((), ())), preferred_element_type=jnp.float32
    )


def contract_cols(left, right):
    return lax.dot_general(
        left, right, (((1,), (1,)), ((), ())), preferred_element_type=jnp.float32
    )


def expert_backward(inputs, gate_vals, w_pair, w_back, hidden_units):
    width = w_back.shape[1]
    rows_in = inputs[:, :width]
    cotangent = inputs[:, width:]
    both = jnp.dot(rows_in, w_pair, preferred_element_type=jnp.float32)
    first = both[:, :hidden_units]
    second = both[:, hidden_units:]
    hidden = (jax.nn.silu(first) * second).astype(jnp.bfloat16)
    output = jnp.dot(hidden, w_back, preferred_element_type=jnp.float32)
    cot_wide = cotangent.astype(jnp.float32)
    grad_gate = jnp.sum(cot_wide * output, axis=1).astype(jnp.bfloat16)
    scaled = (gate_vals.astype(jnp.float32)[:, None] * cot_wide).astype(jnp.bfloat16)
    grad_hidden = contract_cols(scaled, w_back)
    grad_first = grad_hidden * second * silu_slope(first)
    grad_second = grad_hidden * jax.nn.silu(first)
    grad_both = jnp.concatenate([grad_first, grad_second], axis=1).astype(jnp.bfloat16)
    grad_rows = contract_cols(grad_both, w_pair).astype(jnp.bfloat16)
    return (rows_in, hidden, scaled, grad_both, grad_rows, grad_gate)


def block_state(query_rows, grad_rows, counts):
    query_wide = query_rows.astype(jnp.float32)
    grad_wide = grad_rows.astype(jnp.float32) / counts[:, None, None]
    return jnp.einsum("uhj,uhi->hji", query_wide, grad_wide, precision=highest)


def attend_block(query_rows, key_rows, value_rows, grad_rows, prior, later, counts):
    scale_col = counts[:, None, None]
    inverse = 1.0 / counts
    position = jnp.arange(counts.shape[0], dtype=jnp.int32)
    lower = (position[None, :] <= position[:, None]).astype(jnp.float32)
    upper = (position[None, :] >= position[:, None]).astype(jnp.float32) * inverse[None, :]
    mix_query = (
        jnp.einsum("thd,uhd->htu", grad_rows, value_rows, preferred_element_type=jnp.float32)
        * lower
    ).astype(jnp.bfloat16)
    grad_query = (
        jnp.einsum("htu,uhd->thd", mix_query, key_rows, preferred_element_type=jnp.float32)
        + jnp.einsum("thi,hji->thj", grad_rows.astype(jnp.float32), prior, precision=highest)
    ) / scale_col
    mix_key = (
        jnp.einsum("thd,uhd->htu", value_rows, grad_rows, preferred_element_type=jnp.float32)
        * upper
    ).astype(jnp.bfloat16)
    grad_key = jnp.einsum(
        "htu,uhd->thd", mix_key, query_rows, preferred_element_type=jnp.float32
    ) + jnp.einsum("thi,hji->thj", value_rows.astype(jnp.float32), later, precision=highest)
    mix_value = (
        jnp.einsum("thd,uhd->htu", key_rows, query_rows, preferred_element_type=jnp.float32) * upper
    ).astype(jnp.bfloat16)
    grad_value = jnp.einsum(
        "htu,uhd->thd", mix_value, grad_rows, preferred_element_type=jnp.float32
    ) + jnp.einsum("thj,hji->thi", key_rows.astype(jnp.float32), later, precision=highest)
    return (grad_query, grad_key, grad_value)


def on_device(
    attn_query,
    attn_key,
    attn_value,
    prefix_state,
    moe_in,
    grad_out,
    router_gates,
    expert_ids,
    w_gate_up,
    w_down,
    w_out,
):
    groups = lax.axis_size("exp")
    blocks_total = lax.axis_size("ctx")
    local_count = w_gate_up.shape[0]
    flight = local_count * groups
    rows = moe_in.shape[0]
    width = moe_in.shape[1]
    hidden_units = w_down.shape[1]
    top_count = expert_ids.shape[1]
    pair_count = rows * top_count
    capacity = 3 * pair_count // (2 * flight)
    flat_ids = expert_ids.reshape(pair_count)
    member = (flat_ids[:, None] == jnp.arange(flight, dtype=jnp.int32)[None, :]).astype(jnp.int32)
    earlier = jnp.cumsum(member, axis=0) - member
    slot_of = jnp.sum(earlier * member, axis=1)
    target = flat_ids * capacity + slot_of
    placing = (jnp.arange(flight * capacity, dtype=jnp.int32)[:, None] == target[None, :]).astype(
        jnp.bfloat16
    )
    joined = jnp.repeat(jnp.concatenate([moe_in, grad_out], axis=1), top_count, axis=0)
    packed = jnp.dot(placing, joined, preferred_element_type=jnp.float32).astype(jnp.bfloat16)
    gate_slots = (
        jnp.dot(placing, router_gates, preferred_element_type=jnp.float32)
        .astype(jnp.bfloat16)
        .reshape(flight * capacity)
    )
    arrived, gate_arrived = in_one_piece((packed, gate_slots), "exp", 0, 0, 1)
    arrived = arrived.reshape(groups, local_count, capacity, 2 * width)
    gate_arrived = gate_arrived.reshape(groups, local_count, capacity)
    inputs = arrived[:, 0].reshape(groups * capacity, 2 * width)
    gate_vals = gate_arrived[:, 0].reshape(groups * capacity)
    rows_in, hidden, scaled, grad_both, grad_rows, grad_gate = expert_backward(
        inputs, gate_vals, w_gate_up[0], w_down[0], hidden_units
    )
    row_grads = [grad_rows.reshape(groups, capacity, width)]
    gate_grads = [grad_gate.reshape(groups, capacity)]
    pair_sums = [contract_rows(rows_in, grad_both)]
    back_sums = [contract_rows(hidden, scaled)]
    rows_back = jnp.stack(row_grads, axis=1).reshape(flight * capacity, width)
    gates_back = jnp.stack(gate_grads, axis=1).reshape(flight * capacity)
    returned, gate_returned = (
        lax.all_to_all(rows_back, "exp", split_axis=0, concat_axis=0, tiled=True),
        lax.all_to_all(gates_back, "exp", split_axis=0, concat_axis=0, tiled=True),
    )
    pair_grads = contract_rows(placing, returned)
    grad_resid = (
        grad_out.astype(jnp.float32) + pair_grads.reshape(rows, top_count, width).sum(axis=1)
    ).astype(jnp.bfloat16)
    gate_pairs = contract_rows(placing, gate_returned.reshape(flight * capacity, 1))
    grad_gates = gate_pairs.astype(jnp.bfloat16)
    grad_gate_up, grad_down = one_scatter(
        (jnp.stack(pair_sums, axis=0), jnp.stack(back_sums, axis=0)), "ctx", (1, 1)
    )
    attn_grad = contract_cols(lax.all_gather(grad_resid, "exp", axis=0, tiled=True), w_out).astype(
        jnp.bfloat16
    )
    head_dim = prefix_state.shape[-1]
    tok_count = attn_query.shape[0]
    heads_here = attn_query.shape[1] // head_dim
    head_shape = (tok_count, heads_here, head_dim)
    query_rows = attn_query.reshape(head_shape)
    key_rows = attn_key.reshape(head_shape)
    value_rows = attn_value.reshape(head_shape)
    grad_rows = attn_grad.reshape(head_shape)
    block_at = lax.axis_index("ctx")
    total_tokens = tok_count * blocks_total
    counts = (
        3 * total_tokens + block_at * tok_count + jnp.arange(tok_count, dtype=jnp.int32) + 1
    ).astype(jnp.float32)
    local_state = block_state(query_rows, grad_rows, counts)
    piece = lax.all_gather(local_state[None], "ctx", axis=0, tiled=True)
    order = jnp.arange(piece.shape[0], dtype=jnp.int32)
    keep = (order > block_at).astype(jnp.float32)
    later_state = jnp.sum(piece * keep[:, None, None, None], axis=0)
    grad_query, grad_key, grad_value = attend_block(
        query_rows, key_rows, value_rows, grad_rows, prefix_state[0], later_state, counts
    )
    flat_shape = (tok_count, heads_here * head_dim)
    return (
        grad_query.reshape(flat_shape).astype(jnp.bfloat16),
        grad_key.reshape(flat_shape).astype(jnp.bfloat16),
        grad_value.reshape(flat_shape).astype(jnp.bfloat16),
        grad_resid,
        grad_gates,
        grad_gate_up,
        grad_down,
    )


def solution(mesh):
    return jax.shard_map(
        on_device,
        mesh=mesh,
        in_specs=(
            P("ctx", "exp"),
            P("ctx", "exp"),
            P("ctx", "exp"),
            P("ctx", "exp", None, None),
            P(("ctx", "exp"), None),
            P(("ctx", "exp"), None),
            P(("ctx", "exp"), None),
            P(("ctx", "exp"), None),
            P("exp", None, None),
            P("exp", None, None),
            P("exp", None),
        ),
        out_specs=(
            P("ctx", "exp"),
            P("ctx", "exp"),
            P("ctx", "exp"),
            P(("ctx", "exp"), None),
            P(("ctx", "exp"), None),
            P("exp", "ctx", None),
            P("exp", "ctx", None),
        ),
        check_vma=False,
    )
```

profile of v0, /device:TPU:0, one launch (start us, length us, event | category | flops | bytes accessed | tf_op | source)
XLA Modules:
  0.0 308.7 jit_solution(17044022812574908140)
XLA Ops:
  15.8 43.2 %all_to_all.27 = bf16[4,96,4097]{2,1,0:T(8,128)(2,1)S(1)} all-to-all(bf16[4,96,4097]{2,1,0:T(8,128)(2,1)S(1)} %pad_maximum_fusion.1), channel_id=1, replica_groups=mesh['ctx'=32,'exp'=4] {'exp'}, dimensions={0} | all-to-all | bytes 6292992 | tf_op jit(solution)/shard_map/all_to_all | solution.py:16
  62.3 3.1 fusion.15
  65.4 4.4 %all-to-all-start.1 = ((bf16[4,96,2048]{2,1,0:T(8,128)(2,1)}), bf16[4,96,2048]{2,1,0:T(8,128)(2,1)}, u32[]{:S(2)}, u32[]{:S(2)}) async-start(bf16[4,96,2048]{2,1,0:T(8,128)(2,1)} %bitcast.143), calls=%async_computation.1 | async-start | bytes 3145728 | tf_op jit(solution)/shard_map/all_to_all | solution.py:168
  69.8 4.7 %fusion.57 = f32[512,2048]{1,0:T(8,128)} fusion(bf16[384,512]{1,0:T(8,128)(2,1)S(1)} %get-tuple-element.37, f32[384]{0:T(512)S(1)} %convert_reduce_fusion, bf16[384,4097]{1,0:T(8,128)(2,1)} %bitcast.132), kind=kOutput, calls=%fused_computation.71 | convolution fusion | flops 807665664 | bytes 6161920 | tf_op jit(solution)/shard_map/dot_general | solution.py:48
  74.5 5.0 %reshape_transpose_reshape_stack.7 = f32[32,32768]{1,0:T(8,128)} reshape(f32[512,2048]{1,0:T(8,128)} %fusion.57) | data formatting | bytes 8388608 | tf_op jit(solution)/shard_map/reshape;transpose;reshape;stack | solution.py:31
  79.5 7.0 %fusion.29 = f32[2048,1024]{1,0:T(8,128)} fusion(bf16[384,4097]{1,0:T(8,128)(2,1)} %bitcast.133, bf16[384,512]{1,0:T(8,128)(2,1)S(1)} %get-tuple-element.36, bf16[384,512]{1,0:T(8,128)(2,1)S(1)} %get-tuple-element.35), kind=kOutput, calls=%fused_computation.41 | convolution fusion | flops 1612185600 | bytes 10747904 | tf_op jit(solution)/shard_map/dot_general | solution.py:48
  86.5 7.5 %reshape_transpose_reshape_stack.6 = f32[32,65536]{1,0:T(8,128)} reshape(f32[2048,1024]{1,0:T(8,128)} %fusion.29) | data formatting | bytes 16777216 | tf_op jit(solution)/shard_map/reshape;transpose;reshape;stack | solution.py:31
  94.1 3.1 %fusion.18 = bf16[256,2048]{1,0:T(8,128)(2,1)} fusion(bf16[384,2048]{1,0:T(8,128)(2,1)} %bitcast.9, bf16[256,2048]{1,0:T(8,128)(2,1)S(1)} %copy-done.10, s32[256]{0:T(256)S(1)} %multiply_add_fusion), kind=kOutput, calls=%fused_computation.27 | convolution fusion | flops 404324352 | bytes 3671040 | tf_op jit(solution)/shard_map/dot_general | solution.py:48
  97.3 9.3 %pad_maximum_fusion = f32[32,98304]{1,0:T(8,128)} fusion(f32[32,32768]{1,0:T(8,128)} %reshape_transpose_reshape_stack.7, f32[32,65536]{1,0:T(8,128)} %reshape_transpose_reshape_stack.6), kind=kLoop, calls=%fused_computation.4 | loop fusion | flops 3145728 | bytes 25165824 | tf_op jit(solution)/shard_map/concatenate | solution.py:31
  106.6 10.0 %reshape.175 = f32[24576,128]{1,0:T(8,128)} reshape(f32[32,98304]{1,0:T(8,128)} %pad_maximum_fusion) | data formatting | bytes 25165824 | tf_op jit(solution)/shard_map/reshape | solution.py:33
  116.9 31.4 %all-gather.4.cloned.1.call-done = bf16[1024,2048]{1,0:T(8,128)(2,1)} async-done(((bf16[256,2048]{1,0:T(8,128)(2,1)}), bf16[1024,2048]{1,0:T(8,128)(2,1)}) %all-gather.4.cloned.1.call-update) | async-done | bytes 4194320 | tf_op jit(solution)/shard_map/all_gather | solution.py:180
  148.3 5.7 %convolution_convert_fusion.1 = bf16[1024,512]{0,1:T(8,128)(2,1)S(1)} fusion(bf16[1024,2048]{1,0:T(8,128)(2,1)} %all-gather.4.cloned.1.call-done, bf16[512,2048]{1,0:T(8,128)(2,1)} %param.21), kind=kOutput, calls=%fused_computation.40 | convolution fusion | flops 2148007936 | bytes 7340032 | tf_op jit(solution)/shard_map/dot_general | solution.py:54
  158.8 2.5 fusion.10
  165.5 3.4 %all-to-all-start.2 = ((bf16[4,96,1]{1,2,0:T(2,128)(2,1)}), bf16[4,96,1]{1,2,0:T(2,128)(2,1)S(1)}, u32[]{:S(2)}, u32[]{:S(2)}) async-start(bf16[4,96,1]{1,2,0:T(2,128)(2,1)} %convert_element_type.154), calls=%async_computation.2 | async-start | bytes 4096 | tf_op jit(solution)/shard_map/all_to_all | solution.py:169
  169.0 5.2 %all-to-all-done.2 = bf16[4,96,1]{1,2,0:T(2,128)(2,1)S(1)} async-done(((bf16[4,96,1]{1,2,0:T(2,128)(2,1)}), bf16[4,96,1]{1,2,0:T(2,128)(2,1)S(1)}, u32[]{:S(2)}, u32[]{:S(2)}) %all-to-all-start.2) | async-done | bytes 800 | tf_op jit(solution)/shard_map/all_to_all | solution.py:169
  175.0 3.9 %fusion.43 = f32[4,1024,1024]{2,1,0:T(8,128)S(1)} fusion(bf16[1024,4,128]{0,2,1:T(8,128)(2,1)} %bitcast.140, bf16[1024,512]{1,0:T(8,128)(2,1)} %param.13), kind=kOutput, calls=%fused_computation.54 | convolution fusion | flops 1073741824 | bytes 18874368 | tf_op jit(solution)/shard_map/thd,uhd->htu/dot_general | solution.py:92
  179.0 10.9 %fusion.1 = f32[4,1024,128]{1,2,0:T(8,128)} fusion(f32[4,1024,1024]{2,1,0:T(8,128)S(1)} %fusion.43, f32[1024,1024]{1,0:T(8,128)} %fusion.10, bf16[1024,512]{1,0:T(8,128)(2,1)} %param.12), kind=kOutput, calls=%fused_computation.5 | convolution fusion | flops 1082130432 | bytes 24117248 | tf_op jit(solution)/shard_map/htu,uhd->thd/dot_general | solution.py:96
  189.8 4.0 %divide_convert_fusion = bf16[4,1024,128]{1,2,0:T(8,128)(2,1)} fusion(f32[4,1024,128]{1,2,0:T(8,128)} %fusion.1, bf16[1024,4,128]{0,2,1:T(8,128)(2,1)} %bitcast.141, f32[1024]{0:T(1024)S(1)} %add_convert_fusion.1, f32[1,4,128,128]{3,2,1,0:T(8,128)S(1)} %copy-done.12), kind=kOutput, calls=%fused_computation.38 | convolution fusion | flops 806879232 | bytes 4460544 | tf_op jit(solution)/shard_map/thi,hji->thj/dot_general | solution.py:97
  196.1 8.1 %fusion.14 = f32[4,128,1024]{2,1,0:T(8,128)} fusion(bf16[1024,4,128]{0,2,1:T(8,128)(2,1)} %bitcast.142, f32[1024,1024]{0,1:T(8,128)} %fusion.11, bf16[1024,512]{1,0:T(8,128)(2,1)} %param.11, bf16[1024,512]{1,0:T(8,128)(2,1)} %param.12), kind=kOutput, calls=%fused_computation.24 | convolution fusion | flops 2155872256 | bytes 9437184 | tf_op jit(solution)/shard_map/htu,uhd->thd/dot_general | solution.py:109
  204.2 19.6 %reduce-scatter.2.cloned.1.call-done = f32[768,128]{1,0:T(8,128)} async-done(((f32[24576,128]{1,0:T(8,128)}), f32[768,128]{1,0:T(8,128)}) %reduce-scatter.2.cloned.1.call-update) | async-done | bytes 393232 | tf_op jit(solution)/shard_map/reduce_scatter | solution.py:34
  227.1 51.3 %all-gather.6.cloned.1.call-done = f32[128,128,128]{2,1,0:T(8,128)} async-done(((f32[4,128,128]{2,1,0:T(8,128)}), f32[128,128,128]{2,1,0:T(8,128)}) %all-gather.6.cloned.1.call-update) | async-done | bytes 8388624 | tf_op jit(solution)/shard_map/all_gather | solution.py:197
  278.4 4.7 %multiply_reduce_fusion = f32[4,128,128]{2,1,0:T(8,128)S(1)} fusion(f32[32,4,128,128]{3,2,1,0:T(8,128)} %bitcast.135, f32[32]{0:T(128)S(1)} %compare_convert_fusion.1), kind=kLoop, calls=%fused_computation.7 | loop fusion | flops 4128768 | bytes 8650880 | tf_op jit(solution)/shard_map/reduce_sum | solution.py:200
  284.4 8.7 %fusion.22 = bf16[1024,4,128]{0,2,1:T(8,128)(2,1)} fusion(f32[4,128,1024]{2,1,0:T(8,128)S(1)} %fusion.41, f32[4,1024,1024]{2,1,0:T(8,128)} %copy-done.1, f32[1024,1024]{0,1:T(8,128)S(1)} %copy-done.2, bf16[1024,512]{1,0:T(8,128)(2,1)S(1)} %copy-done.9), kind=kOutput, calls=%fused_computation.32 | convolution fusion | flops 1083179008 | bytes 25165824 | tf_op jit(solution)/shard_map/htu,uhd->thd/dot_general | solution.py:103
  295.3 3.6 %add_convert_fusion = bf16[4,128,1024]{2,1,0:T(8,128)(2,1)} fusion(f32[4,128,1024]{2,1,0:T(8,128)} %fusion.14, f32[4,128,128]{2,1,0:T(8,128)S(1)} %multiply_reduce_fusion, bf16[1024,512]{1,0:T(8,128)(2,1)S(1)} %copy-done.6), kind=kOutput, calls=%fused_computation.36 | convolution fusion | flops 806354944 | bytes 4456448 | tf_op jit(solution)/shard_map/thj,hji->thi/dot_general | solution.py:111
  (71 shorter events, 32.6 us)
Async XLA Ops:
  8.0 53.0 %copy-start = (bf16[1,512,2048]{2,1,0:T(8,128)(2,1)S(1)}, bf16[1,512,2048]{2,1,0:T(8,128)(2,1)}, u32[]{:S(2)}) copy-start(bf16[1,512,2048]{2,1,0:T(8,128)(2,1)} %param.20) | copy-start | bytes 6291460
  15.8 43.4 %copy-start.11 = (bf16[1,2048,1024]{2,1,0:T(8,128)(2,1)S(1)}, bf16[1,2048,1024]{2,1,0:T(8,128)(2,1)}, u32[]{:S(2)}) copy-start(bf16[1,2048,1024]{2,1,0:T(8,128)(2,1)} %param.19) | copy-start | bytes 12582916
  59.0 2.0 copy-start.3
  65.4 28.7 %all-to-all-start.1 = ((bf16[4,96,2048]{2,1,0:T(8,128)(2,1)}), bf16[4,96,2048]{2,1,0:T(8,128)(2,1)}, u32[]{:S(2)}, u32[]{:S(2)}) async-start(bf16[4,96,2048]{2,1,0:T(8,128)(2,1)} %bitcast.143), calls=%async_computation.1 | async-start | bytes 3145728 | tf_op jit(solution)/shard_map/all_to_all | solution.py:168
  69.8 78.5 %all-gather.4.cloned.1.call-start = ((), (), s32[]{:S(2)}) async-start(), calls=%async_computation.4 | async-start | bytes 5242880 | tf_op jit(solution)/shard_map/all_gather | solution.py:180
  86.5 7.5 %copy-start.10 = (bf16[256,2048]{1,0:T(8,128)(2,1)S(1)}, bf16[256,2048]{1,0:T(8,128)(2,1)}, u32[]{:S(2)}) copy-start(bf16[256,2048]{1,0:T(8,128)(2,1)} %param.16) | copy-start | bytes 3145732
  97.2 126.6 %reduce-scatter.2.cloned.1.call-start = ((), (), s32[]{:S(2)}) async-start(), calls=%async_computation.5 | async-start | bytes 12976128 | tf_op jit(solution)/shard_map/reduce_scatter | solution.py:34
  116.6 161.8 %all-gather.6.cloned.1.call-start = ((), (), s32[]{:S(2)}) async-start(), calls=%async_computation.6 | async-start | bytes 8650752 | tf_op jit(solution)/shard_map/all_gather | solution.py:197
  116.9 38.1 %copy-start.8 = (bf16[1024,512]{1,0:T(8,128)(2,1)S(1)}, bf16[1024,512]{1,0:T(8,128)(2,1)}, u32[]{:S(2)}) copy-start(bf16[1024,512]{1,0:T(8,128)(2,1)} %param.11) | copy-start | bytes 3145732
  154.0 1.0 copy-start.7
  158.8 5.0 %copy-start.4 = (bf16[4,96,4097]{2,1,0:T(8,128)(2,1)S(1)}, bf16[4,96,4097]{2,1,0:T(8,128)(2,1)}, u32[]{:S(2)}) copy-start(bf16[4,96,4097]{2,1,0:T(8,128)(2,1)} %copy-done.3) | copy-start | bytes 9439492
  165.5 8.6 %all-to-all-start.2 = ((bf16[4,96,1]{1,2,0:T(2,128)(2,1)}), bf16[4,96,1]{1,2,0:T(2,128)(2,1)S(1)}, u32[]{:S(2)}, u32[]{:S(2)}) async-start(bf16[4,96,1]{1,2,0:T(2,128)(2,1)} %convert_element_type.154), calls=%async_computation.2 | async-start | bytes 4096 | tf_op jit(solution)/shard_map/all_to_all | solution.py:169
  178.9 10.9 %copy-start.1 = (f32[4,1024,1024]{2,1,0:T(8,128)}, f32[4,1024,1024]{2,1,0:T(8,128)S(1)}, u32[]{:S(2)}) copy-start(f32[4,1024,1024]{2,1,0:T(8,128)S(1)} %fusion.43) | copy-start | bytes 50331652
  178.9 10.9 %copy-start.12 = (f32[1,4,128,128]{3,2,1,0:T(8,128)S(1)}, f32[1,4,128,128]{3,2,1,0:T(8,128)}, u32[]{:S(2)}) copy-start(f32[1,4,128,128]{3,2,1,0:T(8,128)} %param.14) | copy-start | bytes 786436
  278.4 4.7 %copy-start.5 = (bf16[1024,512]{1,0:T(8,128)(2,1)S(1)}, bf16[1024,512]{1,0:T(8,128)(2,1)}, u32[]{:S(2)}) copy-start(bf16[1024,512]{1,0:T(8,128)(2,1)} %param.13) | copy-start | bytes 3145732
  278.4 5.7 %copy-start.2 = (f32[1024,1024]{0,1:T(8,128)S(1)}, f32[1024,1024]{0,1:T(8,128)}, u32[]{:S(2)}) copy-start(f32[1024,1024]{0,1:T(8,128)} %fusion.11) | copy-start | bytes 12582916
  283.1 1.3 copy-start.9
  284.4 10.9 %copy-start.6 = (bf16[1024,512]{1,0:T(8,128)(2,1)S(1)}, bf16[1024,512]{1,0:T(8,128)(2,1)}, u32[]{:S(2)}) copy-start(bf16[1024,512]{1,0:T(8,128)(2,1)} %param.12) | copy-start | bytes 3145732
Sparse Core Ops, SparseCore 0:
  97.3 50.8 all-gather.3
Sparse Core Ops, SparseCore 1:
  116.7 107.1 reduce-scatter.1
  226.2 52.1 all-gather.5
where the time goes:
time: 311 us; the launch traced here: 309 us
  waiting for transfers between devices  108 us (35%)
  matrix products  73.6 us (24%)
  blocking collectives  43.2 us (14%)
  local copies, waits for them, and re-layouts  37.5 us (12%)
  other arithmetic  22.9 us (7%)
  between operations  15.7 us (5%)
  starting transfers between devices  8.13 us (3%)
    all_gather x1, waiting for transfers between devices, on_device(): piece = lax.all_gather(local_state[None], 'ctx', axis=0, tiled=True)  51.3 us
    all_to_all x1, blocking collectives, in_one_piece(): lax.all_to_all(both, axis, split_axis=split_dim, concat_axis=concat_dim,...  43.2 us
    all_gather x1, waiting for transfers between devices, on_device(): lax.all_gather(grad_resid, 'exp', axis=0, tiled=True)  31.4 us
    reduce_scatter x1, waiting for transfers between devices, one_scatter(): lax.psum_scatter(lines, axis, tiled=True).reshape(-1)  19.6 us
    dot_general x4, matrix products, contract_rows(): lax.dot_general(left, right, (((0,), (0,)), ((), ())), preferred_element_...  15 us
    another operation x2, local copies, waits for them, and re-layouts, one_scatter(): lines = jnp.concatenate([b.reshape(length, -1) for b in pieces], axis=1)  12.5 us
    dot_general x1, matrix products, attend_block(): jnp.einsum('htu,uhd->thd', mix_query, key_rows, preferred_element_type=jn...  10.9 us
    dot_general x3, matrix products, contract_cols(): lax.dot_general(left, right, (((1,), (1,)), ((), ())), preferred_element_...  10.1 us
  transfers between devices with their start and end apart: 5, of which 4 were waited for; matrix products, arithmetic and copies ran while one was open for 30% of the time, Pallas kernels for 0%

commit v1 on v0

v1 whole, which is shorter than its diff:
```python
import functools

import jax
import jax.numpy as jnp
from jax import lax
from jax.experimental import pallas as pl
from jax.experimental.pallas import tpu as pltpu
from jax.sharding import PartitionSpec as P

bf16 = jnp.bfloat16
f32 = jnp.float32
VMEM = pltpu.VMEM
SMEM = pltpu.SMEM
Z, X, C, Y = 4, 4, 2, 4
CAP, ROWS, WIDTH, FF, HD, HEADS, TOK = 96, 256, 2048, 512, 128, 4, 1024
BLOCKS = Z * X * C
LIMIT = 48 * 1024 * 1024


def dot(a, b):
    return lax.dot_general(a, b, (((1,), (0,)), ((), ())), preferred_element_type=f32)


def dot_t(a, b):
    return lax.dot_general(a, b, (((1,), (1,)), ((), ())), preferred_element_type=f32)


def t_dot(a, b):
    return lax.dot_general(a, b, (((0,), (0,)), ((), ())), preferred_element_type=f32)


def split(a):
    hi = a.astype(bf16)
    return hi, (a - hi.astype(f32)).astype(bf16)


def full():
    return pl.BlockSpec(memory_space=VMEM)


def scalars():
    return pl.BlockSpec(memory_space=SMEM)


def call(body, name, outs, ins, flops=0, moved=0, grid=None, in_specs=None, out_specs=None):
    kwargs = {} if grid is None else {"grid": grid}
    return pl.pallas_call(
        body,
        name=name,
        out_shape=[jax.ShapeDtypeStruct(s, t) for s, t in outs],
        in_specs=in_specs or [full() for _ in ins],
        out_specs=out_specs or [full() for _ in outs],
        compiler_params=pltpu.CompilerParams(vmem_limit_bytes=LIMIT),
        cost_estimate=pl.CostEstimate(flops=flops, bytes_accessed=moved, transcendentals=0),
        **kwargs,
    )(*ins)


def pack_body(at_ref, ids_ref, gate_ref, moe_ref, cot_ref, place_ref, *chunks):
    me = at_ref[0]
    ids = ids_ref[...]
    rel = ids - me
    rel = jnp.where(rel < 0, rel + Y, rel)
    lanes = lax.broadcasted_iota(jnp.int32, (ROWS, HD), 1)
    member = (rel == lanes).astype(f32)
    row = lax.broadcasted_iota(jnp.int32, (ROWS, ROWS), 0)
    col = lax.broadcasted_iota(jnp.int32, (ROWS, ROWS), 1)
    earlier = dot((col < row).astype(bf16), member.astype(bf16))
    slot = jnp.sum(earlier * member, axis=1, keepdims=True).astype(jnp.int32)
    target = rel * CAP + slot
    places = lax.broadcasted_iota(jnp.int32, (ROWS, Y * CAP), 1)
    place = (places == target).astype(bf16)
    place_ref[...] = place
    gate = gate_ref[...].astype(f32)
    step = 512
    for j in range(WIDTH // step):
        part = t_dot(place, moe_ref[:, j * step : (j + 1) * step]).astype(bf16)
        for s in range(Y):
            chunks[s][:, j * step : (j + 1) * step] = part[s * CAP : (s + 1) * CAP]
    for j in range(WIDTH // step):
        scaled = (gate * cot_ref[:, j * step : (j + 1) * step].astype(f32)).astype(bf16)
        part = t_dot(place, scaled).astype(bf16)
        for s in range(Y):
            chunks[s][:, WIDTH + j * step : WIDTH + (j + 1) * step] = part[s * CAP : (s + 1) * CAP]


def pack(me, ids, gates, moe_in, grad_out):
    outs = [((ROWS, Y * CAP), bf16)] + [((CAP, 2 * WIDTH), bf16)] * Y
    ins = (me, ids, gates, moe_in, grad_out)
    specs = [scalars()] + [full()] * 4
    return call(pack_body, "pack", outs, ins, 2 * 384 * 256 * 4096, 5 << 20, in_specs=specs)


def expert_body(r0, r1, r2, r3, wp_ref, wb_ref, b0, b1, b2, b3, hid_ref, gb_ref, dot_ref, rows_ref):
    for s, r in enumerate((r0, r1, r2, r3)):
        rows_ref[s * CAP : (s + 1) * CAP, :] = r[...]
    step = 256
    total = jnp.zeros((Y * CAP, 1), f32)
    for j in range(FF // step):
        at, up = j * step, FF + j * step
        first = dot(rows_ref[:, :WIDTH], wp_ref[:, at : at + step])
        second = dot(rows_ref[:, :WIDTH], wp_ref[:, up : up + step])
        grad_hidden = dot_t(rows_ref[:, WIDTH:], wb_ref[at : at + step, :])
        s = 1.0 / (1.0 + jnp.exp(-first))
        silu = first * s
        hidden = (silu * second).astype(bf16)
        hid_ref[:, at : at + step] = hidden
        total += jnp.sum(hidden.astype(f32) * grad_hidden, axis=1, keepdims=True)
        slope = s * (1.0 + first * (1.0 - s))
        gb_ref[:, at : at + step] = (grad_hidden * second * slope).astype(bf16)
        gb_ref[:, up : up + step] = (grad_hidden * silu).astype(bf16)
    dot_ref[...] = jnp.broadcast_to(total, dot_ref.shape)
    for j in range(WIDTH // step):
        at = j * step
        back = dot_t(gb_ref[...], wp_ref[at : at + step, :]).astype(bf16)
        for s, b in enumerate((b0, b1, b2, b3)):
            b[:, at : at + step] = back[s * CAP : (s + 1) * CAP]


def expert(chunks, w_pair, w_back):
    n = Y * CAP
    outs = [((CAP, WIDTH), bf16)] * Y
    outs += [((n, FF), bf16), ((n, 2 * FF), bf16), ((n, HD), f32), ((n, 2 * WIDTH), bf16)]
    return call(expert_body, "expert", outs, (*chunks, w_pair, w_back), 5 * 2 * n * WIDTH * FF, 14 << 20)


def weights_body(core_ref, rows_ref, scaled_ref, gb_ref, hid_ref, keep_ref, send_ref):
    mine = core_ref[0] == 0
    up = t_dot(rows_ref[...], gb_ref[...])
    down = t_dot(hid_ref[...], scaled_ref[...])
    for k in range(X):
        for value, at, wide in (
            (up[k * 128 : k * 128 + 64], up[k * 128 + 64 : k * 128 + 128], None),
            (down[k * 32 : k * 32 + 16], down[k * 32 + 16 : k * 32 + 32], 1),
        ):
            keep = jnp.where(mine, value, at)
            send = jnp.where(mine, at, value).astype(bf16)
            keep = keep.astype(bf16)
            if wide is None:
                keep_ref[0, k, :64, :] = keep
                send_ref[0, k, :64, :] = send
            else:
                keep_ref[0, k, 64:80, :] = keep[:, :1024]
                send_ref[0, k, 64:80, :] = send[:, :1024]
                keep_ref[0, k, 80:96, :] = keep[:, 1024:]
                send_ref[0, k, 80:96, :] = send[:, 1024:]


def weights(core, rows, grad_both, hidden):
    n = Y * CAP
    shape = (Z, X, 96, 1024)
    block = pl.BlockSpec((1, X, 96, 1024), lambda i: (i, 0, 0, 0))
    return call(
        weights_body,
        "weights",
        [(shape, bf16), (shape, bf16)],
        (core, rows, rows, grad_both, hidden),
        3 * 2 * n * WIDTH * FF,
        12 << 20,
        grid=(Z,),
        in_specs=[
            scalars(),
            pl.BlockSpec((n, 512), lambda i: (0, i)),
            pl.BlockSpec((n, WIDTH), lambda i: (0, 1)),
            pl.BlockSpec((n, 2 * FF), lambda i: (0, 0)),
            pl.BlockSpec((n, 128), lambda i: (0, i)),
        ],
        out_specs=[block, block],
    )


def fold_core_body(at_ref, keep_ref, recv_ref, *outs):
    z, x = at_ref[0], at_ref[1]
    for s in range(4):
        xs = lax.rem(x + s, X)
        for k in range(Z):
            a = keep_ref[k, xs, :, :512].astype(f32) + recv_ref[k, xs, :, :512].astype(f32)
            outs[s][k] = a.astype(bf16)
        zs = lax.rem(z + s, Z)
        for k in range(X):
            b = keep_ref[zs, k, :, 512:].astype(f32) + recv_ref[zs, k, :, 512:].astype(f32)
            outs[4 + s][k] = b.astype(bf16)


def fold_axis_body(at_ref, a0, a1, a2, a3, b0, b1, b2, b3, *outs):
    z, x = at_ref[0], at_ref[1]
    for s in range(4):
        for refs, at, base in (((a0, a1, a2, a3), lax.rem(z + s, Z), 0), ((b0, b1, b2, b3), lax.rem(x + s, X), 4)):
            total = refs[0][at].astype(f32) + refs[1][at].astype(f32)
            total = total + refs[2][at].astype(f32) + refs[3][at].astype(f32)
            outs[base + s][...] = total.astype(outs[base + s].dtype)


def fold_last_body(a0, a1, a2, a3, b0, b1, b2, b3, up_ref, down_ref):
    for j, refs in enumerate(((a0, a1, a2, a3), (b0, b1, b2, b3))):
        total = refs[0][...] + refs[1][...].astype(f32) + refs[2][...].astype(f32) + refs[3][...].astype(f32)
        at = j * 512
        up_ref[0, :, at : at + 512] = total[:64]
        down_ref[0, :, at : at + 512] = total[64:80]
        down_ref[0, :, 1024 + at : 1024 + at + 512] = total[80:96]


def project_body(own_ref, rest_ref, resid_ref, out_ref):
    s = pl.program_id(0)

    @pl.when(s == 0)
    def _():
        out_ref[0] = dot_t(resid_ref[...], own_ref[...]).astype(bf16)

    @pl.when(s > 0)
    def _():
        out_ref[0] = dot_t(resid_ref[...], rest_ref[...].reshape(512, WIDTH)).astype(bf16)


def state_body(at_ref, g0, g1, g2, g3, q_ref, grad_ref, state_ref):
    y, block = at_ref[0], at_ref[1]
    ramp = lax.broadcasted_iota(jnp.int32, (ROWS, 1), 0)
    sums = [jnp.zeros((HD, 2 * HD), f32) for _ in range(HEADS)]
    for s, g in enumerate((g0, g1, g2, g3)):
        off = pl.multiple_of(lax.rem(y + s, Y) * ROWS, ROWS)
        inverse = 1.0 / (3 * BLOCKS * TOK + block * TOK + off + ramp + 1).astype(f32)
        grad_ref[pl.ds(off, ROWS), :] = g[...]
        for h in range(HEADS):
            cols = slice(h * HD, (h + 1) * HD)
            hi, lo = split(g[:, cols].astype(f32) * inverse)
            both = jnp.concatenate([hi, lo], axis=1)
            sums[h] += t_dot(q_ref[pl.ds(off, ROWS), cols], both)
    for h in range(HEADS):
        state_ref[h * HD : (h + 1) * HD, :] = sums[h][:, :HD] + sums[h][:, HD:]


SUB = 256
PARTS = TOK // SUB


def inverse_row(block, at):
    ramp = lax.broadcasted_iota(jnp.int32, (1, SUB), 1)
    return 1.0 / (3 * BLOCKS * TOK + block * TOK + at + ramp + 1).astype(f32)


def triangle(lower):
    row = lax.broadcasted_iota(jnp.int32, (SUB, SUB), 0)
    col = lax.broadcasted_iota(jnp.int32, (SUB, SUB), 1)
    return (col <= row) if lower else (col >= row)


def part(ref, i):
    return ref[i * SUB : (i + 1) * SUB, :]


def query_body(at_ref, g_ref, v_ref, k_ref, prior_ref, out_ref):
    block = at_ref[1]
    mask = triangle(True)
    hi, lo = split(prior_ref[0])
    ramp = lax.broadcasted_iota(jnp.int32, (SUB, 1), 0)
    for i in range(PARTS):
        g = part(g_ref, i)
        total = dot_t(g, hi) + dot_t(g, lo)
        for j in range(i + 1):
            mix = dot_t(g, part(v_ref, j))
            if j == i:
                mix = jnp.where(mask, mix, 0.0)
            total += dot(mix.astype(bf16), part(k_ref, j))
        count = (3 * BLOCKS * TOK + block * TOK + i * SUB + ramp + 1).astype(f32)
        out_ref[i * SUB : (i + 1) * SUB, :] = (total / count).astype(bf16)


def mix_body(at_ref, a_ref, b_ref, c_ref, out_ref):
    block = at_ref[1]
    mask = triangle(False)
    inverses = [inverse_row(block, j * SUB) for j in range(PARTS)]
    for i in range(PARTS):
        a = part(a_ref, i)
        total = jnp.zeros((SUB, HD), f32)
        for j in range(i, PARTS):
            mix = dot_t(a, part(b_ref, j)) * inverses[j]
            if j == i:
                mix = jnp.where(mask, mix, 0.0)
            total += dot(mix.astype(bf16), part(c_ref, j))
        out_ref[i * SUB : (i + 1) * SUB, :] = total


def head_call(body, name, ins, out_type, prior=None):
    cols = pl.BlockSpec((TOK, HD), lambda h: (0, h))
    specs = [scalars()] + [cols] * 3
    if prior is not None:
        specs.append(pl.BlockSpec((1, HD, HD), lambda h: (h, 0, 0)))
        ins = (*ins, prior)
    return call(
        body,
        name,
        [((TOK, HEADS * HD), out_type)],
        ins,
        10 * HEADS * 4 * SUB * SUB * HD,
        6 << 20,
        grid=(HEADS,),
        in_specs=specs,
        out_specs=[cols],
    )[0]


def final_body(later_ref, v_ref, k_ref, key_ref, value_ref, out_key, out_value):
    for h in range(HEADS):
        cols = slice(h * HD, (h + 1) * HD)
        hi, lo = split(later_ref[h * HD : (h + 1) * HD, :])
        v, k = v_ref[:, cols], k_ref[:, cols]
        out_key[:, cols] = (key_ref[:, cols] + dot_t(v, hi) + dot_t(v, lo)).astype(bf16)
        out_value[:, cols] = (value_ref[:, cols] + dot(k, hi) + dot(k, lo)).astype(bf16)


def index(z, x, c):
    return (z * X + x) * C + c


def spots():
    return [(z, x, c) for z in range(Z) for x in range(X) for c in range(C)]


def along_y(a, s):
    return lax.ppermute(a, "exp", [(i, (i + s) % Y) for i in range(Y)])


def along_x(a, s):
    return lax.ppermute(a, "ctx", [(index(z, x, c), index(z, (x + s) % X, c)) for z, x, c in spots()])


def along_z(a, s):
    return lax.ppermute(a, "ctx", [(index(z, x, c), index((z + s) % Z, x, c)) for z, x, c in spots()])


def across(a):
    return lax.ppermute(a, "ctx", [(i, i ^ 1) for i in range(BLOCKS)])


def on_device(
    attn_query,
    attn_key,
    attn_value,
    prefix_state,
    moe_in,
    grad_out,
    router_gates,
    expert_ids,
    w_gate_up,
    w_down,
    w_out,
):
    y = lax.axis_index("exp")
    block = lax.axis_index("ctx")
    z, x, c = block // (X * C), (block // C) % X, block % C
    at = jnp.stack([y, block]).astype(jnp.int32)
    spot = jnp.stack([z, x]).astype(jnp.int32)
    core = c.astype(jnp.int32)[None]

    slab = w_out.shape[0] // BLOCKS
    piece = lax.dynamic_slice_in_dim(w_out, block * slab, slab, 0)
    pieces = jnp.concatenate([along_y(piece, s) for s in (1, 2, 3)], axis=0)
    rest = lax.all_gather(pieces[None], "ctx", axis=0, tiled=True)
    rest = rest.reshape(BLOCKS, 3, slab, WIDTH)

    place, *chunks = pack(at, expert_ids, router_gates, moe_in, grad_out)
    held = [chunks[0]] + [along_y(chunks[s], s) for s in (1, 2, 3)]
    b0, b1, b2, b3, hidden, grad_both, dots, rows = expert(held, w_gate_up[0], w_down[0])
    back = [b0] + [along_y(b, -s) for s, b in ((1, b1), (2, b2), (3, b3))]
    dots = dots[:, 0].reshape(Y, 1, CAP)
    dots = [dots[0]] + [along_y(dots[s], -s) for s in (1, 2, 3)]

    pair_grads = dot(place, jnp.concatenate(back, axis=0))
    grad_resid = (grad_out.astype(f32) + pair_grads).astype(bf16)
    picked = jnp.sum(place.astype(f32) * jnp.concatenate(dots, axis=1), axis=1, keepdims=True)
    grad_gates = (picked / router_gates.astype(f32)).astype(bf16)

    per_head = call(
        project_body,
        "project",
        [((Y, ROWS, 512), bf16)],
        (w_out, rest, grad_resid),
        2 * ROWS * WIDTH * WIDTH,
        10 << 20,
        grid=(Y,),
        in_specs=[
            pl.BlockSpec((512, WIDTH), lambda s: (0, 0)),
            pl.BlockSpec((BLOCKS, 1, slab, WIDTH), lambda s: (0, jnp.maximum(s - 1, 0), 0, 0)),
            pl.BlockSpec((ROWS, WIDTH), lambda s: (0, 0)),
        ],
        out_specs=[pl.BlockSpec((1, ROWS, 512), lambda s: (s, 0, 0))],
    )[0]
    grads = [per_head[0]] + [along_y(per_head[s], -s) for s in (1, 2, 3)]
    attn_grad, state = call(
        state_body,
        "state",
        [((TOK, HEADS * HD), bf16), ((HEADS * HD, HD), f32)],
        (at, *grads, attn_query),
        HEADS * 2 * TOK * HD * 2 * HD,
        4 << 20,
        in_specs=[scalars()] + [full()] * 5,
    )

    keep, send = weights(core, rows, grad_both, hidden)
    outs = [((Z, 96, 512), bf16)] * 8
    ins = (spot, keep, across(send))
    specs = [scalars()] + [full()] * 2
    half = call(fold_core_body, "fold_core", outs, ins, 0, 9 << 20, in_specs=specs)
    ins = (spot, half[0], *(along_x(half[s], s) for s in (1, 2, 3)))
    ins = (*ins, half[4], *(along_z(half[4 + s], s) for s in (1, 2, 3)))
    outs = ([((96, 512), f32)] + [((96, 512), bf16)] * 3) * 2
    specs = [scalars()] + [full()] * 8
    half = call(fold_axis_body, "fold_axis", outs, ins, 0, 4 << 20, in_specs=specs)
    ins = (half[0], *(along_z(half[s], s) for s in (1, 2, 3)))
    ins = (*ins, half[4], *(along_x(half[4 + s], s) for s in (1, 2, 3)))
    outs = [((1, 64, 1024), f32), ((1, 16, WIDTH), f32)]
    grad_gate_up, grad_down = call(fold_last_body, "fold_last", outs, ins, 0, 2 << 20)

    other = across(state)
    chip = state + other
    chip16 = chip.astype(bf16)
    from_x = [along_x(chip16, s).astype(f32) for s in (1, 2, 3)]
    line = chip + from_x[0] + from_x[1] + from_x[2]
    line16 = line.astype(bf16)
    from_z = [along_z(line16, s).astype(f32) for s in (1, 2, 3)]
    later = jnp.where(c == 0, other, 0.0)
    for s in (1, 2, 3):
        later += jnp.where(s > x, from_x[s - 1], 0.0) + jnp.where(s > z, from_z[s - 1], 0.0)

    grad_query = head_call(query_body, "grad_query", (at, attn_grad, attn_value, attn_key), bf16, prefix_state[0])
    key_here = head_call(mix_body, "mix_key", (at, attn_value, attn_grad, attn_query), f32)
    value_here = head_call(mix_body, "mix_value", (at, attn_key, attn_query, attn_grad), f32)
    shape = (TOK, HEADS * HD)
    grad_key, grad_value = call(
        final_body,
        "final",
        [(shape, bf16), (shape, bf16)],
        (later, attn_value, attn_key, key_here, value_here),
        HEADS * 8 * TOK * HD * HD,
        8 << 20,
    )
    return (grad_query, grad_key, grad_value, grad_resid, grad_gates, grad_gate_up, grad_down)


def solution(mesh):
    whole = P(("ctx", "exp"), None)
    split_cols = P("ctx", "exp")
    return jax.shard_map(
        on_device,
        mesh=mesh,
        in_specs=(
            split_cols,
            split_cols,
            split_cols,
            P("ctx", "exp", None, None),
            whole,
            whole,
            whole,
            whole,
            P("exp", None, None),
            P("exp", None, None),
            P("exp", None),
        ),
        out_specs=(
            split_cols,
            split_cols,
            split_cols,
            whole,
            whole,
            P("exp", "ctx", None),
            P("exp", "ctx", None),
        ),
        check_vma=False,
    )
```

time: 311 us -> 221 us (0.71)
  matrix products: 73.6 us -> 1.82 us
  Pallas kernels: 0 us -> 58.8 us
  blocking collectives: 43.2 us -> 0 us
  starting transfers between devices: 8.13 us -> 50.3 us
  waiting for transfers between devices: 108 us -> 76 us
  local copies, waits for them, and re-layouts: 37.5 us -> 13.6 us
  other arithmetic: 22.9 us -> 5.39 us
    all_gather x2 -> x1, waiting for transfers between devices: 82.7 us -> 0.01 us  [on_device(): rest = lax.all_gather(pieces[None], 'ctx', axis=0, tiled=True)]
    ppermute x0 -> x35, waiting for transfers between devices: none -> 76 us  [the longest x15 63.1 us: along_y(): return lax.ppermute(a, 'exp', [(i, (i + s) % Y) for i in range(Y)])]
    dot_general x19 -> x1, matrix products: 73.6 us -> 1.82 us  [dot(): lax.dot_general(a, b, (((1,), (0,)), ((), ())), preferred_element_type=f32)]
    pallas_call x0 -> x12, Pallas kernels: none -> 58.8 us  [call(): pl.pallas_call(body, name=name, out_shape=[jax.ShapeDtypeStruct(s, t) for...]
    ppermute x0 -> x35, starting transfers between devices: none -> 50.3 us  [the longest x15 20.4 us: along_y(): return lax.ppermute(a, 'exp', [(i, (i + s) % Y) for i in range(Y)])]
    all_to_all x1 -> x0, blocking collectives: 43.2 us -> none  [in_one_piece(): lax.all_to_all(both, axis, split_axis=split_dim, concat_axis=concat_dim,...]
    reduce_scatter x1 -> x0, waiting for transfers between devices: 19.6 us -> none  [one_scatter(): lax.psum_scatter(lines, axis, tiled=True).reshape(-1)]
    another operation x5 -> x0, local copies, waits for them, and re-layouts: 12.7 us -> none  [the longest x2 12.5 us: one_scatter(): lines = jnp.concatenate([b.reshape(length, -1) for b in pieces], axis=1)]
  transfers between devices with their start and end apart: 5 -> 36, of which waited for: 4 -> 11; matrix products, arithmetic and copies ran while one was open for 30% -> 4% of each run, Pallas kernels for 0% -> 25%
where the time goes in v1:
time: 221 us; the launch traced here: 220 us
  waiting for transfers between devices  76 us (34%)
  Pallas kernels  58.8 us (27%)
  starting transfers between devices  50.3 us (23%)
  between operations  14.3 us (6%)
  local copies, waits for them, and re-layouts  13.6 us (6%)
  other arithmetic  5.39 us (2%)
    ppermute x15, waiting for transfers between devices, along_y(): return lax.ppermute(a, 'exp', [(i, (i + s) % Y) for i in range(Y)])  63.1 us
    pallas_call x12, Pallas kernels, call(): pl.pallas_call(body, name=name, out_shape=[jax.ShapeDtypeStruct(s, t) for...  58.8 us
    ppermute x15, starting transfers between devices, along_y(): return lax.ppermute(a, 'exp', [(i, (i + s) % Y) for i in range(Y)])  20.4 us
    ppermute x9, starting transfers between devices, along_z(): lax.ppermute(a, 'ctx', [(index(z, x, c), index((z + s) % Z, x, c)) for z,...  15.4 us
    ppermute x9, starting transfers between devices, along_x(): lax.ppermute(a, 'ctx', [(index(z, x, c), index(z, (x + s) % X, c)) for z,...  14.5 us
    unnamed x48, local copies, waits for them, and re-layouts  12 us
    ppermute x9, waiting for transfers between devices, along_z(): lax.ppermute(a, 'ctx', [(index(z, x, c), index((z + s) % Z, x, c)) for z,...  6.5 us
    ppermute x9, waiting for transfers between devices, along_x(): lax.ppermute(a, 'ctx', [(index(z, x, c), index(z, (x + s) % X, c)) for z,...  6.46 us
  transfers between devices with their start and end apart: 36, of which 11 were waited for; matrix products, arithmetic and copies ran while one was open for 4% of the time, Pallas kernels for 25%

profile of v1, /device:TPU:0, one launch (start us, length us, event | category | flops | bytes accessed | tf_op | source)
XLA Modules:
  0.0 220.2 jit_solution(4546083124381925388)
XLA Ops:
  9.7 2.9 %collective-permute-start.1 = (bf16[16,2048]{1,0:T(8,128)(2,1)S(1)}, bf16[16,2048]{1,0:T(8,128)(2,1)S(1)}, u32[]{:S(2)}, u32[]{:S(2)}) collective-permute-start(bf16[16,2048]{1,0:T(8,128)(2,1)S(1)} %constant_dynamic-slice_fusion), channel_id=1, source_target_pairs={{0,2},{1,3},{2,0},{3,1},{4,6},{5,7},{6,4},{7,5},{8,10},{9,11},{10,... | collective-permute-start | bytes 196616 | tf_op jit(solution)/shard_map/ppermute | solution.py:320
  21.8 3.1 %pack.1 = (bf16[256,384]{1,0:T(8,128)(2,1)S(1)}, bf16[96,4096]{1,0:T(8,128)(2,1)S(1)}, bf16[96,4096]{1,0:T(8,128)(2,1)}, bf16[96,4096]{1,0:T(8,128)(2,1)}, bf16[96,4096]{1,0:T(8,128)(2,1)S(1)}) custom-call(s32[2]{0:T(128)S(1)} %pad_add_fusion.at_ref, s32[256,1]{1,0:T(8,128)S(1)} %copy.20.ids_ref, bf16[256,1]{1,0:T(8,128)(2,1)S(1)} %copy.21.gate_ref, ...), custom_call_target="tpu_custom_call" | custom-call | flops 805306368 | bytes 5242880 | tf_op jit(solution)/shard_map/pack/pallas_call | solution.py:47
  26.0 3.8 %collective-permute-start.4 = (bf16[96,4096]{1,0:T(8,128)(2,1)}, bf16[96,4096]{1,0:T(8,128)(2,1)S(1)}, u32[]{:S(2)}, u32[]{:S(2)}) collective-permute-start(bf16[96,4096]{1,0:T(8,128)(2,1)} %get-tuple-element.47), channel_id=1, source_target_pairs={{0,2},{1,3},{2,0},{3,1},{4,6},{5,7},{6,4},{7,5},{8,10},{9,11},{10,... | collective-permute-start | bytes 2359304 | tf_op jit(solution)/shard_map/ppermute | solution.py:320
  29.9 17.5 %collective-permute-done.3.r1 = bf16[96,4096]{1,0:T(8,128)(2,1)S(1)} collective-permute-done((bf16[96,4096]{1,0:T(8,128)(2,1)}, bf16[96,4096]{1,0:T(8,128)(2,1)S(1)}, u32[]{:S(2)}, u32[]{:S(2)}) %collective-permute-start.3) | collective-permute-done | bytes 786464 | tf_op jit(solution)/shard_map/ppermute | solution.py:320
  47.4 15.0 %collective-permute-done.4.r2 = bf16[96,4096]{1,0:T(8,128)(2,1)S(1)} collective-permute-done((bf16[96,4096]{1,0:T(8,128)(2,1)}, bf16[96,4096]{1,0:T(8,128)(2,1)S(1)}, u32[]{:S(2)}, u32[]{:S(2)}) %collective-permute-start.4) | collective-permute-done | bytes 786464 | tf_op jit(solution)/shard_map/ppermute | solution.py:320
  63.6 9.1 %expert.1 = (bf16[96,2048]{1,0:T(8,128)(2,1)S(1)}, bf16[96,2048]{1,0:T(8,128)(2,1)}, bf16[96,2048]{1,0:T(8,128)(2,1)S(1)}, bf16[96,2048]{1,0:T(8,128)(2,1)S(1)},...) custom-call(bf16[96,4096]{1,0:T(8,128)(2,1)S(1)} %copy-done.17, ...), custom_call_target="tpu_custom_call" | custom-call | flops 4026531840 | bytes 14680064 | tf_op jit(solution)/shard_map/expert/pallas_call | solution.py:47
  73.5 7.0 %weights.1 = (bf16[4,4,96,1024]{3,2,1,0:T(8,128)(2,1)S(1)}, bf16[4,4,96,1024]{3,2,1,0:T(8,128)(2,1)}) custom-call(s32[1]{0:T(128)} %bitcast.13.core_ref, bf16[384,4096]{1,0:T(8,128)(2,1)} %get-tuple-element.58.rows_ref.scaled_ref, bf16[384,4096]{1,0:T(8,128)(2,1)} %get-tuple-element.58.rows_ref.scaled_ref, bf16[384,1024]{1,0:T(8,128)(2,1)S(1)} %get-tuple-element.59.gb_ref, ...), custom_call_target="tpu_custom_call" | custom-call | flops 2415919104 | bytes 12582912 | tf_op jit(solution)/shard_map/weights/pallas_call | solution.py:47
  82.2 2.7 %collective-permute-start.6 = (bf16[96,2048]{1,0:T(8,128)(2,1)}, bf16[96,2048]{1,0:T(8,128)(2,1)S(1)}, u32[]{:S(2)}, u32[]{:S(2)}) collective-permute-start(bf16[96,2048]{1,0:T(8,128)(2,1)} %get-tuple-element.50), channel_id=1, source_target_pairs={{0,3},{1,0},{2,1},{3,2},{4,7},{5,4},{6,5},{7,6},{8,11},{9,8},{10,9... | collective-permute-start | bytes 1179656 | tf_op jit(solution)/shard_map/ppermute | solution.py:320
  86.5 2.7 %collective-permute-start.19 = (f32[1,96]{1,0:T(1,128)}, f32[1,96]{1,0:T(1,128)}, u32[]{:S(2)}, u32[]{:S(2)}) collective-permute-start(f32[1,96]{1,0:T(1,128)} %bitcast.15), channel_id=1, source_target_pairs={{0,3},{1,0},{2,1},{3,2},{4,7},{5,4},{6,5},{7,6},{8,11},{9,8},{10,9... | collective-permute-start | bytes 1160 | tf_op jit(solution)/shard_map/ppermute | solution.py:320
  89.2 13.4 %collective-permute-done.6 = bf16[96,2048]{1,0:T(8,128)(2,1)S(1)} collective-permute-done((bf16[96,2048]{1,0:T(8,128)(2,1)}, bf16[96,2048]{1,0:T(8,128)(2,1)S(1)}, u32[]{:S(2)}, u32[]{:S(2)}) %collective-permute-start.6) | collective-permute-done | bytes 393248 | tf_op jit(solution)/shard_map/ppermute | solution.py:320
  102.7 3.2 %collective-permute-done.8 = bf16[96,2048]{1,0:T(8,128)(2,1)} collective-permute-done((bf16[96,2048]{1,0:T(8,128)(2,1)S(1)}, bf16[96,2048]{1,0:T(8,128)(2,1)}, u32[]{:S(2)}, u32[]{:S(2)}) %collective-permute-start.8) | collective-permute-done | bytes 393248 | tf_op jit(solution)/shard_map/ppermute | solution.py:320
  107.8 4.9 %fold_core.1 = (bf16[4,96,512]{2,1,0:T(8,128)(2,1)S(1)}, bf16[4,96,512]{2,1,0:T(8,128)(2,1)}, bf16[4,96,512]{2,1,0:T(8,128)(2,1)S(1)}, bf16[4,96,512]{2,1,0:T(8,...) custom-call(s32[2]{0:T(128)S(1)} %pad_add_fusion.1.at_ref, ...), custom_call_target="tpu_custom_call" | custom-call | bytes 9437184 | tf_op jit(solution)/shard_map/fold_core/pallas_call | solution.py:47
  115.7 5.6 %project.1 = bf16[4,256,512]{2,1,0:T(8,128)(2,1)S(1)} custom-call(bf16[512,2048]{1,0:T(8,128)(2,1)S(1)} %copy-done.5, bf16[32,3,16,2048]{3,2,1,0:T(8,128)(2,1)} %bitcast.24, bf16[256,2048]{1,0:T(8,128)(2,1)S(1)} %fusion.resid_ref), custom_call_target="tpu_custom_call" | custom-call | flops 2147483648 | bytes 10485760 | tf_op jit(solution)/shard_map/project/pallas_call | solution.py:47
  125.4 10.9 %collective-permute-done.21 = f32[1,96]{1,0:T(1,128)S(1)} collective-permute-done((f32[1,96]{1,0:T(1,128)S(1)}, f32[1,96]{1,0:T(1,128)S(1)}, u32[]{:S(2)}, u32[]{:S(2)}) %collective-permute-start.21) | collective-permute-done | bytes 416 | tf_op jit(solution)/shard_map/ppermute | solution.py:320
  136.8 2.7 %collective-permute-start.24 = (bf16[4,96,512]{2,1,0:T(8,128)(2,1)S(1)}, bf16[4,96,512]{2,1,0:T(8,128)(2,1)S(1)}, u32[]{:S(2)}, u32[]{:S(2)}) collective-permute-start(bf16[4,96,512]{2,1,0:T(8,128)(2,1)S(1)} %copy-done.14), channel_id=1, source_target_pairs={{0,16},{4,20},{8,24},{12,28},{16,0},{20,4},{24,8},{28,12},{32,48},... | collective-permute-start | bytes 1179656 | tf_op jit(solution)/shard_map/ppermute | solution.py:324
  143.0 3.4 %collective-permute-start.27 = (bf16[4,96,512]{2,1,0:T(8,128)(2,1)}, bf16[4,96,512]{2,1,0:T(8,128)(2,1)}, u32[]{:S(2)}, u32[]{:S(2)}) collective-permute-start(bf16[4,96,512]{2,1,0:T(8,128)(2,1)} %get-tuple-element.69), channel_id=1, source_target_pairs={{0,64},{4,68},{8,72},{12,76},{16,80},{20,84},{24,88},{28,92},{32,9... | collective-permute-start | bytes 1179656 | tf_op jit(solution)/shard_map/ppermute | solution.py:328
  151.1 6.0 %collective-permute-done.25.a3 = bf16[4,96,512]{2,1,0:T(8,128)(2,1)} collective-permute-done((bf16[4,96,512]{2,1,0:T(8,128)(2,1)}, bf16[4,96,512]{2,1,0:T(8,128)(2,1)}, u32[]{:S(2)}, u32[]{:S(2)}) %collective-permute-start.25) | collective-permute-done | bytes 393248 | tf_op jit(solution)/shard_map/ppermute | solution.py:324
  157.1 6.5 %collective-permute-done.27.b2 = bf16[4,96,512]{2,1,0:T(8,128)(2,1)} collective-permute-done((bf16[4,96,512]{2,1,0:T(8,128)(2,1)}, bf16[4,96,512]{2,1,0:T(8,128)(2,1)}, u32[]{:S(2)}, u32[]{:S(2)}) %collective-permute-start.27) | collective-permute-done | bytes 393248 | tf_op jit(solution)/shard_map/ppermute | solution.py:328
  166.8 2.4 %collective-permute-start.30 = (bf16[96,512]{1,0:T(8,128)(2,1)S(1)}, bf16[96,512]{1,0:T(8,128)(2,1)S(1)}, u32[]{:S(2)}, u32[]{:S(2)}) collective-permute-start(bf16[96,512]{1,0:T(8,128)(2,1)S(1)} %get-tuple-element.73), channel_id=1, source_target_pairs={{0,64},{4,68},{8,72},{12,76},{16,80},{20,84},{24,88},{28,92},{32,9... | collective-permute-start | bytes 294920 | tf_op jit(solution)/shard_map/ppermute | solution.py:328
  177.8 2.5 %collective-permute-start.15 = (bf16[512,128]{1,0:T(8,128)(2,1)S(1)}, bf16[512,128]{1,0:T(8,128)(2,1)S(1)}, u32[]{:S(2)}, u32[]{:S(2)}) collective-permute-start(bf16[512,128]{1,0:T(8,128)(2,1)S(1)} %get-tuple-element.85), channel_id=1, source_target_pairs={{0,24},{4,28},{8,0},{12,4},{16,8},{20,12},{24,16},{28,20},{32,56},... | collective-permute-start | bytes 393224 | tf_op jit(solution)/shard_map/ppermute | solution.py:324
  181.8 6.8 %mix_key.1.key_ref = f32[1024,512]{1,0:T(8,128)S(1)} custom-call(s32[2]{0:T(128)S(1)} %pad_add_fusion.at_ref, bf16[1024,512]{1,0:T(8,128)(2,1)S(1)} %copy-done.2, bf16[1024,512]{1,0:T(8,128)(2,1)S(1)} %get-tuple-element.53.g_ref.b_ref.c_ref, bf16[1024,512]{1,0:T(8,128)(2,1)S(1)} %copy-done), custom_call_target="tpu_custom_call" | custom-call | flops 1342177280 | bytes 6291456 | tf_op jit(solution)/shard_map/mix_key/pallas_call | solution.py:47
  192.7 6.8 %mix_value.1.value_ref = f32[1024,512]{1,0:T(8,128)S(1)} custom-call(s32[2]{0:T(128)S(1)} %pad_add_fusion.at_ref, bf16[1024,512]{1,0:T(8,128)(2,1)S(1)} %copy-done.3, bf16[1024,512]{1,0:T(8,128)(2,1)S(1)} %copy-done, bf16[1024,512]{1,0:T(8,128)(2,1)S(1)} %get-tuple-element.53.g_ref.b_ref.c_ref), custom_call_target="tpu_custom_call" | custom-call | flops 1342177280 | bytes 6291456 | tf_op jit(solution)/shard_map/mix_value/pallas_call | solution.py:47
  200.8 7.1 %grad_query.1 = bf16[1024,512]{1,0:T(8,128)(2,1)} custom-call(s32[2]{0:T(128)S(1)} %pad_add_fusion.at_ref, bf16[1024,512]{1,0:T(8,128)(2,1)S(1)} %get-tuple-element.53.g_ref.b_ref.c_ref, bf16[1024,512]{1,0:T(8,128)(2,1)S(1)} %copy-done.2, bf16[1024,512]{1,0:T(8,128)(2,1)S(1)} %copy-done.3, f32[4,128,128]{2,1,0:T(8,128)S(1)} %bitcast.23), custom_call_target="tpu_custom_call" | custom-call | flops 1342177280 | bytes 6291456 | tf_op jit(solution)/shard_map/grad_query/pallas_call | solution.py:47
  209.1 4.3 %final.1 = (bf16[1024,512]{1,0:T(8,128)(2,1)}, bf16[1024,512]{1,0:T(8,128)(2,1)}) custom-call(f32[512,128]{1,0:T(8,128)S(1)} %fusion.11.later_ref, bf16[1024,512]{1,0:T(8,128)(2,1)S(1)} %copy-done.2, bf16[1024,512]{1,0:T(8,128)(2,1)S(1)} %copy-done.3, f32[1024,512]{1,0:T(8,128)S(1)} %mix_key.1.key_ref, f32[1024,512]{1,0:T(8,128)} %copy-done.1), custom_call_target="tpu_custom_call" | custom-call | flops 536870912 | bytes 8388608 | tf_op jit(solution)/shard_map/final/pallas_call | solution.py:47
  (122 shorter events, 55.6 us)
Async XLA Ops:
  7.2 108.5 %all-gather.3.cloned.1.call-start = ((), (), s32[]{:S(2)}) async-start(), calls=%async_computation | async-start | bytes 6488064 | tf_op jit(solution)/shard_map/all_gather | solution.py:358
  25.7 21.7 %collective-permute-start.3 = (bf16[96,4096]{1,0:T(8,128)(2,1)}, bf16[96,4096]{1,0:T(8,128)(2,1)S(1)}, u32[]{:S(2)}, u32[]{:S(2)}) collective-permute-start(bf16[96,4096]{1,0:T(8,128)(2,1)} %get-tuple-element.46), channel_id=1, source_target_pairs={{0,1},{1,2},{2,3},{3,0},{4,5},{5,6},{6,7},{7,4},{8,9},{9,10},{10,1... | collective-permute-start | bytes 2359304 | tf_op jit(solution)/shard_map/ppermute | solution.py:320
  26.0 36.4 %collective-permute-start.4 = (bf16[96,4096]{1,0:T(8,128)(2,1)}, bf16[96,4096]{1,0:T(8,128)(2,1)S(1)}, u32[]{:S(2)}, u32[]{:S(2)}) collective-permute-start(bf16[96,4096]{1,0:T(8,128)(2,1)} %get-tuple-element.47), channel_id=1, source_target_pairs={{0,2},{1,3},{2,0},{3,1},{4,6},{5,7},{6,4},{7,5},{8,10},{9,11},{10,... | collective-permute-start | bytes 2359304 | tf_op jit(solution)/shard_map/ppermute | solution.py:320
  29.7 32.7 %collective-permute-start.5 = (bf16[96,4096]{1,0:T(8,128)(2,1)S(1)}, bf16[96,4096]{1,0:T(8,128)(2,1)S(1)}, u32[]{:S(2)}, u32[]{:S(2)}) collective-permute-start(bf16[96,4096]{1,0:T(8,128)(2,1)S(1)} %get-tuple-element.48), channel_id=1, source_target_pairs={{0,3},{1,0},{2,1},{3,2},{4,7},{5,4},{6,5},{7,6},{8,11},{9,8},{10,9... | collective-permute-start | bytes 2359304 | tf_op jit(solution)/shard_map/ppermute | solution.py:320
  82.2 25.6 %collective-permute-start.22 = (bf16[4,4,96,1024]{3,2,1,0:T(8,128)(2,1)}, bf16[4,4,96,1024]{3,2,1,0:T(8,128)(2,1)}, u32[]{:S(2)}, u32[]{:S(2)}) collective-permute-start(bf16[4,4,96,1024]{3,2,1,0:T(8,128)(2,1)} %get-tuple-element.62), channel_id=1, source_target_pairs={{0,4},{4,0},{8,12},{12,8},{16,20},{20,16},{24,28},{28,24},{32,36},... | collective-permute-start | bytes 9437192 | tf_op jit(solution)/shard_map/ppermute | solution.py:332
  82.2 20.5 %collective-permute-start.6 = (bf16[96,2048]{1,0:T(8,128)(2,1)}, bf16[96,2048]{1,0:T(8,128)(2,1)S(1)}, u32[]{:S(2)}, u32[]{:S(2)}) collective-permute-start(bf16[96,2048]{1,0:T(8,128)(2,1)} %get-tuple-element.50), channel_id=1, source_target_pairs={{0,3},{1,0},{2,1},{3,2},{4,7},{5,4},{6,5},{7,6},{8,11},{9,8},{10,9... | collective-permute-start | bytes 1179656 | tf_op jit(solution)/shard_map/ppermute | solution.py:320
  84.9 17.8 %collective-permute-start.7 = (bf16[96,2048]{1,0:T(8,128)(2,1)S(1)}, bf16[96,2048]{1,0:T(8,128)(2,1)}, u32[]{:S(2)}, u32[]{:S(2)}) collective-permute-start(bf16[96,2048]{1,0:T(8,128)(2,1)S(1)} %get-tuple-element.51), channel_id=1, source_target_pairs={{0,2},{1,3},{2,0},{3,1},{4,6},{5,7},{6,4},{7,5},{8,10},{9,11},{10,... | collective-permute-start | bytes 1179656 | tf_op jit(solution)/shard_map/ppermute | solution.py:320
  85.2 20.7 %collective-permute-start.8 = (bf16[96,2048]{1,0:T(8,128)(2,1)S(1)}, bf16[96,2048]{1,0:T(8,128)(2,1)}, u32[]{:S(2)}, u32[]{:S(2)}) collective-permute-start(bf16[96,2048]{1,0:T(8,128)(2,1)S(1)} %get-tuple-element.52), channel_id=1, source_target_pairs={{0,1},{1,2},{2,3},{3,0},{4,5},{5,6},{6,7},{7,4},{8,9},{9,10},{10,1... | collective-permute-start | bytes 1179656 | tf_op jit(solution)/shard_map/ppermute | solution.py:320
  86.5 36.7 %collective-permute-start.19 = (f32[1,96]{1,0:T(1,128)}, f32[1,96]{1,0:T(1,128)}, u32[]{:S(2)}, u32[]{:S(2)}) collective-permute-start(f32[1,96]{1,0:T(1,128)} %bitcast.15), channel_id=1, source_target_pairs={{0,3},{1,0},{2,1},{3,2},{4,7},{5,4},{6,5},{7,6},{8,11},{9,8},{10,9... | collective-permute-start | bytes 1160 | tf_op jit(solution)/shard_map/ppermute | solution.py:320
  102.6 22.8 %collective-permute-start.20 = (f32[1,96]{1,0:T(1,128)}, f32[1,96]{1,0:T(1,128)}, u32[]{:S(2)}, u32[]{:S(2)}) collective-permute-start(f32[1,96]{1,0:T(1,128)} %bitcast.16), channel_id=1, source_target_pairs={{0,2},{1,3},{2,0},{3,1},{4,6},{5,7},{6,4},{7,5},{8,10},{9,11},{10,... | collective-permute-start | bytes 1160 | tf_op jit(solution)/shard_map/ppermute | solution.py:320
  114.2 25.4 %collective-permute-start.23 = (bf16[4,96,512]{2,1,0:T(8,128)(2,1)}, bf16[4,96,512]{2,1,0:T(8,128)(2,1)}, u32[]{:S(2)}, u32[]{:S(2)}) collective-permute-start(bf16[4,96,512]{2,1,0:T(8,128)(2,1)} %get-tuple-element.64), channel_id=1, source_target_pairs={{0,8},{4,12},{8,16},{12,20},{16,24},{20,28},{24,0},{28,4},{32,40},... | collective-permute-start | bytes 1179656 | tf_op jit(solution)/shard_map/ppermute | solution.py:324
  121.4 19.6 %collective-permute-start.10 = (bf16[256,512]{1,0:T(8,128)(2,1)S(1)}, bf16[256,512]{1,0:T(8,128)(2,1)S(1)}, u32[]{:S(2)}, u32[]{:S(2)}) collective-permute-start(bf16[256,512]{1,0:T(8,128)(2,1)S(1)} %get-tuple-element.88), channel_id=1, source_target_pairs={{0,2},{1,3},{2,0},{3,1},{4,6},{5,7},{6,4},{7,5},{8,10},{9,11},{10,... | collective-permute-start | bytes 786440 | tf_op jit(solution)/shard_map/ppermute | solution.py:320
  122.1 20.9 %collective-permute-start.11 = (bf16[256,512]{1,0:T(8,128)(2,1)S(1)}, bf16[256,512]{1,0:T(8,128)(2,1)S(1)}, u32[]{:S(2)}, u32[]{:S(2)}) collective-permute-start(bf16[256,512]{1,0:T(8,128)(2,1)S(1)} %get-tuple-element.87), channel_id=1, source_target_pairs={{0,1},{1,2},{2,3},{3,0},{4,5},{5,6},{6,7},{7,4},{8,9},{9,10},{10,1... | collective-permute-start | bytes 786440 | tf_op jit(solution)/shard_map/ppermute | solution.py:320
  123.2 23.2 %collective-permute-start.9 = (bf16[256,512]{1,0:T(8,128)(2,1)S(1)}, bf16[256,512]{1,0:T(8,128)(2,1)S(1)}, u32[]{:S(2)}, u32[]{:S(2)}) collective-permute-start(bf16[256,512]{1,0:T(8,128)(2,1)S(1)} %get-tuple-element.89), channel_id=1, source_target_pairs={{0,3},{1,0},{2,1},{3,2},{4,7},{5,4},{6,5},{7,6},{8,11},{9,8},{10,9... | collective-permute-start | bytes 786440 | tf_op jit(solution)/shard_map/ppermute | solution.py:320
  139.6 17.5 %collective-permute-start.25 = (bf16[4,96,512]{2,1,0:T(8,128)(2,1)}, bf16[4,96,512]{2,1,0:T(8,128)(2,1)}, u32[]{:S(2)}, u32[]{:S(2)}) collective-permute-start(bf16[4,96,512]{2,1,0:T(8,128)(2,1)} %get-tuple-element.66), channel_id=1, source_target_pairs={{0,24},{4,28},{8,0},{12,4},{16,8},{20,12},{24,16},{28,20},{32,56},... | collective-permute-start | bytes 1179656 | tf_op jit(solution)/shard_map/ppermute | solution.py:324
  141.0 16.1 %collective-permute-start.26 = (bf16[4,96,512]{2,1,0:T(8,128)(2,1)}, bf16[4,96,512]{2,1,0:T(8,128)(2,1)}, u32[]{:S(2)}, u32[]{:S(2)}) collective-permute-start(bf16[4,96,512]{2,1,0:T(8,128)(2,1)} %get-tuple-element.68), channel_id=1, source_target_pairs={{0,32},{4,36},{8,40},{12,44},{16,48},{20,52},{24,56},{28,60},{32,6... | collective-permute-start | bytes 1179656 | tf_op jit(solution)/shard_map/ppermute | solution.py:328
  143.0 20.6 %collective-permute-start.27 = (bf16[4,96,512]{2,1,0:T(8,128)(2,1)}, bf16[4,96,512]{2,1,0:T(8,128)(2,1)}, u32[]{:S(2)}, u32[]{:S(2)}) collective-permute-start(bf16[4,96,512]{2,1,0:T(8,128)(2,1)} %get-tuple-element.69), channel_id=1, source_target_pairs={{0,64},{4,68},{8,72},{12,76},{16,80},{20,84},{24,88},{28,92},{32,9... | collective-permute-start | bytes 1179656 | tf_op jit(solution)/shard_map/ppermute | solution.py:328
  146.4 17.1 %collective-permute-start.28 = (bf16[4,96,512]{2,1,0:T(8,128)(2,1)}, bf16[4,96,512]{2,1,0:T(8,128)(2,1)}, u32[]{:S(2)}, u32[]{:S(2)}) collective-permute-start(bf16[4,96,512]{2,1,0:T(8,128)(2,1)} %get-tuple-element.70), channel_id=1, source_target_pairs={{0,96},{4,100},{8,104},{12,108},{16,112},{20,116},{24,120},{28,124... | collective-permute-start | bytes 1179656 | tf_op jit(solution)/shard_map/ppermute | solution.py:328
  149.3 21.8 %collective-permute-start.12 = (f32[512,128]{1,0:T(8,128)S(1)}, f32[512,128]{1,0:T(8,128)}, u32[]{:S(2)}, u32[]{:S(2)}) collective-permute-start(f32[512,128]{1,0:T(8,128)S(1)} %get-tuple-element.54), channel_id=1, source_target_pairs={{0,4},{4,0},{8,12},{12,8},{16,20},{20,16},{24,28},{28,24},{32,36},... | collective-permute-start | bytes 786440 | tf_op jit(solution)/shard_map/ppermute | solution.py:332
  174.8 13.8 %collective-permute-start.13 = (bf16[512,128]{1,0:T(8,128)(2,1)S(1)}, bf16[512,128]{1,0:T(8,128)(2,1)S(1)}, u32[]{:S(2)}, u32[]{:S(2)}) collective-permute-start(bf16[512,128]{1,0:T(8,128)(2,1)S(1)} %get-tuple-element.85), channel_id=1, source_target_pairs={{0,8},{4,12},{8,16},{12,20},{16,24},{20,28},{24,0},{28,4},{32,40},... | collective-permute-start | bytes 393224 | tf_op jit(solution)/shard_map/ppermute | solution.py:324
  175.8 12.8 %collective-permute-start.14 = (bf16[512,128]{1,0:T(8,128)(2,1)S(1)}, bf16[512,128]{1,0:T(8,128)(2,1)S(1)}, u32[]{:S(2)}, u32[]{:S(2)}) collective-permute-start(bf16[512,128]{1,0:T(8,128)(2,1)S(1)} %get-tuple-element.85), channel_id=1, source_target_pairs={{0,16},{4,20},{8,24},{12,28},{16,0},{20,4},{24,8},{28,12},{32,48},... | collective-permute-start | bytes 393224 | tf_op jit(solution)/shard_map/ppermute | solution.py:324
  188.7 19.2 %collective-permute-start.16 = (bf16[512,128]{1,0:T(8,128)(2,1)S(1)}, bf16[512,128]{1,0:T(8,128)(2,1)S(1)}, u32[]{:S(2)}, u32[]{:S(2)}) collective-permute-start(bf16[512,128]{1,0:T(8,128)(2,1)S(1)} %fusion.13), channel_id=1, source_target_pairs={{0,32},{4,36},{8,40},{12,44},{16,48},{20,52},{24,56},{28,60},{32,6... | collective-permute-start | bytes 393224 | tf_op jit(solution)/shard_map/ppermute | solution.py:328
  189.5 18.4 %collective-permute-start.17 = (bf16[512,128]{1,0:T(8,128)(2,1)S(1)}, bf16[512,128]{1,0:T(8,128)(2,1)S(1)}, u32[]{:S(2)}, u32[]{:S(2)}) collective-permute-start(bf16[512,128]{1,0:T(8,128)(2,1)S(1)} %fusion.13), channel_id=1, source_target_pairs={{0,64},{4,68},{8,72},{12,76},{16,80},{20,84},{24,88},{28,92},{32,9... | collective-permute-start | bytes 393224 | tf_op jit(solution)/shard_map/ppermute | solution.py:328
  190.7 17.3 %collective-permute-start.18 = (bf16[512,128]{1,0:T(8,128)(2,1)S(1)}, bf16[512,128]{1,0:T(8,128)(2,1)S(1)}, u32[]{:S(2)}, u32[]{:S(2)}) collective-permute-start(bf16[512,128]{1,0:T(8,128)(2,1)S(1)} %fusion.13), channel_id=1, source_target_pairs={{0,96},{4,100},{8,104},{12,108},{16,112},{20,116},{24,120},{28,124... | collective-permute-start | bytes 393224 | tf_op jit(solution)/shard_map/ppermute | solution.py:328
  (35 other events, 436.7 us)
Sparse Core Ops, SparseCore 0:
  17.7 50.9 all-gather.2

commit v2 on v1

v2 whole, which is shorter than its diff:
```python
import jax
import jax.numpy as jnp
from jax import lax
from jax.experimental import pallas as pl
from jax.experimental.pallas import tpu as pltpu
from jax.sharding import PartitionSpec as P

bf16 = jnp.bfloat16
f32 = jnp.float32
VMEM = pltpu.VMEM
SMEM = pltpu.SMEM
Z, X, C, Y = 4, 4, 2, 4
CAP, ROWS, WIDTH, FF, HD, HEADS, TOK = 96, 256, 2048, 512, 128, 4, 1024
BLOCKS = Z * X * C


def dot(a, b):
    return lax.dot_general(a, b, (((1,), (0,)), ((), ())), preferred_element_type=f32)


def dot_t(a, b):
    return lax.dot_general(a, b, (((1,), (1,)), ((), ())), preferred_element_type=f32)


def t_dot(a, b):
    return lax.dot_general(a, b, (((0,), (0,)), ((), ())), preferred_element_type=f32)


def split(a):
    hi = a.astype(bf16)
    return hi, (a - hi.astype(f32)).astype(bf16)


def full():
    return pl.BlockSpec(memory_space=VMEM)


def scalars():
    return pl.BlockSpec(memory_space=SMEM)


def call(body, name, outs, ins, flops=0, moved=0, grid=None, in_specs=None, out_specs=None, limit=24, scratch=()):
    kwargs = {} if grid is None else {"grid": grid}
    return pl.pallas_call(
        body,
        name=name,
        out_shape=[jax.ShapeDtypeStruct(s, t) for s, t in outs],
        in_specs=in_specs or [full() for _ in ins],
        out_specs=out_specs or [full() for _ in outs],
        scratch_shapes=scratch,
        compiler_params=pltpu.CompilerParams(vmem_limit_bytes=limit << 20),
        cost_estimate=pl.CostEstimate(flops=flops, bytes_accessed=moved, transcendentals=0),
        **kwargs,
    )(*ins)


def pack_body(at_ref, ids_ref, gate_ref, moe_ref, cot_ref, place_ref, c0, c1, c2, c3, gate_col):
    @pl.when(pl.program_id(0) == 0)
    def _():
        rel = ids_ref[...] - at_ref[0]
        rel = jnp.where(rel < 0, rel + Y, rel)
        member = (lax.broadcasted_iota(jnp.int32, (8, ROWS), 0) == rel).astype(f32)
        row = lax.broadcasted_iota(jnp.int32, (ROWS, ROWS), 0)
        col = lax.broadcasted_iota(jnp.int32, (ROWS, ROWS), 1)
        earlier = dot(member.astype(bf16), (row < col).astype(bf16))
        slot = jnp.sum(earlier * member, axis=0, keepdims=True).astype(jnp.int32)
        target = rel * CAP + slot
        places = lax.broadcasted_iota(jnp.int32, (Y * CAP, ROWS), 0)
        place_ref[...] = (places == target).astype(bf16)
        gate = gate_ref[...].astype(f32)
        gate_col[...] = jnp.sum(jnp.where(row == col, gate, 0.0), axis=1, keepdims=True)

    place = place_ref[...]
    scaled = (gate_col[...] * cot_ref[...].astype(f32)).astype(bf16)
    for half, rows in enumerate((moe_ref[...], scaled)):
        part = dot(place, rows).astype(bf16)
        for s, chunk in enumerate((c0, c1, c2, c3)):
            chunk[half] = part[s * CAP : (s + 1) * CAP]


def pack(at, ids, gates, moe_in, grad_out):
    step = 512
    outs = [((Y * CAP, ROWS), bf16)] + [((2, CAP, WIDTH), bf16)] * Y
    ins = (at, ids, gates, moe_in, grad_out)
    row = pl.BlockSpec((1, ROWS), lambda j: (0, 0))
    tile = pl.BlockSpec((ROWS, step), lambda j: (0, j))
    return call(
        pack_body,
        "pack",
        outs,
        ins,
        2 * 384 * 256 * 4096,
        5 << 20,
        grid=(WIDTH // step,),
        in_specs=[scalars(), row, row, tile, tile],
        out_specs=[pl.BlockSpec((Y * CAP, ROWS), lambda j: (0, 0))]
        + [pl.BlockSpec((2, CAP, step), lambda j: (0, 0, j))] * Y,
        scratch=[VMEM((ROWS, 1), f32)],
        limit=16,
    )


BACK = WIDTH + 128


def expert_body(r0, r1, r2, r3, wp_ref, wb_ref, b0, b1, b2, b3, hid_ref, gb_ref, rows_ref, cots_ref):
    for s, r in enumerate((r0, r1, r2, r3)):
        rows_ref[s * CAP : (s + 1) * CAP, :] = r[0]
        cots_ref[s * CAP : (s + 1) * CAP, :] = r[1]
    step = 256
    total = jnp.zeros((Y * CAP, 1), f32)
    for j in range(FF // step):
        at, up = j * step, FF + j * step
        first = dot(rows_ref[...], wp_ref[:, at : at + step])
        second = dot(rows_ref[...], wp_ref[:, up : up + step])
        grad_hidden = dot_t(cots_ref[...], wb_ref[at : at + step, :])
        s = 1.0 / (1.0 + jnp.exp(-first))
        silu = first * s
        hidden = (silu * second).astype(bf16)
        hid_ref[:, at : at + step] = hidden
        total += jnp.sum(hidden.astype(f32) * grad_hidden, axis=1, keepdims=True)
        slope = s * (1.0 + first * (1.0 - s))
        gb_ref[:, at : at + step] = (grad_hidden * second * slope).astype(bf16)
        gb_ref[:, up : up + step] = (grad_hidden * silu).astype(bf16)
    backs = (b0, b1, b2, b3)
    hi, lo = split(total)
    lane = lax.broadcasted_iota(jnp.int32, (Y * CAP, 128), 1)
    tail = jnp.where(lane == 0, hi.astype(f32), lo.astype(f32)).astype(bf16)
    for s, b in enumerate(backs):
        b[:, WIDTH:] = tail[s * CAP : (s + 1) * CAP]
    for j in range(WIDTH // step):
        at = j * step
        back = dot_t(gb_ref[...], wp_ref[at : at + step, :]).astype(bf16)
        for s, b in enumerate(backs):
            b[:, at : at + step] = back[s * CAP : (s + 1) * CAP]


def expert(chunks, w_pair, w_back):
    n = Y * CAP
    outs = [((CAP, BACK), bf16)] * Y
    outs += [((n, FF), bf16), ((n, 2 * FF), bf16), ((n, WIDTH), bf16), ((n, WIDTH), bf16)]
    return call(expert_body, "expert", outs, (*chunks, w_pair, w_back), 5 * 2 * n * WIDTH * FF, 14 << 20)


def weights_body(core_ref, rows_ref, scaled_ref, gb_ref, hid_ref, keep_ref, send_ref):
    mine = core_ref[0] == 0
    up = t_dot(rows_ref[...], gb_ref[...])
    down = t_dot(hid_ref[...], scaled_ref[...])
    for k in range(X):
        for even, odd, narrow in (
            (up[k * 128 : k * 128 + 64], up[k * 128 + 64 : k * 128 + 128], True),
            (down[k * 32 : k * 32 + 16], down[k * 32 + 16 : k * 32 + 32], False),
        ):
            keep = jnp.where(mine, even, odd).astype(bf16)
            send = jnp.where(mine, odd, even).astype(bf16)
            for ref, value in ((keep_ref, keep), (send_ref, send)):
                if narrow:
                    ref[k, :64, :] = value
                else:
                    ref[k, 64:80, :] = value[:, :1024]
                    ref[k, 80:96, :] = value[:, 1024:]


def weights(core, rows, scaled, grad_both, hidden):
    n = Y * CAP
    shape = (Z * X, 96, 1024)
    block = pl.BlockSpec((X, 96, 1024), lambda i: (i, 0, 0))
    return call(
        weights_body,
        "weights",
        [(shape, bf16), (shape, bf16)],
        (core, rows, scaled, grad_both, hidden),
        3 * 2 * n * WIDTH * FF,
        12 << 20,
        grid=(Z,),
        in_specs=[
            scalars(),
            pl.BlockSpec((n, 512), lambda i: (0, i)),
            pl.BlockSpec((n, WIDTH), lambda i: (0, 0)),
            pl.BlockSpec((n, 2 * FF), lambda i: (0, 0)),
            pl.BlockSpec((n, 128), lambda i: (0, i)),
        ],
        out_specs=[block, block],
    )


def gather_sum_body(pieces_ref, up_ref, down_ref):
    for j in range(2):
        at = j * 512
        total = pieces_ref[0, :, at : at + 512].astype(f32)
        for k in range(1, Z * X):
            total = total + pieces_ref[k, :, at : at + 512].astype(f32)
        up_ref[0, :, at : at + 512] = total[:64]
        down_ref[0, :, at : at + 512] = total[64:80]
        down_ref[0, :, 1024 + at : 1024 + at + 512] = total[80:96]


def project_body(own_ref, rest_ref, place_ref, gate_ref, cot_ref, r0, r1, r2, r3, resid_ref, gates_ref, *outs):
    step = pl.program_id(0)
    backs = (r0, r1, r2, r3)

    @pl.when(step == 0)
    def _():
        place = place_ref[...]
        wide = 512
        for j in range(WIDTH // wide):
            cols = slice(j * wide, (j + 1) * wide)
            back = jnp.concatenate([b[:, cols] for b in backs], axis=0)
            resid_ref[:, cols] = (cot_ref[:, cols].astype(f32) + t_dot(place, back)).astype(bf16)
        tail = jnp.concatenate([b[:, WIDTH:] for b in backs], axis=0).astype(f32)
        picked = jnp.sum(place.astype(f32) * (tail[:, 0:1] + tail[:, 1:2]), axis=0, keepdims=True)
        gates_ref[...] = (picked / gate_ref[...].astype(f32)).astype(bf16)
        outs[0][...] = dot_t(resid_ref[...], own_ref[...]).astype(bf16)

    for s in range(1, Y):

        @pl.when(step == s)
        def _():
            outs[s][...] = dot_t(resid_ref[...], rest_ref[...].reshape(512, WIDTH)).astype(bf16)


def project(w_out, rest, place, gate_row, grad_out, backs):
    def once(shape):
        return pl.BlockSpec(shape, lambda s: (0,) * len(shape))

    slab = rest.shape[2]
    shapes = [(ROWS, WIDTH), (1, ROWS)] + [(ROWS, 512)] * Y
    return call(
        project_body,
        "project",
        [(s, bf16) for s in shapes],
        (w_out, rest, place, gate_row, grad_out, *backs),
        2 * ROWS * WIDTH * WIDTH + 2 * ROWS * 384 * WIDTH,
        10 << 20,
        grid=(Y,),
        in_specs=[
            once((512, WIDTH)),
            pl.BlockSpec((BLOCKS, 1, slab, WIDTH), lambda s: (0, jnp.maximum(s - 1, 0), 0, 0)),
            once((Y * CAP, ROWS)),
            once((1, ROWS)),
            once((ROWS, WIDTH)),
        ]
        + [once((CAP, BACK))] * Y,
        out_specs=[once(s) for s in shapes],
    )


def state_body(at_ref, g0, g1, g2, g3, q_ref, grad_ref, state_ref):
    y, block = at_ref[0], at_ref[1]
    ramp = lax.broadcasted_iota(jnp.int32, (ROWS, 1), 0)
    sums = [jnp.zeros((HD, 2 * HD), f32) for _ in range(HEADS)]
    for s, g in enumerate((g0, g1, g2, g3)):
        off = pl.multiple_of(lax.rem(y + s, Y) * ROWS, ROWS)
        inverse = 1.0 / (3 * BLOCKS * TOK + block * TOK + off + ramp + 1).astype(f32)
        grad_ref[pl.ds(off, ROWS), :] = g[...]
        for h in range(HEADS):
            cols = slice(h * HD, (h + 1) * HD)
            hi, lo = split(g[:, cols].astype(f32) * inverse)
            both = jnp.concatenate([hi, lo], axis=1)
            sums[h] += t_dot(q_ref[pl.ds(off, ROWS), cols], both)
    for h in range(HEADS):
        state_ref[h * HD : (h + 1) * HD, :] = sums[h][:, :HD] + sums[h][:, HD:]


SUB = 256
PARTS = TOK // SUB
PAIR = 2


def triangle(lower):
    row = lax.broadcasted_iota(jnp.int32, (SUB, SUB), 0)
    col = lax.broadcasted_iota(jnp.int32, (SUB, SUB), 1)
    return (col <= row) if lower else (col >= row)


def query_body(at_ref, g_ref, v_ref, k_ref, prior_ref, out_ref):
    block = at_ref[1]
    mask = triangle(True)
    ramp = lax.broadcasted_iota(jnp.int32, (SUB, 1), 0)
    for h in range(PAIR):
        cols = slice(h * HD, (h + 1) * HD)
        prior = jnp.concatenate(split(prior_ref[h]), axis=0)
        for i in range(PARTS):
            rows, upto = slice(i * SUB, (i + 1) * SUB), (i + 1) * SUB
            g = g_ref[rows, cols]
            mix = dot_t(g, v_ref[:upto, cols])
            edge = jnp.where(mask, mix[:, i * SUB :], 0.0).astype(bf16)
            if i:
                edge = jnp.concatenate([mix[:, : i * SUB].astype(bf16), edge], axis=1)
            before = dot_t(g, prior)
            total = before[:, :HD] + before[:, HD:] + dot(edge, k_ref[:upto, cols])
            count = (3 * BLOCKS * TOK + block * TOK + i * SUB + ramp + 1).astype(f32)
            out_ref[rows, cols] = (total / count).astype(bf16)


def mix_body(at_ref, a_ref, b_ref, c_ref, out_ref):
    block = at_ref[1]
    mask = triangle(False)
    ramp = lax.broadcasted_iota(jnp.int32, (1, TOK), 1)
    inverse = 1.0 / (3 * BLOCKS * TOK + block * TOK + ramp + 1).astype(f32)
    for h in range(PAIR):
        cols = slice(h * HD, (h + 1) * HD)
        for i in range(PARTS):
            at = i * SUB
            rows = slice(at, at + SUB)
            mix = dot_t(a_ref[rows, cols], b_ref[at:, cols]) * inverse[:, at:]
            edge = jnp.where(mask, mix[:, :SUB], 0.0).astype(bf16)
            if i < PARTS - 1:
                edge = jnp.concatenate([edge, mix[:, SUB:].astype(bf16)], axis=1)
            out_ref[rows, cols] = dot(edge, c_ref[at:, cols])


def head_call(body, name, ins, out_type, prior=None):
    cols = pl.BlockSpec((TOK, PAIR * HD), lambda h: (0, h))
    specs = [scalars()] + [cols] * 3
    if prior is not None:
        specs.append(pl.BlockSpec((PAIR, HD, HD), lambda h: (h, 0, 0)))
        ins = (*ins, prior)
    return call(
        body,
        name,
        [((TOK, HEADS * HD), out_type)],
        ins,
        10 * HEADS * 4 * SUB * SUB * HD,
        6 << 20,
        grid=(HEADS // PAIR,),
        in_specs=specs,
        out_specs=[cols],
    )[0]


def final_body(later_ref, v_ref, k_ref, key_ref, value_ref, out_key, out_value):
    hi, lo = split(later_ref[...])
    key = dot_t(v_ref[...], jnp.concatenate([hi, lo], axis=0))
    out_key[...] = (key_ref[...] + key[:, :HD] + key[:, HD:]).astype(bf16)
    value = dot(k_ref[...], jnp.concatenate([hi, lo], axis=1))
    out_value[...] = (value_ref[...] + value[:, :HD] + value[:, HD:]).astype(bf16)


def final(later, values, keys, key_here, value_here):
    cols = pl.BlockSpec((TOK, HD), lambda h: (0, h))
    return call(
        final_body,
        "final",
        [((TOK, HEADS * HD), bf16)] * 2,
        (later, values, keys, key_here, value_here),
        HEADS * 8 * TOK * HD * HD,
        8 << 20,
        grid=(HEADS,),
        in_specs=[pl.BlockSpec((HD, HD), lambda h: (h, 0))] + [cols] * 4,
        out_specs=[cols, cols],
    )


def index(z, x, c):
    return (z * X + x) * C + c


def spots():
    return [(z, x, c) for z in range(Z) for x in range(X) for c in range(C)]


def along_y(a, s):
    return lax.ppermute(a, "exp", [(i, (i + s) % Y) for i in range(Y)])


def along_x(a, s):
    return lax.ppermute(a, "ctx", [(index(z, x, c), index(z, (x + s) % X, c)) for z, x, c in spots()])


def along_z(a, s):
    return lax.ppermute(a, "ctx", [(index(z, x, c), index((z + s) % Z, x, c)) for z, x, c in spots()])


def across(a):
    return lax.ppermute(a, "ctx", [(i, i ^ 1) for i in range(BLOCKS)])


def on_device(
    attn_query,
    attn_key,
    attn_value,
    prefix_state,
    moe_in,
    grad_out,
    router_gates,
    expert_ids,
    w_gate_up,
    w_down,
    w_out,
):
    y = lax.axis_index("exp")
    block = lax.axis_index("ctx")
    z, x, c = block >> 3, (block >> 1) & 3, block & 1
    at = jnp.stack([y, block]).astype(jnp.int32)
    core = c.astype(jnp.int32)[None]

    slab = w_out.shape[0] // BLOCKS
    piece = lax.dynamic_slice_in_dim(w_out, block * slab, slab, 0)
    pieces = jnp.concatenate([along_y(piece, s) for s in (1, 2, 3)], axis=0)
    gate_row = router_gates.reshape(1, ROWS)
    place, *chunks = pack(at, expert_ids.reshape(1, ROWS), gate_row, moe_in, grad_out)
    pieces, chunks[1] = lax.optimization_barrier((pieces, chunks[1]))
    rest = lax.all_gather(pieces[None], "ctx", axis=0, tiled=True)
    rest = rest.reshape(BLOCKS, 3, slab, WIDTH)

    held = [chunks[0]] + [along_y(chunks[s], s) for s in (1, 2, 3)]
    b0, b1, b2, b3, hidden, grad_both, rows, scaled = expert(held, w_gate_up[0], w_down[0])
    backs = [b0] + [along_y(b, -s) for s, b in ((1, b1), (2, b2), (3, b3))]
    keep, send = weights(core, rows, scaled, grad_both, hidden)
    send, backs[1], backs[2], backs[3] = lax.optimization_barrier((send, backs[1], backs[2], backs[3]))
    recv = across(send)

    grad_resid, gates_out, *per_head = project(w_out, rest, place, gate_row, grad_out, backs)
    grad_gates = gates_out.reshape(ROWS, 1)
    grads = [per_head[0]] + [along_y(per_head[s], -s) for s in (1, 2, 3)]
    attn_grad, state = call(
        state_body,
        "state",
        [((TOK, HEADS * HD), bf16), ((HEADS * HD, HD), f32)],
        (at, *grads, attn_query),
        HEADS * 2 * TOK * HD * 2 * HD,
        4 << 20,
        in_specs=[scalars()] + [full()] * 5,
    )

    recv, _ = lax.optimization_barrier((recv, per_head[0]))
    folded = (keep.astype(f32) + recv.astype(f32)).astype(bf16)
    groups = [[index(i, j, k) for i in range(Z) for j in range(X)] for k in range(C)]
    exchanged = lax.all_to_all(folded, "ctx", 0, 0, axis_index_groups=groups, tiled=True)

    other = across(state)
    chip = state + other
    chip16 = chip.astype(bf16)
    from_x = [along_x(chip16, s).astype(f32) for s in (1, 2, 3)]
    line = chip + from_x[0] + from_x[1] + from_x[2]
    line16 = line.astype(bf16)
    from_z = [along_z(line16, s).astype(f32) for s in (1, 2, 3)]
    later = jnp.where(c == 0, other, 0.0)
    for s in (1, 2, 3):
        later += jnp.where(s > x, from_x[s - 1], 0.0) + jnp.where(s > z, from_z[s - 1], 0.0)

    grad_query = head_call(query_body, "grad_query", (at, attn_grad, attn_value, attn_key), bf16, prefix_state[0])
    key_here = head_call(mix_body, "mix_key", (at, attn_value, attn_grad, attn_query), f32)
    value_here = head_call(mix_body, "mix_value", (at, attn_key, attn_query, attn_grad), f32)
    grad_key, grad_value = final(later, attn_value, attn_key, key_here, value_here)

    exchanged, grad_key = lax.optimization_barrier((exchanged, grad_key))
    outs = [((1, 64, 1024), f32), ((1, 16, WIDTH), f32)]
    grad_gate_up, grad_down = call(gather_sum_body, "gather_sum", outs, (exchanged,), 0, 4 << 20)
    return (grad_query, grad_key, grad_value, grad_resid, grad_gates, grad_gate_up, grad_down)


def solution(mesh):
    whole = P(("ctx", "exp"), None)
    split_cols = P("ctx", "exp")
    return jax.shard_map(
        on_device,
        mesh=mesh,
        in_specs=(
            split_cols,
            split_cols,
            split_cols,
            P("ctx", "exp", None, None),
            whole,
            whole,
            whole,
            whole,
            P("exp", None, None),
            P("exp", None, None),
            P("exp", None),
        ),
        out_specs=(
            split_cols,
            split_cols,
            split_cols,
            whole,
            whole,
            P("exp", "ctx", None),
            P("exp", "ctx", None),
        ),
        check_vma=False,
    )
```

time: 221 us -> 211 us (0.955)
  local copies, waits for them, and re-layouts: 13.6 us -> 36.7 us
  Pallas kernels: 58.8 us -> 40.3 us
  starting transfers between devices: 50.3 us -> 35.6 us
  other arithmetic: 5.39 us -> 8.82 us
    unnamed x48 -> x78, local copies, waits for them, and re-layouts: 12 us -> 35.8 us
    pallas_call x12 -> x10, Pallas kernels: 58.8 us -> 40.3 us  [call(): pl.pallas_call(body, name=name, out_shape=[jax.ShapeDtypeStruct(s, t) for...]
    ppermute x9 -> x3, waiting for transfers between devices: 6.46 us -> 18.4 us  [along_x(): lax.ppermute(a, 'ctx', [(index(z, x, c), index(z, (x + s) % X, c)) for z,...]
    ppermute x9 -> x3, starting transfers between devices: 15.4 us -> 5.61 us  [along_z(): lax.ppermute(a, 'ctx', [(index(z, x, c), index((z + s) % Z, x, c)) for z,...]
    ppermute x9 -> x3, starting transfers between devices: 14.5 us -> 5.7 us  [along_x(): lax.ppermute(a, 'ctx', [(index(z, x, c), index(z, (x + s) % X, c)) for z,...]
    ppermute x15 -> x12, waiting for transfers between devices: 63.1 us -> 54.6 us  [along_y(): return lax.ppermute(a, 'exp', [(i, (i + s) % Y) for i in range(Y)])]
    all_to_all x0 -> x1, starting transfers between devices: none -> 7.69 us  [on_device(): lax.all_to_all(folded, 'ctx', 0, 0, axis_index_groups=groups, tiled=True)]
    ppermute x9 -> x3, waiting for transfers between devices: 6.5 us -> 0.01 us  [along_z(): lax.ppermute(a, 'ctx', [(index(z, x, c), index((z + s) % Z, x, c)) for z,...]
  transfers between devices with their start and end apart: 36 -> 22, of which waited for: 11 -> 10; matrix products, arithmetic and copies ran while one was open for 4% -> 1% of each run, Pallas kernels for 25% -> 19%
where the time goes in v2:
time: 211 us; the launch traced here: 210 us
  waiting for transfers between devices  74.6 us (35%)
  Pallas kernels  40.3 us (19%)
  local copies, waits for them, and re-layouts  36.7 us (17%)
  starting transfers between devices  35.6 us (17%)
  between operations  14.2 us (7%)
  other arithmetic  8.82 us (4%)
    ppermute x12, waiting for transfers between devices, along_y(): return lax.ppermute(a, 'exp', [(i, (i + s) % Y) for i in range(Y)])  54.6 us
    pallas_call x10, Pallas kernels, call(): pl.pallas_call(body, name=name, out_shape=[jax.ShapeDtypeStruct(s, t) for...  40.3 us
    unnamed x78, local copies, waits for them, and re-layouts  35.8 us
    ppermute x3, waiting for transfers between devices, along_x(): lax.ppermute(a, 'ctx', [(index(z, x, c), index(z, (x + s) % X, c)) for z,...  18.4 us
    ppermute x12, starting transfers between devices, along_y(): return lax.ppermute(a, 'exp', [(i, (i + s) % Y) for i in range(Y)])  16.6 us
    all_to_all x1, starting transfers between devices, on_device(): lax.all_to_all(folded, 'ctx', 0, 0, axis_index_groups=groups, tiled=True)  7.69 us
    ppermute x3, starting transfers between devices, along_x(): lax.ppermute(a, 'ctx', [(index(z, x, c), index(z, (x + s) % X, c)) for z,...  5.7 us
    ppermute x3, starting transfers between devices, along_z(): lax.ppermute(a, 'ctx', [(index(z, x, c), index((z + s) % Z, x, c)) for z,...  5.61 us
  transfers between devices with their start and end apart: 22, of which 10 were waited for; matrix products, arithmetic and copies ran while one was open for 1% of the time, Pallas kernels for 19%

profile of v2, /device:TPU:0, one launch (start us, length us, event | category | flops | bytes accessed | tf_op | source)
XLA Modules:
  0.0 210.2 jit_solution(1653728547590426174)
XLA Ops:
  9.7 2.9 %collective-permute-start.1 = (bf16[16,2048]{1,0:T(8,128)(2,1)S(1)}, bf16[16,2048]{1,0:T(8,128)(2,1)S(1)}, u32[]{:S(2)}, u32[]{:S(2)}) collective-permute-start(bf16[16,2048]{1,0:T(8,128)(2,1)S(1)} %constant_dynamic-slice_fusion), channel_id=1, source_target_pairs={{0,2},{1,3},{2,0},{3,1},{4,6},{5,7},{6,4},{7,5},{8,10},{9,11},{10,... | collective-permute-start | bytes 196616 | tf_op jit(solution)/shard_map/ppermute | solution.py:364
  17.9 2.7 %pack.1 = (bf16[384,256]{1,0:T(8,128)(2,1)S(1)}, bf16[2,96,2048]{2,1,0:T(8,128)(2,1)S(1)}, bf16[2,96,2048]{2,1,0:T(8,128)(2,1)S(1)}, bf16[2,96,2048]{2,1,0:T(8,128)(2,1)S(1)}, bf16[2,96,2048]{2,1,0:T(8,128)(2,1)S(1)}) custom-call(s32[2]{0:T(128)S(1)} %pad_add_fusion.at_ref, s32[1,256]{1,0:T(1,128)S(1)} %bitcast.16, bf16[1,256]{1,0:T(2,128)(2,1)S(1)} %bitcast.11, ...), custom_call_target="tpu_custom_call" | custom-call | flops 805306368 | bytes 5242880 | tf_op jit(solution)/shard_map/pack/pallas_call | solution.py:44
  25.0 3.1 %collective-permute-start.5 = (bf16[2,96,2048]{2,1,0:T(8,128)(2,1)}, bf16[2,96,2048]{2,1,0:T(8,128)(2,1)S(1)}, u32[]{:S(2)}, u32[]{:S(2)}) collective-permute-start(bf16[2,96,2048]{2,1,0:T(8,128)(2,1)} %copy-done.20), channel_id=1, source_target_pairs={{0,3},{1,0},{2,1},{3,2},{4,7},{5,4},{6,5},{7,6},{8,11},{9,8},{10,9... | collective-permute-start | bytes 2359304 | tf_op jit(solution)/shard_map/ppermute | solution.py:364
  28.1 18.9 %collective-permute-done.4.r2 = bf16[2,96,2048]{2,1,0:T(8,128)(2,1)S(1)} collective-permute-done((bf16[2,96,2048]{2,1,0:T(8,128)(2,1)}, bf16[2,96,2048]{2,1,0:T(8,128)(2,1)S(1)}, u32[]{:S(2)}, u32[]{:S(2)}) %collective-permute-start.4) | collective-permute-done | bytes 786464 | tf_op jit(solution)/shard_map/ppermute | solution.py:364
  47.0 12.4 %collective-permute-done.5.r3 = bf16[2,96,2048]{2,1,0:T(8,128)(2,1)S(1)} collective-permute-done((bf16[2,96,2048]{2,1,0:T(8,128)(2,1)}, bf16[2,96,2048]{2,1,0:T(8,128)(2,1)S(1)}, u32[]{:S(2)}, u32[]{:S(2)}) %collective-permute-start.5) | collective-permute-done | bytes 786464 | tf_op jit(solution)/shard_map/ppermute | solution.py:364
  59.4 2.3 %collective-permute-done.3.r1 = bf16[2,96,2048]{2,1,0:T(8,128)(2,1)S(1)} collective-permute-done((bf16[2,96,2048]{2,1,0:T(8,128)(2,1)S(1)}, bf16[2,96,2048]{2,1,0:T(8,128)(2,1)S(1)}, u32[]{:S(2)}, u32[]{:S(2)}) %collective-permute-start.3) | collective-permute-done | bytes 786464 | tf_op jit(solution)/shard_map/ppermute | solution.py:364
  65.2 5.5 %expert.1 = (bf16[96,2176]{1,0:T(8,128)(2,1)S(1)}, bf16[96,2176]{1,0:T(8,128)(2,1)}, bf16[96,2176]{1,0:T(8,128)(2,1)}, bf16[96,2176]{1,0:T(8,128)(2,1)}, bf16[38...) custom-call(bf16[2,96,2048]{2,1,0:T(8,128)(2,1)S(1)} %copy-done.28, ...), custom_call_target="tpu_custom_call" | custom-call | flops 4026531840 | bytes 14680064 | tf_op jit(solution)/shard_map/expert/pallas_call | solution.py:44
  83.3 5.4 %weights.1 = (bf16[16,96,1024]{2,1,0:T(8,128)(2,1)S(1)}, bf16[16,96,1024]{2,1,0:T(8,128)(2,1)}) custom-call(s32[1]{0:T(128)} %bitcast.7.core_ref, bf16[384,2048]{1,0:T(8,128)(2,1)S(1)} %copy-done.30, bf16[384,2048]{1,0:T(8,128)(2,1)S(1)} %copy-done.32, bf16[384,1024]{1,0:T(8,128)(2,1)S(1)} %copy-done.34, bf16[384,512]{1,0:T(8,128)(2,1)S(1)} %copy-done.36), custom_call_target="tpu_custom_call" | custom-call | flops 2415919104 | bytes 12582912 | tf_op jit(solution)/shard_map/weights/pallas_call | solution.py:44
  90.5 7.6 %collective-permute-done.8.r3 = bf16[96,2176]{1,0:T(8,128)(2,1)} collective-permute-done((bf16[96,2176]{1,0:T(8,128)(2,1)}, bf16[96,2176]{1,0:T(8,128)(2,1)}, u32[]{:S(2)}, u32[]{:S(2)}) %collective-permute-start.8) | collective-permute-done | bytes 417824 | tf_op jit(solution)/shard_map/ppermute | solution.py:364
  98.1 2.8 %copy-done.2 = bf16[1536,2048]{1,0:T(8,128)(2,1)S(1)} copy-done((bf16[1536,2048]{1,0:T(8,128)(2,1)S(1)}, bf16[1536,2048]{1,0:T(8,128)(2,1)}, u32[]{:S(2)}) %copy-start.2) | copy-done | bytes 6291480
  105.7 6.3 %project.1 = (bf16[256,2048]{1,0:T(8,128)(2,1)}, bf16[1,256]{1,0:T(2,128)(2,1)}, bf16[256,512]{1,0:T(8,128)(2,1)S(1)}, bf16[256,512]{1,0:T(8,128)(2,1)S(1)}, bf1...) custom-call(bf16[512,2048]{1,0:T(8,128)(2,1)S(1)} %copy-done.8, bf16[32,3,16,2048]{3,2,1,0:T(8,128)(2,1)S(1)} %bitcast.10, ...), custom_call_target="tpu_custom_call" | custom-call | flops 2550136832 | bytes 10485760 | tf_op jit(solution)/shard_map/project/pallas_call | solution.py:44
  114.1 5.1 %add_convert_fusion = bf16[16,96,1024]{2,1,0:T(8,128)(2,1)} fusion(bf16[16,96,1024]{2,1,0:T(8,128)(2,1)} %collective-permute-done.12, bf16[16,96,1024]{2,1,0:T(8,128)(2,1)S(1)} %get-tuple-element.67), kind=kLoop, calls=%fused_computation | loop fusion | flops 6291456 | bytes 9437184 | tf_op jit(solution)/shard_map/convert_element_type | solution.py:428
  119.2 7.7 %all-to-all-start = ((bf16[16,96,1024]{2,1,0:T(8,128)(2,1)}), bf16[16,96,1024]{2,1,0:T(8,128)(2,1)S(1)}, u32[]{:S(2)}, u32[]{:S(2)}) async-start(bf16[16,96,1024]{2,1,0:T(8,128)(2,1)} %add_convert_fusion), calls=%async_computation | async-start | bytes 6291456 | tf_op jit(solution)/shard_map/all_to_all | solution.py:430
  131.2 6.6 %collective-permute-done.10.g2 = bf16[256,512]{1,0:T(8,128)(2,1)S(1)} collective-permute-done((bf16[256,512]{1,0:T(8,128)(2,1)}, bf16[256,512]{1,0:T(8,128)(2,1)S(1)}, u32[]{:S(2)}, u32[]{:S(2)}) %collective-permute-start.10) | collective-permute-done | bytes 262176 | tf_op jit(solution)/shard_map/ppermute | solution.py:364
  137.9 4.9 %collective-permute-done.11.g3 = bf16[256,512]{1,0:T(8,128)(2,1)S(1)} collective-permute-done((bf16[256,512]{1,0:T(8,128)(2,1)}, bf16[256,512]{1,0:T(8,128)(2,1)S(1)}, u32[]{:S(2)}, u32[]{:S(2)}) %collective-permute-start.11) | collective-permute-done | bytes 262176 | tf_op jit(solution)/shard_map/ppermute | solution.py:364
  150.1 2.7 %collective-permute-start.15 = (bf16[512,128]{1,0:T(8,128)(2,1)}, bf16[512,128]{1,0:T(8,128)(2,1)}, u32[]{:S(2)}, u32[]{:S(2)}) collective-permute-start(bf16[512,128]{1,0:T(8,128)(2,1)} %get-tuple-element.79), channel_id=1, source_target_pairs={{0,16},{4,20},{8,24},{12,28},{16,0},{20,4},{24,8},{28,12},{32,48},... | collective-permute-start | bytes 393224 | tf_op jit(solution)/shard_map/ppermute | solution.py:368
  157.9 4.5 %mix_key.1.key_ref = f32[1024,512]{1,0:T(8,128)S(1)} custom-call(s32[2]{0:T(128)S(1)} %pad_add_fusion.at_ref, bf16[1024,512]{1,0:T(8,128)(2,1)S(1)} %copy-done.3, bf16[1024,512]{1,0:T(8,128)(2,1)S(1)} %copy-done.7, bf16[1024,512]{1,0:T(8,128)(2,1)S(1)} %copy-done.1), custom_call_target="tpu_custom_call" | custom-call | flops 1342177280 | bytes 6291456 | tf_op jit(solution)/shard_map/mix_key/pallas_call | solution.py:44
  162.4 9.8 %collective-permute-done.14 = bf16[512,128]{1,0:T(8,128)(2,1)S(1)} collective-permute-done((bf16[512,128]{1,0:T(8,128)(2,1)}, bf16[512,128]{1,0:T(8,128)(2,1)S(1)}, u32[]{:S(2)}, u32[]{:S(2)}) %collective-permute-start.14) | collective-permute-done | bytes 131104 | tf_op jit(solution)/shard_map/ppermute | solution.py:368
  172.2 8.6 %collective-permute-done.15 = bf16[512,128]{1,0:T(8,128)(2,1)} collective-permute-done((bf16[512,128]{1,0:T(8,128)(2,1)}, bf16[512,128]{1,0:T(8,128)(2,1)}, u32[]{:S(2)}, u32[]{:S(2)}) %collective-permute-start.15) | collective-permute-done | bytes 131104 | tf_op jit(solution)/shard_map/ppermute | solution.py:368
  182.2 3.0 %collective-permute-start.18 = (bf16[512,128]{1,0:T(8,128)(2,1)S(1)}, bf16[512,128]{1,0:T(8,128)(2,1)S(1)}, u32[]{:S(2)}, u32[]{:S(2)}) collective-permute-start(bf16[512,128]{1,0:T(8,128)(2,1)S(1)} %fusion.5), channel_id=1, source_target_pairs={{0,64},{4,68},{8,72},{12,76},{16,80},{20,84},{24,88},{28,92},{32,9... | collective-permute-start | bytes 393224 | tf_op jit(solution)/shard_map/ppermute | solution.py:372
  185.2 2.3 %collective-permute-start.19 = (bf16[512,128]{1,0:T(8,128)(2,1)S(1)}, bf16[512,128]{1,0:T(8,128)(2,1)S(1)}, u32[]{:S(2)}, u32[]{:S(2)}) collective-permute-start(bf16[512,128]{1,0:T(8,128)(2,1)S(1)} %fusion.5), channel_id=1, source_target_pairs={{0,96},{4,100},{8,104},{12,108},{16,112},{20,116},{24,120},{28,124... | collective-permute-start | bytes 393224 | tf_op jit(solution)/shard_map/ppermute | solution.py:372
  187.5 4.5 %mix_value.1.value_ref = f32[1024,512]{1,0:T(8,128)S(1)} custom-call(s32[2]{0:T(128)S(1)} %pad_add_fusion.at_ref, bf16[1024,512]{1,0:T(8,128)(2,1)S(1)} %copy-done.5, bf16[1024,512]{1,0:T(8,128)(2,1)S(1)} %copy-done.1, bf16[1024,512]{1,0:T(8,128)(2,1)S(1)} %copy-done.7), custom_call_target="tpu_custom_call" | custom-call | flops 1342177280 | bytes 6291456 | tf_op jit(solution)/shard_map/mix_value/pallas_call | solution.py:44
  192.1 5.4 %grad_query.1 = bf16[1024,512]{1,0:T(8,128)(2,1)} custom-call(s32[2]{0:T(128)S(1)} %pad_add_fusion.at_ref, bf16[1024,512]{1,0:T(8,128)(2,1)S(1)} %copy-done.7, bf16[1024,512]{1,0:T(8,128)(2,1)S(1)} %copy-done.4, bf16[1024,512]{1,0:T(8,128)(2,1)S(1)} %copy-done.5, f32[4,128,128]{2,1,0:T(8,128)S(1)} %bitcast.15), custom_call_target="tpu_custom_call" | custom-call | flops 1342177280 | bytes 6291456 | tf_op jit(solution)/shard_map/grad_query/pallas_call | solution.py:44
  198.7 3.6 %final.1 = (bf16[1024,512]{1,0:T(8,128)(2,1)}, bf16[1024,512]{1,0:T(8,128)(2,1)}) custom-call(f32[512,128]{1,0:T(8,128)S(1)} %fusion.3.later_ref, bf16[1024,512]{1,0:T(8,128)(2,1)S(1)} %copy-done.4, bf16[1024,512]{1,0:T(8,128)(2,1)S(1)} %copy-done.5, f32[1024,512]{1,0:T(8,128)S(1)} %mix_key.1.key_ref, f32[1024,512]{1,0:T(8,128)S(1)} %mix_value.1.value_ref), custom_call_target="tpu_custom_call" | custom-call | flops 536870912 | bytes 8388608 | tf_op jit(solution)/shard_map/final/pallas_call | solution.py:44
  (116 shorter events, 57.3 us)
Async XLA Ops:
  7.2 91.0 %all-gather.3.cloned.1.call-start = ((), (), s32[]{:S(2)}) async-start(), calls=%async_computation.1 | async-start | bytes 6488064 | tf_op jit(solution)/shard_map/all_gather | solution.py:404
  8.1 15.9 %collective-permute-start = (bf16[16,2048]{1,0:T(8,128)(2,1)S(1)}, bf16[16,2048]{1,0:T(8,128)(2,1)S(1)}, u32[]{:S(2)}, u32[]{:S(2)}) collective-permute-start(bf16[16,2048]{1,0:T(8,128)(2,1)S(1)} %constant_dynamic-slice_fusion), channel_id=1, source_target_pairs={{0,1},{1,2},{2,3},{3,0},{4,5},{5,6},{6,7},{7,4},{8,9},{9,10},{10,1... | collective-permute-start | bytes 196616 | tf_op jit(solution)/shard_map/ppermute | solution.py:364
  9.7 14.2 %collective-permute-start.1 = (bf16[16,2048]{1,0:T(8,128)(2,1)S(1)}, bf16[16,2048]{1,0:T(8,128)(2,1)S(1)}, u32[]{:S(2)}, u32[]{:S(2)}) collective-permute-start(bf16[16,2048]{1,0:T(8,128)(2,1)S(1)} %constant_dynamic-slice_fusion), channel_id=1, source_target_pairs={{0,2},{1,3},{2,0},{3,1},{4,6},{5,7},{6,4},{7,5},{8,10},{9,11},{10,... | collective-permute-start | bytes 196616 | tf_op jit(solution)/shard_map/ppermute | solution.py:364
  12.6 11.3 %collective-permute-start.2 = (bf16[16,2048]{1,0:T(8,128)(2,1)S(1)}, bf16[16,2048]{1,0:T(8,128)(2,1)S(1)}, u32[]{:S(2)}, u32[]{:S(2)}) collective-permute-start(bf16[16,2048]{1,0:T(8,128)(2,1)S(1)} %constant_dynamic-slice_fusion), channel_id=1, source_target_pairs={{0,3},{1,0},{2,1},{3,2},{4,7},{5,4},{6,5},{7,6},{8,11},{9,8},{10,9... | collective-permute-start | bytes 196616 | tf_op jit(solution)/shard_map/ppermute | solution.py:364
  17.9 43.9 %copy-start.18 = (bf16[1,512,2048]{2,1,0:T(8,128)(2,1)S(1)}, bf16[1,512,2048]{2,1,0:T(8,128)(2,1)}, u32[]{:S(2)}) copy-start(bf16[1,512,2048]{2,1,0:T(8,128)(2,1)} %param.20) | copy-start | bytes 6291460
  24.6 22.3 %collective-permute-start.4 = (bf16[2,96,2048]{2,1,0:T(8,128)(2,1)}, bf16[2,96,2048]{2,1,0:T(8,128)(2,1)S(1)}, u32[]{:S(2)}, u32[]{:S(2)}) collective-permute-start(bf16[2,96,2048]{2,1,0:T(8,128)(2,1)} %copy-done.21), channel_id=1, source_target_pairs={{0,2},{1,3},{2,0},{3,1},{4,6},{5,7},{6,4},{7,5},{8,10},{9,11},{10,... | collective-permute-start | bytes 2359304 | tf_op jit(solution)/shard_map/ppermute | solution.py:364
  25.0 34.4 %collective-permute-start.5 = (bf16[2,96,2048]{2,1,0:T(8,128)(2,1)}, bf16[2,96,2048]{2,1,0:T(8,128)(2,1)S(1)}, u32[]{:S(2)}, u32[]{:S(2)}) collective-permute-start(bf16[2,96,2048]{2,1,0:T(8,128)(2,1)} %copy-done.20), channel_id=1, source_target_pairs={{0,3},{1,0},{2,1},{3,2},{4,7},{5,4},{6,5},{7,6},{8,11},{9,8},{10,9... | collective-permute-start | bytes 2359304 | tf_op jit(solution)/shard_map/ppermute | solution.py:364
  28.1 33.7 %collective-permute-start.3 = (bf16[2,96,2048]{2,1,0:T(8,128)(2,1)S(1)}, bf16[2,96,2048]{2,1,0:T(8,128)(2,1)S(1)}, u32[]{:S(2)}, u32[]{:S(2)}) collective-permute-start(bf16[2,96,2048]{2,1,0:T(8,128)(2,1)S(1)} %get-tuple-element.47), channel_id=1, source_target_pairs={{0,1},{1,2},{2,3},{3,0},{4,5},{5,6},{6,7},{7,4},{8,9},{9,10},{10,1... | collective-permute-start | bytes 2359304 | tf_op jit(solution)/shard_map/ppermute | solution.py:364
  75.5 13.2 %collective-permute-start.6 = (bf16[96,2176]{1,0:T(8,128)(2,1)}, bf16[96,2176]{1,0:T(8,128)(2,1)}, u32[]{:S(2)}, u32[]{:S(2)}) collective-permute-start(bf16[96,2176]{1,0:T(8,128)(2,1)} %get-tuple-element.56), channel_id=1, source_target_pairs={{0,3},{1,0},{2,1},{3,2},{4,7},{5,4},{6,5},{7,6},{8,11},{9,8},{10,9... | collective-permute-start | bytes 1253384 | tf_op jit(solution)/shard_map/ppermute | solution.py:364
  76.1 14.4 %collective-permute-start.7 = (bf16[96,2176]{1,0:T(8,128)(2,1)}, bf16[96,2176]{1,0:T(8,128)(2,1)}, u32[]{:S(2)}, u32[]{:S(2)}) collective-permute-start(bf16[96,2176]{1,0:T(8,128)(2,1)} %get-tuple-element.57), channel_id=1, source_target_pairs={{0,2},{1,3},{2,0},{3,1},{4,6},{5,7},{6,4},{7,5},{8,10},{9,11},{10,... | collective-permute-start | bytes 1253384 | tf_op jit(solution)/shard_map/ppermute | solution.py:364
  77.6 20.5 %collective-permute-start.8 = (bf16[96,2176]{1,0:T(8,128)(2,1)}, bf16[96,2176]{1,0:T(8,128)(2,1)}, u32[]{:S(2)}, u32[]{:S(2)}) collective-permute-start(bf16[96,2176]{1,0:T(8,128)(2,1)} %get-tuple-element.58), channel_id=1, source_target_pairs={{0,1},{1,2},{2,3},{3,0},{4,5},{5,6},{6,7},{7,4},{8,9},{9,10},{10,1... | collective-permute-start | bytes 1253384 | tf_op jit(solution)/shard_map/ppermute | solution.py:364
  98.1 16.0 %collective-permute-start.12 = (bf16[16,96,1024]{2,1,0:T(8,128)(2,1)}, bf16[16,96,1024]{2,1,0:T(8,128)(2,1)}, u32[]{:S(2)}, u32[]{:S(2)}) collective-permute-start(bf16[16,96,1024]{2,1,0:T(8,128)(2,1)} %get-tuple-element.68), channel_id=1, source_target_pairs={{0,4},{4,0},{8,12},{12,8},{16,20},{20,16},{24,28},{28,24},{32,36},... | collective-permute-start | bytes 9437192 | tf_op jit(solution)/shard_map/ppermute | solution.py:376
  119.2 83.1 %all-to-all-start = ((bf16[16,96,1024]{2,1,0:T(8,128)(2,1)}), bf16[16,96,1024]{2,1,0:T(8,128)(2,1)S(1)}, u32[]{:S(2)}, u32[]{:S(2)}) async-start(bf16[16,96,1024]{2,1,0:T(8,128)(2,1)} %add_convert_fusion), calls=%async_computation | async-start | bytes 6291456 | tf_op jit(solution)/shard_map/all_to_all | solution.py:430
  126.9 11.0 %collective-permute-start.10 = (bf16[256,512]{1,0:T(8,128)(2,1)}, bf16[256,512]{1,0:T(8,128)(2,1)S(1)}, u32[]{:S(2)}, u32[]{:S(2)}) collective-permute-start(bf16[256,512]{1,0:T(8,128)(2,1)} %copy-done.25), channel_id=1, source_target_pairs={{0,2},{1,3},{2,0},{3,1},{4,6},{5,7},{6,4},{7,5},{8,10},{9,11},{10,... | collective-permute-start | bytes 786440 | tf_op jit(solution)/shard_map/ppermute | solution.py:364
  128.0 14.7 %collective-permute-start.11 = (bf16[256,512]{1,0:T(8,128)(2,1)}, bf16[256,512]{1,0:T(8,128)(2,1)S(1)}, u32[]{:S(2)}, u32[]{:S(2)}) collective-permute-start(bf16[256,512]{1,0:T(8,128)(2,1)} %copy-done.24), channel_id=1, source_target_pairs={{0,1},{1,2},{2,3},{3,0},{4,5},{5,6},{6,7},{7,4},{8,9},{9,10},{10,1... | collective-permute-start | bytes 786440 | tf_op jit(solution)/shard_map/ppermute | solution.py:364
  129.0 13.7 %collective-permute-start.9 = (bf16[256,512]{1,0:T(8,128)(2,1)}, bf16[256,512]{1,0:T(8,128)(2,1)S(1)}, u32[]{:S(2)}, u32[]{:S(2)}) collective-permute-start(bf16[256,512]{1,0:T(8,128)(2,1)} %copy-done.23), channel_id=1, source_target_pairs={{0,3},{1,0},{2,1},{3,2},{4,7},{5,4},{6,5},{7,6},{8,11},{9,8},{10,9... | collective-permute-start | bytes 786440 | tf_op jit(solution)/shard_map/ppermute | solution.py:364
  146.2 1.5 collective-permute-start.13
  148.5 23.7 %collective-permute-start.14 = (bf16[512,128]{1,0:T(8,128)(2,1)}, bf16[512,128]{1,0:T(8,128)(2,1)S(1)}, u32[]{:S(2)}, u32[]{:S(2)}) collective-permute-start(bf16[512,128]{1,0:T(8,128)(2,1)} %get-tuple-element.79), channel_id=1, source_target_pairs={{0,8},{4,12},{8,16},{12,20},{16,24},{20,28},{24,0},{28,4},{32,40},... | collective-permute-start | bytes 393224 | tf_op jit(solution)/shard_map/ppermute | solution.py:368
  150.1 30.8 %collective-permute-start.15 = (bf16[512,128]{1,0:T(8,128)(2,1)}, bf16[512,128]{1,0:T(8,128)(2,1)}, u32[]{:S(2)}, u32[]{:S(2)}) collective-permute-start(bf16[512,128]{1,0:T(8,128)(2,1)} %get-tuple-element.79), channel_id=1, source_target_pairs={{0,16},{4,20},{8,24},{12,28},{16,0},{20,4},{24,8},{28,12},{32,48},... | collective-permute-start | bytes 393224 | tf_op jit(solution)/shard_map/ppermute | solution.py:368
  152.7 28.1 %collective-permute-start.16 = (bf16[512,128]{1,0:T(8,128)(2,1)}, bf16[512,128]{1,0:T(8,128)(2,1)}, u32[]{:S(2)}, u32[]{:S(2)}) collective-permute-start(bf16[512,128]{1,0:T(8,128)(2,1)} %get-tuple-element.79), channel_id=1, source_target_pairs={{0,24},{4,28},{8,0},{12,4},{16,8},{20,12},{24,16},{28,20},{32,56},... | collective-permute-start | bytes 393224 | tf_op jit(solution)/shard_map/ppermute | solution.py:368
  162.4 29.7 %copy-start.4 = (bf16[1024,512]{1,0:T(8,128)(2,1)S(1)}, bf16[1024,512]{1,0:T(8,128)(2,1)}, u32[]{:S(2)}) copy-start(bf16[1024,512]{1,0:T(8,128)(2,1)} %v_ref.3) | copy-start | bytes 3145732
  181.9 15.6 %collective-permute-start.17 = (bf16[512,128]{1,0:T(8,128)(2,1)S(1)}, bf16[512,128]{1,0:T(8,128)(2,1)S(1)}, u32[]{:S(2)}, u32[]{:S(2)}) collective-permute-start(bf16[512,128]{1,0:T(8,128)(2,1)S(1)} %fusion.5), channel_id=1, source_target_pairs={{0,32},{4,36},{8,40},{12,44},{16,48},{20,52},{24,56},{28,60},{32,6... | collective-permute-start | bytes 393224 | tf_op jit(solution)/shard_map/ppermute | solution.py:372
  182.2 15.3 %collective-permute-start.18 = (bf16[512,128]{1,0:T(8,128)(2,1)S(1)}, bf16[512,128]{1,0:T(8,128)(2,1)S(1)}, u32[]{:S(2)}, u32[]{:S(2)}) collective-permute-start(bf16[512,128]{1,0:T(8,128)(2,1)S(1)} %fusion.5), channel_id=1, source_target_pairs={{0,64},{4,68},{8,72},{12,76},{16,80},{20,84},{24,88},{28,92},{32,9... | collective-permute-start | bytes 393224 | tf_op jit(solution)/shard_map/ppermute | solution.py:372
  185.2 12.4 %collective-permute-start.19 = (bf16[512,128]{1,0:T(8,128)(2,1)S(1)}, bf16[512,128]{1,0:T(8,128)(2,1)S(1)}, u32[]{:S(2)}, u32[]{:S(2)}) collective-permute-start(bf16[512,128]{1,0:T(8,128)(2,1)S(1)} %fusion.5), channel_id=1, source_target_pairs={{0,96},{4,100},{8,104},{12,108},{16,112},{20,116},{24,120},{28,124... | collective-permute-start | bytes 393224 | tf_op jit(solution)/shard_map/ppermute | solution.py:372
  (37 other events, 116.2 us)
Sparse Core Ops, SparseCore 0:
  24.8 49.1 all-gather.2

commit v3 on v2

v3 whole, which is shorter than its diff:
```python
import jax
import jax.numpy as jnp
from jax import lax
from jax.experimental import pallas as pl
from jax.experimental.pallas import tpu as pltpu
from jax.sharding import PartitionSpec as P

bf16 = jnp.bfloat16
f32 = jnp.float32
VMEM = pltpu.VMEM
SMEM = pltpu.SMEM
Z, X, C, Y = 4, 4, 2, 4
CAP, ROWS, WIDTH, FF, HD, HEADS, TOK = 96, 256, 2048, 512, 128, 4, 1024
WEIGHT = 4
BLOCKS = Z * X * C


def dot(a, b):
    return lax.dot_general(a, b, (((1,), (0,)), ((), ())), preferred_element_type=f32)


def dot_t(a, b):
    return lax.dot_general(a, b, (((1,), (1,)), ((), ())), preferred_element_type=f32)


def t_dot(a, b):
    return lax.dot_general(a, b, (((0,), (0,)), ((), ())), preferred_element_type=f32)


def split(a):
    hi = a.astype(bf16)
    return hi, (a - hi.astype(f32)).astype(bf16)


def full():
    return pl.BlockSpec(memory_space=VMEM)


def scalars():
    return pl.BlockSpec(memory_space=SMEM)


def call(body, name, outs, ins, flops=0, moved=0, grid=None, in_specs=None, out_specs=None, limit=24, scratch=(), free=()):
    kwargs = {} if grid is None else {"grid": grid}
    specs = in_specs or [full() for _ in ins]
    ins = [
        a if spec.memory_space is SMEM or i in free else pltpu.with_memory_space_constraint(a, pltpu.HBM)
        for i, (a, spec) in enumerate(zip(ins, specs))
    ]
    return pl.pallas_call(
        body,
        name=name,
        out_shape=[pltpu.HBM(s, t) for s, t in outs],
        in_specs=specs,
        out_specs=out_specs or [full() for _ in outs],
        scratch_shapes=scratch,
        compiler_params=pltpu.CompilerParams(vmem_limit_bytes=limit << 20),
        cost_estimate=pl.CostEstimate(flops=WEIGHT * flops, bytes_accessed=WEIGHT * moved, transcendentals=0),
        **kwargs,
    )(*ins)


def pack_body(at_ref, ids_ref, gate_ref, moe_ref, cot_ref, place_ref, c0, c1, c2, c3, gate_col):
    @pl.when(pl.program_id(0) == 0)
    def _():
        rel = ids_ref[...] - at_ref[0]
        rel = jnp.where(rel < 0, rel + Y, rel)
        member = (lax.broadcasted_iota(jnp.int32, (8, ROWS), 0) == rel).astype(f32)
        row = lax.broadcasted_iota(jnp.int32, (ROWS, ROWS), 0)
        col = lax.broadcasted_iota(jnp.int32, (ROWS, ROWS), 1)
        earlier = dot(member.astype(bf16), (row < col).astype(bf16))
        slot = jnp.sum(earlier * member, axis=0, keepdims=True).astype(jnp.int32)
        target = rel * CAP + slot
        places = lax.broadcasted_iota(jnp.int32, (Y * CAP, ROWS), 0)
        place_ref[...] = (places == target).astype(bf16)
        gate = gate_ref[...].astype(f32)
        gate_col[...] = jnp.sum(jnp.where(row == col, gate, 0.0), axis=1, keepdims=True)

    place = place_ref[...]
    scaled = (gate_col[...] * cot_ref[...].astype(f32)).astype(bf16)
    for half, rows in enumerate((moe_ref[...], scaled)):
        part = dot(place, rows).astype(bf16)
        for s, chunk in enumerate((c0, c1, c2, c3)):
            chunk[half] = part[s * CAP : (s + 1) * CAP]


def pack(at, ids, gates, moe_in, grad_out):
    step = 512
    outs = [((Y * CAP, ROWS), bf16)] + [((2, CAP, WIDTH), bf16)] * Y
    ins = (at, ids, gates, moe_in, grad_out)
    row = pl.BlockSpec((1, ROWS), lambda j: (0, 0))
    tile = pl.BlockSpec((ROWS, step), lambda j: (0, j))
    return call(
        pack_body,
        "pack",
        outs,
        ins,
        2 * 384 * 256 * 4096,
        5 << 20,
        grid=(WIDTH // step,),
        in_specs=[scalars(), row, row, tile, tile],
        out_specs=[pl.BlockSpec((Y * CAP, ROWS), lambda j: (0, 0))]
        + [pl.BlockSpec((2, CAP, step), lambda j: (0, 0, j))] * Y,
        scratch=[VMEM((ROWS, 1), f32)],
        limit=16,
    )


BACK = WIDTH + 128
N = Y * CAP
BUNDLE = 2 * WIDTH + 3 * FF
GB, HID = 2 * WIDTH, 2 * WIDTH + 2 * FF
STEP = 256


def expert_body(r0, r1, r2, r3, wp_hbm, wb_hbm, b0, b1, b2, b3, out_hbm, held, back, wp, wb, in_sem, w_sem, out_sem):
    arrived = (r0, r1, r2, r3)
    backs = (b0, b1, b2, b3)
    tiles = FF // STEP

    def incoming(half, s):
        dst = held.at[pl.ds(s * CAP, CAP), pl.ds(half * WIDTH, WIDTH)]
        return pltpu.make_async_copy(arrived[s].at[half], dst, in_sem.at[half * Y + s])

    def weight(j):
        cols, ups = pl.ds(j * STEP, STEP), pl.ds(FF + j * STEP, STEP)
        return (
            pltpu.make_async_copy(wp_hbm.at[0, :, cols], wp.at[:, cols], w_sem.at[3 * j]),
            pltpu.make_async_copy(wp_hbm.at[0, :, ups], wp.at[:, ups], w_sem.at[3 * j + 1]),
            pltpu.make_async_copy(wb_hbm.at[0, cols, :], wb.at[cols, :], w_sem.at[3 * j + 2]),
        )

    for s in range(Y):
        incoming(0, s).start()
    first_tile = weight(0)
    first_tile[0].start()
    first_tile[1].start()
    for s in range(Y):
        incoming(1, s).start()
    first_tile[2].start()
    for j in range(1, tiles):
        for copy in weight(j):
            copy.start()
    for s in range(Y):
        incoming(0, s).wait()
    total = jnp.zeros((N, 1), f32)
    for j in range(tiles):
        at, up = j * STEP, FF + j * STEP
        copies = weight(j)
        copies[0].wait()
        first = dot(held[:, :WIDTH], wp[:, at : at + STEP])
        copies[1].wait()
        second = dot(held[:, :WIDTH], wp[:, up : up + STEP])
        if j == 0:
            for s in range(Y):
                incoming(1, s).wait()
            rows_out = pltpu.make_async_copy(held.at[:, pl.ds(0, GB)], out_hbm.at[:, pl.ds(0, GB)], out_sem.at[0])
            rows_out.start()
        copies[2].wait()
        grad_hidden = dot_t(held[:, WIDTH:GB], wb[at : at + STEP, :])
        s = 1.0 / (1.0 + jnp.exp(-first))
        silu = first * s
        hidden = (silu * second).astype(bf16)
        held[:, HID + at : HID + at + STEP] = hidden
        total += jnp.sum(hidden.astype(f32) * grad_hidden, axis=1, keepdims=True)
        slope = s * (1.0 + first * (1.0 - s))
        held[:, GB + at : GB + at + STEP] = (grad_hidden * second * slope).astype(bf16)
        held[:, GB + up : GB + up + STEP] = (grad_hidden * silu).astype(bf16)
    rest = pl.ds(GB, BUNDLE - GB)
    grads_out = pltpu.make_async_copy(held.at[:, rest], out_hbm.at[:, rest], out_sem.at[1])
    grads_out.start()
    hi, lo = split(total)
    lane = lax.broadcasted_iota(jnp.int32, (N, 128), 1)
    back[:, WIDTH:] = jnp.where(lane == 0, hi.astype(f32), lo.astype(f32)).astype(bf16)
    outgoing = []
    bounds = (0, WIDTH // 2, BACK)
    for part in range(2):
        lo_col, hi_col = bounds[part], bounds[part + 1]
        for at in range(lo_col, min(hi_col, WIDTH), STEP):
            back[:, at : at + STEP] = dot_t(held[:, GB:HID], wp[at : at + STEP, :]).astype(bf16)
        cols = pl.ds(lo_col, hi_col - lo_col)
        for s in range(Y):
            src = back.at[pl.ds(s * CAP, CAP), cols]
            copy = pltpu.make_async_copy(src, backs[s].at[:, cols], out_sem.at[2 + part * Y + s])
            copy.start()
            outgoing.append(copy)
    rows_out.wait()
    grads_out.wait()
    for copy in outgoing:
        copy.wait()


def anywhere():
    return pl.BlockSpec(memory_space=pl.ANY)


def expert(chunks, w_pair, w_back):
    outs = [((CAP, BACK), bf16)] * Y + [((N, BUNDLE), bf16)]
    ins = (*chunks, w_pair, w_back)
    return call(
        expert_body,
        "expert",
        outs,
        ins,
        5 * 2 * N * WIDTH * FF,
        14 << 20,
        in_specs=[anywhere() for _ in ins],
        out_specs=[anywhere() for _ in outs],
        scratch=[
            VMEM((N, BUNDLE), bf16),
            VMEM((N, BACK), bf16),
            VMEM((WIDTH, 2 * FF), bf16),
            VMEM((FF, WIDTH), bf16),
            pltpu.SemaphoreType.DMA((2 * Y,)),
            pltpu.SemaphoreType.DMA((3 * FF // STEP,)),
            pltpu.SemaphoreType.DMA((2 + 2 * Y,)),
        ],
        limit=32,
        free=(1, 2, 3),
    )


def chooser(core, wide, run):
    row = lax.broadcasted_iota(jnp.int32, (wide, wide // 2), 0)
    col = lax.broadcasted_iota(jnp.int32, (wide, wide // 2), 1)
    return (row == (col // run) * (2 * run) + core * run + col % run).astype(bf16)


def weights_body(core_ref, ra, sa, ga, ha, rb, sb, gb, hb, out_ref):
    core = core_ref[0]
    pick_row, pick_hid = chooser(core, 512, 64), chooser(core, 128, 16)
    up = down = None
    for r, s, g, h in ((ra, sa, ga, ha), (rb, sb, gb, hb)):
        rows = dot(r[...], pick_row).astype(bf16)
        hid = dot(h[...], pick_hid).astype(bf16)
        more_up, more_down = t_dot(rows, g[...]), t_dot(hid, s[...])
        up = more_up if up is None else up + more_up
        down = more_down if down is None else down + more_down
    up, down = up.astype(bf16), down.astype(bf16)
    for k in range(X):
        out_ref[k, :64, :] = up[k * 64 : k * 64 + 64]
        out_ref[k, 64:80, :] = down[k * 16 : k * 16 + 16, :1024]
        out_ref[k, 80:96, :] = down[k * 16 : k * 16 + 16, 1024:]


def weights(core, mine, other):
    specs = [
        pl.BlockSpec((N, 512), lambda i: (0, i)),
        pl.BlockSpec((N, WIDTH), lambda i: (0, 1)),
        pl.BlockSpec((N, 2 * FF), lambda i: (0, GB // (2 * FF))),
        pl.BlockSpec((N, 128), lambda i: (0, HID // 128 + i)),
    ]
    return call(
        weights_body,
        "weights",
        [((Z * X, 96, 1024), bf16)],
        (core, *([mine] * 4), *([other] * 4)),
        3 * 2 * N * WIDTH * FF,
        12 << 20,
        grid=(Z,),
        in_specs=[scalars()] + specs + specs,
        out_specs=[pl.BlockSpec((X, 96, 1024), lambda i: (i, 0, 0))],
        limit=32,
    )[0]


def gather_sum_body(pieces_ref, up_ref, down_ref):
    for j in range(2):
        at = j * 512
        total = pieces_ref[0, :, at : at + 512].astype(f32)
        for k in range(1, Z * X):
            total = total + pieces_ref[k, :, at : at + 512].astype(f32)
        up_ref[0, :, at : at + 512] = total[:64]
        down_ref[0, :, at : at + 512] = total[64:80]
        down_ref[0, :, 1024 + at : 1024 + at + 512] = total[80:96]


def project_body(*refs):
    own, rest, place_hbm, gate, cot_hbm, r0, r1, r2, r3, resid_hbm, gates, o0, o1, o2, o3 = refs[:15]
    place, cot, back, w, resid, outs, in_sem, w_sem, out_sem = refs[15:]
    copies = [
        pltpu.make_async_copy(r, back.at[pl.ds(s * CAP, CAP), :], in_sem.at[s]) for s, r in enumerate((r0, r1, r2, r3))
    ]
    copies.append(pltpu.make_async_copy(place_hbm, place, in_sem.at[4]))
    copies.append(pltpu.make_async_copy(cot_hbm, cot, in_sem.at[5]))
    slabs = [pltpu.make_async_copy(own, w.at[0], w_sem.at[0])]
    for s in range(1, Y):
        slabs.append(pltpu.make_async_copy(rest.at[:, s - 1], w.at[s].reshape(rest.shape[0], -1, WIDTH), w_sem.at[s]))
    for copy in copies + slabs:
        copy.start()
    for copy in copies:
        copy.wait()
    wide = 512
    for j in range(WIDTH // wide):
        cols = slice(j * wide, (j + 1) * wide)
        resid[:, cols] = (cot[:, cols].astype(f32) + t_dot(place[...], back[:, cols])).astype(bf16)
    sent = [pltpu.make_async_copy(resid, resid_hbm, out_sem.at[4])]
    sent[0].start()
    tail = back[:, WIDTH:].astype(f32)
    picked = jnp.sum(place[...].astype(f32) * (tail[:, 0:1] + tail[:, 1:2]), axis=0, keepdims=True)
    gates[...] = (picked / gate[...].astype(f32)).astype(bf16)
    for s, out in enumerate((o0, o1, o2, o3)):
        slabs[s].wait()
        outs[s] = dot_t(resid[...], w[s]).astype(bf16)
        copy = pltpu.make_async_copy(outs.at[s], out, out_sem.at[s])
        copy.start()
        sent.append(copy)
    for copy in sent:
        copy.wait()


def project(w_out, rest, place, gate_row, grad_out, backs):
    shapes = [(ROWS, WIDTH), (1, ROWS)] + [(ROWS, 512)] * Y
    ins = (w_out, rest, place, gate_row, grad_out, *backs)
    in_specs, out_specs = [anywhere() for _ in ins], [anywhere() for _ in shapes]
    in_specs[3], out_specs[1] = full(), full()
    return call(
        project_body,
        "project",
        [(s, bf16) for s in shapes],
        ins,
        2 * ROWS * WIDTH * WIDTH + 2 * ROWS * N * WIDTH,
        10 << 20,
        in_specs=in_specs,
        out_specs=out_specs,
        scratch=[
            VMEM((N, ROWS), bf16),
            VMEM((ROWS, WIDTH), bf16),
            VMEM((N, BACK), bf16),
            VMEM((Y, 512, WIDTH), bf16),
            VMEM((ROWS, WIDTH), bf16),
            VMEM((Y, ROWS, 512), bf16),
            pltpu.SemaphoreType.DMA((6,)),
            pltpu.SemaphoreType.DMA((Y,)),
            pltpu.SemaphoreType.DMA((Y + 1,)),
        ],
        limit=32,
    )


def state_body(at_ref, g0, g1, g2, g3, q_ref, grad_ref, state_ref):
    y, block = at_ref[0], at_ref[1]
    ramp = lax.broadcasted_iota(jnp.int32, (ROWS, 1), 0)
    sums = [jnp.zeros((HD, 2 * HD), f32) for _ in range(HEADS)]
    for s, g in enumerate((g0, g1, g2, g3)):
        off = pl.multiple_of(lax.rem(y + s, Y) * ROWS, ROWS)
        inverse = 1.0 / (3 * BLOCKS * TOK + block * TOK + off + ramp + 1).astype(f32)
        grad_ref[pl.ds(off, ROWS), :] = g[...]
        for h in range(HEADS):
            cols = slice(h * HD, (h + 1) * HD)
            hi, lo = split(g[:, cols].astype(f32) * inverse)
            both = jnp.concatenate([hi, lo], axis=1)
            sums[h] += t_dot(q_ref[pl.ds(off, ROWS), cols], both)
    for h in range(HEADS):
        state_ref[h * HD : (h + 1) * HD, :] = sums[h][:, :HD] + sums[h][:, HD:]


SUB = 256
PARTS = TOK // SUB
PAIR = 2


def triangle(lower):
    row = lax.broadcasted_iota(jnp.int32, (SUB, SUB), 0)
    col = lax.broadcasted_iota(jnp.int32, (SUB, SUB), 1)
    return (col <= row) if lower else (col >= row)


def query_part(block, h, g_ref, v_ref, k_ref, prior_ref, out_ref):
    mask = triangle(True)
    ramp = lax.broadcasted_iota(jnp.int32, (SUB, 1), 0)
    cols = slice(h * HD, (h + 1) * HD)
    prior = jnp.concatenate(split(prior_ref[h]), axis=0)
    for i in range(PARTS):
        rows, upto = slice(i * SUB, (i + 1) * SUB), (i + 1) * SUB
        g = g_ref[rows, cols]
        mix = dot_t(g, v_ref[:upto, cols])
        edge = jnp.where(mask, mix[:, i * SUB :], 0.0).astype(bf16)
        if i:
            edge = jnp.concatenate([mix[:, : i * SUB].astype(bf16), edge], axis=1)
        before = dot_t(g, prior)
        total = before[:, :HD] + before[:, HD:] + dot(edge, k_ref[:upto, cols])
        count = (3 * BLOCKS * TOK + block * TOK + i * SUB + ramp + 1).astype(f32)
        out_ref[rows, cols] = (total / count).astype(bf16)


def later_part(block, h, a_ref, b_ref, c_ref, out_ref):
    mask = triangle(False)
    ramp = lax.broadcasted_iota(jnp.int32, (1, TOK), 1)
    inverse = 1.0 / (3 * BLOCKS * TOK + block * TOK + ramp + 1).astype(f32)
    cols = slice(h * HD, (h + 1) * HD)
    for i in range(PARTS):
        at = i * SUB
        rows = slice(at, at + SUB)
        mix = dot_t(a_ref[rows, cols], b_ref[at:, cols]) * inverse[:, at:]
        edge = jnp.where(mask, mix[:, :SUB], 0.0).astype(bf16)
        if i < PARTS - 1:
            edge = jnp.concatenate([edge, mix[:, SUB:].astype(bf16)], axis=1)
        out_ref[rows, cols] = dot(edge, c_ref[at:, cols])


def query_key_body(at_ref, q_ref, k_ref, v_ref, g_ref, prior_ref, out_ref, key_ref):
    block = at_ref[1]
    for h in range(PAIR):
        query_part(block, h, g_ref, v_ref, k_ref, prior_ref, out_ref)
        later_part(block, h, v_ref, g_ref, q_ref, key_ref)


def value_body(at_ref, q_ref, k_ref, g_ref, value_ref):
    for h in range(PAIR):
        later_part(at_ref[1], h, k_ref, q_ref, g_ref, value_ref)


def head_call(body, name, ins, out_types, prior=None):
    cols = pl.BlockSpec((TOK, PAIR * HD), lambda h: (0, h))
    specs = [scalars()] + [cols] * (len(ins) - 1)
    if prior is not None:
        specs.append(pl.BlockSpec((PAIR, HD, HD), lambda h: (h, 0, 0)))
        ins = (*ins, prior)
    return call(
        body,
        name,
        [((TOK, HEADS * HD), t) for t in out_types],
        ins,
        10 * HEADS * 4 * SUB * SUB * HD * len(out_types),
        6 << 20,
        grid=(HEADS // PAIR,),
        in_specs=specs,
        out_specs=[cols] * len(out_types),
    )


def final_body(spot_ref, other, x1, x2, x3, z1, z2, z3, v_ref, k_ref, key_ref, value_ref, out_key, out_value):
    z, x, core = spot_ref[0], spot_ref[1], spot_ref[2]
    later = jnp.where(core == 0, other[...], 0.0)
    for s, a, b in ((1, x1, z1), (2, x2, z2), (3, x3, z3)):
        later += jnp.where(s > x, a[...].astype(f32), 0.0) + jnp.where(s > z, b[...].astype(f32), 0.0)
    hi, lo = split(later)
    key = dot_t(v_ref[...], jnp.concatenate([hi, lo], axis=0))
    out_key[...] = (key_ref[...] + key[:, :HD] + key[:, HD:]).astype(bf16)
    value = dot(k_ref[...], jnp.concatenate([hi, lo], axis=1))
    out_value[...] = (value_ref[...] + value[:, :HD] + value[:, HD:]).astype(bf16)


def final(spot, sums, values, keys, key_here, value_here):
    cols = pl.BlockSpec((TOK, HD), lambda h: (0, h))
    return call(
        final_body,
        "final",
        [((TOK, HEADS * HD), bf16)] * 2,
        (spot, *sums, values, keys, key_here, value_here),
        HEADS * 8 * TOK * HD * HD,
        8 << 20,
        grid=(HEADS,),
        in_specs=[scalars()] + [pl.BlockSpec((HD, HD), lambda h: (h, 0))] * 7 + [cols] * 4,
        out_specs=[cols, cols],
        free=range(1, 8),
    )


def index(z, x, c):
    return (z * X + x) * C + c


def spots():
    return [(z, x, c) for z in range(Z) for x in range(X) for c in range(C)]


def along_y(a, s):
    return lax.ppermute(a, "exp", [(i, (i + s) % Y) for i in range(Y)])


def along_x(a, s):
    return lax.ppermute(a, "ctx", [(index(z, x, c), index(z, (x + s) % X, c)) for z, x, c in spots()])


def along_z(a, s):
    return lax.ppermute(a, "ctx", [(index(z, x, c), index((z + s) % Z, x, c)) for z, x, c in spots()])


def across(a):
    return lax.ppermute(a, "ctx", [(i, i ^ 1) for i in range(BLOCKS)])


def on_device(
    attn_query,
    attn_key,
    attn_value,
    prefix_state,
    moe_in,
    grad_out,
    router_gates,
    expert_ids,
    w_gate_up,
    w_down,
    w_out,
):
    y = lax.axis_index("exp")
    block = lax.axis_index("ctx")
    z, x, c = block >> 3, (block >> 1) & 3, block & 1
    at = jnp.stack([y, block]).astype(jnp.int32)
    spot = jnp.stack([z, x, c]).astype(jnp.int32)
    core = c.astype(jnp.int32)[None]

    slab = w_out.shape[0] // BLOCKS
    piece = lax.dynamic_slice_in_dim(w_out, block * slab, slab, 0)
    pieces = jnp.concatenate([along_y(piece, s) for s in (1, 2, 3)], axis=0)
    gate_row = router_gates.reshape(1, ROWS)
    place, *chunks = pack(at, expert_ids.reshape(1, ROWS), gate_row, moe_in, grad_out)
    pieces, chunks[1] = lax.optimization_barrier((pieces, chunks[1]))
    rest = lax.all_gather(pieces[None], "ctx", axis=0, tiled=True)
    rest = rest.reshape(BLOCKS, 3, slab, WIDTH)

    held = [chunks[0]] + [along_y(chunks[s], s) for s in (1, 2, 3)]
    b0, b1, b2, b3, bundle = expert(held, w_gate_up, w_down)
    backs = [b0] + [along_y(b, -s) for s, b in ((1, b1), (2, b2), (3, b3))]
    other_bundle, backs[1] = lax.optimization_barrier((across(bundle), backs[1]))
    partial = weights(core, bundle, other_bundle)
    groups = [[index(i, j, k) for i in range(Z) for j in range(X)] for k in range(C)]
    exchanged = lax.all_to_all(partial, "ctx", 0, 0, axis_index_groups=groups, tiled=True)

    grad_resid, gates_out, *per_head = project(w_out, rest, place, gate_row, grad_out, backs)
    grad_gates = gates_out.reshape(ROWS, 1)
    grads = [per_head[0]] + [along_y(per_head[s], -s) for s in (1, 2, 3)]
    attn_grad, state = call(
        state_body,
        "state",
        [((TOK, HEADS * HD), bf16), ((HEADS * HD, HD), f32)],
        (at, *grads, attn_query),
        HEADS * 2 * TOK * HD * 2 * HD,
        4 << 20,
        in_specs=[scalars()] + [full()] * 5,
        free=(2, 3, 4),
    )

    other = across(state)
    chip = state + other
    chip16 = chip.astype(bf16)
    from_x = [along_x(chip16, s) for s in (1, 2, 3)]
    line = chip + from_x[0].astype(f32) + from_x[1].astype(f32) + from_x[2].astype(f32)
    line16 = line.astype(bf16)
    ins = (at, attn_query, attn_key, attn_value, attn_grad)
    grad_query, key_here = head_call(query_key_body, "query_key", ins, (bf16, f32), prefix_state[0])
    line16, key_here = lax.optimization_barrier((line16, key_here))
    from_z = [along_z(line16, s) for s in (1, 2, 3)]

    (value_here,) = head_call(value_body, "value", (at, attn_query, attn_key, attn_grad), (f32,))
    sums = (other, *from_x, *from_z)
    grad_key, grad_value = final(spot, sums, attn_value, attn_key, key_here, value_here)

    exchanged, grad_key = lax.optimization_barrier((exchanged, grad_key))
    outs = [((1, 64, 1024), f32), ((1, 16, WIDTH), f32)]
    grad_gate_up, grad_down = call(gather_sum_body, "gather_sum", outs, (exchanged,), 0, 4 << 20, free=(0,))
    return (grad_query, grad_key, grad_value, grad_resid, grad_gates, grad_gate_up, grad_down)


def solution(mesh):
    whole = P(("ctx", "exp"), None)
    split_cols = P("ctx", "exp")
    return jax.shard_map(
        on_device,
        mesh=mesh,
        in_specs=(
            split_cols,
            split_cols,
            split_cols,
            P("ctx", "exp", None, None),
            whole,
            whole,
            whole,
            whole,
            P("exp", None, None),
            P("exp", None, None),
            P("exp", None),
        ),
        out_specs=(
            split_cols,
            split_cols,
            split_cols,
            whole,
            whole,
            P("exp", "ctx", None),
            P("exp", "ctx", None),
        ),
        check_vma=False,
    )
```

time: 211 us -> 174 us (0.82)
  local copies, waits for them, and re-layouts: 36.7 us -> 0.85 us
  Pallas kernels: 40.3 us -> 60.5 us
  waiting for transfers between devices: 74.6 us -> 61.3 us
  other arithmetic: 8.82 us -> 1.92 us
    unnamed x78 -> x2, local copies, waits for them, and re-layouts: 35.8 us -> 0.01 us
    pallas_call x10 -> x9, Pallas kernels: 40.3 us -> 60.5 us  [call(): pl.pallas_call(body, name=name, out_shape=[pltpu.HBM(s, t) for s, t in ou...]
    ppermute x3, waiting for transfers between devices: 18.4 us -> 3.13 us  [along_x(): lax.ppermute(a, 'ctx', [(index(z, x, c), index(z, (x + s) % X, c)) for z,...]
    convert_element_type x1 -> x0, other arithmetic: 5.1 us -> none  [on_device(): folded = (keep.astype(f32) + recv.astype(f32)).astype(bf16)]
  transfers between devices with their start and end apart: 22 -> 22, of which waited for: 10 -> 8; matrix products, arithmetic and copies ran while one was open for 1% -> 1% of each run, Pallas kernels for 19% -> 34%
where the time goes in v3:
time: 174 us; the launch traced here: 173 us
  waiting for transfers between devices  61.3 us (35%)
  Pallas kernels  60.5 us (35%)
  starting transfers between devices  34.8 us (20%)
  between operations  14.1 us (8%)
  other arithmetic  1.92 us (1%)
    pallas_call x9, Pallas kernels, call(): pl.pallas_call(body, name=name, out_shape=[pltpu.HBM(s, t) for s, t in ou...  60.5 us
    ppermute x12, waiting for transfers between devices, along_y(): return lax.ppermute(a, 'exp', [(i, (i + s) % Y) for i in range(Y)])  56.5 us
    ppermute x12, starting transfers between devices, along_y(): return lax.ppermute(a, 'exp', [(i, (i + s) % Y) for i in range(Y)])  14.9 us
    all_to_all x1, starting transfers between devices, on_device(): lax.all_to_all(partial, 'ctx', 0, 0, axis_index_groups=groups, tiled=True)  7.79 us
    ppermute x3, starting transfers between devices, along_z(): lax.ppermute(a, 'ctx', [(index(z, x, c), index((z + s) % Z, x, c)) for z,...  5.87 us
    ppermute x3, starting transfers between devices, along_x(): lax.ppermute(a, 'ctx', [(index(z, x, c), index(z, (x + s) % X, c)) for z,...  5.83 us
  transfers between devices with their start and end apart: 22, of which 8 were waited for; matrix products, arithmetic and copies ran while one was open for 1% of the time, Pallas kernels for 34%

profile of v3, /device:TPU:0, one launch (start us, length us, event | category | flops | bytes accessed | tf_op | source)
XLA Modules:
  0.0 173.5 jit_solution(6282656863207410932)
XLA Ops:
  8.1 1.7 collective-permute-start
  9.7 2.9 %collective-permute-start.1 = (bf16[16,2048]{1,0:T(8,128)(2,1)S(1)}, bf16[16,2048]{1,0:T(8,128)(2,1)S(1)}, u32[]{:S(2)}, u32[]{:S(2)}) collective-permute-start(bf16[16,2048]{1,0:T(8,128)(2,1)S(1)} %constant_dynamic-slice_fusion), channel_id=1, source_target_pairs={{0,2},{1,3},{2,0},{3,1},{4,6},{5,7},{6,4},{7,5},{8,10},{9,11},{10,... | collective-permute-start | bytes 196616 | tf_op jit(solution)/shard_map/ppermute | solution.py:470
  14.1 4.7 %pack.1 = (bf16[384,256]{1,0:T(8,128)(2,1)}, bf16[2,96,2048]{2,1,0:T(8,128)(2,1)}, bf16[2,96,2048]{2,1,0:T(8,128)(2,1)}, bf16[2,96,2048]{2,1,0:T(8,128)(2,1)}, bf16[2,96,2048]{2,1,0:T(8,128)(2,1)}) custom-call(s32[2]{0:T(128)S(1)} %pad_add_fusion.at_ref, s32[1,256]{1,0:T(1,128)} %bitcast.12, bf16[1,256]{1,0:T(2,128)(2,1)} %bitcast.13, ...), custom_call_target="tpu_custom_call" | custom-call | flops 3221225472 | bytes 20971520 | tf_op jit(solution)/shard_map/pack/pallas_call | solution.py:50
  19.9 3.1 %collective-permute-start.5 = (bf16[2,96,2048]{2,1,0:T(8,128)(2,1)}, bf16[2,96,2048]{2,1,0:T(8,128)(2,1)S(1)}, u32[]{:S(2)}, u32[]{:S(2)}) collective-permute-start(bf16[2,96,2048]{2,1,0:T(8,128)(2,1)} %get-tuple-element.45), channel_id=1, source_target_pairs={{0,3},{1,0},{2,1},{3,2},{4,7},{5,4},{6,5},{7,6},{8,11},{9,8},{10,9... | collective-permute-start | bytes 2359304 | tf_op jit(solution)/shard_map/ppermute | solution.py:470
  23.0 18.9 %collective-permute-done.4.r2 = bf16[2,96,2048]{2,1,0:T(8,128)(2,1)S(1)} collective-permute-done((bf16[2,96,2048]{2,1,0:T(8,128)(2,1)}, bf16[2,96,2048]{2,1,0:T(8,128)(2,1)S(1)}, u32[]{:S(2)}, u32[]{:S(2)}) %collective-permute-start.4) | collective-permute-done | bytes 786464 | tf_op jit(solution)/shard_map/ppermute | solution.py:470
  41.8 12.4 %collective-permute-done.5.r3 = bf16[2,96,2048]{2,1,0:T(8,128)(2,1)S(1)} collective-permute-done((bf16[2,96,2048]{2,1,0:T(8,128)(2,1)}, bf16[2,96,2048]{2,1,0:T(8,128)(2,1)S(1)}, u32[]{:S(2)}, u32[]{:S(2)}) %collective-permute-start.5) | collective-permute-done | bytes 786464 | tf_op jit(solution)/shard_map/ppermute | solution.py:470
  54.3 2.3 %collective-permute-done.3.r1 = bf16[2,96,2048]{2,1,0:T(8,128)(2,1)S(1)} collective-permute-done((bf16[2,96,2048]{2,1,0:T(8,128)(2,1)}, bf16[2,96,2048]{2,1,0:T(8,128)(2,1)S(1)}, u32[]{:S(2)}, u32[]{:S(2)}) %collective-permute-start.3) | collective-permute-done | bytes 786464 | tf_op jit(solution)/shard_map/ppermute | solution.py:470
  56.6 10.2 %expert.1 = (bf16[96,2176]{1,0:T(8,128)(2,1)}, bf16[96,2176]{1,0:T(8,128)(2,1)}, bf16[96,2176]{1,0:T(8,128)(2,1)}, bf16[96,2176]{1,0:T(8,128)(2,1)}, bf16[384,5632]{1,0:T(8,128)(2,1)}) custom-call(bf16[2,96,2048]{2,1,0:T(8,128)(2,1)} %get-tuple-element.42.r0, bf16[2,96,2048]{2,1,0:T(8,128)(2,1)S(1)} %collective-permute-done.3.r1, ...), custom_call_target="tpu_custom_call" | custom-call | flops 16106127360 | bytes 58720256 | tf_op jit(solution)/shard_map/expert/pallas_call | solution.py:50
  69.8 10.0 %collective-permute-done.7.refs_6_ = bf16[96,2176]{1,0:T(8,128)(2,1)S(1)} collective-permute-done((bf16[96,2176]{1,0:T(8,128)(2,1)}, bf16[96,2176]{1,0:T(8,128)(2,1)S(1)}, u32[]{:S(2)}, u32[]{:S(2)}) %collective-permute-start.7) | collective-permute-done | bytes 417824 | tf_op jit(solution)/shard_map/ppermute | solution.py:470
  79.8 10.5 %weights.1 = bf16[16,96,1024]{2,1,0:T(8,128)(2,1)} custom-call(s32[1]{0:T(128)} %bitcast.6.core_ref, bf16[384,5632]{1,0:T(8,128)(2,1)} %get-tuple-element.47.ra.sa.ga.ha, bf16[384,5632]{1,0:T(8,128)(2,1)} %get-tuple-element.47.ra.sa.ga.ha, bf16[384,5632]{1,0:T(8,128)(2,1)} %get-tuple-element.47.ra.sa.ga.ha, bf16[384,5632]{1,0:T(8,128)(2,1)} %get-tuple-element.47.ra.sa.ga.ha, ...), custom_call_target="tpu_custom_call" | custom-call | flops 9663676416 | bytes 50331648 | tf_op jit(solution)/shard_map/weights/pallas_call | solution.py:50
  90.3 7.8 %all-to-all-start = ((bf16[16,96,1024]{2,1,0:T(8,128)(2,1)}), bf16[16,96,1024]{2,1,0:T(8,128)(2,1)S(1)}, u32[]{:S(2)}, u32[]{:S(2)}) async-start(bf16[16,96,1024]{2,1,0:T(8,128)(2,1)} %weights.1), calls=%async_computation | async-start | bytes 6291456 | tf_op jit(solution)/shard_map/all_to_all | solution.py:520
  98.1 9.4 %project.1 = (bf16[256,2048]{1,0:T(8,128)(2,1)}, bf16[1,256]{1,0:T(2,128)(2,1)}, bf16[256,512]{1,0:T(8,128)(2,1)}, bf16[256,512]{1,0:T(8,128)(2,1)}, bf16[256,512]{1,0:T(8,128)(2,1)}, /*index=5*/bf16[256,512]{1,0:T(8,128)(2,1)}) custom-call(bf16[512,2048]{1,0:T(8,128)(2,1)} %refs_0_.1, bf16[32,3,16,2048]{3,2,1,0:T(8,128)(2,1)} %bitcast.10, ...), custom_call_target="tpu_custom_call" | custom-call | flops 10200547328 | bytes 41943040 | tf_op jit(solution)/shard_map/project/pallas_call | solution.py:50
  110.4 9.6 %collective-permute-done.10.g1 = bf16[256,512]{1,0:T(8,128)(2,1)S(1)} collective-permute-done((bf16[256,512]{1,0:T(8,128)(2,1)}, bf16[256,512]{1,0:T(8,128)(2,1)S(1)}, u32[]{:S(2)}, u32[]{:S(2)}) %collective-permute-start.10) | collective-permute-done | bytes 262176 | tf_op jit(solution)/shard_map/ppermute | solution.py:470
  120.0 3.3 %collective-permute-done.12.g3 = bf16[256,512]{1,0:T(8,128)(2,1)S(1)} collective-permute-done((bf16[256,512]{1,0:T(8,128)(2,1)}, bf16[256,512]{1,0:T(8,128)(2,1)S(1)}, u32[]{:S(2)}, u32[]{:S(2)}) %collective-permute-start.12) | collective-permute-done | bytes 262176 | tf_op jit(solution)/shard_map/ppermute | solution.py:470
  123.3 3.1 %state.1 = (bf16[1024,512]{1,0:T(8,128)(2,1)}, f32[512,128]{1,0:T(8,128)}) custom-call(s32[2]{0:T(128)S(1)} %pad_add_fusion.at_ref, bf16[256,512]{1,0:T(8,128)(2,1)} %get-tuple-element.52.g0, bf16[256,512]{1,0:T(8,128)(2,1)S(1)} %collective-permute-done.10.g1, bf16[256,512]{1,0:T(8,128)(2,1)S(1)} %collective-permute-done.11.g2, ...), custom_call_target="tpu_custom_call" | custom-call | flops 1073741824 | bytes 16777216 | tf_op jit(solution)/shard_map/state/pallas_call | solution.py:50
  126.4 1.7 collective-permute-done.13.other
  129.1 1.7 collective-permute-start.14
  130.8 2.7 %collective-permute-start.15 = (bf16[512,128]{1,0:T(8,128)(2,1)S(1)}, bf16[512,128]{1,0:T(8,128)(2,1)S(1)}, u32[]{:S(2)}, u32[]{:S(2)}) collective-permute-start(bf16[512,128]{1,0:T(8,128)(2,1)S(1)} %get-tuple-element.71), channel_id=1, source_target_pairs={{0,16},{4,20},{8,24},{12,28},{16,0},{20,4},{24,8},{28,12},{32,48},... | collective-permute-start | bytes 393224 | tf_op jit(solution)/shard_map/ppermute | solution.py:474
  134.9 9.9 %query_key.1 = (bf16[1024,512]{1,0:T(8,128)(2,1)}, f32[1024,512]{1,0:T(8,128)}) custom-call(s32[2]{0:T(128)S(1)} %pad_add_fusion.at_ref, bf16[1024,512]{1,0:T(8,128)(2,1)} %q_ref.5, bf16[1024,512]{1,0:T(8,128)(2,1)} %k_ref.5, bf16[1024,512]{1,0:T(8,128)(2,1)} %v_ref.3, bf16[1024,512]{1,0:T(8,128)(2,1)} %get-tuple-element.56.g_ref, f32[4,128,128]{2,1,0:T(8,128)} %bitcast.11), custom_call_target="tpu_custom_call" | custom-call | flops 10737418240 | bytes 25165824 | tf_op jit(solution)/shard_map/query_key/pallas_call | solution.py:50
  144.8 3.1 %collective-permute-done.15.x2 = bf16[512,128]{1,0:T(8,128)(2,1)S(1)} collective-permute-done((bf16[512,128]{1,0:T(8,128)(2,1)S(1)}, bf16[512,128]{1,0:T(8,128)(2,1)S(1)}, u32[]{:S(2)}, u32[]{:S(2)}) %collective-permute-start.15) | collective-permute-done | bytes 131104 | tf_op jit(solution)/shard_map/ppermute | solution.py:474
  148.6 2.8 %collective-permute-start.18 = (bf16[512,128]{1,0:T(8,128)(2,1)S(1)}, bf16[512,128]{1,0:T(8,128)(2,1)S(1)}, u32[]{:S(2)}, u32[]{:S(2)}) collective-permute-start(bf16[512,128]{1,0:T(8,128)(2,1)S(1)} %add_convert_fusion), channel_id=1, source_target_pairs={{0,64},{4,68},{8,72},{12,76},{16,80},{20,84},{24,88},{28,92},{32,9... | collective-permute-start | bytes 393224 | tf_op jit(solution)/shard_map/ppermute | solution.py:478
  151.4 2.5 %collective-permute-start.19 = (bf16[512,128]{1,0:T(8,128)(2,1)S(1)}, bf16[512,128]{1,0:T(8,128)(2,1)S(1)}, u32[]{:S(2)}, u32[]{:S(2)}) collective-permute-start(bf16[512,128]{1,0:T(8,128)(2,1)S(1)} %add_convert_fusion), channel_id=1, source_target_pairs={{0,96},{4,100},{8,104},{12,108},{16,112},{20,116},{24,120},{28,124... | collective-permute-start | bytes 393224 | tf_op jit(solution)/shard_map/ppermute | solution.py:478
  153.9 6.1 %value.1.value_ref = f32[1024,512]{1,0:T(8,128)} custom-call(s32[2]{0:T(128)S(1)} %pad_add_fusion.at_ref, bf16[1024,512]{1,0:T(8,128)(2,1)} %q_ref.5, bf16[1024,512]{1,0:T(8,128)(2,1)} %k_ref.5, bf16[1024,512]{1,0:T(8,128)(2,1)} %get-tuple-element.56.g_ref), custom_call_target="tpu_custom_call" | custom-call | flops 5368709120 | bytes 25165824 | tf_op jit(solution)/shard_map/value/pallas_call | solution.py:50
  160.1 5.5 %final.1 = (bf16[1024,512]{1,0:T(8,128)(2,1)}, bf16[1024,512]{1,0:T(8,128)(2,1)}) custom-call(s32[3]{0:T(128)S(1)} %pad_add_fusion.1.spot_ref, f32[512,128]{1,0:T(8,128)S(1)} %collective-permute-done.13.other, bf16[512,128]{1,0:T(8,128)(2,1)S(1)} %collective-permute-done.14.x1, bf16[512,128]{1,0:T(8,128)(2,1)S(1)} %collective-permute-done.15.x2, ...), custom_call_target="tpu_custom_call" | custom-call | flops 2147483648 | bytes 33554432 | tf_op jit(solution)/shard_map/final/pallas_call | solution.py:50
  (38 shorter events, 13.6 us)
Async XLA Ops:
  7.2 90.9 %all-gather.3.cloned.1.call-start = ((), (), s32[]{:S(2)}) async-start(), calls=%async_computation.1 | async-start | bytes 6488064 | tf_op jit(solution)/shard_map/all_gather | solution.py:511
  8.1 10.7 %collective-permute-start = (bf16[16,2048]{1,0:T(8,128)(2,1)S(1)}, bf16[16,2048]{1,0:T(8,128)(2,1)S(1)}, u32[]{:S(2)}, u32[]{:S(2)}) collective-permute-start(bf16[16,2048]{1,0:T(8,128)(2,1)S(1)} %constant_dynamic-slice_fusion), channel_id=1, source_target_pairs={{0,1},{1,2},{2,3},{3,0},{4,5},{5,6},{6,7},{7,4},{8,9},{9,10},{10,1... | collective-permute-start | bytes 196616 | tf_op jit(solution)/shard_map/ppermute | solution.py:470
  9.7 9.0 %collective-permute-start.1 = (bf16[16,2048]{1,0:T(8,128)(2,1)S(1)}, bf16[16,2048]{1,0:T(8,128)(2,1)S(1)}, u32[]{:S(2)}, u32[]{:S(2)}) collective-permute-start(bf16[16,2048]{1,0:T(8,128)(2,1)S(1)} %constant_dynamic-slice_fusion), channel_id=1, source_target_pairs={{0,2},{1,3},{2,0},{3,1},{4,6},{5,7},{6,4},{7,5},{8,10},{9,11},{10,... | collective-permute-start | bytes 196616 | tf_op jit(solution)/shard_map/ppermute | solution.py:470
  12.6 6.2 %collective-permute-start.2 = (bf16[16,2048]{1,0:T(8,128)(2,1)S(1)}, bf16[16,2048]{1,0:T(8,128)(2,1)S(1)}, u32[]{:S(2)}, u32[]{:S(2)}) collective-permute-start(bf16[16,2048]{1,0:T(8,128)(2,1)S(1)} %constant_dynamic-slice_fusion), channel_id=1, source_target_pairs={{0,3},{1,0},{2,1},{3,2},{4,7},{5,4},{6,5},{7,6},{8,11},{9,8},{10,9... | collective-permute-start | bytes 196616 | tf_op jit(solution)/shard_map/ppermute | solution.py:470
  19.5 22.3 %collective-permute-start.4 = (bf16[2,96,2048]{2,1,0:T(8,128)(2,1)}, bf16[2,96,2048]{2,1,0:T(8,128)(2,1)S(1)}, u32[]{:S(2)}, u32[]{:S(2)}) collective-permute-start(bf16[2,96,2048]{2,1,0:T(8,128)(2,1)} %get-tuple-element.44), channel_id=1, source_target_pairs={{0,2},{1,3},{2,0},{3,1},{4,6},{5,7},{6,4},{7,5},{8,10},{9,11},{10,... | collective-permute-start | bytes 2359304 | tf_op jit(solution)/shard_map/ppermute | solution.py:470
  19.9 34.4 %collective-permute-start.5 = (bf16[2,96,2048]{2,1,0:T(8,128)(2,1)}, bf16[2,96,2048]{2,1,0:T(8,128)(2,1)S(1)}, u32[]{:S(2)}, u32[]{:S(2)}) collective-permute-start(bf16[2,96,2048]{2,1,0:T(8,128)(2,1)} %get-tuple-element.45), channel_id=1, source_target_pairs={{0,3},{1,0},{2,1},{3,2},{4,7},{5,4},{6,5},{7,6},{8,11},{9,8},{10,9... | collective-permute-start | bytes 2359304 | tf_op jit(solution)/shard_map/ppermute | solution.py:470
  22.9 33.7 %collective-permute-start.3 = (bf16[2,96,2048]{2,1,0:T(8,128)(2,1)}, bf16[2,96,2048]{2,1,0:T(8,128)(2,1)S(1)}, u32[]{:S(2)}, u32[]{:S(2)}) collective-permute-start(bf16[2,96,2048]{2,1,0:T(8,128)(2,1)} %get-tuple-element.43), channel_id=1, source_target_pairs={{0,1},{1,2},{2,3},{3,0},{4,5},{5,6},{6,7},{7,4},{8,9},{9,10},{10,1... | collective-permute-start | bytes 2359304 | tf_op jit(solution)/shard_map/ppermute | solution.py:470
  66.8 13.0 %collective-permute-start.6 = (bf16[384,5632]{1,0:T(8,128)(2,1)}, bf16[384,5632]{1,0:T(8,128)(2,1)}, u32[]{:S(2)}, u32[]{:S(2)}) collective-permute-start(bf16[384,5632]{1,0:T(8,128)(2,1)} %get-tuple-element.47.ra.sa.ga.ha), channel_id=1, source_target_pairs={{0,4},{4,0},{8,12},{12,8},{16,20},{20,16},{24,28},{28,24},{32,36},... | collective-permute-start | bytes 12976136 | tf_op jit(solution)/shard_map/ppermute | solution.py:482
  67.1 12.7 %collective-permute-start.7 = (bf16[96,2176]{1,0:T(8,128)(2,1)}, bf16[96,2176]{1,0:T(8,128)(2,1)S(1)}, u32[]{:S(2)}, u32[]{:S(2)}) collective-permute-start(bf16[96,2176]{1,0:T(8,128)(2,1)} %get-tuple-element.48), channel_id=1, source_target_pairs={{0,3},{1,0},{2,1},{3,2},{4,7},{5,4},{6,5},{7,6},{8,11},{9,8},{10,9... | collective-permute-start | bytes 1253384 | tf_op jit(solution)/shard_map/ppermute | solution.py:470
  67.6 30.5 %collective-permute-start.8 = (bf16[96,2176]{1,0:T(8,128)(2,1)}, bf16[96,2176]{1,0:T(8,128)(2,1)}, u32[]{:S(2)}, u32[]{:S(2)}) collective-permute-start(bf16[96,2176]{1,0:T(8,128)(2,1)} %get-tuple-element.50), channel_id=1, source_target_pairs={{0,2},{1,3},{2,0},{3,1},{4,6},{5,7},{6,4},{7,5},{8,10},{9,11},{10,... | collective-permute-start | bytes 1253384 | tf_op jit(solution)/shard_map/ppermute | solution.py:470
  69.1 29.0 %collective-permute-start.9 = (bf16[96,2176]{1,0:T(8,128)(2,1)}, bf16[96,2176]{1,0:T(8,128)(2,1)}, u32[]{:S(2)}, u32[]{:S(2)}) collective-permute-start(bf16[96,2176]{1,0:T(8,128)(2,1)} %get-tuple-element.51), channel_id=1, source_target_pairs={{0,1},{1,2},{2,3},{3,0},{4,5},{5,6},{6,7},{7,4},{8,9},{9,10},{10,1... | collective-permute-start | bytes 1253384 | tf_op jit(solution)/shard_map/ppermute | solution.py:470
  79.8 10.5 %copy-start = (bf16[96,2176]{1,0:T(8,128)(2,1)}, bf16[96,2176]{1,0:T(8,128)(2,1)S(1)}, u32[]{:S(2)}) copy-start(bf16[96,2176]{1,0:T(8,128)(2,1)S(1)} %collective-permute-done.7.refs_6_) | copy-start | bytes 1253380
  90.3 75.3 %all-to-all-start = ((bf16[16,96,1024]{2,1,0:T(8,128)(2,1)}), bf16[16,96,1024]{2,1,0:T(8,128)(2,1)S(1)}, u32[]{:S(2)}, u32[]{:S(2)}) async-start(bf16[16,96,1024]{2,1,0:T(8,128)(2,1)} %weights.1), calls=%async_computation | async-start | bytes 6291456 | tf_op jit(solution)/shard_map/all_to_all | solution.py:520
  107.6 12.4 %collective-permute-start.10 = (bf16[256,512]{1,0:T(8,128)(2,1)}, bf16[256,512]{1,0:T(8,128)(2,1)S(1)}, u32[]{:S(2)}, u32[]{:S(2)}) collective-permute-start(bf16[256,512]{1,0:T(8,128)(2,1)} %get-tuple-element.53), channel_id=1, source_target_pairs={{0,3},{1,0},{2,1},{3,2},{4,7},{5,4},{6,5},{7,6},{8,11},{9,8},{10,9... | collective-permute-start | bytes 786440 | tf_op jit(solution)/shard_map/ppermute | solution.py:470
  108.9 11.1 %collective-permute-start.11 = (bf16[256,512]{1,0:T(8,128)(2,1)}, bf16[256,512]{1,0:T(8,128)(2,1)S(1)}, u32[]{:S(2)}, u32[]{:S(2)}) collective-permute-start(bf16[256,512]{1,0:T(8,128)(2,1)} %get-tuple-element.54), channel_id=1, source_target_pairs={{0,2},{1,3},{2,0},{3,1},{4,6},{5,7},{6,4},{7,5},{8,10},{9,11},{10,... | collective-permute-start | bytes 786440 | tf_op jit(solution)/shard_map/ppermute | solution.py:470
  109.4 13.9 %collective-permute-start.12 = (bf16[256,512]{1,0:T(8,128)(2,1)}, bf16[256,512]{1,0:T(8,128)(2,1)S(1)}, u32[]{:S(2)}, u32[]{:S(2)}) collective-permute-start(bf16[256,512]{1,0:T(8,128)(2,1)} %get-tuple-element.55), channel_id=1, source_target_pairs={{0,1},{1,2},{2,3},{3,0},{4,5},{5,6},{6,7},{7,4},{8,9},{9,10},{10,1... | collective-permute-start | bytes 786440 | tf_op jit(solution)/shard_map/ppermute | solution.py:470
  126.3 1.7 %collective-permute-start.13 = (f32[512,128]{1,0:T(8,128)}, f32[512,128]{1,0:T(8,128)S(1)}, u32[]{:S(2)}, u32[]{:S(2)}) collective-permute-start(f32[512,128]{1,0:T(8,128)} %get-tuple-element.59), channel_id=1, source_target_pairs={{0,4},{4,0},{8,12},{12,8},{16,20},{20,16},{24,28},{28,24},{32,36},... | collective-permute-start | bytes 786440 | tf_op jit(solution)/shard_map/ppermute | solution.py:482
  129.1 15.7 %collective-permute-start.14 = (bf16[512,128]{1,0:T(8,128)(2,1)S(1)}, bf16[512,128]{1,0:T(8,128)(2,1)S(1)}, u32[]{:S(2)}, u32[]{:S(2)}) collective-permute-start(bf16[512,128]{1,0:T(8,128)(2,1)S(1)} %get-tuple-element.71), channel_id=1, source_target_pairs={{0,8},{4,12},{8,16},{12,20},{16,24},{20,28},{24,0},{28,4},{32,40},... | collective-permute-start | bytes 393224 | tf_op jit(solution)/shard_map/ppermute | solution.py:474
  130.8 17.1 %collective-permute-start.15 = (bf16[512,128]{1,0:T(8,128)(2,1)S(1)}, bf16[512,128]{1,0:T(8,128)(2,1)S(1)}, u32[]{:S(2)}, u32[]{:S(2)}) collective-permute-start(bf16[512,128]{1,0:T(8,128)(2,1)S(1)} %get-tuple-element.71), channel_id=1, source_target_pairs={{0,16},{4,20},{8,24},{12,28},{16,0},{20,4},{24,8},{28,12},{32,48},... | collective-permute-start | bytes 393224 | tf_op jit(solution)/shard_map/ppermute | solution.py:474
  133.5 14.5 %collective-permute-start.16 = (bf16[512,128]{1,0:T(8,128)(2,1)S(1)}, bf16[512,128]{1,0:T(8,128)(2,1)S(1)}, u32[]{:S(2)}, u32[]{:S(2)}) collective-permute-start(bf16[512,128]{1,0:T(8,128)(2,1)S(1)} %get-tuple-element.71), channel_id=1, source_target_pairs={{0,24},{4,28},{8,0},{12,4},{16,8},{20,12},{24,16},{28,20},{32,56},... | collective-permute-start | bytes 393224 | tf_op jit(solution)/shard_map/ppermute | solution.py:474
  148.0 12.0 %collective-permute-start.17 = (bf16[512,128]{1,0:T(8,128)(2,1)S(1)}, bf16[512,128]{1,0:T(8,128)(2,1)S(1)}, u32[]{:S(2)}, u32[]{:S(2)}) collective-permute-start(bf16[512,128]{1,0:T(8,128)(2,1)S(1)} %add_convert_fusion), channel_id=1, source_target_pairs={{0,32},{4,36},{8,40},{12,44},{16,48},{20,52},{24,56},{28,60},{32,6... | collective-permute-start | bytes 393224 | tf_op jit(solution)/shard_map/ppermute | solution.py:478
  148.6 11.4 %collective-permute-start.18 = (bf16[512,128]{1,0:T(8,128)(2,1)S(1)}, bf16[512,128]{1,0:T(8,128)(2,1)S(1)}, u32[]{:S(2)}, u32[]{:S(2)}) collective-permute-start(bf16[512,128]{1,0:T(8,128)(2,1)S(1)} %add_convert_fusion), channel_id=1, source_target_pairs={{0,64},{4,68},{8,72},{12,76},{16,80},{20,84},{24,88},{28,92},{32,9... | collective-permute-start | bytes 393224 | tf_op jit(solution)/shard_map/ppermute | solution.py:478
  151.4 8.7 %collective-permute-start.19 = (bf16[512,128]{1,0:T(8,128)(2,1)S(1)}, bf16[512,128]{1,0:T(8,128)(2,1)S(1)}, u32[]{:S(2)}, u32[]{:S(2)}) collective-permute-start(bf16[512,128]{1,0:T(8,128)(2,1)S(1)} %add_convert_fusion), channel_id=1, source_target_pairs={{0,96},{4,100},{8,104},{12,108},{16,112},{20,116},{24,120},{28,124... | collective-permute-start | bytes 393224 | tf_op jit(solution)/shard_map/ppermute | solution.py:478
Sparse Core Ops, SparseCore 0:
  19.6 53.1 all-gather.2

commit v4 on v3

--- a/solution.py
+++ b/solution.py
@@ -40,7 +40,7 @@
     return pl.BlockSpec(memory_space=SMEM)
 
 
-def call(body, name, outs, ins, flops=0, moved=0, grid=None, in_specs=None, out_specs=None, limit=24, scratch=(), free=()):
+def call(body, name, outs, ins, flops=0, moved=0, grid=None, in_specs=None, out_specs=None, limit=24, scratch=(), free=(), near=False):
     kwargs = {} if grid is None else {"grid": grid}
     specs = in_specs or [full() for _ in ins]
     ins = [
@@ -50,7 +50,7 @@
     return pl.pallas_call(
         body,
         name=name,
-        out_shape=[pltpu.HBM(s, t) for s, t in outs],
+        out_shape=[(VMEM if near else pltpu.HBM)(s, t) for s, t in outs],
         in_specs=specs,
         out_specs=out_specs or [full() for _ in outs],
         scratch_shapes=scratch,
@@ -60,7 +60,7 @@
     )(*ins)
 
 
-def pack_body(at_ref, ids_ref, gate_ref, moe_ref, cot_ref, place_ref, c0, c1, c2, c3, gate_col):
+def pack_body(at_ref, ids_ref, gate_ref, moe_ref, cot_ref, place_ref, turned_ref, c0, c1, c2, c3, gate_col):
     @pl.when(pl.program_id(0) == 0)
     def _():
         rel = ids_ref[...] - at_ref[0]
@@ -73,6 +73,9 @@
         target = rel * CAP + slot
         places = lax.broadcasted_iota(jnp.int32, (Y * CAP, ROWS), 0)
         place_ref[...] = (places == target).astype(bf16)
+        spots_col = jnp.sum(jnp.where(row == col, target.astype(f32), 0.0), axis=1, keepdims=True)
+        lanes = lax.broadcasted_iota(jnp.int32, (ROWS, Y * CAP), 1)
+        turned_ref[...] = (lanes == spots_col.astype(jnp.int32)).astype(bf16)
         gate = gate_ref[...].astype(f32)
         gate_col[...] = jnp.sum(jnp.where(row == col, gate, 0.0), axis=1, keepdims=True)
 
@@ -85,8 +88,8 @@
 
 
 def pack(at, ids, gates, moe_in, grad_out):
-    step = 512
-    outs = [((Y * CAP, ROWS), bf16)] + [((2, CAP, WIDTH), bf16)] * Y
+    step = 1024
+    outs = [((Y * CAP, ROWS), bf16), ((ROWS, Y * CAP), bf16)] + [((2, CAP, WIDTH), bf16)] * Y
     ins = (at, ids, gates, moe_in, grad_out)
     row = pl.BlockSpec((1, ROWS), lambda j: (0, 0))
     tile = pl.BlockSpec((ROWS, step), lambda j: (0, j))
@@ -99,7 +102,7 @@
         5 << 20,
         grid=(WIDTH // step,),
         in_specs=[scalars(), row, row, tile, tile],
-        out_specs=[pl.BlockSpec((Y * CAP, ROWS), lambda j: (0, 0))]
+        out_specs=[pl.BlockSpec((Y * CAP, ROWS), lambda j: (0, 0)), pl.BlockSpec((ROWS, Y * CAP), lambda j: (0, 0))]
         + [pl.BlockSpec((2, CAP, step), lambda j: (0, 0, j))] * Y,
         scratch=[VMEM((ROWS, 1), f32)],
         limit=16,
@@ -113,7 +116,7 @@
 STEP = 256
 
 
-def expert_body(r0, r1, r2, r3, wp_hbm, wb_hbm, b0, b1, b2, b3, out_hbm, held, back, wp, wb, in_sem, w_sem, out_sem):
+def expert_body(r0, r1, r2, r3, wp, wb, b0, b1, b2, b3, out_hbm, held, back, in_sem, out_sem):
     arrived = (r0, r1, r2, r3)
     backs = (b0, b1, b2, b3)
     tiles = FF // STEP
@@ -122,42 +125,23 @@
         dst = held.at[pl.ds(s * CAP, CAP), pl.ds(half * WIDTH, WIDTH)]
         return pltpu.make_async_copy(arrived[s].at[half], dst, in_sem.at[half * Y + s])
 
-    def weight(j):
-        cols, ups = pl.ds(j * STEP, STEP), pl.ds(FF + j * STEP, STEP)
-        return (
-            pltpu.make_async_copy(wp_hbm.at[0, :, cols], wp.at[:, cols], w_sem.at[3 * j]),
-            pltpu.make_async_copy(wp_hbm.at[0, :, ups], wp.at[:, ups], w_sem.at[3 * j + 1]),
-            pltpu.make_async_copy(wb_hbm.at[0, cols, :], wb.at[cols, :], w_sem.at[3 * j + 2]),
-        )
-
     for s in range(Y):
         incoming(0, s).start()
-    first_tile = weight(0)
-    first_tile[0].start()
-    first_tile[1].start()
     for s in range(Y):
         incoming(1, s).start()
-    first_tile[2].start()
-    for j in range(1, tiles):
-        for copy in weight(j):
-            copy.start()
     for s in range(Y):
         incoming(0, s).wait()
     total = jnp.zeros((N, 1), f32)
     for j in range(tiles):
         at, up = j * STEP, FF + j * STEP
-        copies = weight(j)
-        copies[0].wait()
-        first = dot(held[:, :WIDTH], wp[:, at : at + STEP])
-        copies[1].wait()
-        second = dot(held[:, :WIDTH], wp[:, up : up + STEP])
+        first = dot(held[:, :WIDTH], wp[0, :, at : at + STEP])
+        second = dot(held[:, :WIDTH], wp[0, :, up : up + STEP])
         if j == 0:
             for s in range(Y):
                 incoming(1, s).wait()
             rows_out = pltpu.make_async_copy(held.at[:, pl.ds(0, GB)], out_hbm.at[:, pl.ds(0, GB)], out_sem.at[0])
             rows_out.start()
-        copies[2].wait()
-        grad_hidden = dot_t(held[:, WIDTH:GB], wb[at : at + STEP, :])
+        grad_hidden = dot_t(held[:, WIDTH:GB], wb[0, at : at + STEP, :])
         s = 1.0 / (1.0 + jnp.exp(-first))
         silu = first * s
         hidden = (silu * second).astype(bf16)
@@ -177,7 +161,7 @@
     for part in range(2):
         lo_col, hi_col = bounds[part], bounds[part + 1]
         for at in range(lo_col, min(hi_col, WIDTH), STEP):
-            back[:, at : at + STEP] = dot_t(held[:, GB:HID], wp[at : at + STEP, :]).astype(bf16)
+            back[:, at : at + STEP] = dot_t(held[:, GB:HID], wp[0, at : at + STEP, :]).astype(bf16)
         cols = pl.ds(lo_col, hi_col - lo_col)
         for s in range(Y):
             src = back.at[pl.ds(s * CAP, CAP), cols]
@@ -194,6 +178,29 @@
     return pl.BlockSpec(memory_space=pl.ANY)
 
 
+def fetch_body(wp_hbm, wb_hbm, wp, wb, sem):
+    copies = [pltpu.make_async_copy(wp_hbm, wp, sem.at[0]), pltpu.make_async_copy(wb_hbm, wb, sem.at[1])]
+    for copy in copies:
+        copy.start()
+    for copy in copies:
+        copy.wait()
+
+
+def fetch(w_pair, w_back):
+    return call(
+        fetch_body,
+        "fetch",
+        [(w_pair.shape, bf16), (w_back.shape, bf16)],
+        (w_pair, w_back),
+        0,
+        12 << 20,
+        in_specs=[anywhere(), anywhere()],
+        scratch=[pltpu.SemaphoreType.DMA((2,))],
+        limit=16,
+        near=True,
+    )
+
+
 def expert(chunks, w_pair, w_back):
     outs = [((CAP, BACK), bf16)] * Y + [((N, BUNDLE), bf16)]
     ins = (*chunks, w_pair, w_back)
@@ -204,62 +211,79 @@
         ins,
         5 * 2 * N * WIDTH * FF,
         14 << 20,
-        in_specs=[anywhere() for _ in ins],
+        in_specs=[anywhere() for _ in chunks] + [full(), full()],
         out_specs=[anywhere() for _ in outs],
         scratch=[
             VMEM((N, BUNDLE), bf16),
             VMEM((N, BACK), bf16),
-            VMEM((WIDTH, 2 * FF), bf16),
-            VMEM((FF, WIDTH), bf16),
             pltpu.SemaphoreType.DMA((2 * Y,)),
-            pltpu.SemaphoreType.DMA((3 * FF // STEP,)),
             pltpu.SemaphoreType.DMA((2 + 2 * Y,)),
         ],
         limit=32,
-        free=(1, 2, 3),
+        free=(1, 2, 3, 4, 5),
     )
 
 
 def chooser(core, wide, run):
-    row = lax.broadcasted_iota(jnp.int32, (wide, wide // 2), 0)
-    col = lax.broadcasted_iota(jnp.int32, (wide, wide // 2), 1)
-    return (row == (col // run) * (2 * run) + core * run + col % run).astype(bf16)
-
-
-def weights_body(core_ref, ra, sa, ga, ha, rb, sb, gb, hb, out_ref):
+    row = lax.broadcasted_iota(jnp.int32, (wide // 2, wide), 0)
+    col = lax.broadcasted_iota(jnp.int32, (wide // 2, wide), 1)
+    return (col == (row // run) * (2 * run) + core * run + row % run).astype(bf16)
+
+
+def weights_body(core_ref, mine, other, out_hbm, both, rows_t, hid_t, out, in_sem, out_sem):
     core = core_ref[0]
+    copies = []
+    for part, (lo, hi) in enumerate(((0, WIDTH), (HID, BUNDLE), (GB, HID), (WIDTH, GB))):
+        for k, src in enumerate((mine, other)):
+            cols = pl.ds(lo, hi - lo)
+            copy = pltpu.make_async_copy(src.at[:, cols], both.at[pl.ds(k * N, N), cols], in_sem.at[2 * part + k])
+            copy.start()
+            copies.append(copy)
     pick_row, pick_hid = chooser(core, 512, 64), chooser(core, 128, 16)
-    up = down = None
-    for r, s, g, h in ((ra, sa, ga, ha), (rb, sb, gb, hb)):
-        rows = dot(r[...], pick_row).astype(bf16)
-        hid = dot(h[...], pick_hid).astype(bf16)
-        more_up, more_down = t_dot(rows, g[...]), t_dot(hid, s[...])
-        up = more_up if up is None else up + more_up
-        down = more_down if down is None else down + more_down
-    up, down = up.astype(bf16), down.astype(bf16)
-    for k in range(X):
-        out_ref[k, :64, :] = up[k * 64 : k * 64 + 64]
-        out_ref[k, 64:80, :] = down[k * 16 : k * 16 + 16, :1024]
-        out_ref[k, 80:96, :] = down[k * 16 : k * 16 + 16, 1024:]
+    copies[0].wait()
+    copies[1].wait()
+    for i in range(Z):
+        rows_t[i * 256 : (i + 1) * 256, :] = dot_t(pick_row, both[:, i * 512 : (i + 1) * 512]).astype(bf16)
+    copies[2].wait()
+    copies[3].wait()
+    for i in range(Z):
+        hid_t[i * 64 : (i + 1) * 64, :] = dot_t(pick_hid, both[:, HID + i * 128 : HID + (i + 1) * 128]).astype(bf16)
+    copies[4].wait()
+    copies[5].wait()
+    for j in range(4):
+        up = dot(rows_t[...], both[:, GB + j * STEP : GB + (j + 1) * STEP]).astype(bf16)
+        for k in range(Z * X):
+            out[k, :64, j * STEP : (j + 1) * STEP] = up[k * 64 : (k + 1) * 64]
+    copies[6].wait()
+    copies[7].wait()
+    for j in range(8):
+        down = dot(hid_t[...], both[:, WIDTH + j * STEP : WIDTH + (j + 1) * STEP]).astype(bf16)
+        row, col = 64 + 16 * (j // 4), (j % 4) * STEP
+        for k in range(Z * X):
+            out[k, row : row + 16, col : col + STEP] = down[k * 16 : (k + 1) * 16]
+    result = pltpu.make_async_copy(out, out_hbm, out_sem)
+    result.start()
+    result.wait()
 
 
 def weights(core, mine, other):
-    specs = [
-        pl.BlockSpec((N, 512), lambda i: (0, i)),
-        pl.BlockSpec((N, WIDTH), lambda i: (0, 1)),
-        pl.BlockSpec((N, 2 * FF), lambda i: (0, GB // (2 * FF))),
-        pl.BlockSpec((N, 128), lambda i: (0, HID // 128 + i)),
-    ]
     return call(
         weights_body,
         "weights",
         [((Z * X, 96, 1024), bf16)],
-        (core, *([mine] * 4), *([other] * 4)),
+        (core, mine, other),
         3 * 2 * N * WIDTH * FF,
         12 << 20,
-        grid=(Z,),
-        in_specs=[scalars()] + specs + specs,
-        out_specs=[pl.BlockSpec((X, 96, 1024), lambda i: (i, 0, 0))],
+        in_specs=[scalars(), anywhere(), anywhere()],
+        out_specs=[anywhere()],
+        scratch=[
+            VMEM((2 * N, BUNDLE), bf16),
+            VMEM((1024, 2 * N), bf16),
+            VMEM((256, 2 * N), bf16),
+            VMEM((Z * X, 96, 1024), bf16),
+            pltpu.SemaphoreType.DMA((8,)),
+            pltpu.SemaphoreType.DMA,
+        ],
         limit=32,
     )[0]
 
@@ -276,44 +300,46 @@
 
 
 def project_body(*refs):
-    own, rest, place_hbm, gate, cot_hbm, r0, r1, r2, r3, resid_hbm, gates, o0, o1, o2, o3 = refs[:15]
-    place, cot, back, w, resid, outs, in_sem, w_sem, out_sem = refs[15:]
+    own, rest, place_hbm, turned_hbm, gate, cot_hbm, r0, r1, r2, r3, resid_hbm, gates, o0, o1, o2, o3 = refs[:16]
+    place, turned, cot, back, w, resid, outs, in_sem, w_sem, out_sem = refs[16:]
     copies = [
         pltpu.make_async_copy(r, back.at[pl.ds(s * CAP, CAP), :], in_sem.at[s]) for s, r in enumerate((r0, r1, r2, r3))
     ]
-    copies.append(pltpu.make_async_copy(place_hbm, place, in_sem.at[4]))
+    copies.append(pltpu.make_async_copy(turned_hbm, turned, in_sem.at[4]))
+    late = pltpu.make_async_copy(place_hbm, place, in_sem.at[6])
     copies.append(pltpu.make_async_copy(cot_hbm, cot, in_sem.at[5]))
     slabs = [pltpu.make_async_copy(own, w.at[0], w_sem.at[0])]
     for s in range(1, Y):
         slabs.append(pltpu.make_async_copy(rest.at[:, s - 1], w.at[s].reshape(rest.shape[0], -1, WIDTH), w_sem.at[s]))
-    for copy in copies + slabs:
+    for copy in copies + slabs + [late]:
         copy.start()
     for copy in copies:
         copy.wait()
     wide = 512
     for j in range(WIDTH // wide):
         cols = slice(j * wide, (j + 1) * wide)
-        resid[:, cols] = (cot[:, cols].astype(f32) + t_dot(place[...], back[:, cols])).astype(bf16)
+        resid[:, cols] = (cot[:, cols].astype(f32) + dot(turned[...], back[:, cols])).astype(bf16)
     sent = [pltpu.make_async_copy(resid, resid_hbm, out_sem.at[4])]
     sent[0].start()
-    tail = back[:, WIDTH:].astype(f32)
-    picked = jnp.sum(place[...].astype(f32) * (tail[:, 0:1] + tail[:, 1:2]), axis=0, keepdims=True)
-    gates[...] = (picked / gate[...].astype(f32)).astype(bf16)
     for s, out in enumerate((o0, o1, o2, o3)):
         slabs[s].wait()
         outs[s] = dot_t(resid[...], w[s]).astype(bf16)
         copy = pltpu.make_async_copy(outs.at[s], out, out_sem.at[s])
         copy.start()
         sent.append(copy)
+    late.wait()
+    tail = back[:, WIDTH:].astype(f32)
+    picked = jnp.sum(place[...].astype(f32) * (tail[:, 0:1] + tail[:, 1:2]), axis=0, keepdims=True)
+    gates[...] = (picked / gate[...].astype(f32)).astype(bf16)
     for copy in sent:
         copy.wait()
 
 
-def project(w_out, rest, place, gate_row, grad_out, backs):
+def project(w_out, rest, place, turned, gate_row, grad_out, backs):
     shapes = [(ROWS, WIDTH), (1, ROWS)] + [(ROWS, 512)] * Y
-    ins = (w_out, rest, place, gate_row, grad_out, *backs)
+    ins = (w_out, rest, place, turned, gate_row, grad_out, *backs)
     in_specs, out_specs = [anywhere() for _ in ins], [anywhere() for _ in shapes]
-    in_specs[3], out_specs[1] = full(), full()
+    in_specs[4], out_specs[1] = full(), full()
     return call(
         project_body,
         "project",
@@ -325,12 +351,13 @@
         out_specs=out_specs,
         scratch=[
             VMEM((N, ROWS), bf16),
+            VMEM((ROWS, N), bf16),
             VMEM((ROWS, WIDTH), bf16),
             VMEM((N, BACK), bf16),
             VMEM((Y, 512, WIDTH), bf16),
             VMEM((ROWS, WIDTH), bf16),
             VMEM((Y, ROWS, 512), bf16),
-            pltpu.SemaphoreType.DMA((6,)),
+            pltpu.SemaphoreType.DMA((7,)),
             pltpu.SemaphoreType.DMA((Y,)),
             pltpu.SemaphoreType.DMA((Y + 1,)),
         ],
@@ -341,18 +368,30 @@
 def state_body(at_ref, g0, g1, g2, g3, q_ref, grad_ref, state_ref):
     y, block = at_ref[0], at_ref[1]
     ramp = lax.broadcasted_iota(jnp.int32, (ROWS, 1), 0)
-    sums = [jnp.zeros((HD, 2 * HD), f32) for _ in range(HEADS)]
+    total = jnp.zeros((HD, 2 * HD), f32)
     for s, g in enumerate((g0, g1, g2, g3)):
         off = pl.multiple_of(lax.rem(y + s, Y) * ROWS, ROWS)
         inverse = 1.0 / (3 * BLOCKS * TOK + block * TOK + off + ramp + 1).astype(f32)
         grad_ref[pl.ds(off, ROWS), :] = g[...]
-        for h in range(HEADS):
-            cols = slice(h * HD, (h + 1) * HD)
-            hi, lo = split(g[:, cols].astype(f32) * inverse)
-            both = jnp.concatenate([hi, lo], axis=1)
-            sums[h] += t_dot(q_ref[pl.ds(off, ROWS), cols], both)
-    for h in range(HEADS):
-        state_ref[h * HD : (h + 1) * HD, :] = sums[h][:, :HD] + sums[h][:, HD:]
+        both = jnp.concatenate(split(g[...].astype(f32) * inverse), axis=1)
+        total += t_dot(q_ref[pl.ds(off, ROWS), :], both)
+    state_ref[...] = total[:, :HD] + total[:, HD:]
+
+
+def head_state(at, grads, queries):
+    cols = pl.BlockSpec((TOK, HD), lambda h: (0, h))
+    return call(
+        state_body,
+        "state",
+        [((TOK, HEADS * HD), bf16), ((HEADS * HD, HD), f32)],
+        (at, *grads, queries),
+        HEADS * 2 * TOK * HD * 2 * HD,
+        4 << 20,
+        grid=(HEADS,),
+        in_specs=[scalars()] + [pl.BlockSpec((ROWS, HD), lambda h: (0, h))] * Y + [cols],
+        out_specs=[cols, pl.BlockSpec((HD, HD), lambda h: (h, 0))],
+        free=(2, 3, 4),
+    )
 
 
 SUB = 256
@@ -396,7 +435,7 @@
         edge = jnp.where(mask, mix[:, :SUB], 0.0).astype(bf16)
         if i < PARTS - 1:
             edge = jnp.concatenate([edge, mix[:, SUB:].astype(bf16)], axis=1)
-        out_ref[rows, cols] = dot(edge, c_ref[at:, cols])
+        out_ref[rows, cols] = dot(edge, c_ref[at:, cols]).astype(bf16)
 
 
 def query_key_body(at_ref, q_ref, k_ref, v_ref, g_ref, prior_ref, out_ref, key_ref):
@@ -437,9 +476,9 @@
         later += jnp.where(s > x, a[...].astype(f32), 0.0) + jnp.where(s > z, b[...].astype(f32), 0.0)
     hi, lo = split(later)
     key = dot_t(v_ref[...], jnp.concatenate([hi, lo], axis=0))
-    out_key[...] = (key_ref[...] + key[:, :HD] + key[:, HD:]).astype(bf16)
+    out_key[...] = (key_ref[...].astype(f32) + key[:, :HD] + key[:, HD:]).astype(bf16)
     value = dot(k_ref[...], jnp.concatenate([hi, lo], axis=1))
-    out_value[...] = (value_ref[...] + value[:, :HD] + value[:, HD:]).astype(bf16)
+    out_value[...] = (value_ref[...].astype(f32) + value[:, :HD] + value[:, HD:]).astype(bf16)
 
 
 def final(spot, sums, values, keys, key_here, value_here):
@@ -506,32 +545,26 @@
     piece = lax.dynamic_slice_in_dim(w_out, block * slab, slab, 0)
     pieces = jnp.concatenate([along_y(piece, s) for s in (1, 2, 3)], axis=0)
     gate_row = router_gates.reshape(1, ROWS)
-    place, *chunks = pack(at, expert_ids.reshape(1, ROWS), gate_row, moe_in, grad_out)
+    place, turned, *chunks = pack(at, expert_ids.reshape(1, ROWS), gate_row, moe_in, grad_out)
     pieces, chunks[1] = lax.optimization_barrier((pieces, chunks[1]))
     rest = lax.all_gather(pieces[None], "ctx", axis=0, tiled=True)
     rest = rest.reshape(BLOCKS, 3, slab, WIDTH)
 
     held = [chunks[0]] + [along_y(chunks[s], s) for s in (1, 2, 3)]
-    b0, b1, b2, b3, bundle = expert(held, w_gate_up, w_down)
+    w_pair, chunks[0] = lax.optimization_barrier((w_gate_up, chunks[0]))
+    held[0] = chunks[0]
+    w_pair, w_back = fetch(w_pair, w_down)
+    b0, b1, b2, b3, bundle = expert(held, w_pair, w_back)
     backs = [b0] + [along_y(b, -s) for s, b in ((1, b1), (2, b2), (3, b3))]
     other_bundle, backs[1] = lax.optimization_barrier((across(bundle), backs[1]))
     partial = weights(core, bundle, other_bundle)
     groups = [[index(i, j, k) for i in range(Z) for j in range(X)] for k in range(C)]
     exchanged = lax.all_to_all(partial, "ctx", 0, 0, axis_index_groups=groups, tiled=True)
 
-    grad_resid, gates_out, *per_head = project(w_out, rest, place, gate_row, grad_out, backs)
+    grad_resid, gates_out, *per_head = project(w_out, rest, place, turned, gate_row, grad_out, backs)
     grad_gates = gates_out.reshape(ROWS, 1)
     grads = [per_head[0]] + [along_y(per_head[s], -s) for s in (1, 2, 3)]
-    attn_grad, state = call(
-        state_body,
-        "state",
-        [((TOK, HEADS * HD), bf16), ((HEADS * HD, HD), f32)],
-        (at, *grads, attn_query),
-        HEADS * 2 * TOK * HD * 2 * HD,
-        4 << 20,
-        in_specs=[scalars()] + [full()] * 5,
-        free=(2, 3, 4),
-    )
+    attn_grad, state = head_state(at, grads, attn_query)
 
     other = across(state)
     chip = state + other
@@ -540,11 +573,11 @@
     line = chip + from_x[0].astype(f32) + from_x[1].astype(f32) + from_x[2].astype(f32)
     line16 = line.astype(bf16)
     ins = (at, attn_query, attn_key, attn_value, attn_grad)
-    grad_query, key_here = head_call(query_key_body, "query_key", ins, (bf16, f32), prefix_state[0])
+    grad_query, key_here = head_call(query_key_body, "query_key", ins, (bf16, bf16), prefix_state[0])
     line16, key_here = lax.optimization_barrier((line16, key_here))
     from_z = [along_z(line16, s) for s in (1, 2, 3)]
 
-    (value_here,) = head_call(value_body, "value", (at, attn_query, attn_key, attn_grad), (f32,))
+    (value_here,) = head_call(value_body, "value", (at, attn_query, attn_key, attn_grad), (bf16,))
     sums = (other, *from_x, *from_z)
     grad_key, grad_value = final(spot, sums, attn_value, attn_key, key_here, value_here)
 

time: 174 us -> 167 us (0.960)
  Pallas kernels: 60.5 us -> 56 us
  waiting for transfers between devices: 61.3 us -> 58.6 us
    pallas_call x9 -> x10, Pallas kernels: 60.5 us -> 56 us  [call(): pl.pallas_call(body, name=name, out_shape=[(VMEM if near else pltpu.HBM)(...]
    ppermute x12, waiting for transfers between devices: 56.5 us -> 53.7 us  [along_y(): return lax.ppermute(a, 'exp', [(i, (i + s) % Y) for i in range(Y)])]
  transfers between devices with their start and end apart: 22 -> 22, of which waited for: 8 -> 8; matrix products, arithmetic and copies ran while one was open for 1% -> 1% of each run, Pallas kernels for 34% -> 33%
where the time goes in v4:
time: 167 us; the launch traced here: 166 us
  waiting for transfers between devices  58.6 us (35%)
  Pallas kernels  56 us (34%)
  starting transfers between devices  34.9 us (21%)
  between operations  14.2 us (9%)
  other arithmetic  1.89 us (1%)
    pallas_call x10, Pallas kernels, call(): pl.pallas_call(body, name=name, out_shape=[(VMEM if near else pltpu.HBM)(...  56 us
    ppermute x12, waiting for transfers between devices, along_y(): return lax.ppermute(a, 'exp', [(i, (i + s) % Y) for i in range(Y)])  53.7 us
    ppermute x12, starting transfers between devices, along_y(): return lax.ppermute(a, 'exp', [(i, (i + s) % Y) for i in range(Y)])  14.9 us
    all_to_all x1, starting transfers between devices, on_device(): lax.all_to_all(partial, 'ctx', 0, 0, axis_index_groups=groups, tiled=True)  7.81 us
    ppermute x3, starting transfers between devices, along_z(): lax.ppermute(a, 'ctx', [(index(z, x, c), index((z + s) % Z, x, c)) for z,...  6.08 us
    ppermute x3, starting transfers between devices, along_x(): lax.ppermute(a, 'ctx', [(index(z, x, c), index(z, (x + s) % X, c)) for z,...  5.84 us
  transfers between devices with their start and end apart: 22, of which 8 were waited for; matrix products, arithmetic and copies ran while one was open for 1% of the time, Pallas kernels for 33%

profile of v4, /device:TPU:0, one launch (start us, length us, event | category | flops | bytes accessed | tf_op | source)
XLA Modules:
  0.0 166.4 jit_solution(16835195343028363119)
XLA Ops:
  9.7 2.9 %collective-permute-start.1 = (bf16[16,2048]{1,0:T(8,128)(2,1)S(1)}, bf16[16,2048]{1,0:T(8,128)(2,1)S(1)}, u32[]{:S(2)}, u32[]{:S(2)}) collective-permute-start(bf16[16,2048]{1,0:T(8,128)(2,1)S(1)} %constant_dynamic-slice_fusion), channel_id=1, source_target_pairs={{0,2},{1,3},{2,0},{3,1},{4,6},{5,7},{6,4},{7,5},{8,10},{9,11},{10,... | collective-permute-start | bytes 196616 | tf_op jit(solution)/shard_map/ppermute | solution.py:509
  14.1 3.9 %pack.1 = (bf16[384,256]{1,0:T(8,128)(2,1)}, bf16[256,384]{1,0:T(8,128)(2,1)}, bf16[2,96,2048]{2,1,0:T(8,128)(2,1)}, bf16[2,96,2048]{2,1,0:T(8,128)(2,1)}, bf16[...) custom-call(s32[2]{0:T(128)S(1)} %pad_add_fusion.at_ref, s32[1,256]{1,0:T(1,128)} %bitcast.12, ...), custom_call_target="tpu_custom_call" | custom-call | flops 3221225472 | bytes 20971520 | tf_op jit(solution)/shard_map/pack/pallas_call | solution.py:50
  19.2 2.9 %collective-permute-start.5 = (bf16[2,96,2048]{2,1,0:T(8,128)(2,1)}, bf16[2,96,2048]{2,1,0:T(8,128)(2,1)S(1)}, u32[]{:S(2)}, u32[]{:S(2)}) collective-permute-start(bf16[2,96,2048]{2,1,0:T(8,128)(2,1)} %get-tuple-element.52), channel_id=1, source_target_pairs={{0,3},{1,0},{2,1},{3,2},{4,7},{5,4},{6,5},{7,6},{8,11},{9,8},{10,9... | collective-permute-start | bytes 2359304 | tf_op jit(solution)/shard_map/ppermute | solution.py:509
  22.1 2.9 %fetch.1 = (bf16[1,2048,1024]{2,1,0:T(8,128)(2,1)S(1)}, bf16[1,512,2048]{2,1,0:T(8,128)(2,1)S(1)}) custom-call(bf16[1,2048,1024]{2,1,0:T(8,128)(2,1)} %wp_hbm, bf16[1,512,2048]{2,1,0:T(8,128)(2,1)} %wb_hbm.1), custom_call_target="tpu_custom_call" | custom-call | bytes 50331648 | tf_op jit(solution)/shard_map/fetch/pallas_call | solution.py:50
  25.0 16.0 %collective-permute-done.4.r2 = bf16[2,96,2048]{2,1,0:T(8,128)(2,1)S(1)} collective-permute-done((bf16[2,96,2048]{2,1,0:T(8,128)(2,1)}, bf16[2,96,2048]{2,1,0:T(8,128)(2,1)S(1)}, u32[]{:S(2)}, u32[]{:S(2)}) %collective-permute-start.4) | collective-permute-done | bytes 786464 | tf_op jit(solution)/shard_map/ppermute | solution.py:509
  41.0 12.8 %collective-permute-done.5.r3 = bf16[2,96,2048]{2,1,0:T(8,128)(2,1)S(1)} collective-permute-done((bf16[2,96,2048]{2,1,0:T(8,128)(2,1)}, bf16[2,96,2048]{2,1,0:T(8,128)(2,1)S(1)}, u32[]{:S(2)}, u32[]{:S(2)}) %collective-permute-start.5) | collective-permute-done | bytes 786464 | tf_op jit(solution)/shard_map/ppermute | solution.py:509
  53.8 2.0 %collective-permute-done.3.r1 = bf16[2,96,2048]{2,1,0:T(8,128)(2,1)S(1)} collective-permute-done((bf16[2,96,2048]{2,1,0:T(8,128)(2,1)}, bf16[2,96,2048]{2,1,0:T(8,128)(2,1)S(1)}, u32[]{:S(2)}, u32[]{:S(2)}) %collective-permute-start.3) | collective-permute-done | bytes 786464 | tf_op jit(solution)/shard_map/ppermute | solution.py:509
  55.8 6.7 %expert.1 = (bf16[96,2176]{1,0:T(8,128)(2,1)}, bf16[96,2176]{1,0:T(8,128)(2,1)}, bf16[96,2176]{1,0:T(8,128)(2,1)}, bf16[96,2176]{1,0:T(8,128)(2,1)}, bf16[384,5632]{1,0:T(8,128)(2,1)}) custom-call(bf16[2,96,2048]{2,1,0:T(8,128)(2,1)} %get-tuple-element.49.r0, bf16[2,96,2048]{2,1,0:T(8,128)(2,1)S(1)} %collective-permute-done.3.r1, ...), custom_call_target="tpu_custom_call" | custom-call | flops 16106127360 | bytes 58720256 | tf_op jit(solution)/shard_map/expert/pallas_call | solution.py:50
  65.4 10.0 %collective-permute-done.7.refs_7_ = bf16[96,2176]{1,0:T(8,128)(2,1)S(1)} collective-permute-done((bf16[96,2176]{1,0:T(8,128)(2,1)}, bf16[96,2176]{1,0:T(8,128)(2,1)S(1)}, u32[]{:S(2)}, u32[]{:S(2)}) %collective-permute-start.7) | collective-permute-done | bytes 417824 | tf_op jit(solution)/shard_map/ppermute | solution.py:509
  75.4 8.0 %weights.1 = bf16[16,96,1024]{2,1,0:T(8,128)(2,1)} custom-call(s32[1]{0:T(128)} %bitcast.6.core_ref, bf16[384,5632]{1,0:T(8,128)(2,1)} %get-tuple-element.57.mine, bf16[384,5632]{1,0:T(8,128)(2,1)} %collective-permute-done.6.other), custom_call_target="tpu_custom_call" | custom-call | flops 9663676416 | bytes 50331648 | tf_op jit(solution)/shard_map/weights/pallas_call | solution.py:50
  83.4 7.8 %all-to-all-start = ((bf16[16,96,1024]{2,1,0:T(8,128)(2,1)}), bf16[16,96,1024]{2,1,0:T(8,128)(2,1)S(1)}, u32[]{:S(2)}, u32[]{:S(2)}) async-start(bf16[16,96,1024]{2,1,0:T(8,128)(2,1)} %weights.1), calls=%async_computation | async-start | bytes 6291456 | tf_op jit(solution)/shard_map/all_to_all | solution.py:562
  91.3 8.8 %project.1 = (bf16[256,2048]{1,0:T(8,128)(2,1)}, bf16[1,256]{1,0:T(2,128)(2,1)}, bf16[256,512]{1,0:T(8,128)(2,1)}, bf16[256,512]{1,0:T(8,128)(2,1)}, bf16[256,512]{1,0:T(8,128)(2,1)}, /*index=5*/bf16[256,512]{1,0:T(8,128)(2,1)}) custom-call(bf16[512,2048]{1,0:T(8,128)(2,1)} %refs_0_.1, bf16[32,3,16,2048]{3,2,1,0:T(8,128)(2,1)} %bitcast.10, ...), custom_call_target="tpu_custom_call" | custom-call | flops 10200547328 | bytes 41943040 | tf_op jit(solution)/shard_map/project/pallas_call | solution.py:50
  102.9 9.7 %collective-permute-done.10.g1 = bf16[256,512]{1,0:T(8,128)(2,1)S(1)} collective-permute-done((bf16[256,512]{1,0:T(8,128)(2,1)}, bf16[256,512]{1,0:T(8,128)(2,1)S(1)}, u32[]{:S(2)}, u32[]{:S(2)}) %collective-permute-start.10) | collective-permute-done | bytes 262176 | tf_op jit(solution)/shard_map/ppermute | solution.py:509
  112.6 3.3 %collective-permute-done.12.g3 = bf16[256,512]{1,0:T(8,128)(2,1)S(1)} collective-permute-done((bf16[256,512]{1,0:T(8,128)(2,1)}, bf16[256,512]{1,0:T(8,128)(2,1)S(1)}, u32[]{:S(2)}, u32[]{:S(2)}) %collective-permute-start.12) | collective-permute-done | bytes 262176 | tf_op jit(solution)/shard_map/ppermute | solution.py:509
  115.9 4.0 %state.1 = (bf16[1024,512]{1,0:T(8,128)(2,1)}, f32[512,128]{1,0:T(8,128)}) custom-call(s32[2]{0:T(128)S(1)} %pad_add_fusion.at_ref, bf16[256,512]{1,0:T(8,128)(2,1)} %get-tuple-element.62.g0, bf16[256,512]{1,0:T(8,128)(2,1)S(1)} %collective-permute-done.10.g1, bf16[256,512]{1,0:T(8,128)(2,1)S(1)} %collective-permute-done.11.g2, ...), custom_call_target="tpu_custom_call" | custom-call | flops 1073741824 | bytes 16777216 | tf_op jit(solution)/shard_map/state/pallas_call | solution.py:50
  120.0 1.7 %collective-permute-done.13.other = f32[512,128]{1,0:T(8,128)S(1)} collective-permute-done((f32[512,128]{1,0:T(8,128)}, f32[512,128]{1,0:T(8,128)S(1)}, u32[]{:S(2)}, u32[]{:S(2)}) %collective-permute-start.13) | collective-permute-done | bytes 262176 | tf_op jit(solution)/shard_map/ppermute | solution.py:521
  122.7 1.7 %collective-permute-start.14 = (bf16[512,128]{1,0:T(8,128)(2,1)S(1)}, bf16[512,128]{1,0:T(8,128)(2,1)S(1)}, u32[]{:S(2)}, u32[]{:S(2)}) collective-permute-start(bf16[512,128]{1,0:T(8,128)(2,1)S(1)} %get-tuple-element.81), channel_id=1, source_target_pairs={{0,8},{4,12},{8,16},{12,20},{16,24},{20,28},{24,0},{28,4},{32,40},... | collective-permute-start | bytes 393224 | tf_op jit(solution)/shard_map/ppermute | solution.py:513
  124.4 2.7 %collective-permute-start.15 = (bf16[512,128]{1,0:T(8,128)(2,1)S(1)}, bf16[512,128]{1,0:T(8,128)(2,1)S(1)}, u32[]{:S(2)}, u32[]{:S(2)}) collective-permute-start(bf16[512,128]{1,0:T(8,128)(2,1)S(1)} %get-tuple-element.81), channel_id=1, source_target_pairs={{0,16},{4,20},{8,24},{12,28},{16,0},{20,4},{24,8},{28,12},{32,48},... | collective-permute-start | bytes 393224 | tf_op jit(solution)/shard_map/ppermute | solution.py:513
  128.5 9.6 %query_key.1 = (bf16[1024,512]{1,0:T(8,128)(2,1)}, bf16[1024,512]{1,0:T(8,128)(2,1)}) custom-call(s32[2]{0:T(128)S(1)} %pad_add_fusion.at_ref, bf16[1024,512]{1,0:T(8,128)(2,1)} %q_ref.5, bf16[1024,512]{1,0:T(8,128)(2,1)} %k_ref.5, bf16[1024,512]{1,0:T(8,128)(2,1)} %v_ref.3, bf16[1024,512]{1,0:T(8,128)(2,1)} %get-tuple-element.66.g_ref, f32[4,128,128]{2,1,0:T(8,128)} %bitcast.11), custom_call_target="tpu_custom_call" | custom-call | flops 10737418240 | bytes 25165824 | tf_op jit(solution)/shard_map/query_key/pallas_call | solution.py:50
  138.1 3.2 %collective-permute-done.15.x2 = bf16[512,128]{1,0:T(8,128)(2,1)S(1)} collective-permute-done((bf16[512,128]{1,0:T(8,128)(2,1)S(1)}, bf16[512,128]{1,0:T(8,128)(2,1)S(1)}, u32[]{:S(2)}, u32[]{:S(2)}) %collective-permute-start.15) | collective-permute-done | bytes 131104 | tf_op jit(solution)/shard_map/ppermute | solution.py:513
  142.1 2.9 %collective-permute-start.18 = (bf16[512,128]{1,0:T(8,128)(2,1)S(1)}, bf16[512,128]{1,0:T(8,128)(2,1)S(1)}, u32[]{:S(2)}, u32[]{:S(2)}) collective-permute-start(bf16[512,128]{1,0:T(8,128)(2,1)S(1)} %add_convert_fusion), channel_id=1, source_target_pairs={{0,64},{4,68},{8,72},{12,76},{16,80},{20,84},{24,88},{28,92},{32,9... | collective-permute-start | bytes 393224 | tf_op jit(solution)/shard_map/ppermute | solution.py:517
  145.0 2.4 %collective-permute-start.19 = (bf16[512,128]{1,0:T(8,128)(2,1)S(1)}, bf16[512,128]{1,0:T(8,128)(2,1)S(1)}, u32[]{:S(2)}, u32[]{:S(2)}) collective-permute-start(bf16[512,128]{1,0:T(8,128)(2,1)S(1)} %add_convert_fusion), channel_id=1, source_target_pairs={{0,96},{4,100},{8,104},{12,108},{16,112},{20,116},{24,120},{28,124... | collective-permute-start | bytes 393224 | tf_op jit(solution)/shard_map/ppermute | solution.py:517
  147.4 6.0 %value.1.value_ref = bf16[1024,512]{1,0:T(8,128)(2,1)} custom-call(s32[2]{0:T(128)S(1)} %pad_add_fusion.at_ref, bf16[1024,512]{1,0:T(8,128)(2,1)} %q_ref.5, bf16[1024,512]{1,0:T(8,128)(2,1)} %k_ref.5, bf16[1024,512]{1,0:T(8,128)(2,1)} %get-tuple-element.66.g_ref), custom_call_target="tpu_custom_call" | custom-call | flops 5368709120 | bytes 25165824 | tf_op jit(solution)/shard_map/value/pallas_call | solution.py:50
  153.5 5.0 %final.1 = (bf16[1024,512]{1,0:T(8,128)(2,1)}, bf16[1024,512]{1,0:T(8,128)(2,1)}) custom-call(s32[3]{0:T(128)S(1)} %pad_add_fusion.1.spot_ref, f32[512,128]{1,0:T(8,128)S(1)} %collective-permute-done.13.other, bf16[512,128]{1,0:T(8,128)(2,1)S(1)} %collective-permute-done.14.x1, bf16[512,128]{1,0:T(8,128)(2,1)S(1)} %collective-permute-done.15.x2, ...), custom_call_target="tpu_custom_call" | custom-call | flops 2147483648 | bytes 33554432 | tf_op jit(solution)/shard_map/final/pallas_call | solution.py:50
  (39 shorter events, 15.5 us)
Async XLA Ops:
  7.2 84.1 %all-gather.3.cloned.1.call-start = ((), (), s32[]{:S(2)}) async-start(), calls=%async_computation.1 | async-start | bytes 6488064 | tf_op jit(solution)/shard_map/all_gather | solution.py:550
  8.1 9.9 %collective-permute-start = (bf16[16,2048]{1,0:T(8,128)(2,1)S(1)}, bf16[16,2048]{1,0:T(8,128)(2,1)S(1)}, u32[]{:S(2)}, u32[]{:S(2)}) collective-permute-start(bf16[16,2048]{1,0:T(8,128)(2,1)S(1)} %constant_dynamic-slice_fusion), channel_id=1, source_target_pairs={{0,1},{1,2},{2,3},{3,0},{4,5},{5,6},{6,7},{7,4},{8,9},{9,10},{10,1... | collective-permute-start | bytes 196616 | tf_op jit(solution)/shard_map/ppermute | solution.py:509
  9.7 8.2 %collective-permute-start.1 = (bf16[16,2048]{1,0:T(8,128)(2,1)S(1)}, bf16[16,2048]{1,0:T(8,128)(2,1)S(1)}, u32[]{:S(2)}, u32[]{:S(2)}) collective-permute-start(bf16[16,2048]{1,0:T(8,128)(2,1)S(1)} %constant_dynamic-slice_fusion), channel_id=1, source_target_pairs={{0,2},{1,3},{2,0},{3,1},{4,6},{5,7},{6,4},{7,5},{8,10},{9,11},{10,... | collective-permute-start | bytes 196616 | tf_op jit(solution)/shard_map/ppermute | solution.py:509
  12.6 5.3 %collective-permute-start.2 = (bf16[16,2048]{1,0:T(8,128)(2,1)S(1)}, bf16[16,2048]{1,0:T(8,128)(2,1)S(1)}, u32[]{:S(2)}, u32[]{:S(2)}) collective-permute-start(bf16[16,2048]{1,0:T(8,128)(2,1)S(1)} %constant_dynamic-slice_fusion), channel_id=1, source_target_pairs={{0,3},{1,0},{2,1},{3,2},{4,7},{5,4},{6,5},{7,6},{8,11},{9,8},{10,9... | collective-permute-start | bytes 196616 | tf_op jit(solution)/shard_map/ppermute | solution.py:509
  18.7 22.3 %collective-permute-start.4 = (bf16[2,96,2048]{2,1,0:T(8,128)(2,1)}, bf16[2,96,2048]{2,1,0:T(8,128)(2,1)S(1)}, u32[]{:S(2)}, u32[]{:S(2)}) collective-permute-start(bf16[2,96,2048]{2,1,0:T(8,128)(2,1)} %get-tuple-element.51), channel_id=1, source_target_pairs={{0,2},{1,3},{2,0},{3,1},{4,6},{5,7},{6,4},{7,5},{8,10},{9,11},{10,... | collective-permute-start | bytes 2359304 | tf_op jit(solution)/shard_map/ppermute | solution.py:509
  19.2 34.6 %collective-permute-start.5 = (bf16[2,96,2048]{2,1,0:T(8,128)(2,1)}, bf16[2,96,2048]{2,1,0:T(8,128)(2,1)S(1)}, u32[]{:S(2)}, u32[]{:S(2)}) collective-permute-start(bf16[2,96,2048]{2,1,0:T(8,128)(2,1)} %get-tuple-element.52), channel_id=1, source_target_pairs={{0,3},{1,0},{2,1},{3,2},{4,7},{5,4},{6,5},{7,6},{8,11},{9,8},{10,9... | collective-permute-start | bytes 2359304 | tf_op jit(solution)/shard_map/ppermute | solution.py:509
  22.1 33.7 %collective-permute-start.3 = (bf16[2,96,2048]{2,1,0:T(8,128)(2,1)}, bf16[2,96,2048]{2,1,0:T(8,128)(2,1)S(1)}, u32[]{:S(2)}, u32[]{:S(2)}) collective-permute-start(bf16[2,96,2048]{2,1,0:T(8,128)(2,1)} %get-tuple-element.50), channel_id=1, source_target_pairs={{0,1},{1,2},{2,3},{3,0},{4,5},{5,6},{6,7},{7,4},{8,9},{9,10},{10,1... | collective-permute-start | bytes 2359304 | tf_op jit(solution)/shard_map/ppermute | solution.py:509
  62.5 12.9 %collective-permute-start.6 = (bf16[384,5632]{1,0:T(8,128)(2,1)}, bf16[384,5632]{1,0:T(8,128)(2,1)}, u32[]{:S(2)}, u32[]{:S(2)}) collective-permute-start(bf16[384,5632]{1,0:T(8,128)(2,1)} %get-tuple-element.57.mine), channel_id=1, source_target_pairs={{0,4},{4,0},{8,12},{12,8},{16,20},{20,16},{24,28},{28,24},{32,36},... | collective-permute-start | bytes 12976136 | tf_op jit(solution)/shard_map/ppermute | solution.py:521
  62.7 12.7 %collective-permute-start.7 = (bf16[96,2176]{1,0:T(8,128)(2,1)}, bf16[96,2176]{1,0:T(8,128)(2,1)S(1)}, u32[]{:S(2)}, u32[]{:S(2)}) collective-permute-start(bf16[96,2176]{1,0:T(8,128)(2,1)} %get-tuple-element.58), channel_id=1, source_target_pairs={{0,3},{1,0},{2,1},{3,2},{4,7},{5,4},{6,5},{7,6},{8,11},{9,8},{10,9... | collective-permute-start | bytes 1253384 | tf_op jit(solution)/shard_map/ppermute | solution.py:509
  63.3 27.9 %collective-permute-start.8 = (bf16[96,2176]{1,0:T(8,128)(2,1)}, bf16[96,2176]{1,0:T(8,128)(2,1)}, u32[]{:S(2)}, u32[]{:S(2)}) collective-permute-start(bf16[96,2176]{1,0:T(8,128)(2,1)} %get-tuple-element.60), channel_id=1, source_target_pairs={{0,2},{1,3},{2,0},{3,1},{4,6},{5,7},{6,4},{7,5},{8,10},{9,11},{10,... | collective-permute-start | bytes 1253384 | tf_op jit(solution)/shard_map/ppermute | solution.py:509
  64.7 26.5 %collective-permute-start.9 = (bf16[96,2176]{1,0:T(8,128)(2,1)}, bf16[96,2176]{1,0:T(8,128)(2,1)}, u32[]{:S(2)}, u32[]{:S(2)}) collective-permute-start(bf16[96,2176]{1,0:T(8,128)(2,1)} %get-tuple-element.61), channel_id=1, source_target_pairs={{0,1},{1,2},{2,3},{3,0},{4,5},{5,6},{6,7},{7,4},{8,9},{9,10},{10,1... | collective-permute-start | bytes 1253384 | tf_op jit(solution)/shard_map/ppermute | solution.py:509
  75.4 8.0 %copy-start = (bf16[96,2176]{1,0:T(8,128)(2,1)}, bf16[96,2176]{1,0:T(8,128)(2,1)S(1)}, u32[]{:S(2)}) copy-start(bf16[96,2176]{1,0:T(8,128)(2,1)S(1)} %collective-permute-done.7.refs_7_) | copy-start | bytes 1253380
  83.4 75.1 %all-to-all-start = ((bf16[16,96,1024]{2,1,0:T(8,128)(2,1)}), bf16[16,96,1024]{2,1,0:T(8,128)(2,1)S(1)}, u32[]{:S(2)}, u32[]{:S(2)}) async-start(bf16[16,96,1024]{2,1,0:T(8,128)(2,1)} %weights.1), calls=%async_computation | async-start | bytes 6291456 | tf_op jit(solution)/shard_map/all_to_all | solution.py:562
  100.1 12.5 %collective-permute-start.10 = (bf16[256,512]{1,0:T(8,128)(2,1)}, bf16[256,512]{1,0:T(8,128)(2,1)S(1)}, u32[]{:S(2)}, u32[]{:S(2)}) collective-permute-start(bf16[256,512]{1,0:T(8,128)(2,1)} %get-tuple-element.63), channel_id=1, source_target_pairs={{0,3},{1,0},{2,1},{3,2},{4,7},{5,4},{6,5},{7,6},{8,11},{9,8},{10,9... | collective-permute-start | bytes 786440 | tf_op jit(solution)/shard_map/ppermute | solution.py:509
  101.7 11.0 %collective-permute-start.11 = (bf16[256,512]{1,0:T(8,128)(2,1)}, bf16[256,512]{1,0:T(8,128)(2,1)S(1)}, u32[]{:S(2)}, u32[]{:S(2)}) collective-permute-start(bf16[256,512]{1,0:T(8,128)(2,1)} %get-tuple-element.64), channel_id=1, source_target_pairs={{0,2},{1,3},{2,0},{3,1},{4,6},{5,7},{6,4},{7,5},{8,10},{9,11},{10,... | collective-permute-start | bytes 786440 | tf_op jit(solution)/shard_map/ppermute | solution.py:509
  101.9 14.0 %collective-permute-start.12 = (bf16[256,512]{1,0:T(8,128)(2,1)}, bf16[256,512]{1,0:T(8,128)(2,1)S(1)}, u32[]{:S(2)}, u32[]{:S(2)}) collective-permute-start(bf16[256,512]{1,0:T(8,128)(2,1)} %get-tuple-element.65), channel_id=1, source_target_pairs={{0,1},{1,2},{2,3},{3,0},{4,5},{5,6},{6,7},{7,4},{8,9},{9,10},{10,1... | collective-permute-start | bytes 786440 | tf_op jit(solution)/shard_map/ppermute | solution.py:509
  119.9 1.7 %collective-permute-start.13 = (f32[512,128]{1,0:T(8,128)}, f32[512,128]{1,0:T(8,128)S(1)}, u32[]{:S(2)}, u32[]{:S(2)}) collective-permute-start(f32[512,128]{1,0:T(8,128)} %get-tuple-element.69), channel_id=1, source_target_pairs={{0,4},{4,0},{8,12},{12,8},{16,20},{20,16},{24,28},{28,24},{32,36},... | collective-permute-start | bytes 786440 | tf_op jit(solution)/shard_map/ppermute | solution.py:521
  122.7 15.5 %collective-permute-start.14 = (bf16[512,128]{1,0:T(8,128)(2,1)S(1)}, bf16[512,128]{1,0:T(8,128)(2,1)S(1)}, u32[]{:S(2)}, u32[]{:S(2)}) collective-permute-start(bf16[512,128]{1,0:T(8,128)(2,1)S(1)} %get-tuple-element.81), channel_id=1, source_target_pairs={{0,8},{4,12},{8,16},{12,20},{16,24},{20,28},{24,0},{28,4},{32,40},... | collective-permute-start | bytes 393224 | tf_op jit(solution)/shard_map/ppermute | solution.py:513
  124.4 16.9 %collective-permute-start.15 = (bf16[512,128]{1,0:T(8,128)(2,1)S(1)}, bf16[512,128]{1,0:T(8,128)(2,1)S(1)}, u32[]{:S(2)}, u32[]{:S(2)}) collective-permute-start(bf16[512,128]{1,0:T(8,128)(2,1)S(1)} %get-tuple-element.81), channel_id=1, source_target_pairs={{0,16},{4,20},{8,24},{12,28},{16,0},{20,4},{24,8},{28,12},{32,48},... | collective-permute-start | bytes 393224 | tf_op jit(solution)/shard_map/ppermute | solution.py:513
  127.0 14.3 %collective-permute-start.16 = (bf16[512,128]{1,0:T(8,128)(2,1)S(1)}, bf16[512,128]{1,0:T(8,128)(2,1)S(1)}, u32[]{:S(2)}, u32[]{:S(2)}) collective-permute-start(bf16[512,128]{1,0:T(8,128)(2,1)S(1)} %get-tuple-element.81), channel_id=1, source_target_pairs={{0,24},{4,28},{8,0},{12,4},{16,8},{20,12},{24,16},{28,20},{32,56},... | collective-permute-start | bytes 393224 | tf_op jit(solution)/shard_map/ppermute | solution.py:513
  141.4 12.1 %collective-permute-start.17 = (bf16[512,128]{1,0:T(8,128)(2,1)S(1)}, bf16[512,128]{1,0:T(8,128)(2,1)S(1)}, u32[]{:S(2)}, u32[]{:S(2)}) collective-permute-start(bf16[512,128]{1,0:T(8,128)(2,1)S(1)} %add_convert_fusion), channel_id=1, source_target_pairs={{0,32},{4,36},{8,40},{12,44},{16,48},{20,52},{24,56},{28,60},{32,6... | collective-permute-start | bytes 393224 | tf_op jit(solution)/shard_map/ppermute | solution.py:517
  142.1 11.3 %collective-permute-start.18 = (bf16[512,128]{1,0:T(8,128)(2,1)S(1)}, bf16[512,128]{1,0:T(8,128)(2,1)S(1)}, u32[]{:S(2)}, u32[]{:S(2)}) collective-permute-start(bf16[512,128]{1,0:T(8,128)(2,1)S(1)} %add_convert_fusion), channel_id=1, source_target_pairs={{0,64},{4,68},{8,72},{12,76},{16,80},{20,84},{24,88},{28,92},{32,9... | collective-permute-start | bytes 393224 | tf_op jit(solution)/shard_map/ppermute | solution.py:517
  145.0 8.5 %collective-permute-start.19 = (bf16[512,128]{1,0:T(8,128)(2,1)S(1)}, bf16[512,128]{1,0:T(8,128)(2,1)S(1)}, u32[]{:S(2)}, u32[]{:S(2)}) collective-permute-start(bf16[512,128]{1,0:T(8,128)(2,1)S(1)} %add_convert_fusion), channel_id=1, source_target_pairs={{0,96},{4,100},{8,104},{12,108},{16,112},{20,116},{24,120},{28,124... | collective-permute-start | bytes 393224 | tf_op jit(solution)/shard_map/ppermute | solution.py:517
Sparse Core Ops, SparseCore 0:
  18.8 52.6 all-gather.2

commit v5 on v4

--- a/solution.py
+++ b/solution.py
@@ -40,17 +40,17 @@
     return pl.BlockSpec(memory_space=SMEM)
 
 
-def call(body, name, outs, ins, flops=0, moved=0, grid=None, in_specs=None, out_specs=None, limit=24, scratch=(), free=(), near=False):
+def call(body, name, outs, ins, flops=0, moved=0, grid=None, in_specs=None, out_specs=None, limit=24, scratch=(), free=(), near=(), held=()):
     kwargs = {} if grid is None else {"grid": grid}
     specs = in_specs or [full() for _ in ins]
     ins = [
-        a if spec.memory_space is SMEM or i in free else pltpu.with_memory_space_constraint(a, pltpu.HBM)
+        a if spec.memory_space is SMEM or i in free else pltpu.with_memory_space_constraint(a, VMEM if i in held else pltpu.HBM)
         for i, (a, spec) in enumerate(zip(ins, specs))
     ]
     return pl.pallas_call(
         body,
         name=name,
-        out_shape=[(VMEM if near else pltpu.HBM)(s, t) for s, t in outs],
+        out_shape=[(VMEM if near is True or i in near else pltpu.HBM)(s, t) for i, (s, t) in enumerate(outs)],
         in_specs=specs,
         out_specs=out_specs or [full() for _ in outs],
         scratch_shapes=scratch,
@@ -116,7 +116,7 @@
 STEP = 256
 
 
-def expert_body(r0, r1, r2, r3, wp, wb, b0, b1, b2, b3, out_hbm, held, back, in_sem, out_sem):
+def expert_body(r0, r1, r2, r3, wp, wb, b0, b1, b2, b3, held, back, in_sem, out_sem):
     arrived = (r0, r1, r2, r3)
     backs = (b0, b1, b2, b3)
     tiles = FF // STEP
@@ -139,8 +139,6 @@
         if j == 0:
             for s in range(Y):
                 incoming(1, s).wait()
-            rows_out = pltpu.make_async_copy(held.at[:, pl.ds(0, GB)], out_hbm.at[:, pl.ds(0, GB)], out_sem.at[0])
-            rows_out.start()
         grad_hidden = dot_t(held[:, WIDTH:GB], wb[0, at : at + STEP, :])
         s = 1.0 / (1.0 + jnp.exp(-first))
         silu = first * s
@@ -150,9 +148,6 @@
         slope = s * (1.0 + first * (1.0 - s))
         held[:, GB + at : GB + at + STEP] = (grad_hidden * second * slope).astype(bf16)
         held[:, GB + up : GB + up + STEP] = (grad_hidden * silu).astype(bf16)
-    rest = pl.ds(GB, BUNDLE - GB)
-    grads_out = pltpu.make_async_copy(held.at[:, rest], out_hbm.at[:, rest], out_sem.at[1])
-    grads_out.start()
     hi, lo = split(total)
     lane = lax.broadcasted_iota(jnp.int32, (N, 128), 1)
     back[:, WIDTH:] = jnp.where(lane == 0, hi.astype(f32), lo.astype(f32)).astype(bf16)
@@ -165,11 +160,9 @@
         cols = pl.ds(lo_col, hi_col - lo_col)
         for s in range(Y):
             src = back.at[pl.ds(s * CAP, CAP), cols]
-            copy = pltpu.make_async_copy(src, backs[s].at[:, cols], out_sem.at[2 + part * Y + s])
+            copy = pltpu.make_async_copy(src, backs[s].at[:, cols], out_sem.at[part * Y + s])
             copy.start()
             outgoing.append(copy)
-    rows_out.wait()
-    grads_out.wait()
     for copy in outgoing:
         copy.wait()
 
@@ -178,25 +171,27 @@
     return pl.BlockSpec(memory_space=pl.ANY)
 
 
-def fetch_body(wp_hbm, wb_hbm, wp, wb, sem):
-    copies = [pltpu.make_async_copy(wp_hbm, wp, sem.at[0]), pltpu.make_async_copy(wb_hbm, wb, sem.at[1])]
+def fetch_body(*refs):
+    half = len(refs) // 2
+    sem = refs[-1]
+    copies = [pltpu.make_async_copy(refs[i], refs[half + i], sem.at[i]) for i in range(half)]
     for copy in copies:
         copy.start()
     for copy in copies:
         copy.wait()
 
 
-def fetch(w_pair, w_back):
+def fetch(*arrays):
     return call(
         fetch_body,
         "fetch",
-        [(w_pair.shape, bf16), (w_back.shape, bf16)],
-        (w_pair, w_back),
+        [(a.shape, a.dtype) for a in arrays],
+        arrays,
         0,
         12 << 20,
-        in_specs=[anywhere(), anywhere()],
-        scratch=[pltpu.SemaphoreType.DMA((2,))],
-        limit=16,
+        in_specs=[anywhere() for _ in arrays],
+        scratch=[pltpu.SemaphoreType.DMA((len(arrays),))],
+        limit=2,
         near=True,
     )
 
@@ -212,15 +207,16 @@
         5 * 2 * N * WIDTH * FF,
         14 << 20,
         in_specs=[anywhere() for _ in chunks] + [full(), full()],
-        out_specs=[anywhere() for _ in outs],
+        out_specs=[anywhere()] * Y + [full()],
         scratch=[
-            VMEM((N, BUNDLE), bf16),
             VMEM((N, BACK), bf16),
             pltpu.SemaphoreType.DMA((2 * Y,)),
-            pltpu.SemaphoreType.DMA((2 + 2 * Y,)),
+            pltpu.SemaphoreType.DMA((2 * Y,)),
         ],
-        limit=32,
-        free=(1, 2, 3, 4, 5),
+        limit=16,
+        free=(1, 2, 3),
+        held=(4, 5),
+        near=(Y,),
     )
 
 
@@ -230,61 +226,53 @@
     return (col == (row // run) * (2 * run) + core * run + row % run).astype(bf16)
 
 
-def weights_body(core_ref, mine, other, out_hbm, both, rows_t, hid_t, out, in_sem, out_sem):
-    core = core_ref[0]
-    copies = []
-    for part, (lo, hi) in enumerate(((0, WIDTH), (HID, BUNDLE), (GB, HID), (WIDTH, GB))):
-        for k, src in enumerate((mine, other)):
-            cols = pl.ds(lo, hi - lo)
-            copy = pltpu.make_async_copy(src.at[:, cols], both.at[pl.ds(k * N, N), cols], in_sem.at[2 * part + k])
-            copy.start()
-            copies.append(copy)
+def weights_body(at_ref, mine, other, out_hbm, out, rows_t, hid_t, sem):
+    core = at_ref[4]
     pick_row, pick_hid = chooser(core, 512, 64), chooser(core, 128, 16)
-    copies[0].wait()
-    copies[1].wait()
-    for i in range(Z):
-        rows_t[i * 256 : (i + 1) * 256, :] = dot_t(pick_row, both[:, i * 512 : (i + 1) * 512]).astype(bf16)
-    copies[2].wait()
-    copies[3].wait()
-    for i in range(Z):
-        hid_t[i * 64 : (i + 1) * 64, :] = dot_t(pick_hid, both[:, HID + i * 128 : HID + (i + 1) * 128]).astype(bf16)
-    copies[4].wait()
-    copies[5].wait()
+    for k, src in enumerate((mine, other)):
+        for i in range(Z):
+            rows_t[k, i * 256 : (i + 1) * 256, :] = dot_t(pick_row, src[:, i * 512 : (i + 1) * 512]).astype(bf16)
+            cols = slice(HID + i * 128, HID + (i + 1) * 128)
+            hid_t[k, i * 64 : (i + 1) * 64, :] = dot_t(pick_hid, src[:, cols]).astype(bf16)
     for j in range(4):
-        up = dot(rows_t[...], both[:, GB + j * STEP : GB + (j + 1) * STEP]).astype(bf16)
+        cols = slice(GB + j * STEP, GB + (j + 1) * STEP)
+        up = (dot(rows_t[0], mine[:, cols]) + dot(rows_t[1], other[:, cols])).astype(bf16)
         for k in range(Z * X):
             out[k, :64, j * STEP : (j + 1) * STEP] = up[k * 64 : (k + 1) * 64]
-    copies[6].wait()
-    copies[7].wait()
+    copies = [pltpu.make_async_copy(out.at[:, pl.ds(0, 64)], out_hbm.at[:, pl.ds(0, 64)], sem.at[0])]
+    copies[0].start()
     for j in range(8):
-        down = dot(hid_t[...], both[:, WIDTH + j * STEP : WIDTH + (j + 1) * STEP]).astype(bf16)
+        cols = slice(WIDTH + j * STEP, WIDTH + (j + 1) * STEP)
+        down = (dot(hid_t[0], mine[:, cols]) + dot(hid_t[1], other[:, cols])).astype(bf16)
         row, col = 64 + 16 * (j // 4), (j % 4) * STEP
         for k in range(Z * X):
             out[k, row : row + 16, col : col + STEP] = down[k * 16 : (k + 1) * 16]
-    result = pltpu.make_async_copy(out, out_hbm, out_sem)
-    result.start()
-    result.wait()
-
-
-def weights(core, mine, other):
+        if j % 4 == 3:
+            part = pl.ds(row, 16)
+            copies.append(pltpu.make_async_copy(out.at[:, part], out_hbm.at[:, part], sem.at[1 + j // 4]))
+            copies[-1].start()
+    for copy in copies:
+        copy.wait()
+
+
+def weights(at, mine, other):
     return call(
         weights_body,
         "weights",
         [((Z * X, 96, 1024), bf16)],
-        (core, mine, other),
+        (at, mine, other),
         3 * 2 * N * WIDTH * FF,
         12 << 20,
-        in_specs=[scalars(), anywhere(), anywhere()],
+        in_specs=[scalars(), full(), full()],
         out_specs=[anywhere()],
         scratch=[
-            VMEM((2 * N, BUNDLE), bf16),
-            VMEM((1024, 2 * N), bf16),
-            VMEM((256, 2 * N), bf16),
             VMEM((Z * X, 96, 1024), bf16),
-            pltpu.SemaphoreType.DMA((8,)),
-            pltpu.SemaphoreType.DMA,
+            VMEM((2, 1024, N), bf16),
+            VMEM((2, 256, N), bf16),
+            pltpu.SemaphoreType.DMA((3,)),
         ],
-        limit=32,
+        limit=16,
+        held=(1, 2),
     )[0]
 
 
@@ -301,7 +289,7 @@
 
 def project_body(*refs):
     own, rest, place_hbm, turned_hbm, gate, cot_hbm, r0, r1, r2, r3, resid_hbm, gates, o0, o1, o2, o3 = refs[:16]
-    place, turned, cot, back, w, resid, outs, in_sem, w_sem, out_sem = refs[16:]
+    place, turned, cot, back, w, resid, in_sem, w_sem, out_sem = refs[16:]
     copies = [
         pltpu.make_async_copy(r, back.at[pl.ds(s * CAP, CAP), :], in_sem.at[s]) for s, r in enumerate((r0, r1, r2, r3))
     ]
@@ -319,14 +307,11 @@
     for j in range(WIDTH // wide):
         cols = slice(j * wide, (j + 1) * wide)
         resid[:, cols] = (cot[:, cols].astype(f32) + dot(turned[...], back[:, cols])).astype(bf16)
-    sent = [pltpu.make_async_copy(resid, resid_hbm, out_sem.at[4])]
+    sent = [pltpu.make_async_copy(resid, resid_hbm, out_sem)]
     sent[0].start()
     for s, out in enumerate((o0, o1, o2, o3)):
         slabs[s].wait()
-        outs[s] = dot_t(resid[...], w[s]).astype(bf16)
-        copy = pltpu.make_async_copy(outs.at[s], out, out_sem.at[s])
-        copy.start()
-        sent.append(copy)
+        out[...] = dot_t(resid[...], w[s]).astype(bf16)
     late.wait()
     tail = back[:, WIDTH:].astype(f32)
     picked = jnp.sum(place[...].astype(f32) * (tail[:, 0:1] + tail[:, 1:2]), axis=0, keepdims=True)
@@ -339,7 +324,8 @@
     shapes = [(ROWS, WIDTH), (1, ROWS)] + [(ROWS, 512)] * Y
     ins = (w_out, rest, place, turned, gate_row, grad_out, *backs)
     in_specs, out_specs = [anywhere() for _ in ins], [anywhere() for _ in shapes]
-    in_specs[4], out_specs[1] = full(), full()
+    in_specs[4] = full()
+    out_specs[1:] = [full()] * 5
     return call(
         project_body,
         "project",
@@ -356,30 +342,32 @@
             VMEM((N, BACK), bf16),
             VMEM((Y, 512, WIDTH), bf16),
             VMEM((ROWS, WIDTH), bf16),
-            VMEM((Y, ROWS, 512), bf16),
             pltpu.SemaphoreType.DMA((7,)),
             pltpu.SemaphoreType.DMA((Y,)),
-            pltpu.SemaphoreType.DMA((Y + 1,)),
+            pltpu.SemaphoreType.DMA,
         ],
-        limit=32,
+        limit=20,
+        near=(2, 3, 4, 5),
     )
 
 
 def state_body(at_ref, g0, g1, g2, g3, q_ref, grad_ref, state_ref):
     y, block = at_ref[0], at_ref[1]
     ramp = lax.broadcasted_iota(jnp.int32, (ROWS, 1), 0)
-    total = jnp.zeros((HD, 2 * HD), f32)
+    sums = [jnp.zeros((HD, 2 * HD), f32) for _ in range(HEADS)]
     for s, g in enumerate((g0, g1, g2, g3)):
         off = pl.multiple_of(lax.rem(y + s, Y) * ROWS, ROWS)
         inverse = 1.0 / (3 * BLOCKS * TOK + block * TOK + off + ramp + 1).astype(f32)
         grad_ref[pl.ds(off, ROWS), :] = g[...]
-        both = jnp.concatenate(split(g[...].astype(f32) * inverse), axis=1)
-        total += t_dot(q_ref[pl.ds(off, ROWS), :], both)
-    state_ref[...] = total[:, :HD] + total[:, HD:]
+        for h in range(HEADS):
+            cols = slice(h * HD, (h + 1) * HD)
+            both = jnp.concatenate(split(g[:, cols].astype(f32) * inverse), axis=1)
+            sums[h] += t_dot(q_ref[pl.ds(off, ROWS), cols], both)
+    for h in range(HEADS):
+        state_ref[h * HD : (h + 1) * HD, :] = sums[h][:, :HD] + sums[h][:, HD:]
 
 
 def head_state(at, grads, queries):
-    cols = pl.BlockSpec((TOK, HD), lambda h: (0, h))
     return call(
         state_body,
         "state",
@@ -387,11 +375,21 @@
         (at, *grads, queries),
         HEADS * 2 * TOK * HD * 2 * HD,
         4 << 20,
-        grid=(HEADS,),
-        in_specs=[scalars()] + [pl.BlockSpec((ROWS, HD), lambda h: (0, h))] * Y + [cols],
-        out_specs=[cols, pl.BlockSpec((HD, HD), lambda h: (h, 0))],
-        free=(2, 3, 4),
-    )
+        in_specs=[scalars()] + [full()] * 5,
+        limit=8,
+        held=(1, 2, 3, 4, 5),
+        near=(0, 1),
+    )
+
+
+def chip_body(state, other, chip, chip16):
+    chip[...] = state[...] + other[...]
+    chip16[...] = chip[...].astype(bf16)
+
+
+def line_body(chip, x1, x2, x3, line16):
+    total = chip[...] + x1[...].astype(f32) + x2[...].astype(f32) + x3[...].astype(f32)
+    line16[...] = total.astype(bf16)
 
 
 SUB = 256
@@ -440,49 +438,54 @@
 
 def query_key_body(at_ref, q_ref, k_ref, v_ref, g_ref, prior_ref, out_ref, key_ref):
     block = at_ref[1]
-    for h in range(PAIR):
+    for h in range(HEADS):
         query_part(block, h, g_ref, v_ref, k_ref, prior_ref, out_ref)
         later_part(block, h, v_ref, g_ref, q_ref, key_ref)
 
 
 def value_body(at_ref, q_ref, k_ref, g_ref, value_ref):
-    for h in range(PAIR):
+    for h in range(HEADS):
         later_part(at_ref[1], h, k_ref, q_ref, g_ref, value_ref)
 
 
-def head_call(body, name, ins, out_types, prior=None):
-    cols = pl.BlockSpec((TOK, PAIR * HD), lambda h: (0, h))
-    specs = [scalars()] + [cols] * (len(ins) - 1)
-    if prior is not None:
-        specs.append(pl.BlockSpec((PAIR, HD, HD), lambda h: (h, 0, 0)))
-        ins = (*ins, prior)
+def head_call(body, name, ins, outs, near):
     return call(
         body,
         name,
-        [((TOK, HEADS * HD), t) for t in out_types],
+        [((TOK, HEADS * HD), bf16)] * outs,
         ins,
-        10 * HEADS * 4 * SUB * SUB * HD * len(out_types),
+        10 * HEADS * 4 * SUB * SUB * HD * outs,
         6 << 20,
-        grid=(HEADS // PAIR,),
-        in_specs=specs,
-        out_specs=[cols] * len(out_types),
-    )
-
-
-def final_body(spot_ref, other, x1, x2, x3, z1, z2, z3, v_ref, k_ref, key_ref, value_ref, out_key, out_value):
-    z, x, core = spot_ref[0], spot_ref[1], spot_ref[2]
-    later = jnp.where(core == 0, other[...], 0.0)
-    for s, a, b in ((1, x1, z1), (2, x2, z2), (3, x3, z3)):
-        later += jnp.where(s > x, a[...].astype(f32), 0.0) + jnp.where(s > z, b[...].astype(f32), 0.0)
-    hi, lo = split(later)
-    key = dot_t(v_ref[...], jnp.concatenate([hi, lo], axis=0))
-    out_key[...] = (key_ref[...].astype(f32) + key[:, :HD] + key[:, HD:]).astype(bf16)
-    value = dot(k_ref[...], jnp.concatenate([hi, lo], axis=1))
-    out_value[...] = (value_ref[...].astype(f32) + value[:, :HD] + value[:, HD:]).astype(bf16)
+        in_specs=[scalars()] + [full()] * (len(ins) - 1),
+        limit=16,
+        held=range(1, len(ins)),
+        near=(near,),
+    )
+
+
+def final_body(spot_ref, other, x1, x2, x3, z1, z2, z3, v_ref, k_ref, key_ref, value_ref, key_hbm, value_hbm, outs, sem):
+    z, x, core = spot_ref[2], spot_ref[3], spot_ref[4]
+    copies = []
+    for h in range(HEADS):
+        rows, cols = slice(h * HD, (h + 1) * HD), slice(h * HD, (h + 1) * HD)
+        later = jnp.where(core == 0, other[rows], 0.0)
+        for s, a, b in ((1, x1, z1), (2, x2, z2), (3, x3, z3)):
+            later += jnp.where(s > x, a[rows].astype(f32), 0.0) + jnp.where(s > z, b[rows].astype(f32), 0.0)
+        hi, lo = split(later)
+        key = dot_t(v_ref[:, cols], jnp.concatenate([hi, lo], axis=0))
+        outs[0, :, cols] = (key_ref[:, cols].astype(f32) + key[:, :HD] + key[:, HD:]).astype(bf16)
+        value = dot(k_ref[:, cols], jnp.concatenate([hi, lo], axis=1))
+        outs[1, :, cols] = (value_ref[:, cols].astype(f32) + value[:, :HD] + value[:, HD:]).astype(bf16)
+        here = pl.ds(h * HD, HD)
+        for k, out in enumerate((key_hbm, value_hbm)):
+            copy = pltpu.make_async_copy(outs.at[k, :, here], out.at[:, here], sem.at[2 * h + k])
+            copy.start()
+            copies.append(copy)
+    for copy in copies:
+        copy.wait()
 
 
 def final(spot, sums, values, keys, key_here, value_here):
-    cols = pl.BlockSpec((TOK, HD), lambda h: (0, h))
     return call(
         final_body,
         "final",
@@ -490,10 +493,11 @@
         (spot, *sums, values, keys, key_here, value_here),
         HEADS * 8 * TOK * HD * HD,
         8 << 20,
-        grid=(HEADS,),
-        in_specs=[scalars()] + [pl.BlockSpec((HD, HD), lambda h: (h, 0))] * 7 + [cols] * 4,
-        out_specs=[cols, cols],
-        free=range(1, 8),
+        in_specs=[scalars()] + [full()] * 11,
+        out_specs=[anywhere()] * 2,
+        scratch=[VMEM((2, TOK, HEADS * HD), bf16), pltpu.SemaphoreType.DMA((2 * HEADS,))],
+        limit=12,
+        held=range(1, 12),
     )
 
 
@@ -537,9 +541,7 @@
     y = lax.axis_index("exp")
     block = lax.axis_index("ctx")
     z, x, c = block >> 3, (block >> 1) & 3, block & 1
-    at = jnp.stack([y, block]).astype(jnp.int32)
-    spot = jnp.stack([z, x, c]).astype(jnp.int32)
-    core = c.astype(jnp.int32)[None]
+    at = jnp.stack([y, block, z, x, c]).astype(jnp.int32)
 
     slab = w_out.shape[0] // BLOCKS
     piece = lax.dynamic_slice_in_dim(w_out, block * slab, slab, 0)
@@ -553,33 +555,34 @@
     held = [chunks[0]] + [along_y(chunks[s], s) for s in (1, 2, 3)]
     w_pair, chunks[0] = lax.optimization_barrier((w_gate_up, chunks[0]))
     held[0] = chunks[0]
+    prior = prefix_state[0]
     w_pair, w_back = fetch(w_pair, w_down)
+    queries, keys, values = attn_query, attn_key, attn_value
     b0, b1, b2, b3, bundle = expert(held, w_pair, w_back)
     backs = [b0] + [along_y(b, -s) for s, b in ((1, b1), (2, b2), (3, b3))]
     other_bundle, backs[1] = lax.optimization_barrier((across(bundle), backs[1]))
-    partial = weights(core, bundle, other_bundle)
+    partial = weights(at, bundle, other_bundle)
     groups = [[index(i, j, k) for i in range(Z) for j in range(X)] for k in range(C)]
     exchanged = lax.all_to_all(partial, "ctx", 0, 0, axis_index_groups=groups, tiled=True)
 
     grad_resid, gates_out, *per_head = project(w_out, rest, place, turned, gate_row, grad_out, backs)
     grad_gates = gates_out.reshape(ROWS, 1)
     grads = [per_head[0]] + [along_y(per_head[s], -s) for s in (1, 2, 3)]
-    attn_grad, state = head_state(at, grads, attn_query)
+    attn_grad, state = head_state(at, grads, queries)
 
     other = across(state)
-    chip = state + other
-    chip16 = chip.astype(bf16)
+    size = (HEADS * HD, HD)
+    outs = [(size, f32), (size, bf16)]
+    chip, chip16 = call(chip_body, "chip", outs, (state, other), limit=4, held=(0, 1), near=(0, 1))
     from_x = [along_x(chip16, s) for s in (1, 2, 3)]
-    line = chip + from_x[0].astype(f32) + from_x[1].astype(f32) + from_x[2].astype(f32)
-    line16 = line.astype(bf16)
-    ins = (at, attn_query, attn_key, attn_value, attn_grad)
-    grad_query, key_here = head_call(query_key_body, "query_key", ins, (bf16, bf16), prefix_state[0])
-    line16, key_here = lax.optimization_barrier((line16, key_here))
+    ins = (at, queries, keys, values, attn_grad, prior)
+    grad_query, key_here = head_call(query_key_body, "query_key", ins, 2, 1)
+    chip, key_here = lax.optimization_barrier((chip, key_here))
+    (line16,) = call(line_body, "line", [(size, bf16)], (chip, *from_x), limit=4, held=range(4), near=(0,))
     from_z = [along_z(line16, s) for s in (1, 2, 3)]
-
-    (value_here,) = head_call(value_body, "value", (at, attn_query, attn_key, attn_grad), (bf16,))
+    (value_here,) = head_call(value_body, "value", (at, queries, keys, attn_grad), 1, 0)
     sums = (other, *from_x, *from_z)
-    grad_key, grad_value = final(spot, sums, attn_value, attn_key, key_here, value_here)
+    grad_key, grad_value = final(at, sums, values, keys, key_here, value_here)
 
     exchanged, grad_key = lax.optimization_barrier((exchanged, grad_key))
     outs = [((1, 64, 1024), f32), ((1, 16, WIDTH), f32)]

time: 167 us -> 161 us (0.964)
  Pallas kernels: 56 us -> 45.6 us
  waiting for transfers between devices: 58.6 us -> 64.2 us
    pallas_call x10 -> x12, Pallas kernels: 56 us -> 45.6 us  [call(): pl.pallas_call(body, name=name, out_shape=[(VMEM if near is True or i in...]
    ppermute x3, waiting for transfers between devices: 3.19 us -> 9 us  [along_x(): lax.ppermute(a, 'ctx', [(index(z, x, c), index(z, (x + s) % X, c)) for z,...]
  transfers between devices with their start and end apart: 22 -> 22, of which waited for: 8 -> 10; matrix products, arithmetic and copies ran while one was open for 1% -> 0% of each run, Pallas kernels for 33% -> 28%
where the time goes in v5:
time: 161 us; the launch traced here: 160 us
  waiting for transfers between devices  64.2 us (40%)
  Pallas kernels  45.6 us (28%)
  starting transfers between devices  34.8 us (22%)
  between operations  14.2 us (9%)
    ppermute x12, waiting for transfers between devices, along_y(): return lax.ppermute(a, 'exp', [(i, (i + s) % Y) for i in range(Y)])  53.6 us
    pallas_call x12, Pallas kernels, call(): pl.pallas_call(body, name=name, out_shape=[(VMEM if near is True or i in...  45.6 us
    ppermute x12, starting transfers between devices, along_y(): return lax.ppermute(a, 'exp', [(i, (i + s) % Y) for i in range(Y)])  14.9 us
    ppermute x3, waiting for transfers between devices, along_x(): lax.ppermute(a, 'ctx', [(index(z, x, c), index(z, (x + s) % X, c)) for z,...  9 us
    all_to_all x1, starting transfers between devices, on_device(): lax.all_to_all(partial, 'ctx', 0, 0, axis_index_groups=groups, tiled=True)  7.82 us
    ppermute x3, starting transfers between devices, along_z(): lax.ppermute(a, 'ctx', [(index(z, x, c), index((z + s) % Z, x, c)) for z,...  5.94 us
    ppermute x3, starting transfers between devices, along_x(): lax.ppermute(a, 'ctx', [(index(z, x, c), index(z, (x + s) % X, c)) for z,...  5.85 us
  transfers between devices with their start and end apart: 22, of which 10 were waited for; matrix products, arithmetic and copies ran while one was open for 0% of the time, Pallas kernels for 28%

profile of v5, /device:TPU:0, one launch (start us, length us, event | category | flops | bytes accessed | tf_op | source)
XLA Modules:
  0.0 160.5 jit_solution(18206910642413915420)
XLA Ops:
  8.1 1.7 %collective-permute-start = (bf16[16,2048]{1,0:T(8,128)(2,1)S(1)}, bf16[16,2048]{1,0:T(8,128)(2,1)S(1)}, u32[]{:S(2)}, u32[]{:S(2)}) collective-permute-start(bf16[16,2048]{1,0:T(8,128)(2,1)S(1)} %constant_dynamic-slice_fusion), channel_id=1, source_target_pairs={{0,1},{1,2},{2,3},{3,0},{4,5},{5,6},{6,7},{7,4},{8,9},{9,10},{10,1... | collective-permute-start | bytes 196616 | tf_op jit(solution)/shard_map/ppermute | solution.py:513
  9.7 2.9 %collective-permute-start.1 = (bf16[16,2048]{1,0:T(8,128)(2,1)S(1)}, bf16[16,2048]{1,0:T(8,128)(2,1)S(1)}, u32[]{:S(2)}, u32[]{:S(2)}) collective-permute-start(bf16[16,2048]{1,0:T(8,128)(2,1)S(1)} %constant_dynamic-slice_fusion), channel_id=1, source_target_pairs={{0,2},{1,3},{2,0},{3,1},{4,6},{5,7},{6,4},{7,5},{8,10},{9,11},{10,... | collective-permute-start | bytes 196616 | tf_op jit(solution)/shard_map/ppermute | solution.py:513
  14.1 3.9 %pack.1 = (bf16[384,256]{1,0:T(8,128)(2,1)}, bf16[256,384]{1,0:T(8,128)(2,1)}, bf16[2,96,2048]{2,1,0:T(8,128)(2,1)}, bf16[2,96,2048]{2,1,0:T(8,128)(2,1)}, bf16[...) custom-call(s32[5]{0:T(128)S(1)} %stack.23.at_ref.spot_ref, s32[1,256]{1,0:T(1,128)} %bitcast.12, ...), custom_call_target="tpu_custom_call" | custom-call | flops 3221225472 | bytes 20971520 | tf_op jit(solution)/shard_map/pack/pallas_call | solution.py:50
  19.2 2.9 %collective-permute-start.5 = (bf16[2,96,2048]{2,1,0:T(8,128)(2,1)}, bf16[2,96,2048]{2,1,0:T(8,128)(2,1)S(1)}, u32[]{:S(2)}, u32[]{:S(2)}) collective-permute-start(bf16[2,96,2048]{2,1,0:T(8,128)(2,1)} %get-tuple-element.54), channel_id=1, source_target_pairs={{0,3},{1,0},{2,1},{3,2},{4,7},{5,4},{6,5},{7,6},{8,11},{9,8},{10,9... | collective-permute-start | bytes 2359304 | tf_op jit(solution)/shard_map/ppermute | solution.py:513
  22.1 2.9 %fetch.1 = (bf16[1,2048,1024]{2,1,0:T(8,128)(2,1)S(1)}, bf16[1,512,2048]{2,1,0:T(8,128)(2,1)S(1)}) custom-call(bf16[1,2048,1024]{2,1,0:T(8,128)(2,1)} %refs_0_.1, bf16[1,512,2048]{2,1,0:T(8,128)(2,1)} %refs_1_.1), custom_call_target="tpu_custom_call" | custom-call | bytes 50331648 | tf_op jit(solution)/shard_map/fetch/pallas_call | solution.py:50
  25.0 16.0 %collective-permute-done.4.r2 = bf16[2,96,2048]{2,1,0:T(8,128)(2,1)S(1)} collective-permute-done((bf16[2,96,2048]{2,1,0:T(8,128)(2,1)}, bf16[2,96,2048]{2,1,0:T(8,128)(2,1)S(1)}, u32[]{:S(2)}, u32[]{:S(2)}) %collective-permute-start.4) | collective-permute-done | bytes 786464 | tf_op jit(solution)/shard_map/ppermute | solution.py:513
  41.0 12.8 %collective-permute-done.5.r3 = bf16[2,96,2048]{2,1,0:T(8,128)(2,1)S(1)} collective-permute-done((bf16[2,96,2048]{2,1,0:T(8,128)(2,1)}, bf16[2,96,2048]{2,1,0:T(8,128)(2,1)S(1)}, u32[]{:S(2)}, u32[]{:S(2)}) %collective-permute-start.5) | collective-permute-done | bytes 786464 | tf_op jit(solution)/shard_map/ppermute | solution.py:513
  53.8 2.0 %collective-permute-done.3.r1 = bf16[2,96,2048]{2,1,0:T(8,128)(2,1)S(1)} collective-permute-done((bf16[2,96,2048]{2,1,0:T(8,128)(2,1)}, bf16[2,96,2048]{2,1,0:T(8,128)(2,1)S(1)}, u32[]{:S(2)}, u32[]{:S(2)}) %collective-permute-start.3) | collective-permute-done | bytes 786464 | tf_op jit(solution)/shard_map/ppermute | solution.py:513
  55.8 6.7 %expert.1 = (bf16[96,2176]{1,0:T(8,128)(2,1)}, bf16[96,2176]{1,0:T(8,128)(2,1)}, bf16[96,2176]{1,0:T(8,128)(2,1)}, bf16[96,2176]{1,0:T(8,128)(2,1)}, bf16[384,5632]{1,0:T(8,128)(2,1)S(1)}) custom-call(bf16[2,96,2048]{2,1,0:T(8,128)(2,1)} %get-tuple-element.51.r0, bf16[2,96,2048]{2,1,0:T(8,128)(2,1)S(1)} %collective-permute-done.3.r1, ...), custom_call_target="tpu_custom_call" | custom-call | flops 16106127360 | bytes 58720256 | tf_op jit(solution)/shard_map/expert/pallas_call | solution.py:50
  65.4 10.1 %collective-permute-done.7.refs_7_ = bf16[96,2176]{1,0:T(8,128)(2,1)} collective-permute-done((bf16[96,2176]{1,0:T(8,128)(2,1)}, bf16[96,2176]{1,0:T(8,128)(2,1)}, u32[]{:S(2)}, u32[]{:S(2)}) %collective-permute-start.7) | collective-permute-done | bytes 417824 | tf_op jit(solution)/shard_map/ppermute | solution.py:513
  75.5 6.5 %weights.1 = bf16[16,96,1024]{2,1,0:T(8,128)(2,1)} custom-call(s32[5]{0:T(128)S(1)} %stack.23.at_ref.spot_ref, bf16[384,5632]{1,0:T(8,128)(2,1)S(1)} %get-tuple-element.59.mine, bf16[384,5632]{1,0:T(8,128)(2,1)S(1)} %collective-permute-done.6.other), custom_call_target="tpu_custom_call" | custom-call | flops 9663676416 | bytes 50331648 | tf_op jit(solution)/shard_map/weights/pallas_call | solution.py:50
  82.0 7.8 %all-to-all-start = ((bf16[16,96,1024]{2,1,0:T(8,128)(2,1)}), bf16[16,96,1024]{2,1,0:T(8,128)(2,1)S(1)}, u32[]{:S(2)}, u32[]{:S(2)}) async-start(bf16[16,96,1024]{2,1,0:T(8,128)(2,1)} %weights.1), calls=%async_computation | async-start | bytes 6291456 | tf_op jit(solution)/shard_map/all_to_all | solution.py:566
  89.9 8.4 %project.1 = (bf16[256,2048]{1,0:T(8,128)(2,1)}, bf16[1,256]{1,0:T(2,128)(2,1)}, bf16[256,512]{1,0:T(8,128)(2,1)S(1)}, bf16[256,512]{1,0:T(8,128)(2,1)S(1)}, bf1...) custom-call(bf16[512,2048]{1,0:T(8,128)(2,1)} %refs_0_.2, bf16[32,3,16,2048]{3,2,1,0:T(8,128)(2,1)} %bitcast.11, ...), custom_call_target="tpu_custom_call" | custom-call | flops 10200547328 | bytes 41943040 | tf_op jit(solution)/shard_map/project/pallas_call | solution.py:50
  101.1 9.4 %collective-permute-done.10.g1 = bf16[256,512]{1,0:T(8,128)(2,1)S(1)} collective-permute-done((bf16[256,512]{1,0:T(8,128)(2,1)S(1)}, bf16[256,512]{1,0:T(8,128)(2,1)S(1)}, u32[]{:S(2)}, u32[]{:S(2)}) %collective-permute-start.10) | collective-permute-done | bytes 262176 | tf_op jit(solution)/shard_map/ppermute | solution.py:513
  110.6 3.3 %collective-permute-done.12.g3 = bf16[256,512]{1,0:T(8,128)(2,1)S(1)} collective-permute-done((bf16[256,512]{1,0:T(8,128)(2,1)S(1)}, bf16[256,512]{1,0:T(8,128)(2,1)S(1)}, u32[]{:S(2)}, u32[]{:S(2)}) %collective-permute-start.12) | collective-permute-done | bytes 262176 | tf_op jit(solution)/shard_map/ppermute | solution.py:513
  116.8 1.7 %collective-permute-start.14 = (bf16[512,128]{1,0:T(8,128)(2,1)S(1)}, bf16[512,128]{1,0:T(8,128)(2,1)S(1)}, u32[]{:S(2)}, u32[]{:S(2)}) collective-permute-start(bf16[512,128]{1,0:T(8,128)(2,1)S(1)} %get-tuple-element.72), channel_id=1, source_target_pairs={{0,8},{4,12},{8,16},{12,20},{16,24},{20,28},{24,0},{28,4},{32,40},... | collective-permute-start | bytes 393224 | tf_op jit(solution)/shard_map/ppermute | solution.py:517
  118.5 2.7 %collective-permute-start.15 = (bf16[512,128]{1,0:T(8,128)(2,1)S(1)}, bf16[512,128]{1,0:T(8,128)(2,1)S(1)}, u32[]{:S(2)}, u32[]{:S(2)}) collective-permute-start(bf16[512,128]{1,0:T(8,128)(2,1)S(1)} %get-tuple-element.72), channel_id=1, source_target_pairs={{0,16},{4,20},{8,24},{12,28},{16,0},{20,4},{24,8},{28,12},{32,48},... | collective-permute-start | bytes 393224 | tf_op jit(solution)/shard_map/ppermute | solution.py:517
  122.6 8.1 %query_key.1 = (bf16[1024,512]{1,0:T(8,128)(2,1)}, bf16[1024,512]{1,0:T(8,128)(2,1)S(1)}) custom-call(s32[5]{0:T(128)S(1)} %stack.23.at_ref.spot_ref, bf16[1024,512]{1,0:T(8,128)(2,1)S(1)} %copy-done, bf16[1024,512]{1,0:T(8,128)(2,1)S(1)} %copy-done.1, bf16[1024,512]{1,0:T(8,128)(2,1)S(1)} %copy-done.2, bf16[1024,512]{1,0:T(8,128)(2,1)S(1)} %get-tuple-element.68.g_ref, ...), custom_call_target="tpu_custom_call" | custom-call | flops 10737418240 | bytes 25165824 | tf_op jit(solution)/shard_map/query_key/pallas_call | solution.py:50
  130.7 2.6 %collective-permute-done.14.x1 = bf16[512,128]{1,0:T(8,128)(2,1)S(1)} collective-permute-done((bf16[512,128]{1,0:T(8,128)(2,1)S(1)}, bf16[512,128]{1,0:T(8,128)(2,1)S(1)}, u32[]{:S(2)}, u32[]{:S(2)}) %collective-permute-start.14) | collective-permute-done | bytes 131104 | tf_op jit(solution)/shard_map/ppermute | solution.py:517
  133.3 6.4 %collective-permute-done.15.x2 = bf16[512,128]{1,0:T(8,128)(2,1)S(1)} collective-permute-done((bf16[512,128]{1,0:T(8,128)(2,1)S(1)}, bf16[512,128]{1,0:T(8,128)(2,1)S(1)}, u32[]{:S(2)}, u32[]{:S(2)}) %collective-permute-start.15) | collective-permute-done | bytes 131104 | tf_op jit(solution)/shard_map/ppermute | solution.py:517
  140.4 2.8 %collective-permute-start.18 = (bf16[512,128]{1,0:T(8,128)(2,1)S(1)}, bf16[512,128]{1,0:T(8,128)(2,1)S(1)}, u32[]{:S(2)}, u32[]{:S(2)}) collective-permute-start(bf16[512,128]{1,0:T(8,128)(2,1)S(1)} %line.1), channel_id=1, source_target_pairs={{0,64},{4,68},{8,72},{12,76},{16,80},{20,84},{24,88},{28,92},{32,9... | collective-permute-start | bytes 393224 | tf_op jit(solution)/shard_map/ppermute | solution.py:521
  143.2 2.5 %collective-permute-start.19 = (bf16[512,128]{1,0:T(8,128)(2,1)S(1)}, bf16[512,128]{1,0:T(8,128)(2,1)S(1)}, u32[]{:S(2)}, u32[]{:S(2)}) collective-permute-start(bf16[512,128]{1,0:T(8,128)(2,1)S(1)} %line.1), channel_id=1, source_target_pairs={{0,96},{4,100},{8,104},{12,108},{16,112},{20,116},{24,120},{28,124... | collective-permute-start | bytes 393224 | tf_op jit(solution)/shard_map/ppermute | solution.py:521
  145.7 4.1 %value.1.value_ref = bf16[1024,512]{1,0:T(8,128)(2,1)S(1)} custom-call(s32[5]{0:T(128)S(1)} %stack.23.at_ref.spot_ref, bf16[1024,512]{1,0:T(8,128)(2,1)S(1)} %copy-done, bf16[1024,512]{1,0:T(8,128)(2,1)S(1)} %copy-done.1, bf16[1024,512]{1,0:T(8,128)(2,1)S(1)} %get-tuple-element.68.g_ref), custom_call_target="tpu_custom_call" | custom-call | flops 5368709120 | bytes 25165824 | tf_op jit(solution)/shard_map/value/pallas_call | solution.py:50
  149.9 2.7 %final.1 = (bf16[1024,512]{1,0:T(8,128)(2,1)}, bf16[1024,512]{1,0:T(8,128)(2,1)}) custom-call(s32[5]{0:T(128)S(1)} %stack.23.at_ref.spot_ref, f32[512,128]{1,0:T(8,128)S(1)} %collective-permute-done.13.other, bf16[512,128]{1,0:T(8,128)(2,1)S(1)} %collective-permute-done.14.x1, bf16[512,128]{1,0:T(8,128)(2,1)S(1)} %collective-permute-done.15.x2, ...), custom_call_target="tpu_custom_call" | custom-call | flops 2147483648 | bytes 33554432 | tf_op jit(solution)/shard_map/final/pallas_call | solution.py:50
  (44 shorter events, 15.6 us)
Async XLA Ops:
  7.2 82.7 %all-gather.3.cloned.1.call-start = ((), (), s32[]{:S(2)}) async-start(), calls=%async_computation.1 | async-start | bytes 6488064 | tf_op jit(solution)/shard_map/all_gather | solution.py:552
  8.1 9.9 %collective-permute-start = (bf16[16,2048]{1,0:T(8,128)(2,1)S(1)}, bf16[16,2048]{1,0:T(8,128)(2,1)S(1)}, u32[]{:S(2)}, u32[]{:S(2)}) collective-permute-start(bf16[16,2048]{1,0:T(8,128)(2,1)S(1)} %constant_dynamic-slice_fusion), channel_id=1, source_target_pairs={{0,1},{1,2},{2,3},{3,0},{4,5},{5,6},{6,7},{7,4},{8,9},{9,10},{10,1... | collective-permute-start | bytes 196616 | tf_op jit(solution)/shard_map/ppermute | solution.py:513
  9.7 8.2 %collective-permute-start.1 = (bf16[16,2048]{1,0:T(8,128)(2,1)S(1)}, bf16[16,2048]{1,0:T(8,128)(2,1)S(1)}, u32[]{:S(2)}, u32[]{:S(2)}) collective-permute-start(bf16[16,2048]{1,0:T(8,128)(2,1)S(1)} %constant_dynamic-slice_fusion), channel_id=1, source_target_pairs={{0,2},{1,3},{2,0},{3,1},{4,6},{5,7},{6,4},{7,5},{8,10},{9,11},{10,... | collective-permute-start | bytes 196616 | tf_op jit(solution)/shard_map/ppermute | solution.py:513
  12.6 5.3 %collective-permute-start.2 = (bf16[16,2048]{1,0:T(8,128)(2,1)S(1)}, bf16[16,2048]{1,0:T(8,128)(2,1)S(1)}, u32[]{:S(2)}, u32[]{:S(2)}) collective-permute-start(bf16[16,2048]{1,0:T(8,128)(2,1)S(1)} %constant_dynamic-slice_fusion), channel_id=1, source_target_pairs={{0,3},{1,0},{2,1},{3,2},{4,7},{5,4},{6,5},{7,6},{8,11},{9,8},{10,9... | collective-permute-start | bytes 196616 | tf_op jit(solution)/shard_map/ppermute | solution.py:513
  18.7 22.3 %collective-permute-start.4 = (bf16[2,96,2048]{2,1,0:T(8,128)(2,1)}, bf16[2,96,2048]{2,1,0:T(8,128)(2,1)S(1)}, u32[]{:S(2)}, u32[]{:S(2)}) collective-permute-start(bf16[2,96,2048]{2,1,0:T(8,128)(2,1)} %get-tuple-element.53), channel_id=1, source_target_pairs={{0,2},{1,3},{2,0},{3,1},{4,6},{5,7},{6,4},{7,5},{8,10},{9,11},{10,... | collective-permute-start | bytes 2359304 | tf_op jit(solution)/shard_map/ppermute | solution.py:513
  19.2 34.6 %collective-permute-start.5 = (bf16[2,96,2048]{2,1,0:T(8,128)(2,1)}, bf16[2,96,2048]{2,1,0:T(8,128)(2,1)S(1)}, u32[]{:S(2)}, u32[]{:S(2)}) collective-permute-start(bf16[2,96,2048]{2,1,0:T(8,128)(2,1)} %get-tuple-element.54), channel_id=1, source_target_pairs={{0,3},{1,0},{2,1},{3,2},{4,7},{5,4},{6,5},{7,6},{8,11},{9,8},{10,9... | collective-permute-start | bytes 2359304 | tf_op jit(solution)/shard_map/ppermute | solution.py:513
  22.1 33.7 %collective-permute-start.3 = (bf16[2,96,2048]{2,1,0:T(8,128)(2,1)}, bf16[2,96,2048]{2,1,0:T(8,128)(2,1)S(1)}, u32[]{:S(2)}, u32[]{:S(2)}) collective-permute-start(bf16[2,96,2048]{2,1,0:T(8,128)(2,1)} %get-tuple-element.52), channel_id=1, source_target_pairs={{0,1},{1,2},{2,3},{3,0},{4,5},{5,6},{6,7},{7,4},{8,9},{9,10},{10,1... | collective-permute-start | bytes 2359304 | tf_op jit(solution)/shard_map/ppermute | solution.py:513
  62.5 13.0 %collective-permute-start.6 = (bf16[384,5632]{1,0:T(8,128)(2,1)S(1)}, bf16[384,5632]{1,0:T(8,128)(2,1)S(1)}, u32[]{:S(2)}, u32[]{:S(2)}) collective-permute-start(bf16[384,5632]{1,0:T(8,128)(2,1)S(1)} %get-tuple-element.59.mine), channel_id=1, source_target_pairs={{0,4},{4,0},{8,12},{12,8},{16,20},{20,16},{24,28},{28,24},{32,36},... | collective-permute-start | bytes 12976136 | tf_op jit(solution)/shard_map/ppermute | solution.py:525
  62.7 12.8 %collective-permute-start.7 = (bf16[96,2176]{1,0:T(8,128)(2,1)}, bf16[96,2176]{1,0:T(8,128)(2,1)}, u32[]{:S(2)}, u32[]{:S(2)}) collective-permute-start(bf16[96,2176]{1,0:T(8,128)(2,1)} %get-tuple-element.60), channel_id=1, source_target_pairs={{0,3},{1,0},{2,1},{3,2},{4,7},{5,4},{6,5},{7,6},{8,11},{9,8},{10,9... | collective-permute-start | bytes 1253384 | tf_op jit(solution)/shard_map/ppermute | solution.py:513
  63.3 26.5 %collective-permute-start.8 = (bf16[96,2176]{1,0:T(8,128)(2,1)}, bf16[96,2176]{1,0:T(8,128)(2,1)}, u32[]{:S(2)}, u32[]{:S(2)}) collective-permute-start(bf16[96,2176]{1,0:T(8,128)(2,1)} %get-tuple-element.62), channel_id=1, source_target_pairs={{0,2},{1,3},{2,0},{3,1},{4,6},{5,7},{6,4},{7,5},{8,10},{9,11},{10,... | collective-permute-start | bytes 1253384 | tf_op jit(solution)/shard_map/ppermute | solution.py:513
  64.7 25.1 %collective-permute-start.9 = (bf16[96,2176]{1,0:T(8,128)(2,1)}, bf16[96,2176]{1,0:T(8,128)(2,1)}, u32[]{:S(2)}, u32[]{:S(2)}) collective-permute-start(bf16[96,2176]{1,0:T(8,128)(2,1)} %get-tuple-element.63), channel_id=1, source_target_pairs={{0,1},{1,2},{2,3},{3,0},{4,5},{5,6},{6,7},{7,4},{8,9},{9,10},{10,1... | collective-permute-start | bytes 1253384 | tf_op jit(solution)/shard_map/ppermute | solution.py:513
  82.0 70.6 %all-to-all-start = ((bf16[16,96,1024]{2,1,0:T(8,128)(2,1)}), bf16[16,96,1024]{2,1,0:T(8,128)(2,1)S(1)}, u32[]{:S(2)}, u32[]{:S(2)}) async-start(bf16[16,96,1024]{2,1,0:T(8,128)(2,1)} %weights.1), calls=%async_computation | async-start | bytes 6291456 | tf_op jit(solution)/shard_map/all_to_all | solution.py:566
  98.2 24.4 %copy-start.1 = (bf16[1024,512]{1,0:T(8,128)(2,1)S(1)}, bf16[1024,512]{1,0:T(8,128)(2,1)}, u32[]{:S(2)}) copy-start(bf16[1024,512]{1,0:T(8,128)(2,1)} %k_ref.5) | copy-start | bytes 3145732
  98.2 24.4 %copy-start.2 = (bf16[1024,512]{1,0:T(8,128)(2,1)S(1)}, bf16[1024,512]{1,0:T(8,128)(2,1)}, u32[]{:S(2)}) copy-start(bf16[1024,512]{1,0:T(8,128)(2,1)} %v_ref.3) | copy-start | bytes 3145732
  98.2 12.2 %collective-permute-start.10 = (bf16[256,512]{1,0:T(8,128)(2,1)S(1)}, bf16[256,512]{1,0:T(8,128)(2,1)S(1)}, u32[]{:S(2)}, u32[]{:S(2)}) collective-permute-start(bf16[256,512]{1,0:T(8,128)(2,1)S(1)} %get-tuple-element.65), channel_id=1, source_target_pairs={{0,3},{1,0},{2,1},{3,2},{4,7},{5,4},{6,5},{7,6},{8,11},{9,8},{10,9... | collective-permute-start | bytes 786440 | tf_op jit(solution)/shard_map/ppermute | solution.py:513
  99.8 10.8 %collective-permute-start.11 = (bf16[256,512]{1,0:T(8,128)(2,1)S(1)}, bf16[256,512]{1,0:T(8,128)(2,1)S(1)}, u32[]{:S(2)}, u32[]{:S(2)}) collective-permute-start(bf16[256,512]{1,0:T(8,128)(2,1)S(1)} %get-tuple-element.66), channel_id=1, source_target_pairs={{0,2},{1,3},{2,0},{3,1},{4,6},{5,7},{6,4},{7,5},{8,10},{9,11},{10,... | collective-permute-start | bytes 786440 | tf_op jit(solution)/shard_map/ppermute | solution.py:513
  99.9 13.9 %collective-permute-start.12 = (bf16[256,512]{1,0:T(8,128)(2,1)S(1)}, bf16[256,512]{1,0:T(8,128)(2,1)S(1)}, u32[]{:S(2)}, u32[]{:S(2)}) collective-permute-start(bf16[256,512]{1,0:T(8,128)(2,1)S(1)} %get-tuple-element.67), channel_id=1, source_target_pairs={{0,1},{1,2},{2,3},{3,0},{4,5},{5,6},{6,7},{7,4},{8,9},{9,10},{10,1... | collective-permute-start | bytes 786440 | tf_op jit(solution)/shard_map/ppermute | solution.py:513
  115.1 1.6 %collective-permute-start.13 = (f32[512,128]{1,0:T(8,128)S(1)}, f32[512,128]{1,0:T(8,128)S(1)}, u32[]{:S(2)}, u32[]{:S(2)}) collective-permute-start(f32[512,128]{1,0:T(8,128)S(1)} %get-tuple-element.71.state), channel_id=1, source_target_pairs={{0,4},{4,0},{8,12},{12,8},{16,20},{20,16},{24,28},{28,24},{32,36},... | collective-permute-start | bytes 786440 | tf_op jit(solution)/shard_map/ppermute | solution.py:525
  116.8 16.5 %collective-permute-start.14 = (bf16[512,128]{1,0:T(8,128)(2,1)S(1)}, bf16[512,128]{1,0:T(8,128)(2,1)S(1)}, u32[]{:S(2)}, u32[]{:S(2)}) collective-permute-start(bf16[512,128]{1,0:T(8,128)(2,1)S(1)} %get-tuple-element.72), channel_id=1, source_target_pairs={{0,8},{4,12},{8,16},{12,20},{16,24},{20,28},{24,0},{28,4},{32,40},... | collective-permute-start | bytes 393224 | tf_op jit(solution)/shard_map/ppermute | solution.py:517
  118.5 21.2 %collective-permute-start.15 = (bf16[512,128]{1,0:T(8,128)(2,1)S(1)}, bf16[512,128]{1,0:T(8,128)(2,1)S(1)}, u32[]{:S(2)}, u32[]{:S(2)}) collective-permute-start(bf16[512,128]{1,0:T(8,128)(2,1)S(1)} %get-tuple-element.72), channel_id=1, source_target_pairs={{0,16},{4,20},{8,24},{12,28},{16,0},{20,4},{24,8},{28,12},{32,48},... | collective-permute-start | bytes 393224 | tf_op jit(solution)/shard_map/ppermute | solution.py:517
  121.1 18.6 %collective-permute-start.16 = (bf16[512,128]{1,0:T(8,128)(2,1)S(1)}, bf16[512,128]{1,0:T(8,128)(2,1)S(1)}, u32[]{:S(2)}, u32[]{:S(2)}) collective-permute-start(bf16[512,128]{1,0:T(8,128)(2,1)S(1)} %get-tuple-element.72), channel_id=1, source_target_pairs={{0,24},{4,28},{8,0},{12,4},{16,8},{20,12},{24,16},{28,20},{32,56},... | collective-permute-start | bytes 393224 | tf_op jit(solution)/shard_map/ppermute | solution.py:517
  139.8 10.0 %collective-permute-start.17 = (bf16[512,128]{1,0:T(8,128)(2,1)S(1)}, bf16[512,128]{1,0:T(8,128)(2,1)S(1)}, u32[]{:S(2)}, u32[]{:S(2)}) collective-permute-start(bf16[512,128]{1,0:T(8,128)(2,1)S(1)} %line.1), channel_id=1, source_target_pairs={{0,32},{4,36},{8,40},{12,44},{16,48},{20,52},{24,56},{28,60},{32,6... | collective-permute-start | bytes 393224 | tf_op jit(solution)/shard_map/ppermute | solution.py:521
  140.4 9.4 %collective-permute-start.18 = (bf16[512,128]{1,0:T(8,128)(2,1)S(1)}, bf16[512,128]{1,0:T(8,128)(2,1)S(1)}, u32[]{:S(2)}, u32[]{:S(2)}) collective-permute-start(bf16[512,128]{1,0:T(8,128)(2,1)S(1)} %line.1), channel_id=1, source_target_pairs={{0,64},{4,68},{8,72},{12,76},{16,80},{20,84},{24,88},{28,92},{32,9... | collective-permute-start | bytes 393224 | tf_op jit(solution)/shard_map/ppermute | solution.py:521
  143.2 6.6 %collective-permute-start.19 = (bf16[512,128]{1,0:T(8,128)(2,1)S(1)}, bf16[512,128]{1,0:T(8,128)(2,1)S(1)}, u32[]{:S(2)}, u32[]{:S(2)}) collective-permute-start(bf16[512,128]{1,0:T(8,128)(2,1)S(1)} %line.1), channel_id=1, source_target_pairs={{0,96},{4,100},{8,104},{12,108},{16,112},{20,116},{24,120},{28,124... | collective-permute-start | bytes 393224 | tf_op jit(solution)/shard_map/ppermute | solution.py:521
  (2 other events, 48.4 us)
Sparse Core Ops, SparseCore 0:
  18.8 52.6 all-gather.2

commit v6 on v5

--- a/solution.py
+++ b/solution.py
@@ -11,7 +11,8 @@
 SMEM = pltpu.SMEM
 Z, X, C, Y = 4, 4, 2, 4
 CAP, ROWS, WIDTH, FF, HD, HEADS, TOK = 96, 256, 2048, 512, 128, 4, 1024
-WEIGHT = 4
+WEIGHT = 3
+EARLY = ("pack", "fetch", "expert", "down_grad", "up_grad")
 BLOCKS = Z * X * C
 
 
@@ -41,6 +42,7 @@
 
 
 def call(body, name, outs, ins, flops=0, moved=0, grid=None, in_specs=None, out_specs=None, limit=24, scratch=(), free=(), near=(), held=()):
+    weight = 4 if name in EARLY else WEIGHT
     kwargs = {} if grid is None else {"grid": grid}
     specs = in_specs or [full() for _ in ins]
     ins = [
@@ -55,7 +57,7 @@
         out_specs=out_specs or [full() for _ in outs],
         scratch_shapes=scratch,
         compiler_params=pltpu.CompilerParams(vmem_limit_bytes=limit << 20),
-        cost_estimate=pl.CostEstimate(flops=WEIGHT * flops, bytes_accessed=WEIGHT * moved, transcendentals=0),
+        cost_estimate=pl.CostEstimate(flops=weight * flops, bytes_accessed=weight * moved, transcendentals=0),
         **kwargs,
     )(*ins)
 
@@ -111,18 +113,19 @@
 
 BACK = WIDTH + 128
 N = Y * CAP
-BUNDLE = 2 * WIDTH + 3 * FF
-GB, HID = 2 * WIDTH, 2 * WIDTH + 2 * FF
+BUNDLE = WIDTH + 2 * FF
+SIDE = WIDTH + FF
+GB = HID = WIDTH
 STEP = 256
 
 
-def expert_body(r0, r1, r2, r3, wp, wb, b0, b1, b2, b3, held, back, in_sem, out_sem):
+def expert_body(r0, r1, r2, r3, wp, wb, b0, b1, b2, b3, held, side, back, in_sem, out_sem):
     arrived = (r0, r1, r2, r3)
     backs = (b0, b1, b2, b3)
     tiles = FF // STEP
 
     def incoming(half, s):
-        dst = held.at[pl.ds(s * CAP, CAP), pl.ds(half * WIDTH, WIDTH)]
+        dst = (side if half else held).at[pl.ds(s * CAP, CAP), pl.ds(0, WIDTH)]
         return pltpu.make_async_copy(arrived[s].at[half], dst, in_sem.at[half * Y + s])
 
     for s in range(Y):
@@ -139,11 +142,11 @@
         if j == 0:
             for s in range(Y):
                 incoming(1, s).wait()
-        grad_hidden = dot_t(held[:, WIDTH:GB], wb[0, at : at + STEP, :])
+        grad_hidden = dot_t(side[:, :WIDTH], wb[0, at : at + STEP, :])
         s = 1.0 / (1.0 + jnp.exp(-first))
         silu = first * s
         hidden = (silu * second).astype(bf16)
-        held[:, HID + at : HID + at + STEP] = hidden
+        side[:, HID + at : HID + at + STEP] = hidden
         total += jnp.sum(hidden.astype(f32) * grad_hidden, axis=1, keepdims=True)
         slope = s * (1.0 + first * (1.0 - s))
         held[:, GB + at : GB + at + STEP] = (grad_hidden * second * slope).astype(bf16)
@@ -156,7 +159,7 @@
     for part in range(2):
         lo_col, hi_col = bounds[part], bounds[part + 1]
         for at in range(lo_col, min(hi_col, WIDTH), STEP):
-            back[:, at : at + STEP] = dot_t(held[:, GB:HID], wp[0, at : at + STEP, :]).astype(bf16)
+            back[:, at : at + STEP] = dot_t(held[:, GB:], wp[0, at : at + STEP, :]).astype(bf16)
         cols = pl.ds(lo_col, hi_col - lo_col)
         for s in range(Y):
             src = back.at[pl.ds(s * CAP, CAP), cols]
@@ -197,7 +200,7 @@
 
 
 def expert(chunks, w_pair, w_back):
-    outs = [((CAP, BACK), bf16)] * Y + [((N, BUNDLE), bf16)]
+    outs = [((CAP, BACK), bf16)] * Y + [((N, BUNDLE), bf16), ((N, SIDE), bf16)]
     ins = (*chunks, w_pair, w_back)
     return call(
         expert_body,
@@ -207,7 +210,7 @@
         5 * 2 * N * WIDTH * FF,
         14 << 20,
         in_specs=[anywhere() for _ in chunks] + [full(), full()],
-        out_specs=[anywhere()] * Y + [full()],
+        out_specs=[anywhere()] * Y + [full()] * 2,
         scratch=[
             VMEM((N, BACK), bf16),
             pltpu.SemaphoreType.DMA((2 * Y,)),
@@ -216,7 +219,7 @@
         limit=16,
         free=(1, 2, 3),
         held=(4, 5),
-        near=(Y,),
+        near=(Y, Y + 1),
     )
 
 
@@ -226,65 +229,79 @@
     return (col == (row // run) * (2 * run) + core * run + row % run).astype(bf16)
 
 
-def weights_body(at_ref, mine, other, out_hbm, out, rows_t, hid_t, sem):
-    core = at_ref[4]
-    pick_row, pick_hid = chooser(core, 512, 64), chooser(core, 128, 16)
+def down_body(side, out_hbm, out, hid_t, sem):
+    row = lax.broadcasted_iota(jnp.int32, (FF, FF), 0)
+    col = lax.broadcasted_iota(jnp.int32, (FF, FF), 1)
+    hid_t[...] = dot_t((row == col).astype(bf16), side[:, HID:]).astype(bf16)
+    copies = []
+    for j in range(WIDTH // 512):
+        cols = slice(j * 512, (j + 1) * 512)
+        out[:, cols] = dot(hid_t[...], side[:, cols]).astype(bf16)
+        here = pl.ds(j * 512, 512)
+        copies.append(pltpu.make_async_copy(out.at[:, here], out_hbm.at[:, here], sem.at[j]))
+        copies[-1].start()
+    for copy in copies:
+        copy.wait()
+
+
+def down_grad(side):
+    return call(
+        down_body,
+        "down_grad",
+        [((FF, WIDTH), bf16)],
+        (side,),
+        2 * N * WIDTH * FF,
+        4 << 20,
+        in_specs=[full()],
+        out_specs=[anywhere()],
+        scratch=[VMEM((FF, WIDTH), bf16), VMEM((FF, N), bf16), pltpu.SemaphoreType.DMA((4,))],
+        limit=8,
+        held=(0,),
+    )[0]
+
+
+def up_body(at_ref, mine, other, out_hbm, out, rows_t, sem):
+    pick_row = chooser(at_ref[4], 512, 64)
     for k, src in enumerate((mine, other)):
         for i in range(Z):
             rows_t[k, i * 256 : (i + 1) * 256, :] = dot_t(pick_row, src[:, i * 512 : (i + 1) * 512]).astype(bf16)
-            cols = slice(HID + i * 128, HID + (i + 1) * 128)
-            hid_t[k, i * 64 : (i + 1) * 64, :] = dot_t(pick_hid, src[:, cols]).astype(bf16)
+    copies = []
     for j in range(4):
         cols = slice(GB + j * STEP, GB + (j + 1) * STEP)
         up = (dot(rows_t[0], mine[:, cols]) + dot(rows_t[1], other[:, cols])).astype(bf16)
         for k in range(Z * X):
-            out[k, :64, j * STEP : (j + 1) * STEP] = up[k * 64 : (k + 1) * 64]
-    copies = [pltpu.make_async_copy(out.at[:, pl.ds(0, 64)], out_hbm.at[:, pl.ds(0, 64)], sem.at[0])]
-    copies[0].start()
-    for j in range(8):
-        cols = slice(WIDTH + j * STEP, WIDTH + (j + 1) * STEP)
-        down = (dot(hid_t[0], mine[:, cols]) + dot(hid_t[1], other[:, cols])).astype(bf16)
-        row, col = 64 + 16 * (j // 4), (j % 4) * STEP
-        for k in range(Z * X):
-            out[k, row : row + 16, col : col + STEP] = down[k * 16 : (k + 1) * 16]
-        if j % 4 == 3:
-            part = pl.ds(row, 16)
-            copies.append(pltpu.make_async_copy(out.at[:, part], out_hbm.at[:, part], sem.at[1 + j // 4]))
-            copies[-1].start()
+            out[k, :, j * STEP : (j + 1) * STEP] = up[k * 64 : (k + 1) * 64]
+        here = pl.ds(j * STEP, STEP)
+        copies.append(pltpu.make_async_copy(out.at[:, :, here], out_hbm.at[:, :, here], sem.at[j]))
+        copies[-1].start()
     for copy in copies:
         copy.wait()
 
 
-def weights(at, mine, other):
-    return call(
-        weights_body,
-        "weights",
-        [((Z * X, 96, 1024), bf16)],
+def up_grad(at, mine, other):
+    shape = (Z * X, 64, 1024)
+    return call(
+        up_body,
+        "up_grad",
+        [(shape, bf16)],
         (at, mine, other),
-        3 * 2 * N * WIDTH * FF,
-        12 << 20,
+        2 * 2 * N * WIDTH * FF,
+        8 << 20,
         in_specs=[scalars(), full(), full()],
         out_specs=[anywhere()],
-        scratch=[
-            VMEM((Z * X, 96, 1024), bf16),
-            VMEM((2, 1024, N), bf16),
-            VMEM((2, 256, N), bf16),
-            pltpu.SemaphoreType.DMA((3,)),
-        ],
-        limit=16,
+        scratch=[VMEM(shape, bf16), VMEM((2, 1024, N), bf16), pltpu.SemaphoreType.DMA((4,))],
+        limit=12,
         held=(1, 2),
     )[0]
 
 
-def gather_sum_body(pieces_ref, up_ref, down_ref):
+def gather_sum_body(pieces_ref, up_ref):
     for j in range(2):
-        at = j * 512
-        total = pieces_ref[0, :, at : at + 512].astype(f32)
+        cols = slice(j * 512, (j + 1) * 512)
+        total = pieces_ref[0, :, cols].astype(f32)
         for k in range(1, Z * X):
-            total = total + pieces_ref[k, :, at : at + 512].astype(f32)
-        up_ref[0, :, at : at + 512] = total[:64]
-        down_ref[0, :, at : at + 512] = total[64:80]
-        down_ref[0, :, 1024 + at : 1024 + at + 512] = total[80:96]
+            total = total + pieces_ref[k, :, cols].astype(f32)
+        up_ref[0, :, cols] = total
 
 
 def project_body(*refs):
@@ -558,10 +575,12 @@
     prior = prefix_state[0]
     w_pair, w_back = fetch(w_pair, w_down)
     queries, keys, values = attn_query, attn_key, attn_value
-    b0, b1, b2, b3, bundle = expert(held, w_pair, w_back)
+    b0, b1, b2, b3, bundle, side = expert(held, w_pair, w_back)
     backs = [b0] + [along_y(b, -s) for s, b in ((1, b1), (2, b2), (3, b3))]
-    other_bundle, backs[1] = lax.optimization_barrier((across(bundle), backs[1]))
-    partial = weights(at, bundle, other_bundle)
+    down = lax.psum_scatter(down_grad(side), "ctx", scatter_dimension=0, tiled=True)
+    other_bundle = across(bundle)
+    partial = up_grad(at, bundle, other_bundle)
+    _, backs[2], backs[3] = lax.optimization_barrier((partial, backs[2], backs[3]))
     groups = [[index(i, j, k) for i in range(Z) for j in range(X)] for k in range(C)]
     exchanged = lax.all_to_all(partial, "ctx", 0, 0, axis_index_groups=groups, tiled=True)
 
@@ -584,9 +603,10 @@
     sums = (other, *from_x, *from_z)
     grad_key, grad_value = final(at, sums, values, keys, key_here, value_here)
 
-    exchanged, grad_key = lax.optimization_barrier((exchanged, grad_key))
-    outs = [((1, 64, 1024), f32), ((1, 16, WIDTH), f32)]
-    grad_gate_up, grad_down = call(gather_sum_body, "gather_sum", outs, (exchanged,), 0, 4 << 20, free=(0,))
+    exchanged, down, grad_key = lax.optimization_barrier((exchanged, down, grad_key))
+    outs = [((1, 64, 1024), f32)]
+    (grad_gate_up,) = call(gather_sum_body, "gather_sum", outs, (exchanged,), 0, 4 << 20, limit=8, free=(0,))
+    grad_down = down.astype(f32)[None]
     return (grad_query, grad_key, grad_value, grad_resid, grad_gates, grad_gate_up, grad_down)
 
 

time: 161 us -> 163 us (1.012)
  waiting for transfers between devices: 64.2 us -> 58.2 us
  Pallas kernels: 45.6 us -> 50.1 us
  starting transfers between devices: 34.8 us -> 37.4 us
    reduce_scatter x0 -> x1, waiting for transfers between devices: none -> 11.9 us  [on_device(): lax.psum_scatter(down_grad(side), 'ctx', scatter_dimension=0, tiled=True)]
    ppermute x12, waiting for transfers between devices: 53.6 us -> 44.3 us  [along_y(): return lax.ppermute(a, 'exp', [(i, (i + s) % Y) for i in range(Y)])]
    ppermute x3, waiting for transfers between devices: 9 us -> 0.01 us  [along_x(): lax.ppermute(a, 'ctx', [(index(z, x, c), index(z, (x + s) % X, c)) for z,...]
    pallas_call x12 -> x13, Pallas kernels: 45.6 us -> 50.1 us  [call(): pl.pallas_call(body, name=name, out_shape=[(VMEM if near is True or i in...]
    ppermute x12, starting transfers between devices: 14.9 us -> 16.7 us  [along_y(): return lax.ppermute(a, 'exp', [(i, (i + s) % Y) for i in range(Y)])]
  transfers between devices with their start and end apart: 22 -> 23, of which waited for: 10 -> 10; matrix products, arithmetic and copies ran while one was open for 0% -> 0% of each run, Pallas kernels for 28% -> 30%
where the time goes in v6:
time: 163 us
  waiting for transfers between devices  58.2 us (36%)
  Pallas kernels  50.1 us (31%)
  starting transfers between devices  37.4 us (23%)
  between operations  14.2 us (9%)
  local copies, waits for them, and re-layouts  1.82 us (1%)
    pallas_call x13, Pallas kernels, call(): pl.pallas_call(body, name=name, out_shape=[(VMEM if near is True or i in...  50.1 us
    ppermute x12, waiting for transfers between devices, along_y(): return lax.ppermute(a, 'exp', [(i, (i + s) % Y) for i in range(Y)])  44.3 us
    ppermute x12, starting transfers between devices, along_y(): return lax.ppermute(a, 'exp', [(i, (i + s) % Y) for i in range(Y)])  16.7 us
    reduce_scatter x1, waiting for transfers between devices, on_device(): lax.psum_scatter(down_grad(side), 'ctx', scatter_dimension=0, tiled=True)  11.9 us
    all_to_all x1, starting transfers between devices, on_device(): lax.all_to_all(partial, 'ctx', 0, 0, axis_index_groups=groups, tiled=True)  7.91 us
    ppermute x3, starting transfers between devices, along_z(): lax.ppermute(a, 'ctx', [(index(z, x, c), index((z + s) % Z, x, c)) for z,...  6.59 us
    ppermute x3, starting transfers between devices, along_x(): lax.ppermute(a, 'ctx', [(index(z, x, c), index(z, (x + s) % X, c)) for z,...  5.83 us
  transfers between devices with their start and end apart: 23, of which 10 were waited for; matrix products, arithmetic and copies ran while one was open for 0% of the time, Pallas kernels for 30%

profile of v6, /device:TPU:0, one launch (start us, length us, event | category | flops | bytes accessed | tf_op | source)
XLA Modules:
  0.0 163.1 jit_solution(7722743913992956909)
XLA Ops:
  8.1 1.7 %collective-permute-start = (bf16[16,2048]{1,0:T(8,128)(2,1)S(1)}, bf16[16,2048]{1,0:T(8,128)(2,1)S(1)}, u32[]{:S(2)}, u32[]{:S(2)}) collective-permute-start(bf16[16,2048]{1,0:T(8,128)(2,1)S(1)} %constant_dynamic-slice_fusion), channel_id=1, source_target_pairs={{0,1},{1,2},{2,3},{3,0},{4,5},{5,6},{6,7},{7,4},{8,9},{9,10},{10,1... | collective-permute-start | bytes 196616 | tf_op jit(solution)/shard_map/ppermute | solution.py:530
  9.7 2.9 %collective-permute-start.1 = (bf16[16,2048]{1,0:T(8,128)(2,1)S(1)}, bf16[16,2048]{1,0:T(8,128)(2,1)S(1)}, u32[]{:S(2)}, u32[]{:S(2)}) collective-permute-start(bf16[16,2048]{1,0:T(8,128)(2,1)S(1)} %constant_dynamic-slice_fusion), channel_id=1, source_target_pairs={{0,2},{1,3},{2,0},{3,1},{4,6},{5,7},{6,4},{7,5},{8,10},{9,11},{10,... | collective-permute-start | bytes 196616 | tf_op jit(solution)/shard_map/ppermute | solution.py:530
  14.1 3.9 %pack.1 = (bf16[384,256]{1,0:T(8,128)(2,1)}, bf16[256,384]{1,0:T(8,128)(2,1)}, bf16[2,96,2048]{2,1,0:T(8,128)(2,1)}, bf16[2,96,2048]{2,1,0:T(8,128)(2,1)}, bf16[...) custom-call(s32[5]{0:T(128)S(1)} %stack.23.at_ref.spot_ref, s32[1,256]{1,0:T(1,128)} %bitcast.15, ...), custom_call_target="tpu_custom_call" | custom-call | flops 3221225472 | bytes 20971520 | tf_op jit(solution)/shard_map/pack/pallas_call | solution.py:52
  19.2 2.9 %collective-permute-start.5 = (bf16[2,96,2048]{2,1,0:T(8,128)(2,1)}, bf16[2,96,2048]{2,1,0:T(8,128)(2,1)S(1)}, u32[]{:S(2)}, u32[]{:S(2)}) collective-permute-start(bf16[2,96,2048]{2,1,0:T(8,128)(2,1)} %get-tuple-element.54), channel_id=1, source_target_pairs={{0,3},{1,0},{2,1},{3,2},{4,7},{5,4},{6,5},{7,6},{8,11},{9,8},{10,9... | collective-permute-start | bytes 2359304 | tf_op jit(solution)/shard_map/ppermute | solution.py:530
  22.2 2.9 %fetch.1 = (bf16[1,2048,1024]{2,1,0:T(8,128)(2,1)S(1)}, bf16[1,512,2048]{2,1,0:T(8,128)(2,1)S(1)}) custom-call(bf16[1,2048,1024]{2,1,0:T(8,128)(2,1)} %refs_0_.1, bf16[1,512,2048]{2,1,0:T(8,128)(2,1)} %refs_1_.1), custom_call_target="tpu_custom_call" | custom-call | bytes 50331648 | tf_op jit(solution)/shard_map/fetch/pallas_call | solution.py:52
  25.1 16.0 %collective-permute-done.4.r2 = bf16[2,96,2048]{2,1,0:T(8,128)(2,1)S(1)} collective-permute-done((bf16[2,96,2048]{2,1,0:T(8,128)(2,1)}, bf16[2,96,2048]{2,1,0:T(8,128)(2,1)S(1)}, u32[]{:S(2)}, u32[]{:S(2)}) %collective-permute-start.4) | collective-permute-done | bytes 786464 | tf_op jit(solution)/shard_map/ppermute | solution.py:530
  41.1 12.8 %collective-permute-done.5.r3 = bf16[2,96,2048]{2,1,0:T(8,128)(2,1)S(1)} collective-permute-done((bf16[2,96,2048]{2,1,0:T(8,128)(2,1)}, bf16[2,96,2048]{2,1,0:T(8,128)(2,1)S(1)}, u32[]{:S(2)}, u32[]{:S(2)}) %collective-permute-start.5) | collective-permute-done | bytes 786464 | tf_op jit(solution)/shard_map/ppermute | solution.py:530
  53.8 2.0 %collective-permute-done.3.r1 = bf16[2,96,2048]{2,1,0:T(8,128)(2,1)S(1)} collective-permute-done((bf16[2,96,2048]{2,1,0:T(8,128)(2,1)}, bf16[2,96,2048]{2,1,0:T(8,128)(2,1)S(1)}, u32[]{:S(2)}, u32[]{:S(2)}) %collective-permute-start.3) | collective-permute-done | bytes 786464 | tf_op jit(solution)/shard_map/ppermute | solution.py:530
  55.8 8.2 %expert.1 = (bf16[96,2176]{1,0:T(8,128)(2,1)}, bf16[96,2176]{1,0:T(8,128)(2,1)}, bf16[96,2176]{1,0:T(8,128)(2,1)}, bf16[96,2176]{1,0:T(8,128)(2,1)}, bf16[384,30...) custom-call(bf16[2,96,2048]{2,1,0:T(8,128)(2,1)} %get-tuple-element.51.r0, ...), custom_call_target="tpu_custom_call" | custom-call | flops 16106127360 | bytes 58720256 | tf_op jit(solution)/shard_map/expert/pallas_call | solution.py:52
  65.7 3.0 %collective-permute-start.6 = (bf16[96,2176]{1,0:T(8,128)(2,1)}, bf16[96,2176]{1,0:T(8,128)(2,1)S(1)}, u32[]{:S(2)}, u32[]{:S(2)}) collective-permute-start(bf16[96,2176]{1,0:T(8,128)(2,1)} %get-tuple-element.59), channel_id=1, source_target_pairs={{0,3},{1,0},{2,1},{3,2},{4,7},{5,4},{6,5},{7,6},{8,11},{9,8},{10,9... | collective-permute-start | bytes 1253384 | tf_op jit(solution)/shard_map/ppermute | solution.py:530
  68.7 2.4 %down_grad.1 = bf16[512,2048]{1,0:T(8,128)(2,1)} custom-call(bf16[384,2560]{1,0:T(8,128)(2,1)S(1)} %get-tuple-element.71.side), custom_call_target="tpu_custom_call" | custom-call | flops 3221225472 | bytes 16777216 | tf_op jit(solution)/shard_map/down_grad/pallas_call | solution.py:52
  71.2 7.0 %up_grad.1 = bf16[16,64,1024]{2,1,0:T(8,128)(2,1)} custom-call(s32[5]{0:T(128)S(1)} %stack.23.at_ref.spot_ref, bf16[384,3072]{1,0:T(8,128)(2,1)} %get-tuple-element.60.mine, bf16[384,3072]{1,0:T(8,128)(2,1)} %collective-permute-done.7.other), custom_call_target="tpu_custom_call" | custom-call | flops 6442450944 | bytes 33554432 | tf_op jit(solution)/shard_map/up_grad/pallas_call | solution.py:52
  78.2 7.9 %all-to-all-start = ((bf16[16,64,1024]{2,1,0:T(8,128)(2,1)}), bf16[16,64,1024]{2,1,0:T(8,128)(2,1)S(1)}, u32[]{:S(2)}, u32[]{:S(2)}) async-start(bf16[16,64,1024]{2,1,0:T(8,128)(2,1)} %up_grad.1), calls=%async_computation | async-start | bytes 4194304 | tf_op jit(solution)/shard_map/all_to_all | solution.py:585
  87.7 8.5 %project.1 = (bf16[256,2048]{1,0:T(8,128)(2,1)}, bf16[1,256]{1,0:T(2,128)(2,1)}, bf16[256,512]{1,0:T(8,128)(2,1)S(1)}, bf16[256,512]{1,0:T(8,128)(2,1)S(1)}, bf1...) custom-call(bf16[512,2048]{1,0:T(8,128)(2,1)} %refs_0_.2, bf16[32,3,16,2048]{3,2,1,0:T(8,128)(2,1)} %bitcast.14, ...), custom_call_target="tpu_custom_call" | custom-call | flops 7650410496 | bytes 31457280 | tf_op jit(solution)/shard_map/project/pallas_call | solution.py:52
  99.0 6.4 %collective-permute-done.10.g1 = bf16[256,512]{1,0:T(8,128)(2,1)S(1)} collective-permute-done((bf16[256,512]{1,0:T(8,128)(2,1)S(1)}, bf16[256,512]{1,0:T(8,128)(2,1)S(1)}, u32[]{:S(2)}, u32[]{:S(2)}) %collective-permute-start.10) | collective-permute-done | bytes 262176 | tf_op jit(solution)/shard_map/ppermute | solution.py:530
  105.4 2.2 %collective-permute-done.11.g2 = bf16[256,512]{1,0:T(8,128)(2,1)S(1)} collective-permute-done((bf16[256,512]{1,0:T(8,128)(2,1)S(1)}, bf16[256,512]{1,0:T(8,128)(2,1)S(1)}, u32[]{:S(2)}, u32[]{:S(2)}) %collective-permute-start.11) | collective-permute-done | bytes 262176 | tf_op jit(solution)/shard_map/ppermute | solution.py:530
  107.6 4.2 %collective-permute-done.12.g3 = bf16[256,512]{1,0:T(8,128)(2,1)S(1)} collective-permute-done((bf16[256,512]{1,0:T(8,128)(2,1)S(1)}, bf16[256,512]{1,0:T(8,128)(2,1)S(1)}, u32[]{:S(2)}, u32[]{:S(2)}) %collective-permute-start.12) | collective-permute-done | bytes 262176 | tf_op jit(solution)/shard_map/ppermute | solution.py:530
  116.5 2.7 %collective-permute-start.15 = (bf16[512,128]{1,0:T(8,128)(2,1)S(1)}, bf16[512,128]{1,0:T(8,128)(2,1)S(1)}, u32[]{:S(2)}, u32[]{:S(2)}) collective-permute-start(bf16[512,128]{1,0:T(8,128)(2,1)S(1)} %get-tuple-element.73), channel_id=1, source_target_pairs={{0,16},{4,20},{8,24},{12,28},{16,0},{20,4},{24,8},{28,12},{32,48},... | collective-permute-start | bytes 393224 | tf_op jit(solution)/shard_map/ppermute | solution.py:534
  120.6 8.2 %query_key.1 = (bf16[1024,512]{1,0:T(8,128)(2,1)}, bf16[1024,512]{1,0:T(8,128)(2,1)S(1)}) custom-call(s32[5]{0:T(128)S(1)} %stack.23.at_ref.spot_ref, bf16[1024,512]{1,0:T(8,128)(2,1)S(1)} %copy-done, bf16[1024,512]{1,0:T(8,128)(2,1)S(1)} %copy-done.1, bf16[1024,512]{1,0:T(8,128)(2,1)S(1)} %copy-done.2, bf16[1024,512]{1,0:T(8,128)(2,1)S(1)} %get-tuple-element.69.g_ref, ...), custom_call_target="tpu_custom_call" | custom-call | flops 8053063680 | bytes 18874368 | tf_op jit(solution)/shard_map/query_key/pallas_call | solution.py:52
  128.9 2.0 %collective-permute-start.17 = (bf16[512,128]{1,0:T(8,128)(2,1)S(1)}, bf16[512,128]{1,0:T(8,128)(2,1)S(1)}, u32[]{:S(2)}, u32[]{:S(2)}) collective-permute-start(bf16[512,128]{1,0:T(8,128)(2,1)S(1)} %line.1), channel_id=1, source_target_pairs={{0,32},{4,36},{8,40},{12,44},{16,48},{20,52},{24,56},{28,60},{32,6... | collective-permute-start | bytes 393224 | tf_op jit(solution)/shard_map/ppermute | solution.py:538
  130.9 3.7 %collective-permute-start.18 = (bf16[512,128]{1,0:T(8,128)(2,1)S(1)}, bf16[512,128]{1,0:T(8,128)(2,1)S(1)}, u32[]{:S(2)}, u32[]{:S(2)}) collective-permute-start(bf16[512,128]{1,0:T(8,128)(2,1)S(1)} %line.1), channel_id=1, source_target_pairs={{0,64},{4,68},{8,72},{12,76},{16,80},{20,84},{24,88},{28,92},{32,9... | collective-permute-start | bytes 393224 | tf_op jit(solution)/shard_map/ppermute | solution.py:538
  135.5 4.1 %value.1.value_ref = bf16[1024,512]{1,0:T(8,128)(2,1)S(1)} custom-call(s32[5]{0:T(128)S(1)} %stack.23.at_ref.spot_ref, bf16[1024,512]{1,0:T(8,128)(2,1)S(1)} %copy-done, bf16[1024,512]{1,0:T(8,128)(2,1)S(1)} %copy-done.1, bf16[1024,512]{1,0:T(8,128)(2,1)S(1)} %get-tuple-element.69.g_ref), custom_call_target="tpu_custom_call" | custom-call | flops 4026531840 | bytes 18874368 | tf_op jit(solution)/shard_map/value/pallas_call | solution.py:52
  140.0 2.7 %final.1 = (bf16[1024,512]{1,0:T(8,128)(2,1)}, bf16[1024,512]{1,0:T(8,128)(2,1)}) custom-call(s32[5]{0:T(128)S(1)} %stack.23.at_ref.spot_ref, f32[512,128]{1,0:T(8,128)S(1)} %collective-permute-done.13.other, bf16[512,128]{1,0:T(8,128)(2,1)S(1)} %collective-permute-done.14.x1, bf16[512,128]{1,0:T(8,128)(2,1)S(1)} %collective-permute-done.15.x2, ...), custom_call_target="tpu_custom_call" | custom-call | flops 1610612736 | bytes 25165824 | tf_op jit(solution)/shard_map/final/pallas_call | solution.py:52
  142.7 11.9 %reduce-scatter.2.cloned.1.call-done = bf16[16,2048]{1,0:T(8,128)(2,1)} async-done(((bf16[512,2048]{1,0:T(8,128)(2,1)}), bf16[16,2048]{1,0:T(8,128)(2,1)}) %reduce-scatter.2.cloned.1.call-update) | async-done | bytes 65552 | tf_op jit(solution)/shard_map/reduce_scatter | solution.py:580
  (57 shorter events, 18.9 us)
Async XLA Ops:
  7.2 79.6 %all-gather.3.cloned.1.call-start = ((), (), s32[]{:S(2)}) async-start(), calls=%async_computation.3 | async-start | bytes 6488064 | tf_op jit(solution)/shard_map/all_gather | solution.py:569
  8.1 9.9 %collective-permute-start = (bf16[16,2048]{1,0:T(8,128)(2,1)S(1)}, bf16[16,2048]{1,0:T(8,128)(2,1)S(1)}, u32[]{:S(2)}, u32[]{:S(2)}) collective-permute-start(bf16[16,2048]{1,0:T(8,128)(2,1)S(1)} %constant_dynamic-slice_fusion), channel_id=1, source_target_pairs={{0,1},{1,2},{2,3},{3,0},{4,5},{5,6},{6,7},{7,4},{8,9},{9,10},{10,1... | collective-permute-start | bytes 196616 | tf_op jit(solution)/shard_map/ppermute | solution.py:530
  9.7 8.2 %collective-permute-start.1 = (bf16[16,2048]{1,0:T(8,128)(2,1)S(1)}, bf16[16,2048]{1,0:T(8,128)(2,1)S(1)}, u32[]{:S(2)}, u32[]{:S(2)}) collective-permute-start(bf16[16,2048]{1,0:T(8,128)(2,1)S(1)} %constant_dynamic-slice_fusion), channel_id=1, source_target_pairs={{0,2},{1,3},{2,0},{3,1},{4,6},{5,7},{6,4},{7,5},{8,10},{9,11},{10,... | collective-permute-start | bytes 196616 | tf_op jit(solution)/shard_map/ppermute | solution.py:530
  12.6 5.3 %collective-permute-start.2 = (bf16[16,2048]{1,0:T(8,128)(2,1)S(1)}, bf16[16,2048]{1,0:T(8,128)(2,1)S(1)}, u32[]{:S(2)}, u32[]{:S(2)}) collective-permute-start(bf16[16,2048]{1,0:T(8,128)(2,1)S(1)} %constant_dynamic-slice_fusion), channel_id=1, source_target_pairs={{0,3},{1,0},{2,1},{3,2},{4,7},{5,4},{6,5},{7,6},{8,11},{9,8},{10,9... | collective-permute-start | bytes 196616 | tf_op jit(solution)/shard_map/ppermute | solution.py:530
  18.7 135.9 %reduce-scatter.2.cloned.1.call-start = ((), (), s32[]{:S(2)}) async-start(), calls=%async_computation.2 | async-start | bytes 2162688 | tf_op jit(solution)/shard_map/reduce_scatter | solution.py:580
  18.7 22.3 %collective-permute-start.4 = (bf16[2,96,2048]{2,1,0:T(8,128)(2,1)}, bf16[2,96,2048]{2,1,0:T(8,128)(2,1)S(1)}, u32[]{:S(2)}, u32[]{:S(2)}) collective-permute-start(bf16[2,96,2048]{2,1,0:T(8,128)(2,1)} %get-tuple-element.53), channel_id=1, source_target_pairs={{0,2},{1,3},{2,0},{3,1},{4,6},{5,7},{6,4},{7,5},{8,10},{9,11},{10,... | collective-permute-start | bytes 2359304 | tf_op jit(solution)/shard_map/ppermute | solution.py:530
  19.2 34.6 %collective-permute-start.5 = (bf16[2,96,2048]{2,1,0:T(8,128)(2,1)}, bf16[2,96,2048]{2,1,0:T(8,128)(2,1)S(1)}, u32[]{:S(2)}, u32[]{:S(2)}) collective-permute-start(bf16[2,96,2048]{2,1,0:T(8,128)(2,1)} %get-tuple-element.54), channel_id=1, source_target_pairs={{0,3},{1,0},{2,1},{3,2},{4,7},{5,4},{6,5},{7,6},{8,11},{9,8},{10,9... | collective-permute-start | bytes 2359304 | tf_op jit(solution)/shard_map/ppermute | solution.py:530
  22.2 33.7 %collective-permute-start.3 = (bf16[2,96,2048]{2,1,0:T(8,128)(2,1)}, bf16[2,96,2048]{2,1,0:T(8,128)(2,1)S(1)}, u32[]{:S(2)}, u32[]{:S(2)}) collective-permute-start(bf16[2,96,2048]{2,1,0:T(8,128)(2,1)} %get-tuple-element.52), channel_id=1, source_target_pairs={{0,1},{1,2},{2,3},{3,0},{4,5},{5,6},{6,7},{7,4},{8,9},{9,10},{10,1... | collective-permute-start | bytes 2359304 | tf_op jit(solution)/shard_map/ppermute | solution.py:530
  64.0 7.2 %collective-permute-start.7 = (bf16[384,3072]{1,0:T(8,128)(2,1)}, bf16[384,3072]{1,0:T(8,128)(2,1)}, u32[]{:S(2)}, u32[]{:S(2)}) collective-permute-start(bf16[384,3072]{1,0:T(8,128)(2,1)} %get-tuple-element.60.mine), channel_id=1, source_target_pairs={{0,4},{4,0},{8,12},{12,8},{16,20},{20,16},{24,28},{28,24},{32,36},... | collective-permute-start | bytes 7077896 | tf_op jit(solution)/shard_map/ppermute | solution.py:542
  64.2 21.9 %collective-permute-start.8 = (bf16[96,2176]{1,0:T(8,128)(2,1)}, bf16[96,2176]{1,0:T(8,128)(2,1)S(1)}, u32[]{:S(2)}, u32[]{:S(2)}) collective-permute-start(bf16[96,2176]{1,0:T(8,128)(2,1)} %get-tuple-element.61), channel_id=1, source_target_pairs={{0,2},{1,3},{2,0},{3,1},{4,6},{5,7},{6,4},{7,5},{8,10},{9,11},{10,... | collective-permute-start | bytes 1253384 | tf_op jit(solution)/shard_map/ppermute | solution.py:530
  65.5 21.3 %collective-permute-start.9 = (bf16[96,2176]{1,0:T(8,128)(2,1)}, bf16[96,2176]{1,0:T(8,128)(2,1)S(1)}, u32[]{:S(2)}, u32[]{:S(2)}) collective-permute-start(bf16[96,2176]{1,0:T(8,128)(2,1)} %get-tuple-element.62), channel_id=1, source_target_pairs={{0,1},{1,2},{2,3},{3,0},{4,5},{5,6},{6,7},{7,4},{8,9},{9,10},{10,1... | collective-permute-start | bytes 1253384 | tf_op jit(solution)/shard_map/ppermute | solution.py:530
  65.7 21.1 %collective-permute-start.6 = (bf16[96,2176]{1,0:T(8,128)(2,1)}, bf16[96,2176]{1,0:T(8,128)(2,1)S(1)}, u32[]{:S(2)}, u32[]{:S(2)}) collective-permute-start(bf16[96,2176]{1,0:T(8,128)(2,1)} %get-tuple-element.59), channel_id=1, source_target_pairs={{0,3},{1,0},{2,1},{3,2},{4,7},{5,4},{6,5},{7,6},{8,11},{9,8},{10,9... | collective-permute-start | bytes 1253384 | tf_op jit(solution)/shard_map/ppermute | solution.py:530
  78.2 76.5 %all-to-all-start = ((bf16[16,64,1024]{2,1,0:T(8,128)(2,1)}), bf16[16,64,1024]{2,1,0:T(8,128)(2,1)S(1)}, u32[]{:S(2)}, u32[]{:S(2)}) async-start(bf16[16,64,1024]{2,1,0:T(8,128)(2,1)} %up_grad.1), calls=%async_computation | async-start | bytes 4194304 | tf_op jit(solution)/shard_map/all_to_all | solution.py:585
  96.2 24.5 %copy-start.1 = (bf16[1024,512]{1,0:T(8,128)(2,1)S(1)}, bf16[1024,512]{1,0:T(8,128)(2,1)}, u32[]{:S(2)}) copy-start(bf16[1024,512]{1,0:T(8,128)(2,1)} %k_ref.5) | copy-start | bytes 3145732
  96.2 9.2 %collective-permute-start.10 = (bf16[256,512]{1,0:T(8,128)(2,1)S(1)}, bf16[256,512]{1,0:T(8,128)(2,1)S(1)}, u32[]{:S(2)}, u32[]{:S(2)}) collective-permute-start(bf16[256,512]{1,0:T(8,128)(2,1)S(1)} %get-tuple-element.66), channel_id=1, source_target_pairs={{0,3},{1,0},{2,1},{3,2},{4,7},{5,4},{6,5},{7,6},{8,11},{9,8},{10,9... | collective-permute-start | bytes 786440 | tf_op jit(solution)/shard_map/ppermute | solution.py:530
  96.9 10.8 %collective-permute-start.11 = (bf16[256,512]{1,0:T(8,128)(2,1)S(1)}, bf16[256,512]{1,0:T(8,128)(2,1)S(1)}, u32[]{:S(2)}, u32[]{:S(2)}) collective-permute-start(bf16[256,512]{1,0:T(8,128)(2,1)S(1)} %get-tuple-element.67), channel_id=1, source_target_pairs={{0,2},{1,3},{2,0},{3,1},{4,6},{5,7},{6,4},{7,5},{8,10},{9,11},{10,... | collective-permute-start | bytes 786440 | tf_op jit(solution)/shard_map/ppermute | solution.py:530
  98.2 13.6 %collective-permute-start.12 = (bf16[256,512]{1,0:T(8,128)(2,1)S(1)}, bf16[256,512]{1,0:T(8,128)(2,1)S(1)}, u32[]{:S(2)}, u32[]{:S(2)}) collective-permute-start(bf16[256,512]{1,0:T(8,128)(2,1)S(1)} %get-tuple-element.68), channel_id=1, source_target_pairs={{0,1},{1,2},{2,3},{3,0},{4,5},{5,6},{6,7},{7,4},{8,9},{9,10},{10,1... | collective-permute-start | bytes 786440 | tf_op jit(solution)/shard_map/ppermute | solution.py:530
  113.1 1.6 collective-permute-start.13
  114.8 14.0 %collective-permute-start.14 = (bf16[512,128]{1,0:T(8,128)(2,1)S(1)}, bf16[512,128]{1,0:T(8,128)(2,1)S(1)}, u32[]{:S(2)}, u32[]{:S(2)}) collective-permute-start(bf16[512,128]{1,0:T(8,128)(2,1)S(1)} %get-tuple-element.73), channel_id=1, source_target_pairs={{0,8},{4,12},{8,16},{12,20},{16,24},{20,28},{24,0},{28,4},{32,40},... | collective-permute-start | bytes 393224 | tf_op jit(solution)/shard_map/ppermute | solution.py:534
  116.5 12.4 %collective-permute-start.15 = (bf16[512,128]{1,0:T(8,128)(2,1)S(1)}, bf16[512,128]{1,0:T(8,128)(2,1)S(1)}, u32[]{:S(2)}, u32[]{:S(2)}) collective-permute-start(bf16[512,128]{1,0:T(8,128)(2,1)S(1)} %get-tuple-element.73), channel_id=1, source_target_pairs={{0,16},{4,20},{8,24},{12,28},{16,0},{20,4},{24,8},{28,12},{32,48},... | collective-permute-start | bytes 393224 | tf_op jit(solution)/shard_map/ppermute | solution.py:534
  119.2 9.6 %collective-permute-start.16 = (bf16[512,128]{1,0:T(8,128)(2,1)S(1)}, bf16[512,128]{1,0:T(8,128)(2,1)S(1)}, u32[]{:S(2)}, u32[]{:S(2)}) collective-permute-start(bf16[512,128]{1,0:T(8,128)(2,1)S(1)} %get-tuple-element.73), channel_id=1, source_target_pairs={{0,24},{4,28},{8,0},{12,4},{16,8},{20,12},{24,16},{28,20},{32,56},... | collective-permute-start | bytes 393224 | tf_op jit(solution)/shard_map/ppermute | solution.py:534
  128.9 10.7 %collective-permute-start.17 = (bf16[512,128]{1,0:T(8,128)(2,1)S(1)}, bf16[512,128]{1,0:T(8,128)(2,1)S(1)}, u32[]{:S(2)}, u32[]{:S(2)}) collective-permute-start(bf16[512,128]{1,0:T(8,128)(2,1)S(1)} %line.1), channel_id=1, source_target_pairs={{0,32},{4,36},{8,40},{12,44},{16,48},{20,52},{24,56},{28,60},{32,6... | collective-permute-start | bytes 393224 | tf_op jit(solution)/shard_map/ppermute | solution.py:538
  130.9 9.1 %collective-permute-start.18 = (bf16[512,128]{1,0:T(8,128)(2,1)S(1)}, bf16[512,128]{1,0:T(8,128)(2,1)S(1)}, u32[]{:S(2)}, u32[]{:S(2)}) collective-permute-start(bf16[512,128]{1,0:T(8,128)(2,1)S(1)} %line.1), channel_id=1, source_target_pairs={{0,64},{4,68},{8,72},{12,76},{16,80},{20,84},{24,88},{28,92},{32,9... | collective-permute-start | bytes 393224 | tf_op jit(solution)/shard_map/ppermute | solution.py:538
  134.5 5.5 %collective-permute-start.19 = (bf16[512,128]{1,0:T(8,128)(2,1)S(1)}, bf16[512,128]{1,0:T(8,128)(2,1)S(1)}, u32[]{:S(2)}, u32[]{:S(2)}) collective-permute-start(bf16[512,128]{1,0:T(8,128)(2,1)S(1)} %line.1), channel_id=1, source_target_pairs={{0,96},{4,100},{8,104},{12,108},{16,112},{20,116},{24,120},{28,124... | collective-permute-start | bytes 393224 | tf_op jit(solution)/shard_map/ppermute | solution.py:538
  (7 other events, 76.4 us)
Sparse Core Ops, SparseCore 0:
  18.8 50.7 all-gather.2
  73.2 81.4 reduce-scatter.1

commit v7 on v5

--- a/solution.py
+++ b/solution.py
@@ -12,6 +12,7 @@
 Z, X, C, Y = 4, 4, 2, 4
 CAP, ROWS, WIDTH, FF, HD, HEADS, TOK = 96, 256, 2048, 512, 128, 4, 1024
 WEIGHT = 4
+EARLY = ("pack", "fetch", "expert", "weights")
 BLOCKS = Z * X * C
 
 
@@ -41,6 +42,7 @@
 
 
 def call(body, name, outs, ins, flops=0, moved=0, grid=None, in_specs=None, out_specs=None, limit=24, scratch=(), free=(), near=(), held=()):
+    weight = 4 if name in EARLY else WEIGHT
     kwargs = {} if grid is None else {"grid": grid}
     specs = in_specs or [full() for _ in ins]
     ins = [
@@ -55,7 +57,7 @@
         out_specs=out_specs or [full() for _ in outs],
         scratch_shapes=scratch,
         compiler_params=pltpu.CompilerParams(vmem_limit_bytes=limit << 20),
-        cost_estimate=pl.CostEstimate(flops=WEIGHT * flops, bytes_accessed=WEIGHT * moved, transcendentals=0),
+        cost_estimate=pl.CostEstimate(flops=weight * flops, bytes_accessed=weight * moved, transcendentals=0),
         **kwargs,
     )(*ins)
 
@@ -351,7 +353,7 @@
     )
 
 
-def state_body(at_ref, g0, g1, g2, g3, q_ref, grad_ref, state_ref):
+def state_body(at_ref, g0, g1, g2, g3, q_ref, grad_ref, keep_ref, send_ref):
     y, block = at_ref[0], at_ref[1]
     ramp = lax.broadcasted_iota(jnp.int32, (ROWS, 1), 0)
     sums = [jnp.zeros((HD, 2 * HD), f32) for _ in range(HEADS)]
@@ -363,22 +365,26 @@
             cols = slice(h * HD, (h + 1) * HD)
             both = jnp.concatenate(split(g[:, cols].astype(f32) * inverse), axis=1)
             sums[h] += t_dot(q_ref[pl.ds(off, ROWS), cols], both)
-    for h in range(HEADS):
-        state_ref[h * HD : (h + 1) * HD, :] = sums[h][:, :HD] + sums[h][:, HD:]
+    sums = [total[:, :HD] + total[:, HD:] for total in sums]
+    first = at_ref[4] == 0
+    for h in range(HEADS // 2):
+        rows = slice(h * HD, (h + 1) * HD)
+        keep_ref[rows, :] = jnp.where(first, sums[h], sums[h + 2])
+        send_ref[rows, :] = jnp.where(first, sums[h + 2], sums[h])
 
 
 def head_state(at, grads, queries):
     return call(
         state_body,
         "state",
-        [((TOK, HEADS * HD), bf16), ((HEADS * HD, HD), f32)],
+        [((TOK, HEADS * HD), bf16), ((HEADS * HD // 2, HD), f32), ((HEADS * HD // 2, HD), f32)],
         (at, *grads, queries),
         HEADS * 2 * TOK * HD * 2 * HD,
         4 << 20,
         in_specs=[scalars()] + [full()] * 5,
         limit=8,
         held=(1, 2, 3, 4, 5),
-        near=(0, 1),
+        near=(0, 1, 2),
     )
 
 
@@ -463,15 +469,21 @@
     )
 
 
-def final_body(spot_ref, other, x1, x2, x3, z1, z2, z3, v_ref, k_ref, key_ref, value_ref, key_hbm, value_hbm, outs, sem):
+def later_body(spot_ref, keep, other, x1, x2, x3, z1, z2, z3, own, send):
     z, x, core = spot_ref[2], spot_ref[3], spot_ref[4]
+    later = jnp.zeros(keep.shape, f32)
+    for s, a, b in ((1, x1, z1), (2, x2, z2), (3, x3, z3)):
+        later += jnp.where(s > x, a[...].astype(f32), 0.0) + jnp.where(s > z, b[...].astype(f32), 0.0)
+    own[...] = later + jnp.where(core == 0, other[...], 0.0)
+    send[...] = later + jnp.where(core == 1, keep[...], 0.0)
+
+
+def final_body(spot_ref, own, got, v_ref, k_ref, key_ref, value_ref, key_hbm, value_hbm, outs, sem):
+    core = spot_ref[4]
     copies = []
     for h in range(HEADS):
-        rows, cols = slice(h * HD, (h + 1) * HD), slice(h * HD, (h + 1) * HD)
-        later = jnp.where(core == 0, other[rows], 0.0)
-        for s, a, b in ((1, x1, z1), (2, x2, z2), (3, x3, z3)):
-            later += jnp.where(s > x, a[rows].astype(f32), 0.0) + jnp.where(s > z, b[rows].astype(f32), 0.0)
-        hi, lo = split(later)
+        rows, cols = slice((h % 2) * HD, (h % 2 + 1) * HD), slice(h * HD, (h + 1) * HD)
+        hi, lo = split(jnp.where(core == h // 2, own[rows], got[rows]))
         key = dot_t(v_ref[:, cols], jnp.concatenate([hi, lo], axis=0))
         outs[0, :, cols] = (key_ref[:, cols].astype(f32) + key[:, :HD] + key[:, HD:]).astype(bf16)
         value = dot(k_ref[:, cols], jnp.concatenate([hi, lo], axis=1))
@@ -493,11 +505,11 @@
         (spot, *sums, values, keys, key_here, value_here),
         HEADS * 8 * TOK * HD * HD,
         8 << 20,
-        in_specs=[scalars()] + [full()] * 11,
+        in_specs=[scalars()] + [full()] * 6,
         out_specs=[anywhere()] * 2,
         scratch=[VMEM((2, TOK, HEADS * HD), bf16), pltpu.SemaphoreType.DMA((2 * HEADS,))],
         limit=12,
-        held=range(1, 12),
+        held=range(1, 7),
     )
 
 
@@ -560,20 +572,20 @@
     queries, keys, values = attn_query, attn_key, attn_value
     b0, b1, b2, b3, bundle = expert(held, w_pair, w_back)
     backs = [b0] + [along_y(b, -s) for s, b in ((1, b1), (2, b2), (3, b3))]
-    other_bundle, backs[1] = lax.optimization_barrier((across(bundle), backs[1]))
-    partial = weights(at, bundle, other_bundle)
+    partial = weights(at, bundle, across(bundle))
+    _, backs[2], backs[3] = lax.optimization_barrier((partial, backs[2], backs[3]))
     groups = [[index(i, j, k) for i in range(Z) for j in range(X)] for k in range(C)]
     exchanged = lax.all_to_all(partial, "ctx", 0, 0, axis_index_groups=groups, tiled=True)
 
     grad_resid, gates_out, *per_head = project(w_out, rest, place, turned, gate_row, grad_out, backs)
     grad_gates = gates_out.reshape(ROWS, 1)
     grads = [per_head[0]] + [along_y(per_head[s], -s) for s in (1, 2, 3)]
-    attn_grad, state = head_state(at, grads, queries)
-
-    other = across(state)
-    size = (HEADS * HD, HD)
+    attn_grad, mine, send = head_state(at, grads, queries)
+
+    other = across(send)
+    size = (HEADS * HD // 2, HD)
     outs = [(size, f32), (size, bf16)]
-    chip, chip16 = call(chip_body, "chip", outs, (state, other), limit=4, held=(0, 1), near=(0, 1))
+    chip, chip16 = call(chip_body, "chip", outs, (mine, other), limit=4, held=(0, 1), near=(0, 1))
     from_x = [along_x(chip16, s) for s in (1, 2, 3)]
     ins = (at, queries, keys, values, attn_grad, prior)
     grad_query, key_here = head_call(query_key_body, "query_key", ins, 2, 1)
@@ -581,8 +593,11 @@
     (line16,) = call(line_body, "line", [(size, bf16)], (chip, *from_x), limit=4, held=range(4), near=(0,))
     from_z = [along_z(line16, s) for s in (1, 2, 3)]
     (value_here,) = head_call(value_body, "value", (at, queries, keys, attn_grad), 1, 0)
-    sums = (other, *from_x, *from_z)
-    grad_key, grad_value = final(at, sums, values, keys, key_here, value_here)
+    value_here, from_z[2] = lax.optimization_barrier((value_here, from_z[2]))
+    ins = (at, mine, other, *from_x, *from_z)
+    specs = [scalars()] + [full()] * 8
+    own, send = call(later_body, "later", [(size, f32)] * 2, ins, in_specs=specs, limit=4, held=range(1, 9), near=(0, 1))
+    grad_key, grad_value = final(at, (own, across(send)), values, keys, key_here, value_here)
 
     exchanged, grad_key = lax.optimization_barrier((exchanged, grad_key))
     outs = [((1, 64, 1024), f32), ((1, 16, WIDTH), f32)]

time: 161 us -> 158 us (0.981)
  waiting for transfers between devices: 64.2 us -> 59.6 us
    ppermute x12, waiting for transfers between devices: 53.6 us -> 44.5 us  [along_y(): return lax.ppermute(a, 'exp', [(i, (i + s) % Y) for i in range(Y)])]
    ppermute x2 -> x3, waiting for transfers between devices: 1.52 us -> 5.96 us  [across(): return lax.ppermute(a, 'ctx', [(i, i ^ 1) for i in range(BLOCKS)])]
    ppermute x12, starting transfers between devices: 14.9 us -> 16.7 us  [along_y(): return lax.ppermute(a, 'exp', [(i, (i + s) % Y) for i in range(Y)])]
    pallas_call x12 -> x13, Pallas kernels: 45.6 us -> 46.2 us  [call(): pl.pallas_call(body, name=name, out_shape=[(VMEM if near is True or i in...]
  transfers between devices with their start and end apart: 22 -> 23, of which waited for: 10 -> 12; matrix products, arithmetic and copies ran while one was open for 0% -> 0% of each run, Pallas kernels for 28% -> 29%
where the time goes in v7:
time: 158 us; the launch traced here: 157 us
  waiting for transfers between devices  59.6 us (38%)
  Pallas kernels  46.2 us (29%)
  starting transfers between devices  35.4 us (22%)
  between operations  14.2 us (9%)
    pallas_call x13, Pallas kernels, call(): pl.pallas_call(body, name=name, out_shape=[(VMEM if near is True or i in...  46.2 us
    ppermute x12, waiting for transfers between devices, along_y(): return lax.ppermute(a, 'exp', [(i, (i + s) % Y) for i in range(Y)])  44.5 us
    ppermute x12, starting transfers between devices, along_y(): return lax.ppermute(a, 'exp', [(i, (i + s) % Y) for i in range(Y)])  16.7 us
    ppermute x3, waiting for transfers between devices, along_x(): lax.ppermute(a, 'ctx', [(index(z, x, c), index(z, (x + s) % X, c)) for z,...  9.12 us
    all_to_all x1, starting transfers between devices, on_device(): lax.all_to_all(partial, 'ctx', 0, 0, axis_index_groups=groups, tiled=True)  7.6 us
    ppermute x3, waiting for transfers between devices, across(): return lax.ppermute(a, 'ctx', [(i, i ^ 1) for i in range(BLOCKS)])  5.96 us
    ppermute x3, starting transfers between devices, along_x(): lax.ppermute(a, 'ctx', [(index(z, x, c), index(z, (x + s) % X, c)) for z,...  5.81 us
    ppermute x3, starting transfers between devices, along_z(): lax.ppermute(a, 'ctx', [(index(z, x, c), index((z + s) % Z, x, c)) for z,...  4.91 us
  transfers between devices with their start and end apart: 23, of which 12 were waited for; matrix products, arithmetic and copies ran while one was open for 0% of the time, Pallas kernels for 29%

profile of v7, /device:TPU:0, one launch (start us, length us, event | category | flops | bytes accessed | tf_op | source)
XLA Modules:
  0.0 157.1 jit_solution(7079547238853860879)
XLA Ops:
  8.1 1.7 %collective-permute-start = (bf16[16,2048]{1,0:T(8,128)(2,1)S(1)}, bf16[16,2048]{1,0:T(8,128)(2,1)S(1)}, u32[]{:S(2)}, u32[]{:S(2)}) collective-permute-start(bf16[16,2048]{1,0:T(8,128)(2,1)S(1)} %constant_dynamic-slice_fusion), channel_id=1, source_target_pairs={{0,1},{1,2},{2,3},{3,0},{4,5},{5,6},{6,7},{7,4},{8,9},{9,10},{10,1... | collective-permute-start | bytes 196616 | tf_op jit(solution)/shard_map/ppermute | solution.py:525
  9.7 2.9 %collective-permute-start.1 = (bf16[16,2048]{1,0:T(8,128)(2,1)S(1)}, bf16[16,2048]{1,0:T(8,128)(2,1)S(1)}, u32[]{:S(2)}, u32[]{:S(2)}) collective-permute-start(bf16[16,2048]{1,0:T(8,128)(2,1)S(1)} %constant_dynamic-slice_fusion), channel_id=1, source_target_pairs={{0,2},{1,3},{2,0},{3,1},{4,6},{5,7},{6,4},{7,5},{8,10},{9,11},{10,... | collective-permute-start | bytes 196616 | tf_op jit(solution)/shard_map/ppermute | solution.py:525
  14.1 3.9 %pack.1 = (bf16[384,256]{1,0:T(8,128)(2,1)}, bf16[256,384]{1,0:T(8,128)(2,1)}, bf16[2,96,2048]{2,1,0:T(8,128)(2,1)}, bf16[2,96,2048]{2,1,0:T(8,128)(2,1)}, bf16[...) custom-call(s32[5]{0:T(128)S(1)} %stack.23.at_ref.spot_ref, s32[1,256]{1,0:T(1,128)} %bitcast.12, ...), custom_call_target="tpu_custom_call" | custom-call | flops 3221225472 | bytes 20971520 | tf_op jit(solution)/shard_map/pack/pallas_call | solution.py:52
  19.2 2.9 %collective-permute-start.5 = (bf16[2,96,2048]{2,1,0:T(8,128)(2,1)}, bf16[2,96,2048]{2,1,0:T(8,128)(2,1)S(1)}, u32[]{:S(2)}, u32[]{:S(2)}) collective-permute-start(bf16[2,96,2048]{2,1,0:T(8,128)(2,1)} %get-tuple-element.59), channel_id=1, source_target_pairs={{0,3},{1,0},{2,1},{3,2},{4,7},{5,4},{6,5},{7,6},{8,11},{9,8},{10,9... | collective-permute-start | bytes 2359304 | tf_op jit(solution)/shard_map/ppermute | solution.py:525
  22.1 2.9 %fetch.1 = (bf16[1,2048,1024]{2,1,0:T(8,128)(2,1)S(1)}, bf16[1,512,2048]{2,1,0:T(8,128)(2,1)S(1)}) custom-call(bf16[1,2048,1024]{2,1,0:T(8,128)(2,1)} %refs_0_.1, bf16[1,512,2048]{2,1,0:T(8,128)(2,1)} %refs_1_.1), custom_call_target="tpu_custom_call" | custom-call | bytes 50331648 | tf_op jit(solution)/shard_map/fetch/pallas_call | solution.py:52
  25.0 16.0 %collective-permute-done.4.r2 = bf16[2,96,2048]{2,1,0:T(8,128)(2,1)S(1)} collective-permute-done((bf16[2,96,2048]{2,1,0:T(8,128)(2,1)}, bf16[2,96,2048]{2,1,0:T(8,128)(2,1)S(1)}, u32[]{:S(2)}, u32[]{:S(2)}) %collective-permute-start.4) | collective-permute-done | bytes 786464 | tf_op jit(solution)/shard_map/ppermute | solution.py:525
  41.0 12.8 %collective-permute-done.5.r3 = bf16[2,96,2048]{2,1,0:T(8,128)(2,1)S(1)} collective-permute-done((bf16[2,96,2048]{2,1,0:T(8,128)(2,1)}, bf16[2,96,2048]{2,1,0:T(8,128)(2,1)S(1)}, u32[]{:S(2)}, u32[]{:S(2)}) %collective-permute-start.5) | collective-permute-done | bytes 786464 | tf_op jit(solution)/shard_map/ppermute | solution.py:525
  53.8 2.0 %collective-permute-done.3.r1 = bf16[2,96,2048]{2,1,0:T(8,128)(2,1)S(1)} collective-permute-done((bf16[2,96,2048]{2,1,0:T(8,128)(2,1)}, bf16[2,96,2048]{2,1,0:T(8,128)(2,1)S(1)}, u32[]{:S(2)}, u32[]{:S(2)}) %collective-permute-start.3) | collective-permute-done | bytes 786464 | tf_op jit(solution)/shard_map/ppermute | solution.py:525
  55.8 6.7 %expert.1 = (bf16[96,2176]{1,0:T(8,128)(2,1)}, bf16[96,2176]{1,0:T(8,128)(2,1)}, bf16[96,2176]{1,0:T(8,128)(2,1)}, bf16[96,2176]{1,0:T(8,128)(2,1)}, bf16[384,5632]{1,0:T(8,128)(2,1)S(1)}) custom-call(bf16[2,96,2048]{2,1,0:T(8,128)(2,1)} %get-tuple-element.56.r0, bf16[2,96,2048]{2,1,0:T(8,128)(2,1)S(1)} %collective-permute-done.3.r1, ...), custom_call_target="tpu_custom_call" | custom-call | flops 16106127360 | bytes 58720256 | tf_op jit(solution)/shard_map/expert/pallas_call | solution.py:52
  64.1 3.1 %collective-permute-start.6 = (bf16[96,2176]{1,0:T(8,128)(2,1)}, bf16[96,2176]{1,0:T(8,128)(2,1)}, u32[]{:S(2)}, u32[]{:S(2)}) collective-permute-start(bf16[96,2176]{1,0:T(8,128)(2,1)} %get-tuple-element.64), channel_id=1, source_target_pairs={{0,3},{1,0},{2,1},{3,2},{4,7},{5,4},{6,5},{7,6},{8,11},{9,8},{10,9... | collective-permute-start | bytes 1253384 | tf_op jit(solution)/shard_map/ppermute | solution.py:525
  67.2 3.3 %collective-permute-done.7.other = bf16[384,5632]{1,0:T(8,128)(2,1)S(1)} collective-permute-done((bf16[384,5632]{1,0:T(8,128)(2,1)S(1)}, bf16[384,5632]{1,0:T(8,128)(2,1)S(1)}, u32[]{:S(2)}, u32[]{:S(2)}) %collective-permute-start.7) | collective-permute-done | bytes 4325408 | tf_op jit(solution)/shard_map/ppermute | solution.py:537
  70.5 6.5 %weights.1 = bf16[16,96,1024]{2,1,0:T(8,128)(2,1)} custom-call(s32[5]{0:T(128)S(1)} %stack.23.at_ref.spot_ref, bf16[384,5632]{1,0:T(8,128)(2,1)S(1)} %get-tuple-element.65.mine, bf16[384,5632]{1,0:T(8,128)(2,1)S(1)} %collective-permute-done.7.other), custom_call_target="tpu_custom_call" | custom-call | flops 9663676416 | bytes 50331648 | tf_op jit(solution)/shard_map/weights/pallas_call | solution.py:52
  77.0 7.6 %all-to-all-start = ((bf16[16,96,1024]{2,1,0:T(8,128)(2,1)}), bf16[16,96,1024]{2,1,0:T(8,128)(2,1)S(1)}, u32[]{:S(2)}, u32[]{:S(2)}) async-start(bf16[16,96,1024]{2,1,0:T(8,128)(2,1)} %weights.1), calls=%async_computation | async-start | bytes 6291456 | tf_op jit(solution)/shard_map/all_to_all | solution.py:578
  85.4 8.4 %project.1 = (bf16[256,2048]{1,0:T(8,128)(2,1)}, bf16[1,256]{1,0:T(2,128)(2,1)}, bf16[256,512]{1,0:T(8,128)(2,1)S(1)}, bf16[256,512]{1,0:T(8,128)(2,1)S(1)}, bf1...) custom-call(bf16[512,2048]{1,0:T(8,128)(2,1)} %refs_0_.2, bf16[32,3,16,2048]{3,2,1,0:T(8,128)(2,1)} %bitcast.11, ...), custom_call_target="tpu_custom_call" | custom-call | flops 10200547328 | bytes 41943040 | tf_op jit(solution)/shard_map/project/pallas_call | solution.py:52
  96.6 6.4 %collective-permute-done.10.g1 = bf16[256,512]{1,0:T(8,128)(2,1)S(1)} collective-permute-done((bf16[256,512]{1,0:T(8,128)(2,1)S(1)}, bf16[256,512]{1,0:T(8,128)(2,1)S(1)}, u32[]{:S(2)}, u32[]{:S(2)}) %collective-permute-start.10) | collective-permute-done | bytes 262176 | tf_op jit(solution)/shard_map/ppermute | solution.py:525
  103.0 2.2 %collective-permute-done.11.g2 = bf16[256,512]{1,0:T(8,128)(2,1)S(1)} collective-permute-done((bf16[256,512]{1,0:T(8,128)(2,1)S(1)}, bf16[256,512]{1,0:T(8,128)(2,1)S(1)}, u32[]{:S(2)}, u32[]{:S(2)}) %collective-permute-start.11) | collective-permute-done | bytes 262176 | tf_op jit(solution)/shard_map/ppermute | solution.py:525
  105.3 4.3 %collective-permute-done.12.g3 = bf16[256,512]{1,0:T(8,128)(2,1)S(1)} collective-permute-done((bf16[256,512]{1,0:T(8,128)(2,1)S(1)}, bf16[256,512]{1,0:T(8,128)(2,1)S(1)}, u32[]{:S(2)}, u32[]{:S(2)}) %collective-permute-start.12) | collective-permute-done | bytes 262176 | tf_op jit(solution)/shard_map/ppermute | solution.py:525
  113.9 2.7 %collective-permute-start.15 = (bf16[256,128]{1,0:T(8,128)(2,1)S(1)}, bf16[256,128]{1,0:T(8,128)(2,1)S(1)}, u32[]{:S(2)}, u32[]{:S(2)}) collective-permute-start(bf16[256,128]{1,0:T(8,128)(2,1)S(1)} %get-tuple-element.78), channel_id=1, source_target_pairs={{0,16},{4,20},{8,24},{12,28},{16,0},{20,4},{24,8},{28,12},{32,48},... | collective-permute-start | bytes 196616 | tf_op jit(solution)/shard_map/ppermute | solution.py:529
  118.1 8.1 %query_key.1 = (bf16[1024,512]{1,0:T(8,128)(2,1)}, bf16[1024,512]{1,0:T(8,128)(2,1)S(1)}) custom-call(s32[5]{0:T(128)S(1)} %stack.23.at_ref.spot_ref, bf16[1024,512]{1,0:T(8,128)(2,1)S(1)} %copy-done, bf16[1024,512]{1,0:T(8,128)(2,1)S(1)} %copy-done.1, bf16[1024,512]{1,0:T(8,128)(2,1)S(1)} %copy-done.2, bf16[1024,512]{1,0:T(8,128)(2,1)S(1)} %get-tuple-element.74.g_ref, ...), custom_call_target="tpu_custom_call" | custom-call | flops 10737418240 | bytes 25165824 | tf_op jit(solution)/shard_map/query_key/pallas_call | solution.py:52
  126.2 2.1 %collective-permute-done.14.x1 = bf16[256,128]{1,0:T(8,128)(2,1)S(1)} collective-permute-done((bf16[256,128]{1,0:T(8,128)(2,1)S(1)}, bf16[256,128]{1,0:T(8,128)(2,1)S(1)}, u32[]{:S(2)}, u32[]{:S(2)}) %collective-permute-start.14) | collective-permute-done | bytes 65568 | tf_op jit(solution)/shard_map/ppermute | solution.py:529
  128.3 7.0 %collective-permute-done.15.x2 = bf16[256,128]{1,0:T(8,128)(2,1)S(1)} collective-permute-done((bf16[256,128]{1,0:T(8,128)(2,1)S(1)}, bf16[256,128]{1,0:T(8,128)(2,1)S(1)}, u32[]{:S(2)}, u32[]{:S(2)}) %collective-permute-start.15) | collective-permute-done | bytes 65568 | tf_op jit(solution)/shard_map/ppermute | solution.py:529
  137.5 2.8 %collective-permute-start.18 = (bf16[256,128]{1,0:T(8,128)(2,1)S(1)}, bf16[256,128]{1,0:T(8,128)(2,1)S(1)}, u32[]{:S(2)}, u32[]{:S(2)}) collective-permute-start(bf16[256,128]{1,0:T(8,128)(2,1)S(1)} %line.1), channel_id=1, source_target_pairs={{0,64},{4,68},{8,72},{12,76},{16,80},{20,84},{24,88},{28,92},{32,9... | collective-permute-start | bytes 196616 | tf_op jit(solution)/shard_map/ppermute | solution.py:533
  140.3 4.1 %value.1.value_ref = bf16[1024,512]{1,0:T(8,128)(2,1)S(1)} custom-call(s32[5]{0:T(128)S(1)} %stack.23.at_ref.spot_ref, bf16[1024,512]{1,0:T(8,128)(2,1)S(1)} %copy-done, bf16[1024,512]{1,0:T(8,128)(2,1)S(1)} %copy-done.1, bf16[1024,512]{1,0:T(8,128)(2,1)S(1)} %get-tuple-element.74.g_ref), custom_call_target="tpu_custom_call" | custom-call | flops 5368709120 | bytes 25165824 | tf_op jit(solution)/shard_map/value/pallas_call | solution.py:52
  146.5 2.7 %final.1 = (bf16[1024,512]{1,0:T(8,128)(2,1)}, bf16[1024,512]{1,0:T(8,128)(2,1)}) custom-call(s32[5]{0:T(128)S(1)} %stack.23.at_ref.spot_ref, f32[256,128]{1,0:T(8,128)S(1)} %get-tuple-element.83.own, f32[256,128]{1,0:T(8,128)S(1)} %collective-permute-done.20.got, bf16[1024,512]{1,0:T(8,128)(2,1)S(1)} %copy-done.2, bf16[1024,512]{1,0:T(8,128)(2,1)S(1)} %copy-done.1, ...), custom_call_target="tpu_custom_call" | custom-call | flops 2147483648 | bytes 33554432 | tf_op jit(solution)/shard_map/final/pallas_call | solution.py:52
  (47 shorter events, 19.9 us)
Async XLA Ops:
  7.2 78.2 %all-gather.3.cloned.1.call-start = ((), (), s32[]{:S(2)}) async-start(), calls=%async_computation.1 | async-start | bytes 6488064 | tf_op jit(solution)/shard_map/all_gather | solution.py:564
  8.1 9.9 %collective-permute-start = (bf16[16,2048]{1,0:T(8,128)(2,1)S(1)}, bf16[16,2048]{1,0:T(8,128)(2,1)S(1)}, u32[]{:S(2)}, u32[]{:S(2)}) collective-permute-start(bf16[16,2048]{1,0:T(8,128)(2,1)S(1)} %constant_dynamic-slice_fusion), channel_id=1, source_target_pairs={{0,1},{1,2},{2,3},{3,0},{4,5},{5,6},{6,7},{7,4},{8,9},{9,10},{10,1... | collective-permute-start | bytes 196616 | tf_op jit(solution)/shard_map/ppermute | solution.py:525
  9.7 8.2 %collective-permute-start.1 = (bf16[16,2048]{1,0:T(8,128)(2,1)S(1)}, bf16[16,2048]{1,0:T(8,128)(2,1)S(1)}, u32[]{:S(2)}, u32[]{:S(2)}) collective-permute-start(bf16[16,2048]{1,0:T(8,128)(2,1)S(1)} %constant_dynamic-slice_fusion), channel_id=1, source_target_pairs={{0,2},{1,3},{2,0},{3,1},{4,6},{5,7},{6,4},{7,5},{8,10},{9,11},{10,... | collective-permute-start | bytes 196616 | tf_op jit(solution)/shard_map/ppermute | solution.py:525
  12.6 5.3 %collective-permute-start.2 = (bf16[16,2048]{1,0:T(8,128)(2,1)S(1)}, bf16[16,2048]{1,0:T(8,128)(2,1)S(1)}, u32[]{:S(2)}, u32[]{:S(2)}) collective-permute-start(bf16[16,2048]{1,0:T(8,128)(2,1)S(1)} %constant_dynamic-slice_fusion), channel_id=1, source_target_pairs={{0,3},{1,0},{2,1},{3,2},{4,7},{5,4},{6,5},{7,6},{8,11},{9,8},{10,9... | collective-permute-start | bytes 196616 | tf_op jit(solution)/shard_map/ppermute | solution.py:525
  18.7 22.3 %collective-permute-start.4 = (bf16[2,96,2048]{2,1,0:T(8,128)(2,1)}, bf16[2,96,2048]{2,1,0:T(8,128)(2,1)S(1)}, u32[]{:S(2)}, u32[]{:S(2)}) collective-permute-start(bf16[2,96,2048]{2,1,0:T(8,128)(2,1)} %get-tuple-element.58), channel_id=1, source_target_pairs={{0,2},{1,3},{2,0},{3,1},{4,6},{5,7},{6,4},{7,5},{8,10},{9,11},{10,... | collective-permute-start | bytes 2359304 | tf_op jit(solution)/shard_map/ppermute | solution.py:525
  19.2 34.6 %collective-permute-start.5 = (bf16[2,96,2048]{2,1,0:T(8,128)(2,1)}, bf16[2,96,2048]{2,1,0:T(8,128)(2,1)S(1)}, u32[]{:S(2)}, u32[]{:S(2)}) collective-permute-start(bf16[2,96,2048]{2,1,0:T(8,128)(2,1)} %get-tuple-element.59), channel_id=1, source_target_pairs={{0,3},{1,0},{2,1},{3,2},{4,7},{5,4},{6,5},{7,6},{8,11},{9,8},{10,9... | collective-permute-start | bytes 2359304 | tf_op jit(solution)/shard_map/ppermute | solution.py:525
  22.1 33.7 %collective-permute-start.3 = (bf16[2,96,2048]{2,1,0:T(8,128)(2,1)}, bf16[2,96,2048]{2,1,0:T(8,128)(2,1)S(1)}, u32[]{:S(2)}, u32[]{:S(2)}) collective-permute-start(bf16[2,96,2048]{2,1,0:T(8,128)(2,1)} %get-tuple-element.57), channel_id=1, source_target_pairs={{0,1},{1,2},{2,3},{3,0},{4,5},{5,6},{6,7},{7,4},{8,9},{9,10},{10,1... | collective-permute-start | bytes 2359304 | tf_op jit(solution)/shard_map/ppermute | solution.py:525
  62.5 8.0 %collective-permute-start.7 = (bf16[384,5632]{1,0:T(8,128)(2,1)S(1)}, bf16[384,5632]{1,0:T(8,128)(2,1)S(1)}, u32[]{:S(2)}, u32[]{:S(2)}) collective-permute-start(bf16[384,5632]{1,0:T(8,128)(2,1)S(1)} %get-tuple-element.65.mine), channel_id=1, source_target_pairs={{0,4},{4,0},{8,12},{12,8},{16,20},{20,16},{24,28},{28,24},{32,36},... | collective-permute-start | bytes 12976136 | tf_op jit(solution)/shard_map/ppermute | solution.py:537
  62.7 21.9 %collective-permute-start.8 = (bf16[96,2176]{1,0:T(8,128)(2,1)}, bf16[96,2176]{1,0:T(8,128)(2,1)}, u32[]{:S(2)}, u32[]{:S(2)}) collective-permute-start(bf16[96,2176]{1,0:T(8,128)(2,1)} %get-tuple-element.66), channel_id=1, source_target_pairs={{0,2},{1,3},{2,0},{3,1},{4,6},{5,7},{6,4},{7,5},{8,10},{9,11},{10,... | collective-permute-start | bytes 1253384 | tf_op jit(solution)/shard_map/ppermute | solution.py:525
  64.0 21.4 %collective-permute-start.9 = (bf16[96,2176]{1,0:T(8,128)(2,1)}, bf16[96,2176]{1,0:T(8,128)(2,1)}, u32[]{:S(2)}, u32[]{:S(2)}) collective-permute-start(bf16[96,2176]{1,0:T(8,128)(2,1)} %get-tuple-element.67), channel_id=1, source_target_pairs={{0,1},{1,2},{2,3},{3,0},{4,5},{5,6},{6,7},{7,4},{8,9},{9,10},{10,1... | collective-permute-start | bytes 1253384 | tf_op jit(solution)/shard_map/ppermute | solution.py:525
  64.1 21.2 %collective-permute-start.6 = (bf16[96,2176]{1,0:T(8,128)(2,1)}, bf16[96,2176]{1,0:T(8,128)(2,1)}, u32[]{:S(2)}, u32[]{:S(2)}) collective-permute-start(bf16[96,2176]{1,0:T(8,128)(2,1)} %get-tuple-element.64), channel_id=1, source_target_pairs={{0,3},{1,0},{2,1},{3,2},{4,7},{5,4},{6,5},{7,6},{8,11},{9,8},{10,9... | collective-permute-start | bytes 1253384 | tf_op jit(solution)/shard_map/ppermute | solution.py:525
  77.0 72.1 %all-to-all-start = ((bf16[16,96,1024]{2,1,0:T(8,128)(2,1)}), bf16[16,96,1024]{2,1,0:T(8,128)(2,1)S(1)}, u32[]{:S(2)}, u32[]{:S(2)}) async-start(bf16[16,96,1024]{2,1,0:T(8,128)(2,1)} %weights.1), calls=%async_computation | async-start | bytes 6291456 | tf_op jit(solution)/shard_map/all_to_all | solution.py:578
  93.7 24.4 %copy-start.1 = (bf16[1024,512]{1,0:T(8,128)(2,1)S(1)}, bf16[1024,512]{1,0:T(8,128)(2,1)}, u32[]{:S(2)}) copy-start(bf16[1024,512]{1,0:T(8,128)(2,1)} %k_ref.5) | copy-start | bytes 3145732
  93.8 9.2 %collective-permute-start.10 = (bf16[256,512]{1,0:T(8,128)(2,1)S(1)}, bf16[256,512]{1,0:T(8,128)(2,1)S(1)}, u32[]{:S(2)}, u32[]{:S(2)}) collective-permute-start(bf16[256,512]{1,0:T(8,128)(2,1)S(1)} %get-tuple-element.71), channel_id=1, source_target_pairs={{0,3},{1,0},{2,1},{3,2},{4,7},{5,4},{6,5},{7,6},{8,11},{9,8},{10,9... | collective-permute-start | bytes 786440 | tf_op jit(solution)/shard_map/ppermute | solution.py:525
  94.5 10.8 %collective-permute-start.11 = (bf16[256,512]{1,0:T(8,128)(2,1)S(1)}, bf16[256,512]{1,0:T(8,128)(2,1)S(1)}, u32[]{:S(2)}, u32[]{:S(2)}) collective-permute-start(bf16[256,512]{1,0:T(8,128)(2,1)S(1)} %get-tuple-element.72), channel_id=1, source_target_pairs={{0,2},{1,3},{2,0},{3,1},{4,6},{5,7},{6,4},{7,5},{8,10},{9,11},{10,... | collective-permute-start | bytes 786440 | tf_op jit(solution)/shard_map/ppermute | solution.py:525
  95.9 13.7 %collective-permute-start.12 = (bf16[256,512]{1,0:T(8,128)(2,1)S(1)}, bf16[256,512]{1,0:T(8,128)(2,1)S(1)}, u32[]{:S(2)}, u32[]{:S(2)}) collective-permute-start(bf16[256,512]{1,0:T(8,128)(2,1)S(1)} %get-tuple-element.73), channel_id=1, source_target_pairs={{0,1},{1,2},{2,3},{3,0},{4,5},{5,6},{6,7},{7,4},{8,9},{9,10},{10,1... | collective-permute-start | bytes 786440 | tf_op jit(solution)/shard_map/ppermute | solution.py:525
  110.8 1.4 collective-permute-start.13
  112.3 16.0 %collective-permute-start.14 = (bf16[256,128]{1,0:T(8,128)(2,1)S(1)}, bf16[256,128]{1,0:T(8,128)(2,1)S(1)}, u32[]{:S(2)}, u32[]{:S(2)}) collective-permute-start(bf16[256,128]{1,0:T(8,128)(2,1)S(1)} %get-tuple-element.78), channel_id=1, source_target_pairs={{0,8},{4,12},{8,16},{12,20},{16,24},{20,28},{24,0},{28,4},{32,40},... | collective-permute-start | bytes 196616 | tf_op jit(solution)/shard_map/ppermute | solution.py:529
  113.9 21.4 %collective-permute-start.15 = (bf16[256,128]{1,0:T(8,128)(2,1)S(1)}, bf16[256,128]{1,0:T(8,128)(2,1)S(1)}, u32[]{:S(2)}, u32[]{:S(2)}) collective-permute-start(bf16[256,128]{1,0:T(8,128)(2,1)S(1)} %get-tuple-element.78), channel_id=1, source_target_pairs={{0,16},{4,20},{8,24},{12,28},{16,0},{20,4},{24,8},{28,12},{32,48},... | collective-permute-start | bytes 196616 | tf_op jit(solution)/shard_map/ppermute | solution.py:529
  116.7 18.7 %collective-permute-start.16 = (bf16[256,128]{1,0:T(8,128)(2,1)S(1)}, bf16[256,128]{1,0:T(8,128)(2,1)S(1)}, u32[]{:S(2)}, u32[]{:S(2)}) collective-permute-start(bf16[256,128]{1,0:T(8,128)(2,1)S(1)} %get-tuple-element.78), channel_id=1, source_target_pairs={{0,24},{4,28},{8,0},{12,4},{16,8},{20,12},{24,16},{28,20},{32,56},... | collective-permute-start | bytes 196616 | tf_op jit(solution)/shard_map/ppermute | solution.py:529
  135.4 9.0 %collective-permute-start.19 = (bf16[256,128]{1,0:T(8,128)(2,1)S(1)}, bf16[256,128]{1,0:T(8,128)(2,1)S(1)}, u32[]{:S(2)}, u32[]{:S(2)}) collective-permute-start(bf16[256,128]{1,0:T(8,128)(2,1)S(1)} %line.1), channel_id=1, source_target_pairs={{0,96},{4,100},{8,104},{12,108},{16,112},{20,116},{24,120},{28,124... | collective-permute-start | bytes 196616 | tf_op jit(solution)/shard_map/ppermute | solution.py:533
  137.0 7.4 %collective-permute-start.17 = (bf16[256,128]{1,0:T(8,128)(2,1)S(1)}, bf16[256,128]{1,0:T(8,128)(2,1)S(1)}, u32[]{:S(2)}, u32[]{:S(2)}) collective-permute-start(bf16[256,128]{1,0:T(8,128)(2,1)S(1)} %line.1), channel_id=1, source_target_pairs={{0,32},{4,36},{8,40},{12,44},{16,48},{20,52},{24,56},{28,60},{32,6... | collective-permute-start | bytes 196616 | tf_op jit(solution)/shard_map/ppermute | solution.py:533
  137.5 6.9 %collective-permute-start.18 = (bf16[256,128]{1,0:T(8,128)(2,1)S(1)}, bf16[256,128]{1,0:T(8,128)(2,1)S(1)}, u32[]{:S(2)}, u32[]{:S(2)}) collective-permute-start(bf16[256,128]{1,0:T(8,128)(2,1)S(1)} %line.1), channel_id=1, source_target_pairs={{0,64},{4,68},{8,72},{12,76},{16,80},{20,84},{24,88},{28,92},{32,9... | collective-permute-start | bytes 196616 | tf_op jit(solution)/shard_map/ppermute | solution.py:533
  145.0 1.4 collective-permute-start.20
  (3 other events, 72.9 us)
Sparse Core Ops, SparseCore 0:
  18.8 52.6 all-gather.2

commit v8 on v5

--- a/solution.py
+++ b/solution.py
@@ -11,7 +11,8 @@
 SMEM = pltpu.SMEM
 Z, X, C, Y = 4, 4, 2, 4
 CAP, ROWS, WIDTH, FF, HD, HEADS, TOK = 96, 256, 2048, 512, 128, 4, 1024
-WEIGHT = 4
+WEIGHT = 3
+EARLY = ("pack", "fetch", "expert", "own_weights", "weights")
 BLOCKS = Z * X * C
 
 
@@ -41,6 +42,7 @@
 
 
 def call(body, name, outs, ins, flops=0, moved=0, grid=None, in_specs=None, out_specs=None, limit=24, scratch=(), free=(), near=(), held=()):
+    weight = 4 if name in EARLY else WEIGHT
     kwargs = {} if grid is None else {"grid": grid}
     specs = in_specs or [full() for _ in ins]
     ins = [
@@ -55,7 +57,7 @@
         out_specs=out_specs or [full() for _ in outs],
         scratch_shapes=scratch,
         compiler_params=pltpu.CompilerParams(vmem_limit_bytes=limit << 20),
-        cost_estimate=pl.CostEstimate(flops=WEIGHT * flops, bytes_accessed=WEIGHT * moved, transcendentals=0),
+        cost_estimate=pl.CostEstimate(flops=weight * flops, bytes_accessed=weight * moved, transcendentals=0),
         **kwargs,
     )(*ins)
 
@@ -226,24 +228,51 @@
     return (col == (row // run) * (2 * run) + core * run + row % run).astype(bf16)
 
 
-def weights_body(at_ref, mine, other, out_hbm, out, rows_t, hid_t, sem):
-    core = at_ref[4]
+def turn(core, src, rows_t, hid_t):
     pick_row, pick_hid = chooser(core, 512, 64), chooser(core, 128, 16)
-    for k, src in enumerate((mine, other)):
-        for i in range(Z):
-            rows_t[k, i * 256 : (i + 1) * 256, :] = dot_t(pick_row, src[:, i * 512 : (i + 1) * 512]).astype(bf16)
-            cols = slice(HID + i * 128, HID + (i + 1) * 128)
-            hid_t[k, i * 64 : (i + 1) * 64, :] = dot_t(pick_hid, src[:, cols]).astype(bf16)
+    for i in range(Z):
+        rows_t[i * 256 : (i + 1) * 256, :] = dot_t(pick_row, src[:, i * 512 : (i + 1) * 512]).astype(bf16)
+        cols = slice(HID + i * 128, HID + (i + 1) * 128)
+        hid_t[i * 64 : (i + 1) * 64, :] = dot_t(pick_hid, src[:, cols]).astype(bf16)
+
+
+def own_weights_body(at_ref, mine, up_ref, down_ref, rows_t, hid_t):
+    turn(at_ref[4], mine, rows_t, hid_t)
     for j in range(4):
-        cols = slice(GB + j * STEP, GB + (j + 1) * STEP)
-        up = (dot(rows_t[0], mine[:, cols]) + dot(rows_t[1], other[:, cols])).astype(bf16)
+        up_ref[:, j * STEP : (j + 1) * STEP] = dot(rows_t[...], mine[:, GB + j * STEP : GB + (j + 1) * STEP])
+    for j in range(8):
+        at = WIDTH + j * STEP
+        down_ref[:, j * STEP : (j + 1) * STEP] = dot(hid_t[...], mine[:, at : at + STEP])
+
+
+def own_weights(at, mine):
+    return call(
+        own_weights_body,
+        "own_weights",
+        [((1024, 1024), f32), ((256, WIDTH), f32)],
+        (at, mine),
+        3 * N * WIDTH * FF,
+        10 << 20,
+        in_specs=[scalars(), full()],
+        scratch=[VMEM((1024, N), bf16), VMEM((256, N), bf16)],
+        limit=8,
+        held=(1,),
+        near=(0, 1),
+    )
+
+
+def weights_body(at_ref, up_ref, down_ref, other, out_hbm, out, rows_t, hid_t, sem):
+    turn(at_ref[4], other, rows_t, hid_t)
+    for j in range(4):
+        here = slice(j * STEP, (j + 1) * STEP)
+        up = (up_ref[:, here] + dot(rows_t[...], other[:, GB + j * STEP : GB + (j + 1) * STEP])).astype(bf16)
         for k in range(Z * X):
-            out[k, :64, j * STEP : (j + 1) * STEP] = up[k * 64 : (k + 1) * 64]
+            out[k, :64, here] = up[k * 64 : (k + 1) * 64]
     copies = [pltpu.make_async_copy(out.at[:, pl.ds(0, 64)], out_hbm.at[:, pl.ds(0, 64)], sem.at[0])]
     copies[0].start()
     for j in range(8):
-        cols = slice(WIDTH + j * STEP, WIDTH + (j + 1) * STEP)
-        down = (dot(hid_t[0], mine[:, cols]) + dot(hid_t[1], other[:, cols])).astype(bf16)
+        here, at = slice(j * STEP, (j + 1) * STEP), WIDTH + j * STEP
+        down = (down_ref[:, here] + dot(hid_t[...], other[:, at : at + STEP])).astype(bf16)
         row, col = 64 + 16 * (j // 4), (j % 4) * STEP
         for k in range(Z * X):
             out[k, row : row + 16, col : col + STEP] = down[k * 16 : (k + 1) * 16]
@@ -255,24 +284,24 @@
         copy.wait()
 
 
-def weights(at, mine, other):
+def weights(at, own, other):
     return call(
         weights_body,
         "weights",
         [((Z * X, 96, 1024), bf16)],
-        (at, mine, other),
-        3 * 2 * N * WIDTH * FF,
-        12 << 20,
-        in_specs=[scalars(), full(), full()],
+        (at, *own, other),
+        3 * N * WIDTH * FF,
+        10 << 20,
+        in_specs=[scalars(), full(), full(), full()],
         out_specs=[anywhere()],
         scratch=[
             VMEM((Z * X, 96, 1024), bf16),
-            VMEM((2, 1024, N), bf16),
-            VMEM((2, 256, N), bf16),
+            VMEM((1024, N), bf16),
+            VMEM((256, N), bf16),
             pltpu.SemaphoreType.DMA((3,)),
         ],
-        limit=16,
-        held=(1, 2),
+        limit=12,
+        held=(1, 2, 3),
     )[0]
 
 
@@ -560,8 +589,8 @@
     queries, keys, values = attn_query, attn_key, attn_value
     b0, b1, b2, b3, bundle = expert(held, w_pair, w_back)
     backs = [b0] + [along_y(b, -s) for s, b in ((1, b1), (2, b2), (3, b3))]
-    other_bundle, backs[1] = lax.optimization_barrier((across(bundle), backs[1]))
-    partial = weights(at, bundle, other_bundle)
+    partial = weights(at, own_weights(at, bundle), across(bundle))
+    _, backs[2], backs[3] = lax.optimization_barrier((partial, backs[2], backs[3]))
     groups = [[index(i, j, k) for i in range(Z) for j in range(X)] for k in range(C)]
     exchanged = lax.all_to_all(partial, "ctx", 0, 0, axis_index_groups=groups, tiled=True)
 

time: 161 us -> 155 us (0.963)
  waiting for transfers between devices: 64.2 us -> 55.9 us
  starting transfers between devices: 34.8 us -> 36.6 us
    ppermute x12, waiting for transfers between devices: 53.6 us -> 46.3 us  [along_y(): return lax.ppermute(a, 'exp', [(i, (i + s) % Y) for i in range(Y)])]
    ppermute x12, starting transfers between devices: 14.9 us -> 16.7 us  [along_y(): return lax.ppermute(a, 'exp', [(i, (i + s) % Y) for i in range(Y)])]
    pallas_call x12 -> x13, Pallas kernels: 45.6 us -> 46.9 us  [call(): pl.pallas_call(body, name=name, out_shape=[(VMEM if near is True or i in...]
  transfers between devices with their start and end apart: 22 -> 22, of which waited for: 10 -> 10; matrix products, arithmetic and copies ran while one was open for 0% -> 0% of each run, Pallas kernels for 28% -> 30%
where the time goes in v8:
time: 155 us
  waiting for transfers between devices  55.9 us (36%)
  Pallas kernels  46.9 us (30%)
  starting transfers between devices  36.6 us (24%)
  between operations  14.2 us (9%)
    pallas_call x13, Pallas kernels, call(): pl.pallas_call(body, name=name, out_shape=[(VMEM if near is True or i in...  46.9 us
    ppermute x12, waiting for transfers between devices, along_y(): return lax.ppermute(a, 'exp', [(i, (i + s) % Y) for i in range(Y)])  46.3 us
    ppermute x12, starting transfers between devices, along_y(): return lax.ppermute(a, 'exp', [(i, (i + s) % Y) for i in range(Y)])  16.7 us
    ppermute x3, waiting for transfers between devices, along_x(): lax.ppermute(a, 'ctx', [(index(z, x, c), index(z, (x + s) % X, c)) for z,...  7.99 us
    all_to_all x1, starting transfers between devices, on_device(): lax.all_to_all(partial, 'ctx', 0, 0, axis_index_groups=groups, tiled=True)  7.9 us
    ppermute x3, starting transfers between devices, along_z(): lax.ppermute(a, 'ctx', [(index(z, x, c), index((z + s) % Z, x, c)) for z,...  5.82 us
    ppermute x3, starting transfers between devices, along_x(): lax.ppermute(a, 'ctx', [(index(z, x, c), index(z, (x + s) % X, c)) for z,...  5.8 us
  transfers between devices with their start and end apart: 22, of which 10 were waited for; matrix products, arithmetic and copies ran while one was open for 0% of the time, Pallas kernels for 30%

profile of v8, /device:TPU:0, one launch (start us, length us, event | category | flops | bytes accessed | tf_op | source)
XLA Modules:
  0.0 155.2 jit_solution(15644554841677880219)
XLA Ops:
  9.7 2.9 %collective-permute-start.1 = (bf16[16,2048]{1,0:T(8,128)(2,1)S(1)}, bf16[16,2048]{1,0:T(8,128)(2,1)S(1)}, u32[]{:S(2)}, u32[]{:S(2)}) collective-permute-start(bf16[16,2048]{1,0:T(8,128)(2,1)S(1)} %constant_dynamic-slice_fusion), channel_id=1, source_target_pairs={{0,2},{1,3},{2,0},{3,1},{4,6},{5,7},{6,4},{7,5},{8,10},{9,11},{10,... | collective-permute-start | bytes 196616 | tf_op jit(solution)/shard_map/ppermute | solution.py:542
  14.1 3.9 %pack.1 = (bf16[384,256]{1,0:T(8,128)(2,1)}, bf16[256,384]{1,0:T(8,128)(2,1)}, bf16[2,96,2048]{2,1,0:T(8,128)(2,1)}, bf16[2,96,2048]{2,1,0:T(8,128)(2,1)}, bf16[...) custom-call(s32[5]{0:T(128)S(1)} %stack.23.at_ref.spot_ref, s32[1,256]{1,0:T(1,128)} %bitcast.12, ...), custom_call_target="tpu_custom_call" | custom-call | flops 3221225472 | bytes 20971520 | tf_op jit(solution)/shard_map/pack/pallas_call | solution.py:52
  19.2 2.9 %collective-permute-start.5 = (bf16[2,96,2048]{2,1,0:T(8,128)(2,1)}, bf16[2,96,2048]{2,1,0:T(8,128)(2,1)S(1)}, u32[]{:S(2)}, u32[]{:S(2)}) collective-permute-start(bf16[2,96,2048]{2,1,0:T(8,128)(2,1)} %get-tuple-element.56), channel_id=1, source_target_pairs={{0,3},{1,0},{2,1},{3,2},{4,7},{5,4},{6,5},{7,6},{8,11},{9,8},{10,9... | collective-permute-start | bytes 2359304 | tf_op jit(solution)/shard_map/ppermute | solution.py:542
  22.1 2.9 %fetch.1 = (bf16[1,2048,1024]{2,1,0:T(8,128)(2,1)S(1)}, bf16[1,512,2048]{2,1,0:T(8,128)(2,1)S(1)}) custom-call(bf16[1,2048,1024]{2,1,0:T(8,128)(2,1)} %refs_0_.1, bf16[1,512,2048]{2,1,0:T(8,128)(2,1)} %refs_1_.1), custom_call_target="tpu_custom_call" | custom-call | bytes 50331648 | tf_op jit(solution)/shard_map/fetch/pallas_call | solution.py:52
  25.0 16.0 %collective-permute-done.4.r2 = bf16[2,96,2048]{2,1,0:T(8,128)(2,1)S(1)} collective-permute-done((bf16[2,96,2048]{2,1,0:T(8,128)(2,1)}, bf16[2,96,2048]{2,1,0:T(8,128)(2,1)S(1)}, u32[]{:S(2)}, u32[]{:S(2)}) %collective-permute-start.4) | collective-permute-done | bytes 786464 | tf_op jit(solution)/shard_map/ppermute | solution.py:542
  41.0 12.8 %collective-permute-done.5.r3 = bf16[2,96,2048]{2,1,0:T(8,128)(2,1)S(1)} collective-permute-done((bf16[2,96,2048]{2,1,0:T(8,128)(2,1)}, bf16[2,96,2048]{2,1,0:T(8,128)(2,1)S(1)}, u32[]{:S(2)}, u32[]{:S(2)}) %collective-permute-start.5) | collective-permute-done | bytes 786464 | tf_op jit(solution)/shard_map/ppermute | solution.py:542
  53.8 2.0 %collective-permute-done.3.r1 = bf16[2,96,2048]{2,1,0:T(8,128)(2,1)S(1)} collective-permute-done((bf16[2,96,2048]{2,1,0:T(8,128)(2,1)}, bf16[2,96,2048]{2,1,0:T(8,128)(2,1)S(1)}, u32[]{:S(2)}, u32[]{:S(2)}) %collective-permute-start.3) | collective-permute-done | bytes 786464 | tf_op jit(solution)/shard_map/ppermute | solution.py:542
  55.8 6.7 %expert.1 = (bf16[96,2176]{1,0:T(8,128)(2,1)}, bf16[96,2176]{1,0:T(8,128)(2,1)}, bf16[96,2176]{1,0:T(8,128)(2,1)}, bf16[96,2176]{1,0:T(8,128)(2,1)}, bf16[384,5632]{1,0:T(8,128)(2,1)S(1)}) custom-call(bf16[2,96,2048]{2,1,0:T(8,128)(2,1)} %get-tuple-element.53.r0, bf16[2,96,2048]{2,1,0:T(8,128)(2,1)S(1)} %collective-permute-done.3.r1, ...), custom_call_target="tpu_custom_call" | custom-call | flops 16106127360 | bytes 58720256 | tf_op jit(solution)/shard_map/expert/pallas_call | solution.py:52
  64.2 3.1 %collective-permute-start.6 = (bf16[96,2176]{1,0:T(8,128)(2,1)}, bf16[96,2176]{1,0:T(8,128)(2,1)}, u32[]{:S(2)}, u32[]{:S(2)}) collective-permute-start(bf16[96,2176]{1,0:T(8,128)(2,1)} %get-tuple-element.61), channel_id=1, source_target_pairs={{0,3},{1,0},{2,1},{3,2},{4,7},{5,4},{6,5},{7,6},{8,11},{9,8},{10,9... | collective-permute-start | bytes 1253384 | tf_op jit(solution)/shard_map/ppermute | solution.py:542
  67.3 3.2 %own_weights.1 = (f32[1024,1024]{1,0:T(8,128)S(1)}, f32[256,2048]{1,0:T(8,128)S(1)}) custom-call(s32[5]{0:T(128)S(1)} %stack.23.at_ref.spot_ref, bf16[384,5632]{1,0:T(8,128)(2,1)S(1)} %get-tuple-element.62.mine), custom_call_target="tpu_custom_call" | custom-call | flops 4831838208 | bytes 41943040 | tf_op jit(solution)/shard_map/own_weights/pallas_call | solution.py:52
  70.5 4.4 %weights.1 = bf16[16,96,1024]{2,1,0:T(8,128)(2,1)} custom-call(s32[5]{0:T(128)S(1)} %stack.23.at_ref.spot_ref, f32[1024,1024]{1,0:T(8,128)S(1)} %get-tuple-element.63.up_ref, f32[256,2048]{1,0:T(8,128)S(1)} %get-tuple-element.64.down_ref, bf16[384,5632]{1,0:T(8,128)(2,1)S(1)} %collective-permute-done.7.other), custom_call_target="tpu_custom_call" | custom-call | flops 4831838208 | bytes 41943040 | tf_op jit(solution)/shard_map/weights/pallas_call | solution.py:52
  74.9 7.9 %all-to-all-start = ((bf16[16,96,1024]{2,1,0:T(8,128)(2,1)}), bf16[16,96,1024]{2,1,0:T(8,128)(2,1)S(1)}, u32[]{:S(2)}, u32[]{:S(2)}) async-start(bf16[16,96,1024]{2,1,0:T(8,128)(2,1)} %weights.1), calls=%async_computation | async-start | bytes 6291456 | tf_op jit(solution)/shard_map/all_to_all | solution.py:595
  82.8 2.6 %collective-permute-done.9.refs_9_ = bf16[96,2176]{1,0:T(8,128)(2,1)} collective-permute-done((bf16[96,2176]{1,0:T(8,128)(2,1)}, bf16[96,2176]{1,0:T(8,128)(2,1)}, u32[]{:S(2)}, u32[]{:S(2)}) %collective-permute-start.9) | collective-permute-done | bytes 417824 | tf_op jit(solution)/shard_map/ppermute | solution.py:542
  85.4 8.3 %project.1 = (bf16[256,2048]{1,0:T(8,128)(2,1)}, bf16[1,256]{1,0:T(2,128)(2,1)}, bf16[256,512]{1,0:T(8,128)(2,1)S(1)}, bf16[256,512]{1,0:T(8,128)(2,1)S(1)}, bf1...) custom-call(bf16[512,2048]{1,0:T(8,128)(2,1)} %refs_0_.2, bf16[32,3,16,2048]{3,2,1,0:T(8,128)(2,1)} %bitcast.11, ...), custom_call_target="tpu_custom_call" | custom-call | flops 7650410496 | bytes 31457280 | tf_op jit(solution)/shard_map/project/pallas_call | solution.py:52
  96.7 6.4 %collective-permute-done.10.g1 = bf16[256,512]{1,0:T(8,128)(2,1)S(1)} collective-permute-done((bf16[256,512]{1,0:T(8,128)(2,1)S(1)}, bf16[256,512]{1,0:T(8,128)(2,1)S(1)}, u32[]{:S(2)}, u32[]{:S(2)}) %collective-permute-start.10) | collective-permute-done | bytes 262176 | tf_op jit(solution)/shard_map/ppermute | solution.py:542
  103.1 2.2 %collective-permute-done.11.g2 = bf16[256,512]{1,0:T(8,128)(2,1)S(1)} collective-permute-done((bf16[256,512]{1,0:T(8,128)(2,1)S(1)}, bf16[256,512]{1,0:T(8,128)(2,1)S(1)}, u32[]{:S(2)}, u32[]{:S(2)}) %collective-permute-start.11) | collective-permute-done | bytes 262176 | tf_op jit(solution)/shard_map/ppermute | solution.py:542
  105.3 4.3 %collective-permute-done.12.g3 = bf16[256,512]{1,0:T(8,128)(2,1)S(1)} collective-permute-done((bf16[256,512]{1,0:T(8,128)(2,1)S(1)}, bf16[256,512]{1,0:T(8,128)(2,1)S(1)}, u32[]{:S(2)}, u32[]{:S(2)}) %collective-permute-start.12) | collective-permute-done | bytes 262176 | tf_op jit(solution)/shard_map/ppermute | solution.py:542
  114.2 2.7 %collective-permute-start.15 = (bf16[512,128]{1,0:T(8,128)(2,1)S(1)}, bf16[512,128]{1,0:T(8,128)(2,1)S(1)}, u32[]{:S(2)}, u32[]{:S(2)}) collective-permute-start(bf16[512,128]{1,0:T(8,128)(2,1)S(1)} %get-tuple-element.76), channel_id=1, source_target_pairs={{0,16},{4,20},{8,24},{12,28},{16,0},{20,4},{24,8},{28,12},{32,48},... | collective-permute-start | bytes 393224 | tf_op jit(solution)/shard_map/ppermute | solution.py:546
  118.4 8.2 %query_key.1 = (bf16[1024,512]{1,0:T(8,128)(2,1)}, bf16[1024,512]{1,0:T(8,128)(2,1)S(1)}) custom-call(s32[5]{0:T(128)S(1)} %stack.23.at_ref.spot_ref, bf16[1024,512]{1,0:T(8,128)(2,1)S(1)} %copy-done, bf16[1024,512]{1,0:T(8,128)(2,1)S(1)} %copy-done.1, bf16[1024,512]{1,0:T(8,128)(2,1)S(1)} %copy-done.2, bf16[1024,512]{1,0:T(8,128)(2,1)S(1)} %get-tuple-element.73.g_ref, ...), custom_call_target="tpu_custom_call" | custom-call | flops 8053063680 | bytes 18874368 | tf_op jit(solution)/shard_map/query_key/pallas_call | solution.py:52
  127.6 6.9 %collective-permute-done.15.x2 = bf16[512,128]{1,0:T(8,128)(2,1)S(1)} collective-permute-done((bf16[512,128]{1,0:T(8,128)(2,1)S(1)}, bf16[512,128]{1,0:T(8,128)(2,1)S(1)}, u32[]{:S(2)}, u32[]{:S(2)}) %collective-permute-start.15) | collective-permute-done | bytes 131104 | tf_op jit(solution)/shard_map/ppermute | solution.py:546
  135.0 3.0 %collective-permute-start.18 = (bf16[512,128]{1,0:T(8,128)(2,1)S(1)}, bf16[512,128]{1,0:T(8,128)(2,1)S(1)}, u32[]{:S(2)}, u32[]{:S(2)}) collective-permute-start(bf16[512,128]{1,0:T(8,128)(2,1)S(1)} %line.1), channel_id=1, source_target_pairs={{0,64},{4,68},{8,72},{12,76},{16,80},{20,84},{24,88},{28,92},{32,9... | collective-permute-start | bytes 393224 | tf_op jit(solution)/shard_map/ppermute | solution.py:550
  138.0 2.4 %collective-permute-start.19 = (bf16[512,128]{1,0:T(8,128)(2,1)S(1)}, bf16[512,128]{1,0:T(8,128)(2,1)S(1)}, u32[]{:S(2)}, u32[]{:S(2)}) collective-permute-start(bf16[512,128]{1,0:T(8,128)(2,1)S(1)} %line.1), channel_id=1, source_target_pairs={{0,96},{4,100},{8,104},{12,108},{16,112},{20,116},{24,120},{28,124... | collective-permute-start | bytes 393224 | tf_op jit(solution)/shard_map/ppermute | solution.py:550
  140.4 4.1 %value.1.value_ref = bf16[1024,512]{1,0:T(8,128)(2,1)S(1)} custom-call(s32[5]{0:T(128)S(1)} %stack.23.at_ref.spot_ref, bf16[1024,512]{1,0:T(8,128)(2,1)S(1)} %copy-done, bf16[1024,512]{1,0:T(8,128)(2,1)S(1)} %copy-done.1, bf16[1024,512]{1,0:T(8,128)(2,1)S(1)} %get-tuple-element.73.g_ref), custom_call_target="tpu_custom_call" | custom-call | flops 4026531840 | bytes 18874368 | tf_op jit(solution)/shard_map/value/pallas_call | solution.py:52
  144.6 2.7 %final.1 = (bf16[1024,512]{1,0:T(8,128)(2,1)}, bf16[1024,512]{1,0:T(8,128)(2,1)}) custom-call(s32[5]{0:T(128)S(1)} %stack.23.at_ref.spot_ref, f32[512,128]{1,0:T(8,128)S(1)} %collective-permute-done.13.other, bf16[512,128]{1,0:T(8,128)(2,1)S(1)} %collective-permute-done.14.x1, bf16[512,128]{1,0:T(8,128)(2,1)S(1)} %collective-permute-done.15.x2, ...), custom_call_target="tpu_custom_call" | custom-call | flops 1610612736 | bytes 25165824 | tf_op jit(solution)/shard_map/final/pallas_call | solution.py:52
  (45 shorter events, 18.4 us)
Async XLA Ops:
  7.2 78.3 %all-gather.3.cloned.1.call-start = ((), (), s32[]{:S(2)}) async-start(), calls=%async_computation.1 | async-start | bytes 6488064 | tf_op jit(solution)/shard_map/all_gather | solution.py:581
  8.1 9.9 %collective-permute-start = (bf16[16,2048]{1,0:T(8,128)(2,1)S(1)}, bf16[16,2048]{1,0:T(8,128)(2,1)S(1)}, u32[]{:S(2)}, u32[]{:S(2)}) collective-permute-start(bf16[16,2048]{1,0:T(8,128)(2,1)S(1)} %constant_dynamic-slice_fusion), channel_id=1, source_target_pairs={{0,1},{1,2},{2,3},{3,0},{4,5},{5,6},{6,7},{7,4},{8,9},{9,10},{10,1... | collective-permute-start | bytes 196616 | tf_op jit(solution)/shard_map/ppermute | solution.py:542
  9.7 8.2 %collective-permute-start.1 = (bf16[16,2048]{1,0:T(8,128)(2,1)S(1)}, bf16[16,2048]{1,0:T(8,128)(2,1)S(1)}, u32[]{:S(2)}, u32[]{:S(2)}) collective-permute-start(bf16[16,2048]{1,0:T(8,128)(2,1)S(1)} %constant_dynamic-slice_fusion), channel_id=1, source_target_pairs={{0,2},{1,3},{2,0},{3,1},{4,6},{5,7},{6,4},{7,5},{8,10},{9,11},{10,... | collective-permute-start | bytes 196616 | tf_op jit(solution)/shard_map/ppermute | solution.py:542
  12.6 5.3 %collective-permute-start.2 = (bf16[16,2048]{1,0:T(8,128)(2,1)S(1)}, bf16[16,2048]{1,0:T(8,128)(2,1)S(1)}, u32[]{:S(2)}, u32[]{:S(2)}) collective-permute-start(bf16[16,2048]{1,0:T(8,128)(2,1)S(1)} %constant_dynamic-slice_fusion), channel_id=1, source_target_pairs={{0,3},{1,0},{2,1},{3,2},{4,7},{5,4},{6,5},{7,6},{8,11},{9,8},{10,9... | collective-permute-start | bytes 196616 | tf_op jit(solution)/shard_map/ppermute | solution.py:542
  18.7 22.3 %collective-permute-start.4 = (bf16[2,96,2048]{2,1,0:T(8,128)(2,1)}, bf16[2,96,2048]{2,1,0:T(8,128)(2,1)S(1)}, u32[]{:S(2)}, u32[]{:S(2)}) collective-permute-start(bf16[2,96,2048]{2,1,0:T(8,128)(2,1)} %get-tuple-element.55), channel_id=1, source_target_pairs={{0,2},{1,3},{2,0},{3,1},{4,6},{5,7},{6,4},{7,5},{8,10},{9,11},{10,... | collective-permute-start | bytes 2359304 | tf_op jit(solution)/shard_map/ppermute | solution.py:542
  19.2 34.6 %collective-permute-start.5 = (bf16[2,96,2048]{2,1,0:T(8,128)(2,1)}, bf16[2,96,2048]{2,1,0:T(8,128)(2,1)S(1)}, u32[]{:S(2)}, u32[]{:S(2)}) collective-permute-start(bf16[2,96,2048]{2,1,0:T(8,128)(2,1)} %get-tuple-element.56), channel_id=1, source_target_pairs={{0,3},{1,0},{2,1},{3,2},{4,7},{5,4},{6,5},{7,6},{8,11},{9,8},{10,9... | collective-permute-start | bytes 2359304 | tf_op jit(solution)/shard_map/ppermute | solution.py:542
  22.1 33.7 %collective-permute-start.3 = (bf16[2,96,2048]{2,1,0:T(8,128)(2,1)}, bf16[2,96,2048]{2,1,0:T(8,128)(2,1)S(1)}, u32[]{:S(2)}, u32[]{:S(2)}) collective-permute-start(bf16[2,96,2048]{2,1,0:T(8,128)(2,1)} %get-tuple-element.54), channel_id=1, source_target_pairs={{0,1},{1,2},{2,3},{3,0},{4,5},{5,6},{6,7},{7,4},{8,9},{9,10},{10,1... | collective-permute-start | bytes 2359304 | tf_op jit(solution)/shard_map/ppermute | solution.py:542
  62.5 7.9 %collective-permute-start.7 = (bf16[384,5632]{1,0:T(8,128)(2,1)S(1)}, bf16[384,5632]{1,0:T(8,128)(2,1)S(1)}, u32[]{:S(2)}, u32[]{:S(2)}) collective-permute-start(bf16[384,5632]{1,0:T(8,128)(2,1)S(1)} %get-tuple-element.62.mine), channel_id=1, source_target_pairs={{0,4},{4,0},{8,12},{12,8},{16,20},{20,16},{24,28},{28,24},{32,36},... | collective-permute-start | bytes 12976136 | tf_op jit(solution)/shard_map/ppermute | solution.py:554
  62.7 20.1 %collective-permute-start.8 = (bf16[96,2176]{1,0:T(8,128)(2,1)}, bf16[96,2176]{1,0:T(8,128)(2,1)}, u32[]{:S(2)}, u32[]{:S(2)}) collective-permute-start(bf16[96,2176]{1,0:T(8,128)(2,1)} %get-tuple-element.65), channel_id=1, source_target_pairs={{0,2},{1,3},{2,0},{3,1},{4,6},{5,7},{6,4},{7,5},{8,10},{9,11},{10,... | collective-permute-start | bytes 1253384 | tf_op jit(solution)/shard_map/ppermute | solution.py:542
  64.0 21.4 %collective-permute-start.9 = (bf16[96,2176]{1,0:T(8,128)(2,1)}, bf16[96,2176]{1,0:T(8,128)(2,1)}, u32[]{:S(2)}, u32[]{:S(2)}) collective-permute-start(bf16[96,2176]{1,0:T(8,128)(2,1)} %get-tuple-element.66), channel_id=1, source_target_pairs={{0,1},{1,2},{2,3},{3,0},{4,5},{5,6},{6,7},{7,4},{8,9},{9,10},{10,1... | collective-permute-start | bytes 1253384 | tf_op jit(solution)/shard_map/ppermute | solution.py:542
  64.2 21.2 %collective-permute-start.6 = (bf16[96,2176]{1,0:T(8,128)(2,1)}, bf16[96,2176]{1,0:T(8,128)(2,1)}, u32[]{:S(2)}, u32[]{:S(2)}) collective-permute-start(bf16[96,2176]{1,0:T(8,128)(2,1)} %get-tuple-element.61), channel_id=1, source_target_pairs={{0,3},{1,0},{2,1},{3,2},{4,7},{5,4},{6,5},{7,6},{8,11},{9,8},{10,9... | collective-permute-start | bytes 1253384 | tf_op jit(solution)/shard_map/ppermute | solution.py:542
  74.9 72.4 %all-to-all-start = ((bf16[16,96,1024]{2,1,0:T(8,128)(2,1)}), bf16[16,96,1024]{2,1,0:T(8,128)(2,1)S(1)}, u32[]{:S(2)}, u32[]{:S(2)}) async-start(bf16[16,96,1024]{2,1,0:T(8,128)(2,1)} %weights.1), calls=%async_computation | async-start | bytes 6291456 | tf_op jit(solution)/shard_map/all_to_all | solution.py:595
  93.8 24.6 %copy-start.1 = (bf16[1024,512]{1,0:T(8,128)(2,1)S(1)}, bf16[1024,512]{1,0:T(8,128)(2,1)}, u32[]{:S(2)}) copy-start(bf16[1024,512]{1,0:T(8,128)(2,1)} %k_ref.5) | copy-start | bytes 3145732
  93.8 24.6 %copy-start.2 = (bf16[1024,512]{1,0:T(8,128)(2,1)S(1)}, bf16[1024,512]{1,0:T(8,128)(2,1)}, u32[]{:S(2)}) copy-start(bf16[1024,512]{1,0:T(8,128)(2,1)} %v_ref.3) | copy-start | bytes 3145732
  93.8 9.2 %collective-permute-start.10 = (bf16[256,512]{1,0:T(8,128)(2,1)S(1)}, bf16[256,512]{1,0:T(8,128)(2,1)S(1)}, u32[]{:S(2)}, u32[]{:S(2)}) collective-permute-start(bf16[256,512]{1,0:T(8,128)(2,1)S(1)} %get-tuple-element.70), channel_id=1, source_target_pairs={{0,3},{1,0},{2,1},{3,2},{4,7},{5,4},{6,5},{7,6},{8,11},{9,8},{10,9... | collective-permute-start | bytes 786440 | tf_op jit(solution)/shard_map/ppermute | solution.py:542
  94.6 10.8 %collective-permute-start.11 = (bf16[256,512]{1,0:T(8,128)(2,1)S(1)}, bf16[256,512]{1,0:T(8,128)(2,1)S(1)}, u32[]{:S(2)}, u32[]{:S(2)}) collective-permute-start(bf16[256,512]{1,0:T(8,128)(2,1)S(1)} %get-tuple-element.71), channel_id=1, source_target_pairs={{0,2},{1,3},{2,0},{3,1},{4,6},{5,7},{6,4},{7,5},{8,10},{9,11},{10,... | collective-permute-start | bytes 786440 | tf_op jit(solution)/shard_map/ppermute | solution.py:542
  96.0 13.7 %collective-permute-start.12 = (bf16[256,512]{1,0:T(8,128)(2,1)S(1)}, bf16[256,512]{1,0:T(8,128)(2,1)S(1)}, u32[]{:S(2)}, u32[]{:S(2)}) collective-permute-start(bf16[256,512]{1,0:T(8,128)(2,1)S(1)} %get-tuple-element.72), channel_id=1, source_target_pairs={{0,1},{1,2},{2,3},{3,0},{4,5},{5,6},{6,7},{7,4},{8,9},{9,10},{10,1... | collective-permute-start | bytes 786440 | tf_op jit(solution)/shard_map/ppermute | solution.py:542
  110.9 1.6 %collective-permute-start.13 = (f32[512,128]{1,0:T(8,128)S(1)}, f32[512,128]{1,0:T(8,128)S(1)}, u32[]{:S(2)}, u32[]{:S(2)}) collective-permute-start(f32[512,128]{1,0:T(8,128)S(1)} %get-tuple-element.75.state), channel_id=1, source_target_pairs={{0,4},{4,0},{8,12},{12,8},{16,20},{20,16},{24,28},{28,24},{32,36},... | collective-permute-start | bytes 786440 | tf_op jit(solution)/shard_map/ppermute | solution.py:554
  112.6 15.1 %collective-permute-start.14 = (bf16[512,128]{1,0:T(8,128)(2,1)S(1)}, bf16[512,128]{1,0:T(8,128)(2,1)S(1)}, u32[]{:S(2)}, u32[]{:S(2)}) collective-permute-start(bf16[512,128]{1,0:T(8,128)(2,1)S(1)} %get-tuple-element.76), channel_id=1, source_target_pairs={{0,8},{4,12},{8,16},{12,20},{16,24},{20,28},{24,0},{28,4},{32,40},... | collective-permute-start | bytes 393224 | tf_op jit(solution)/shard_map/ppermute | solution.py:546
  114.2 20.3 %collective-permute-start.15 = (bf16[512,128]{1,0:T(8,128)(2,1)S(1)}, bf16[512,128]{1,0:T(8,128)(2,1)S(1)}, u32[]{:S(2)}, u32[]{:S(2)}) collective-permute-start(bf16[512,128]{1,0:T(8,128)(2,1)S(1)} %get-tuple-element.76), channel_id=1, source_target_pairs={{0,16},{4,20},{8,24},{12,28},{16,0},{20,4},{24,8},{28,12},{32,48},... | collective-permute-start | bytes 393224 | tf_op jit(solution)/shard_map/ppermute | solution.py:546
  116.9 17.6 %collective-permute-start.16 = (bf16[512,128]{1,0:T(8,128)(2,1)S(1)}, bf16[512,128]{1,0:T(8,128)(2,1)S(1)}, u32[]{:S(2)}, u32[]{:S(2)}) collective-permute-start(bf16[512,128]{1,0:T(8,128)(2,1)S(1)} %get-tuple-element.76), channel_id=1, source_target_pairs={{0,24},{4,28},{8,0},{12,4},{16,8},{20,12},{24,16},{28,20},{32,56},... | collective-permute-start | bytes 393224 | tf_op jit(solution)/shard_map/ppermute | solution.py:546
  134.6 9.9 %collective-permute-start.17 = (bf16[512,128]{1,0:T(8,128)(2,1)S(1)}, bf16[512,128]{1,0:T(8,128)(2,1)S(1)}, u32[]{:S(2)}, u32[]{:S(2)}) collective-permute-start(bf16[512,128]{1,0:T(8,128)(2,1)S(1)} %line.1), channel_id=1, source_target_pairs={{0,32},{4,36},{8,40},{12,44},{16,48},{20,52},{24,56},{28,60},{32,6... | collective-permute-start | bytes 393224 | tf_op jit(solution)/shard_map/ppermute | solution.py:550
  135.0 9.5 %collective-permute-start.18 = (bf16[512,128]{1,0:T(8,128)(2,1)S(1)}, bf16[512,128]{1,0:T(8,128)(2,1)S(1)}, u32[]{:S(2)}, u32[]{:S(2)}) collective-permute-start(bf16[512,128]{1,0:T(8,128)(2,1)S(1)} %line.1), channel_id=1, source_target_pairs={{0,64},{4,68},{8,72},{12,76},{16,80},{20,84},{24,88},{28,92},{32,9... | collective-permute-start | bytes 393224 | tf_op jit(solution)/shard_map/ppermute | solution.py:550
  138.0 6.5 %collective-permute-start.19 = (bf16[512,128]{1,0:T(8,128)(2,1)S(1)}, bf16[512,128]{1,0:T(8,128)(2,1)S(1)}, u32[]{:S(2)}, u32[]{:S(2)}) collective-permute-start(bf16[512,128]{1,0:T(8,128)(2,1)S(1)} %line.1), channel_id=1, source_target_pairs={{0,96},{4,100},{8,104},{12,108},{16,112},{20,116},{24,120},{28,124... | collective-permute-start | bytes 393224 | tf_op jit(solution)/shard_map/ppermute | solution.py:550
  (2 other events, 48.7 us)
Sparse Core Ops, SparseCore 0:
  18.8 52.7 all-gather.2

commit v9 on v8

--- a/solution.py
+++ b/solution.py
@@ -62,53 +62,63 @@
     )(*ins)
 
 
-def pack_body(at_ref, ids_ref, gate_ref, moe_ref, cot_ref, place_ref, turned_ref, c0, c1, c2, c3, gate_col):
-    @pl.when(pl.program_id(0) == 0)
-    def _():
-        rel = ids_ref[...] - at_ref[0]
-        rel = jnp.where(rel < 0, rel + Y, rel)
-        member = (lax.broadcasted_iota(jnp.int32, (8, ROWS), 0) == rel).astype(f32)
-        row = lax.broadcasted_iota(jnp.int32, (ROWS, ROWS), 0)
-        col = lax.broadcasted_iota(jnp.int32, (ROWS, ROWS), 1)
-        earlier = dot(member.astype(bf16), (row < col).astype(bf16))
-        slot = jnp.sum(earlier * member, axis=0, keepdims=True).astype(jnp.int32)
-        target = rel * CAP + slot
-        places = lax.broadcasted_iota(jnp.int32, (Y * CAP, ROWS), 0)
-        place_ref[...] = (places == target).astype(bf16)
-        spots_col = jnp.sum(jnp.where(row == col, target.astype(f32), 0.0), axis=1, keepdims=True)
-        lanes = lax.broadcasted_iota(jnp.int32, (ROWS, Y * CAP), 1)
-        turned_ref[...] = (lanes == spots_col.astype(jnp.int32)).astype(bf16)
-        gate = gate_ref[...].astype(f32)
-        gate_col[...] = jnp.sum(jnp.where(row == col, gate, 0.0), axis=1, keepdims=True)
-
-    place = place_ref[...]
-    scaled = (gate_col[...] * cot_ref[...].astype(f32)).astype(bf16)
-    for half, rows in enumerate((moe_ref[...], scaled)):
-        part = dot(place, rows).astype(bf16)
-        for s, chunk in enumerate((c0, c1, c2, c3)):
-            chunk[half] = part[s * CAP : (s + 1) * CAP]
+def pack_body(at_ref, ids_ref, gate_ref, moe_hbm, cot_hbm, place_ref, turned_ref, c0, c1, c2, c3, moe, cot, sem):
+    half = WIDTH // 2
+    copies = []
+    for k in range(2):
+        cols = pl.ds(k * half, half)
+        copies.append(pltpu.make_async_copy(moe_hbm.at[:, cols], moe.at[:, cols], sem.at[k]))
+        copies.append(pltpu.make_async_copy(cot_hbm.at[:, cols], cot.at[:, cols], sem.at[2 + k]))
+    for copy in copies:
+        copy.start()
+    rel = ids_ref[...] - at_ref[0]
+    rel = jnp.where(rel < 0, rel + Y, rel)
+    member = (lax.broadcasted_iota(jnp.int32, (8, ROWS), 0) == rel).astype(f32)
+    row = lax.broadcasted_iota(jnp.int32, (ROWS, ROWS), 0)
+    col = lax.broadcasted_iota(jnp.int32, (ROWS, ROWS), 1)
+    earlier = dot(member.astype(bf16), (row < col).astype(bf16))
+    slot = jnp.sum(earlier * member, axis=0, keepdims=True).astype(jnp.int32)
+    target = rel * CAP + slot
+    places = lax.broadcasted_iota(jnp.int32, (Y * CAP, ROWS), 0)
+    place_ref[...] = (places == target).astype(bf16)
+    spots_col = jnp.sum(jnp.where(row == col, target.astype(f32), 0.0), axis=1, keepdims=True)
+    lanes = lax.broadcasted_iota(jnp.int32, (ROWS, Y * CAP), 1)
+    turned_ref[...] = (lanes == spots_col.astype(jnp.int32)).astype(bf16)
+    gate = gate_ref[...].astype(f32)
+    gate_col = jnp.sum(jnp.where(row == col, gate, 0.0), axis=1, keepdims=True)
+    step = 512
+    for j in range(WIDTH // step):
+        cols = slice(j * step, (j + 1) * step)
+        if j % 2 == 0:
+            copies[j].wait()
+            copies[j + 1].wait()
+        scaled = (gate_col * cot[:, cols].astype(f32)).astype(bf16)
+        for part, rows in enumerate((moe[:, cols], scaled)):
+            packed = dot(place_ref[...], rows).astype(bf16)
+            for s, chunk in enumerate((c0, c1, c2, c3)):
+                chunk[part, :, cols] = packed[s * CAP : (s + 1) * CAP]
 
 
 def pack(at, ids, gates, moe_in, grad_out):
-    step = 1024
     outs = [((Y * CAP, ROWS), bf16), ((ROWS, Y * CAP), bf16)] + [((2, CAP, WIDTH), bf16)] * Y
-    ins = (at, ids, gates, moe_in, grad_out)
-    row = pl.BlockSpec((1, ROWS), lambda j: (0, 0))
-    tile = pl.BlockSpec((ROWS, step), lambda j: (0, j))
     return call(
         pack_body,
         "pack",
         outs,
-        ins,
+        (at, ids, gates, moe_in, grad_out),
         2 * 384 * 256 * 4096,
         5 << 20,
-        grid=(WIDTH // step,),
-        in_specs=[scalars(), row, row, tile, tile],
-        out_specs=[pl.BlockSpec((Y * CAP, ROWS), lambda j: (0, 0)), pl.BlockSpec((ROWS, Y * CAP), lambda j: (0, 0))]
-        + [pl.BlockSpec((2, CAP, step), lambda j: (0, 0, j))] * Y,
-        scratch=[VMEM((ROWS, 1), f32)],
-        limit=16,
-    )
+        in_specs=[scalars(), full(), full(), anywhere(), anywhere()],
+        scratch=[VMEM((ROWS, WIDTH), bf16), VMEM((ROWS, WIDTH), bf16), pltpu.SemaphoreType.DMA((4,))],
+        limit=10,
+        near=(3, 4, 5),
+    )
+
+
+def join_body(a, b, c, out):
+    rows = a.shape[0]
+    for k, ref in enumerate((a, b, c)):
+        out[k * rows : (k + 1) * rows, :] = ref[...]
 
 
 BACK = WIDTH + 128
@@ -574,10 +584,12 @@
 
     slab = w_out.shape[0] // BLOCKS
     piece = lax.dynamic_slice_in_dim(w_out, block * slab, slab, 0)
-    pieces = jnp.concatenate([along_y(piece, s) for s in (1, 2, 3)], axis=0)
+    pieces = [along_y(piece, s) for s in (1, 2, 3)]
     gate_row = router_gates.reshape(1, ROWS)
     place, turned, *chunks = pack(at, expert_ids.reshape(1, ROWS), gate_row, moe_in, grad_out)
-    pieces, chunks[1] = lax.optimization_barrier((pieces, chunks[1]))
+    pieces[0], place = lax.optimization_barrier((pieces[0], place))
+    outs = [((3 * slab, WIDTH), bf16)]
+    (pieces,) = call(join_body, "join", outs, pieces, limit=2, free=range(3))
     rest = lax.all_gather(pieces[None], "ctx", axis=0, tiled=True)
     rest = rest.reshape(BLOCKS, 3, slab, WIDTH)
 

time: 155 us -> 156 us (level)
    pallas_call x13 -> x14, Pallas kernels: 46.9 us -> 47.4 us  [call(): pl.pallas_call(body, name=name, out_shape=[(VMEM if near is True or i in...]
  transfers between devices with their start and end apart: 22 -> 22, of which waited for: 10 -> 7; matrix products, arithmetic and copies ran while one was open for 0% -> 0% of each run, Pallas kernels for 30% -> 29%
where the time goes in v9:
time: 156 us
  waiting for transfers between devices  56.3 us (36%)
  Pallas kernels  47.4 us (30%)
  starting transfers between devices  36.8 us (24%)
  between operations  14.3 us (9%)
    ppermute x12, waiting for transfers between devices, along_y(): return lax.ppermute(a, 'exp', [(i, (i + s) % Y) for i in range(Y)])  47.5 us
    pallas_call x14, Pallas kernels, call(): pl.pallas_call(body, name=name, out_shape=[(VMEM if near is True or i in...  47.4 us
    ppermute x12, starting transfers between devices, along_y(): return lax.ppermute(a, 'exp', [(i, (i + s) % Y) for i in range(Y)])  17.4 us
    all_to_all x1, starting transfers between devices, on_device(): lax.all_to_all(partial, 'ctx', 0, 0, axis_index_groups=groups, tiled=True)  7.89 us
    ppermute x3, waiting for transfers between devices, along_x(): lax.ppermute(a, 'ctx', [(index(z, x, c), index(z, (x + s) % X, c)) for z,...  7.24 us
    ppermute x3, starting transfers between devices, along_x(): lax.ppermute(a, 'ctx', [(index(z, x, c), index(z, (x + s) % X, c)) for z,...  5.7 us
    ppermute x3, starting transfers between devices, along_z(): lax.ppermute(a, 'ctx', [(index(z, x, c), index((z + s) % Z, x, c)) for z,...  5.61 us
  transfers between devices with their start and end apart: 22, of which 7 were waited for; matrix products, arithmetic and copies ran while one was open for 0% of the time, Pallas kernels for 29%

profile of v9, /device:TPU:0, one launch (start us, length us, event | category | flops | bytes accessed | tf_op | source)
XLA Modules:
  0.0 155.8 jit_solution(13209176521364153264)
XLA Ops:
  8.1 1.7 %collective-permute-start = (bf16[16,2048]{1,0:T(8,128)(2,1)S(1)}, bf16[16,2048]{1,0:T(8,128)(2,1)S(1)}, u32[]{:S(2)}, u32[]{:S(2)}) collective-permute-start(bf16[16,2048]{1,0:T(8,128)(2,1)S(1)} %constant_dynamic-slice_fusion), channel_id=1, source_target_pairs={{0,1},{1,2},{2,3},{3,0},{4,5},{5,6},{6,7},{7,4},{8,9},{9,10},{10,1... | collective-permute-start | bytes 196616 | tf_op jit(solution)/shard_map/ppermute | solution.py:552
  9.7 2.9 %collective-permute-start.1 = (bf16[16,2048]{1,0:T(8,128)(2,1)S(1)}, bf16[16,2048]{1,0:T(8,128)(2,1)S(1)}, u32[]{:S(2)}, u32[]{:S(2)}) collective-permute-start(bf16[16,2048]{1,0:T(8,128)(2,1)S(1)} %constant_dynamic-slice_fusion), channel_id=1, source_target_pairs={{0,2},{1,3},{2,0},{3,1},{4,6},{5,7},{6,4},{7,5},{8,10},{9,11},{10,... | collective-permute-start | bytes 196616 | tf_op jit(solution)/shard_map/ppermute | solution.py:552
  14.1 3.9 %pack.1 = (bf16[384,256]{1,0:T(8,128)(2,1)}, bf16[256,384]{1,0:T(8,128)(2,1)}, bf16[2,96,2048]{2,1,0:T(8,128)(2,1)}, bf16[2,96,2048]{2,1,0:T(8,128)(2,1)S(1)}, b...) custom-call(s32[5]{0:T(128)S(1)} %stack.23.at_ref.spot_ref, s32[1,256]{1,0:T(1,128)} %bitcast.12, ...), custom_call_target="tpu_custom_call" | custom-call | flops 3221225472 | bytes 20971520 | tf_op jit(solution)/shard_map/pack/pallas_call | solution.py:52
  19.5 2.2 %collective-permute-start.4 = (bf16[2,96,2048]{2,1,0:T(8,128)(2,1)S(1)}, bf16[2,96,2048]{2,1,0:T(8,128)(2,1)S(1)}, u32[]{:S(2)}, u32[]{:S(2)}) collective-permute-start(bf16[2,96,2048]{2,1,0:T(8,128)(2,1)S(1)} %get-tuple-element.55), channel_id=1, source_target_pairs={{0,2},{1,3},{2,0},{3,1},{4,6},{5,7},{6,4},{7,5},{8,10},{9,11},{10,... | collective-permute-start | bytes 2359304 | tf_op jit(solution)/shard_map/ppermute | solution.py:552
  22.2 2.9 %fetch.1 = (bf16[1,2048,1024]{2,1,0:T(8,128)(2,1)S(1)}, bf16[1,512,2048]{2,1,0:T(8,128)(2,1)S(1)}) custom-call(bf16[1,2048,1024]{2,1,0:T(8,128)(2,1)} %refs_0_.1, bf16[1,512,2048]{2,1,0:T(8,128)(2,1)} %refs_1_.1), custom_call_target="tpu_custom_call" | custom-call | bytes 50331648 | tf_op jit(solution)/shard_map/fetch/pallas_call | solution.py:52
  25.1 30.2 %collective-permute-done.3.r1 = bf16[2,96,2048]{2,1,0:T(8,128)(2,1)S(1)} collective-permute-done((bf16[2,96,2048]{2,1,0:T(8,128)(2,1)S(1)}, bf16[2,96,2048]{2,1,0:T(8,128)(2,1)S(1)}, u32[]{:S(2)}, u32[]{:S(2)}) %collective-permute-start.3) | collective-permute-done | bytes 786464 | tf_op jit(solution)/shard_map/ppermute | solution.py:552
  55.9 6.7 %expert.1 = (bf16[96,2176]{1,0:T(8,128)(2,1)}, bf16[96,2176]{1,0:T(8,128)(2,1)}, bf16[96,2176]{1,0:T(8,128)(2,1)}, bf16[96,2176]{1,0:T(8,128)(2,1)}, bf16[384,5632]{1,0:T(8,128)(2,1)S(1)}) custom-call(bf16[2,96,2048]{2,1,0:T(8,128)(2,1)} %get-tuple-element.53.r0, bf16[2,96,2048]{2,1,0:T(8,128)(2,1)S(1)} %collective-permute-done.3.r1, ...), custom_call_target="tpu_custom_call" | custom-call | flops 16106127360 | bytes 58720256 | tf_op jit(solution)/shard_map/expert/pallas_call | solution.py:52
  63.9 2.3 %collective-permute-start.9 = (bf16[96,2176]{1,0:T(8,128)(2,1)}, bf16[96,2176]{1,0:T(8,128)(2,1)}, u32[]{:S(2)}, u32[]{:S(2)}) collective-permute-start(bf16[96,2176]{1,0:T(8,128)(2,1)} %get-tuple-element.66), channel_id=1, source_target_pairs={{0,1},{1,2},{2,3},{3,0},{4,5},{5,6},{6,7},{7,4},{8,9},{9,10},{10,1... | collective-permute-start | bytes 1253384 | tf_op jit(solution)/shard_map/ppermute | solution.py:552
  67.1 3.2 %own_weights.1 = (f32[1024,1024]{1,0:T(8,128)S(1)}, f32[256,2048]{1,0:T(8,128)S(1)}) custom-call(s32[5]{0:T(128)S(1)} %stack.23.at_ref.spot_ref, bf16[384,5632]{1,0:T(8,128)(2,1)S(1)} %get-tuple-element.62.mine), custom_call_target="tpu_custom_call" | custom-call | flops 4831838208 | bytes 41943040 | tf_op jit(solution)/shard_map/own_weights/pallas_call | solution.py:52
  70.3 4.4 %weights.1 = bf16[16,96,1024]{2,1,0:T(8,128)(2,1)} custom-call(s32[5]{0:T(128)S(1)} %stack.23.at_ref.spot_ref, f32[1024,1024]{1,0:T(8,128)S(1)} %get-tuple-element.63.up_ref, f32[256,2048]{1,0:T(8,128)S(1)} %get-tuple-element.64.down_ref, bf16[384,5632]{1,0:T(8,128)(2,1)S(1)} %collective-permute-done.7.other), custom_call_target="tpu_custom_call" | custom-call | flops 4831838208 | bytes 41943040 | tf_op jit(solution)/shard_map/weights/pallas_call | solution.py:52
  74.7 7.9 %all-to-all-start = ((bf16[16,96,1024]{2,1,0:T(8,128)(2,1)}), bf16[16,96,1024]{2,1,0:T(8,128)(2,1)S(1)}, u32[]{:S(2)}, u32[]{:S(2)}) async-start(bf16[16,96,1024]{2,1,0:T(8,128)(2,1)} %weights.1), calls=%async_computation | async-start | bytes 6291456 | tf_op jit(solution)/shard_map/all_to_all | solution.py:607
  82.6 2.9 %collective-permute-done.9.refs_9_ = bf16[96,2176]{1,0:T(8,128)(2,1)} collective-permute-done((bf16[96,2176]{1,0:T(8,128)(2,1)}, bf16[96,2176]{1,0:T(8,128)(2,1)}, u32[]{:S(2)}, u32[]{:S(2)}) %collective-permute-start.9) | collective-permute-done | bytes 417824 | tf_op jit(solution)/shard_map/ppermute | solution.py:552
  85.5 8.3 %project.1 = (bf16[256,2048]{1,0:T(8,128)(2,1)}, bf16[1,256]{1,0:T(2,128)(2,1)}, bf16[256,512]{1,0:T(8,128)(2,1)S(1)}, bf16[256,512]{1,0:T(8,128)(2,1)S(1)}, bf1...) custom-call(bf16[512,2048]{1,0:T(8,128)(2,1)} %refs_0_.2, bf16[32,3,16,2048]{3,2,1,0:T(8,128)(2,1)} %bitcast.11, ...), custom_call_target="tpu_custom_call" | custom-call | flops 7650410496 | bytes 31457280 | tf_op jit(solution)/shard_map/project/pallas_call | solution.py:52
  93.9 2.6 %collective-permute-start.10 = (bf16[256,512]{1,0:T(8,128)(2,1)S(1)}, bf16[256,512]{1,0:T(8,128)(2,1)S(1)}, u32[]{:S(2)}, u32[]{:S(2)}) collective-permute-start(bf16[256,512]{1,0:T(8,128)(2,1)S(1)} %get-tuple-element.70), channel_id=1, source_target_pairs={{0,3},{1,0},{2,1},{3,2},{4,7},{5,4},{6,5},{7,6},{8,11},{9,8},{10,9... | collective-permute-start | bytes 786440 | tf_op jit(solution)/shard_map/ppermute | solution.py:552
  97.5 10.4 %collective-permute-done.10.g1 = bf16[256,512]{1,0:T(8,128)(2,1)S(1)} collective-permute-done((bf16[256,512]{1,0:T(8,128)(2,1)S(1)}, bf16[256,512]{1,0:T(8,128)(2,1)S(1)}, u32[]{:S(2)}, u32[]{:S(2)}) %collective-permute-start.10) | collective-permute-done | bytes 262176 | tf_op jit(solution)/shard_map/ppermute | solution.py:552
  108.0 3.4 %collective-permute-done.12.g3 = bf16[256,512]{1,0:T(8,128)(2,1)S(1)} collective-permute-done((bf16[256,512]{1,0:T(8,128)(2,1)S(1)}, bf16[256,512]{1,0:T(8,128)(2,1)S(1)}, u32[]{:S(2)}, u32[]{:S(2)}) %collective-permute-start.12) | collective-permute-done | bytes 262176 | tf_op jit(solution)/shard_map/ppermute | solution.py:552
  114.3 1.5 collective-permute-start.14
  115.8 2.7 %collective-permute-start.15 = (bf16[512,128]{1,0:T(8,128)(2,1)S(1)}, bf16[512,128]{1,0:T(8,128)(2,1)S(1)}, u32[]{:S(2)}, u32[]{:S(2)}) collective-permute-start(bf16[512,128]{1,0:T(8,128)(2,1)S(1)} %get-tuple-element.76), channel_id=1, source_target_pairs={{0,16},{4,20},{8,24},{12,28},{16,0},{20,4},{24,8},{28,12},{32,48},... | collective-permute-start | bytes 393224 | tf_op jit(solution)/shard_map/ppermute | solution.py:556
  120.0 8.1 %query_key.1 = (bf16[1024,512]{1,0:T(8,128)(2,1)}, bf16[1024,512]{1,0:T(8,128)(2,1)S(1)}) custom-call(s32[5]{0:T(128)S(1)} %stack.23.at_ref.spot_ref, bf16[1024,512]{1,0:T(8,128)(2,1)S(1)} %copy-done, bf16[1024,512]{1,0:T(8,128)(2,1)S(1)} %copy-done.1, bf16[1024,512]{1,0:T(8,128)(2,1)S(1)} %copy-done.2, bf16[1024,512]{1,0:T(8,128)(2,1)S(1)} %get-tuple-element.73.g_ref, ...), custom_call_target="tpu_custom_call" | custom-call | flops 8053063680 | bytes 18874368 | tf_op jit(solution)/shard_map/query_key/pallas_call | solution.py:52
  128.1 7.2 %collective-permute-done.15.x2 = bf16[512,128]{1,0:T(8,128)(2,1)S(1)} collective-permute-done((bf16[512,128]{1,0:T(8,128)(2,1)S(1)}, bf16[512,128]{1,0:T(8,128)(2,1)S(1)}, u32[]{:S(2)}, u32[]{:S(2)}) %collective-permute-start.15) | collective-permute-done | bytes 131104 | tf_op jit(solution)/shard_map/ppermute | solution.py:556
  135.7 2.9 %collective-permute-start.18 = (bf16[512,128]{1,0:T(8,128)(2,1)S(1)}, bf16[512,128]{1,0:T(8,128)(2,1)S(1)}, u32[]{:S(2)}, u32[]{:S(2)}) collective-permute-start(bf16[512,128]{1,0:T(8,128)(2,1)S(1)} %line.1), channel_id=1, source_target_pairs={{0,64},{4,68},{8,72},{12,76},{16,80},{20,84},{24,88},{28,92},{32,9... | collective-permute-start | bytes 393224 | tf_op jit(solution)/shard_map/ppermute | solution.py:560
  138.6 2.4 %collective-permute-start.19 = (bf16[512,128]{1,0:T(8,128)(2,1)S(1)}, bf16[512,128]{1,0:T(8,128)(2,1)S(1)}, u32[]{:S(2)}, u32[]{:S(2)}) collective-permute-start(bf16[512,128]{1,0:T(8,128)(2,1)S(1)} %line.1), channel_id=1, source_target_pairs={{0,96},{4,100},{8,104},{12,108},{16,112},{20,116},{24,120},{28,124... | collective-permute-start | bytes 393224 | tf_op jit(solution)/shard_map/ppermute | solution.py:560
  141.0 4.1 %value.1.value_ref = bf16[1024,512]{1,0:T(8,128)(2,1)S(1)} custom-call(s32[5]{0:T(128)S(1)} %stack.23.at_ref.spot_ref, bf16[1024,512]{1,0:T(8,128)(2,1)S(1)} %copy-done, bf16[1024,512]{1,0:T(8,128)(2,1)S(1)} %copy-done.1, bf16[1024,512]{1,0:T(8,128)(2,1)S(1)} %get-tuple-element.73.g_ref), custom_call_target="tpu_custom_call" | custom-call | flops 4026531840 | bytes 18874368 | tf_op jit(solution)/shard_map/value/pallas_call | solution.py:52
  145.1 2.7 %final.1 = (bf16[1024,512]{1,0:T(8,128)(2,1)}, bf16[1024,512]{1,0:T(8,128)(2,1)}) custom-call(s32[5]{0:T(128)S(1)} %stack.23.at_ref.spot_ref, f32[512,128]{1,0:T(8,128)S(1)} %collective-permute-done.13.other, bf16[512,128]{1,0:T(8,128)(2,1)S(1)} %collective-permute-done.14.x1, bf16[512,128]{1,0:T(8,128)(2,1)S(1)} %collective-permute-done.15.x2, ...), custom_call_target="tpu_custom_call" | custom-call | flops 1610612736 | bytes 25165824 | tf_op jit(solution)/shard_map/final/pallas_call | solution.py:52
  (45 shorter events, 14.0 us)
Async XLA Ops:
  7.2 78.4 %all-gather.3.cloned.1.call-start = ((), (), s32[]{:S(2)}) async-start(), calls=%async_computation.1 | async-start | bytes 6488064 | tf_op jit(solution)/shard_map/all_gather | solution.py:593
  8.1 9.9 %collective-permute-start = (bf16[16,2048]{1,0:T(8,128)(2,1)S(1)}, bf16[16,2048]{1,0:T(8,128)(2,1)S(1)}, u32[]{:S(2)}, u32[]{:S(2)}) collective-permute-start(bf16[16,2048]{1,0:T(8,128)(2,1)S(1)} %constant_dynamic-slice_fusion), channel_id=1, source_target_pairs={{0,1},{1,2},{2,3},{3,0},{4,5},{5,6},{6,7},{7,4},{8,9},{9,10},{10,1... | collective-permute-start | bytes 196616 | tf_op jit(solution)/shard_map/ppermute | solution.py:552
  9.7 8.3 %collective-permute-start.1 = (bf16[16,2048]{1,0:T(8,128)(2,1)S(1)}, bf16[16,2048]{1,0:T(8,128)(2,1)S(1)}, u32[]{:S(2)}, u32[]{:S(2)}) collective-permute-start(bf16[16,2048]{1,0:T(8,128)(2,1)S(1)} %constant_dynamic-slice_fusion), channel_id=1, source_target_pairs={{0,2},{1,3},{2,0},{3,1},{4,6},{5,7},{6,4},{7,5},{8,10},{9,11},{10,... | collective-permute-start | bytes 196616 | tf_op jit(solution)/shard_map/ppermute | solution.py:552
  12.6 5.4 %collective-permute-start.2 = (bf16[16,2048]{1,0:T(8,128)(2,1)S(1)}, bf16[16,2048]{1,0:T(8,128)(2,1)S(1)}, u32[]{:S(2)}, u32[]{:S(2)}) collective-permute-start(bf16[16,2048]{1,0:T(8,128)(2,1)S(1)} %constant_dynamic-slice_fusion), channel_id=1, source_target_pairs={{0,3},{1,0},{2,1},{3,2},{4,7},{5,4},{6,5},{7,6},{8,11},{9,8},{10,9... | collective-permute-start | bytes 196616 | tf_op jit(solution)/shard_map/ppermute | solution.py:552
  18.7 36.6 %collective-permute-start.3 = (bf16[2,96,2048]{2,1,0:T(8,128)(2,1)S(1)}, bf16[2,96,2048]{2,1,0:T(8,128)(2,1)S(1)}, u32[]{:S(2)}, u32[]{:S(2)}) collective-permute-start(bf16[2,96,2048]{2,1,0:T(8,128)(2,1)S(1)} %get-tuple-element.54), channel_id=1, source_target_pairs={{0,1},{1,2},{2,3},{3,0},{4,5},{5,6},{6,7},{7,4},{8,9},{9,10},{10,1... | collective-permute-start | bytes 2359304 | tf_op jit(solution)/shard_map/ppermute | solution.py:552
  19.5 35.8 %collective-permute-start.4 = (bf16[2,96,2048]{2,1,0:T(8,128)(2,1)S(1)}, bf16[2,96,2048]{2,1,0:T(8,128)(2,1)S(1)}, u32[]{:S(2)}, u32[]{:S(2)}) collective-permute-start(bf16[2,96,2048]{2,1,0:T(8,128)(2,1)S(1)} %get-tuple-element.55), channel_id=1, source_target_pairs={{0,2},{1,3},{2,0},{3,1},{4,6},{5,7},{6,4},{7,5},{8,10},{9,11},{10,... | collective-permute-start | bytes 2359304 | tf_op jit(solution)/shard_map/ppermute | solution.py:552
  21.7 34.2 %collective-permute-start.5 = (bf16[2,96,2048]{2,1,0:T(8,128)(2,1)S(1)}, bf16[2,96,2048]{2,1,0:T(8,128)(2,1)S(1)}, u32[]{:S(2)}, u32[]{:S(2)}) collective-permute-start(bf16[2,96,2048]{2,1,0:T(8,128)(2,1)S(1)} %get-tuple-element.56), channel_id=1, source_target_pairs={{0,3},{1,0},{2,1},{3,2},{4,7},{5,4},{6,5},{7,6},{8,11},{9,8},{10,9... | collective-permute-start | bytes 2359304 | tf_op jit(solution)/shard_map/ppermute | solution.py:552
  62.6 7.7 %collective-permute-start.7 = (bf16[384,5632]{1,0:T(8,128)(2,1)S(1)}, bf16[384,5632]{1,0:T(8,128)(2,1)S(1)}, u32[]{:S(2)}, u32[]{:S(2)}) collective-permute-start(bf16[384,5632]{1,0:T(8,128)(2,1)S(1)} %get-tuple-element.62.mine), channel_id=1, source_target_pairs={{0,4},{4,0},{8,12},{12,8},{16,20},{20,16},{24,28},{28,24},{32,36},... | collective-permute-start | bytes 12976136 | tf_op jit(solution)/shard_map/ppermute | solution.py:564
  62.7 19.9 %collective-permute-start.8 = (bf16[96,2176]{1,0:T(8,128)(2,1)}, bf16[96,2176]{1,0:T(8,128)(2,1)}, u32[]{:S(2)}, u32[]{:S(2)}) collective-permute-start(bf16[96,2176]{1,0:T(8,128)(2,1)} %get-tuple-element.65), channel_id=1, source_target_pairs={{0,2},{1,3},{2,0},{3,1},{4,6},{5,7},{6,4},{7,5},{8,10},{9,11},{10,... | collective-permute-start | bytes 1253384 | tf_op jit(solution)/shard_map/ppermute | solution.py:552
  63.9 21.7 %collective-permute-start.9 = (bf16[96,2176]{1,0:T(8,128)(2,1)}, bf16[96,2176]{1,0:T(8,128)(2,1)}, u32[]{:S(2)}, u32[]{:S(2)}) collective-permute-start(bf16[96,2176]{1,0:T(8,128)(2,1)} %get-tuple-element.66), channel_id=1, source_target_pairs={{0,1},{1,2},{2,3},{3,0},{4,5},{5,6},{6,7},{7,4},{8,9},{9,10},{10,1... | collective-permute-start | bytes 1253384 | tf_op jit(solution)/shard_map/ppermute | solution.py:552
  66.2 19.3 %collective-permute-start.6 = (bf16[96,2176]{1,0:T(8,128)(2,1)}, bf16[96,2176]{1,0:T(8,128)(2,1)}, u32[]{:S(2)}, u32[]{:S(2)}) collective-permute-start(bf16[96,2176]{1,0:T(8,128)(2,1)} %get-tuple-element.61), channel_id=1, source_target_pairs={{0,3},{1,0},{2,1},{3,2},{4,7},{5,4},{6,5},{7,6},{8,11},{9,8},{10,9... | collective-permute-start | bytes 1253384 | tf_op jit(solution)/shard_map/ppermute | solution.py:552
  74.7 73.1 %all-to-all-start = ((bf16[16,96,1024]{2,1,0:T(8,128)(2,1)}), bf16[16,96,1024]{2,1,0:T(8,128)(2,1)S(1)}, u32[]{:S(2)}, u32[]{:S(2)}) async-start(bf16[16,96,1024]{2,1,0:T(8,128)(2,1)} %weights.1), calls=%async_computation | async-start | bytes 6291456 | tf_op jit(solution)/shard_map/all_to_all | solution.py:607
  93.9 26.1 %copy-start.1 = (bf16[1024,512]{1,0:T(8,128)(2,1)S(1)}, bf16[1024,512]{1,0:T(8,128)(2,1)}, u32[]{:S(2)}) copy-start(bf16[1024,512]{1,0:T(8,128)(2,1)} %k_ref.5) | copy-start | bytes 3145732
  93.9 26.1 %copy-start.2 = (bf16[1024,512]{1,0:T(8,128)(2,1)S(1)}, bf16[1024,512]{1,0:T(8,128)(2,1)}, u32[]{:S(2)}) copy-start(bf16[1024,512]{1,0:T(8,128)(2,1)} %v_ref.3) | copy-start | bytes 3145732
  93.9 14.0 %collective-permute-start.10 = (bf16[256,512]{1,0:T(8,128)(2,1)S(1)}, bf16[256,512]{1,0:T(8,128)(2,1)S(1)}, u32[]{:S(2)}, u32[]{:S(2)}) collective-permute-start(bf16[256,512]{1,0:T(8,128)(2,1)S(1)} %get-tuple-element.70), channel_id=1, source_target_pairs={{0,3},{1,0},{2,1},{3,2},{4,7},{5,4},{6,5},{7,6},{8,11},{9,8},{10,9... | collective-permute-start | bytes 786440 | tf_op jit(solution)/shard_map/ppermute | solution.py:552
  96.6 11.4 %collective-permute-start.11 = (bf16[256,512]{1,0:T(8,128)(2,1)S(1)}, bf16[256,512]{1,0:T(8,128)(2,1)S(1)}, u32[]{:S(2)}, u32[]{:S(2)}) collective-permute-start(bf16[256,512]{1,0:T(8,128)(2,1)S(1)} %get-tuple-element.71), channel_id=1, source_target_pairs={{0,2},{1,3},{2,0},{3,1},{4,6},{5,7},{6,4},{7,5},{8,10},{9,11},{10,... | collective-permute-start | bytes 786440 | tf_op jit(solution)/shard_map/ppermute | solution.py:552
  96.6 14.8 %collective-permute-start.12 = (bf16[256,512]{1,0:T(8,128)(2,1)S(1)}, bf16[256,512]{1,0:T(8,128)(2,1)S(1)}, u32[]{:S(2)}, u32[]{:S(2)}) collective-permute-start(bf16[256,512]{1,0:T(8,128)(2,1)S(1)} %get-tuple-element.72), channel_id=1, source_target_pairs={{0,1},{1,2},{2,3},{3,0},{4,5},{5,6},{6,7},{7,4},{8,9},{9,10},{10,1... | collective-permute-start | bytes 786440 | tf_op jit(solution)/shard_map/ppermute | solution.py:552
  112.6 1.6 %collective-permute-start.13 = (f32[512,128]{1,0:T(8,128)S(1)}, f32[512,128]{1,0:T(8,128)S(1)}, u32[]{:S(2)}, u32[]{:S(2)}) collective-permute-start(f32[512,128]{1,0:T(8,128)S(1)} %get-tuple-element.75.state), channel_id=1, source_target_pairs={{0,4},{4,0},{8,12},{12,8},{16,20},{20,16},{24,28},{28,24},{32,36},... | collective-permute-start | bytes 786440 | tf_op jit(solution)/shard_map/ppermute | solution.py:564
  114.3 13.8 %collective-permute-start.14 = (bf16[512,128]{1,0:T(8,128)(2,1)S(1)}, bf16[512,128]{1,0:T(8,128)(2,1)S(1)}, u32[]{:S(2)}, u32[]{:S(2)}) collective-permute-start(bf16[512,128]{1,0:T(8,128)(2,1)S(1)} %get-tuple-element.76), channel_id=1, source_target_pairs={{0,8},{4,12},{8,16},{12,20},{16,24},{20,28},{24,0},{28,4},{32,40},... | collective-permute-start | bytes 393224 | tf_op jit(solution)/shard_map/ppermute | solution.py:556
  115.8 19.5 %collective-permute-start.15 = (bf16[512,128]{1,0:T(8,128)(2,1)S(1)}, bf16[512,128]{1,0:T(8,128)(2,1)S(1)}, u32[]{:S(2)}, u32[]{:S(2)}) collective-permute-start(bf16[512,128]{1,0:T(8,128)(2,1)S(1)} %get-tuple-element.76), channel_id=1, source_target_pairs={{0,16},{4,20},{8,24},{12,28},{16,0},{20,4},{24,8},{28,12},{32,48},... | collective-permute-start | bytes 393224 | tf_op jit(solution)/shard_map/ppermute | solution.py:556
  118.5 16.8 %collective-permute-start.16 = (bf16[512,128]{1,0:T(8,128)(2,1)S(1)}, bf16[512,128]{1,0:T(8,128)(2,1)S(1)}, u32[]{:S(2)}, u32[]{:S(2)}) collective-permute-start(bf16[512,128]{1,0:T(8,128)(2,1)S(1)} %get-tuple-element.76), channel_id=1, source_target_pairs={{0,24},{4,28},{8,0},{12,4},{16,8},{20,12},{24,16},{28,20},{32,56},... | collective-permute-start | bytes 393224 | tf_op jit(solution)/shard_map/ppermute | solution.py:556
  135.4 9.7 %collective-permute-start.17 = (bf16[512,128]{1,0:T(8,128)(2,1)S(1)}, bf16[512,128]{1,0:T(8,128)(2,1)S(1)}, u32[]{:S(2)}, u32[]{:S(2)}) collective-permute-start(bf16[512,128]{1,0:T(8,128)(2,1)S(1)} %line.1), channel_id=1, source_target_pairs={{0,32},{4,36},{8,40},{12,44},{16,48},{20,52},{24,56},{28,60},{32,6... | collective-permute-start | bytes 393224 | tf_op jit(solution)/shard_map/ppermute | solution.py:560
  135.7 9.4 %collective-permute-start.18 = (bf16[512,128]{1,0:T(8,128)(2,1)S(1)}, bf16[512,128]{1,0:T(8,128)(2,1)S(1)}, u32[]{:S(2)}, u32[]{:S(2)}) collective-permute-start(bf16[512,128]{1,0:T(8,128)(2,1)S(1)} %line.1), channel_id=1, source_target_pairs={{0,64},{4,68},{8,72},{12,76},{16,80},{20,84},{24,88},{28,92},{32,9... | collective-permute-start | bytes 393224 | tf_op jit(solution)/shard_map/ppermute | solution.py:560
  138.6 6.5 %collective-permute-start.19 = (bf16[512,128]{1,0:T(8,128)(2,1)S(1)}, bf16[512,128]{1,0:T(8,128)(2,1)S(1)}, u32[]{:S(2)}, u32[]{:S(2)}) collective-permute-start(bf16[512,128]{1,0:T(8,128)(2,1)S(1)} %line.1), channel_id=1, source_target_pairs={{0,96},{4,100},{8,104},{12,108},{16,112},{20,116},{24,120},{28,124... | collective-permute-start | bytes 393224 | tf_op jit(solution)/shard_map/ppermute | solution.py:560
  (2 other events, 51.8 us)
Sparse Core Ops, SparseCore 0:
  18.9 52.6 all-gather.2

commit v10 on v8

--- a/solution.py
+++ b/solution.py
@@ -118,29 +118,19 @@
 STEP = 256
 
 
-def expert_body(r0, r1, r2, r3, wp, wb, b0, b1, b2, b3, held, back, in_sem, out_sem):
+def expert_body(r0, r1, r2, r3, wp, wb, b0, b1, b2, b3, held, back, out_sem):
     arrived = (r0, r1, r2, r3)
     backs = (b0, b1, b2, b3)
     tiles = FF // STEP
 
-    def incoming(half, s):
-        dst = held.at[pl.ds(s * CAP, CAP), pl.ds(half * WIDTH, WIDTH)]
-        return pltpu.make_async_copy(arrived[s].at[half], dst, in_sem.at[half * Y + s])
-
-    for s in range(Y):
-        incoming(0, s).start()
-    for s in range(Y):
-        incoming(1, s).start()
-    for s in range(Y):
-        incoming(0, s).wait()
+    for s, r in enumerate(arrived):
+        held[s * CAP : (s + 1) * CAP, :WIDTH] = r[0]
+        held[s * CAP : (s + 1) * CAP, WIDTH:GB] = r[1]
     total = jnp.zeros((N, 1), f32)
     for j in range(tiles):
         at, up = j * STEP, FF + j * STEP
         first = dot(held[:, :WIDTH], wp[0, :, at : at + STEP])
         second = dot(held[:, :WIDTH], wp[0, :, up : up + STEP])
-        if j == 0:
-            for s in range(Y):
-                incoming(1, s).wait()
         grad_hidden = dot_t(held[:, WIDTH:GB], wb[0, at : at + STEP, :])
         s = 1.0 / (1.0 + jnp.exp(-first))
         silu = first * s
@@ -208,16 +198,14 @@
         ins,
         5 * 2 * N * WIDTH * FF,
         14 << 20,
-        in_specs=[anywhere() for _ in chunks] + [full(), full()],
+        in_specs=[full()] * (Y + 2),
         out_specs=[anywhere()] * Y + [full()],
         scratch=[
             VMEM((N, BACK), bf16),
             pltpu.SemaphoreType.DMA((2 * Y,)),
-            pltpu.SemaphoreType.DMA((2 * Y,)),
         ],
         limit=16,
-        free=(1, 2, 3),
-        held=(4, 5),
+        held=range(6),
         near=(Y,),
     )
 

time: 155 us -> 156 us (level)
  waiting for transfers between devices: 55.9 us -> 58.7 us
    ppermute x3, waiting for transfers between devices: 7.99 us -> 9.93 us  [along_x(): lax.ppermute(a, 'ctx', [(index(z, x, c), index(z, (x + s) % X, c)) for z,...]
  transfers between devices with their start and end apart: 22 -> 22, of which waited for: 10 -> 11; matrix products, arithmetic and copies ran while one was open for 0% -> 0% of each run, Pallas kernels for 30% -> 29%
where the time goes in v10:
time: 156 us
  waiting for transfers between devices  58.7 us (38%)
  Pallas kernels  45.6 us (29%)
  starting transfers between devices  35.4 us (23%)
  between operations  14.2 us (9%)
    ppermute x12, waiting for transfers between devices, along_y(): return lax.ppermute(a, 'exp', [(i, (i + s) % Y) for i in range(Y)])  46.1 us
    pallas_call x13, Pallas kernels, call(): pl.pallas_call(body, name=name, out_shape=[(VMEM if near is True or i in...  45.6 us
    ppermute x12, starting transfers between devices, along_y(): return lax.ppermute(a, 'exp', [(i, (i + s) % Y) for i in range(Y)])  16.7 us
    ppermute x3, waiting for transfers between devices, along_x(): lax.ppermute(a, 'ctx', [(index(z, x, c), index(z, (x + s) % X, c)) for z,...  9.93 us
    all_to_all x1, starting transfers between devices, on_device(): lax.all_to_all(partial, 'ctx', 0, 0, axis_index_groups=groups, tiled=True)  7.05 us
    ppermute x3, starting transfers between devices, along_x(): lax.ppermute(a, 'ctx', [(index(z, x, c), index(z, (x + s) % X, c)) for z,...  5.79 us
    ppermute x3, starting transfers between devices, along_z(): lax.ppermute(a, 'ctx', [(index(z, x, c), index((z + s) % Z, x, c)) for z,...  5.52 us
  transfers between devices with their start and end apart: 22, of which 11 were waited for; matrix products, arithmetic and copies ran while one was open for 0% of the time, Pallas kernels for 29%

profile of v10, /device:TPU:0, one launch (start us, length us, event | category | flops | bytes accessed | tf_op | source)
XLA Modules:
  0.0 155.5 jit_solution(11882167819626754062)
XLA Ops:
  9.7 2.9 %collective-permute-start.1 = (bf16[16,2048]{1,0:T(8,128)(2,1)S(1)}, bf16[16,2048]{1,0:T(8,128)(2,1)S(1)}, u32[]{:S(2)}, u32[]{:S(2)}) collective-permute-start(bf16[16,2048]{1,0:T(8,128)(2,1)S(1)} %constant_dynamic-slice_fusion), channel_id=1, source_target_pairs={{0,2},{1,3},{2,0},{3,1},{4,6},{5,7},{6,4},{7,5},{8,10},{9,11},{10,... | collective-permute-start | bytes 196616 | tf_op jit(solution)/shard_map/ppermute | solution.py:530
  14.1 3.9 %pack.1 = (bf16[384,256]{1,0:T(8,128)(2,1)}, bf16[256,384]{1,0:T(8,128)(2,1)}, bf16[2,96,2048]{2,1,0:T(8,128)(2,1)}, bf16[2,96,2048]{2,1,0:T(8,128)(2,1)}, bf16[...) custom-call(s32[5]{0:T(128)S(1)} %stack.23.at_ref.spot_ref, s32[1,256]{1,0:T(1,128)} %bitcast.12, ...), custom_call_target="tpu_custom_call" | custom-call | flops 3221225472 | bytes 20971520 | tf_op jit(solution)/shard_map/pack/pallas_call | solution.py:52
  19.2 2.9 %collective-permute-start.5 = (bf16[2,96,2048]{2,1,0:T(8,128)(2,1)}, bf16[2,96,2048]{2,1,0:T(8,128)(2,1)S(1)}, u32[]{:S(2)}, u32[]{:S(2)}) collective-permute-start(bf16[2,96,2048]{2,1,0:T(8,128)(2,1)} %get-tuple-element.56), channel_id=1, source_target_pairs={{0,3},{1,0},{2,1},{3,2},{4,7},{5,4},{6,5},{7,6},{8,11},{9,8},{10,9... | collective-permute-start | bytes 2359304 | tf_op jit(solution)/shard_map/ppermute | solution.py:530
  22.1 2.9 %fetch.1 = (bf16[1,2048,1024]{2,1,0:T(8,128)(2,1)S(1)}, bf16[1,512,2048]{2,1,0:T(8,128)(2,1)S(1)}) custom-call(bf16[1,2048,1024]{2,1,0:T(8,128)(2,1)} %refs_0_.1, bf16[1,512,2048]{2,1,0:T(8,128)(2,1)} %refs_1_.1), custom_call_target="tpu_custom_call" | custom-call | bytes 50331648 | tf_op jit(solution)/shard_map/fetch/pallas_call | solution.py:52
  25.1 15.9 %collective-permute-done.4.r2 = bf16[2,96,2048]{2,1,0:T(8,128)(2,1)S(1)} collective-permute-done((bf16[2,96,2048]{2,1,0:T(8,128)(2,1)}, bf16[2,96,2048]{2,1,0:T(8,128)(2,1)S(1)}, u32[]{:S(2)}, u32[]{:S(2)}) %collective-permute-start.4) | collective-permute-done | bytes 786464 | tf_op jit(solution)/shard_map/ppermute | solution.py:530
  41.0 12.8 %collective-permute-done.5.r3 = bf16[2,96,2048]{2,1,0:T(8,128)(2,1)S(1)} collective-permute-done((bf16[2,96,2048]{2,1,0:T(8,128)(2,1)}, bf16[2,96,2048]{2,1,0:T(8,128)(2,1)S(1)}, u32[]{:S(2)}, u32[]{:S(2)}) %collective-permute-start.5) | collective-permute-done | bytes 786464 | tf_op jit(solution)/shard_map/ppermute | solution.py:530
  53.8 2.0 %collective-permute-done.3.r1 = bf16[2,96,2048]{2,1,0:T(8,128)(2,1)S(1)} collective-permute-done((bf16[2,96,2048]{2,1,0:T(8,128)(2,1)}, bf16[2,96,2048]{2,1,0:T(8,128)(2,1)S(1)}, u32[]{:S(2)}, u32[]{:S(2)}) %collective-permute-start.3) | collective-permute-done | bytes 786464 | tf_op jit(solution)/shard_map/ppermute | solution.py:530
  55.8 5.5 %expert.1 = (bf16[96,2176]{1,0:T(8,128)(2,1)}, bf16[96,2176]{1,0:T(8,128)(2,1)}, bf16[96,2176]{1,0:T(8,128)(2,1)}, bf16[96,2176]{1,0:T(8,128)(2,1)}, bf16[384,5632]{1,0:T(8,128)(2,1)S(1)}) custom-call(bf16[2,96,2048]{2,1,0:T(8,128)(2,1)S(1)} %copy-done.4, bf16[2,96,2048]{2,1,0:T(8,128)(2,1)S(1)} %collective-permute-done.3.r1, ...), custom_call_target="tpu_custom_call" | custom-call | flops 16106127360 | bytes 58720256 | tf_op jit(solution)/shard_map/expert/pallas_call | solution.py:52
  62.9 3.1 %collective-permute-start.6 = (bf16[96,2176]{1,0:T(8,128)(2,1)}, bf16[96,2176]{1,0:T(8,128)(2,1)}, u32[]{:S(2)}, u32[]{:S(2)}) collective-permute-start(bf16[96,2176]{1,0:T(8,128)(2,1)} %get-tuple-element.61), channel_id=1, source_target_pairs={{0,3},{1,0},{2,1},{3,2},{4,7},{5,4},{6,5},{7,6},{8,11},{9,8},{10,9... | collective-permute-start | bytes 1253384 | tf_op jit(solution)/shard_map/ppermute | solution.py:530
  66.0 3.2 %own_weights.1 = (f32[1024,1024]{1,0:T(8,128)S(1)}, f32[256,2048]{1,0:T(8,128)S(1)}) custom-call(s32[5]{0:T(128)S(1)} %stack.23.at_ref.spot_ref, bf16[384,5632]{1,0:T(8,128)(2,1)S(1)} %get-tuple-element.62.mine), custom_call_target="tpu_custom_call" | custom-call | flops 4831838208 | bytes 41943040 | tf_op jit(solution)/shard_map/own_weights/pallas_call | solution.py:52
  70.2 4.4 %weights.1 = bf16[16,96,1024]{2,1,0:T(8,128)(2,1)} custom-call(s32[5]{0:T(128)S(1)} %stack.23.at_ref.spot_ref, f32[1024,1024]{1,0:T(8,128)S(1)} %get-tuple-element.63.up_ref, f32[256,2048]{1,0:T(8,128)S(1)} %get-tuple-element.64.down_ref, bf16[384,5632]{1,0:T(8,128)(2,1)S(1)} %collective-permute-done.7.other), custom_call_target="tpu_custom_call" | custom-call | flops 4831838208 | bytes 41943040 | tf_op jit(solution)/shard_map/weights/pallas_call | solution.py:52
  74.6 7.1 %all-to-all-start = ((bf16[16,96,1024]{2,1,0:T(8,128)(2,1)}), bf16[16,96,1024]{2,1,0:T(8,128)(2,1)S(1)}, u32[]{:S(2)}, u32[]{:S(2)}) async-start(bf16[16,96,1024]{2,1,0:T(8,128)(2,1)} %weights.1), calls=%async_computation | async-start | bytes 6291456 | tf_op jit(solution)/shard_map/all_to_all | solution.py:583
  81.7 2.5 %collective-permute-done.9.refs_9_ = bf16[96,2176]{1,0:T(8,128)(2,1)} collective-permute-done((bf16[96,2176]{1,0:T(8,128)(2,1)}, bf16[96,2176]{1,0:T(8,128)(2,1)}, u32[]{:S(2)}, u32[]{:S(2)}) %collective-permute-start.9) | collective-permute-done | bytes 417824 | tf_op jit(solution)/shard_map/ppermute | solution.py:530
  84.1 8.3 %project.1 = (bf16[256,2048]{1,0:T(8,128)(2,1)}, bf16[1,256]{1,0:T(2,128)(2,1)}, bf16[256,512]{1,0:T(8,128)(2,1)S(1)}, bf16[256,512]{1,0:T(8,128)(2,1)S(1)}, bf1...) custom-call(bf16[512,2048]{1,0:T(8,128)(2,1)} %refs_0_.2, bf16[32,3,16,2048]{3,2,1,0:T(8,128)(2,1)} %bitcast.11, ...), custom_call_target="tpu_custom_call" | custom-call | flops 7650410496 | bytes 31457280 | tf_op jit(solution)/shard_map/project/pallas_call | solution.py:52
  95.4 6.4 %collective-permute-done.10.g1 = bf16[256,512]{1,0:T(8,128)(2,1)S(1)} collective-permute-done((bf16[256,512]{1,0:T(8,128)(2,1)S(1)}, bf16[256,512]{1,0:T(8,128)(2,1)S(1)}, u32[]{:S(2)}, u32[]{:S(2)}) %collective-permute-start.10) | collective-permute-done | bytes 262176 | tf_op jit(solution)/shard_map/ppermute | solution.py:530
  101.8 2.2 %collective-permute-done.11.g2 = bf16[256,512]{1,0:T(8,128)(2,1)S(1)} collective-permute-done((bf16[256,512]{1,0:T(8,128)(2,1)S(1)}, bf16[256,512]{1,0:T(8,128)(2,1)S(1)}, u32[]{:S(2)}, u32[]{:S(2)}) %collective-permute-start.11) | collective-permute-done | bytes 262176 | tf_op jit(solution)/shard_map/ppermute | solution.py:530
  104.0 4.3 %collective-permute-done.12.g3 = bf16[256,512]{1,0:T(8,128)(2,1)S(1)} collective-permute-done((bf16[256,512]{1,0:T(8,128)(2,1)S(1)}, bf16[256,512]{1,0:T(8,128)(2,1)S(1)}, u32[]{:S(2)}, u32[]{:S(2)}) %collective-permute-start.12) | collective-permute-done | bytes 262176 | tf_op jit(solution)/shard_map/ppermute | solution.py:530
  112.9 2.7 %collective-permute-start.15 = (bf16[512,128]{1,0:T(8,128)(2,1)S(1)}, bf16[512,128]{1,0:T(8,128)(2,1)S(1)}, u32[]{:S(2)}, u32[]{:S(2)}) collective-permute-start(bf16[512,128]{1,0:T(8,128)(2,1)S(1)} %get-tuple-element.76), channel_id=1, source_target_pairs={{0,16},{4,20},{8,24},{12,28},{16,0},{20,4},{24,8},{28,12},{32,48},... | collective-permute-start | bytes 393224 | tf_op jit(solution)/shard_map/ppermute | solution.py:534
  117.1 8.2 %query_key.1 = (bf16[1024,512]{1,0:T(8,128)(2,1)}, bf16[1024,512]{1,0:T(8,128)(2,1)S(1)}) custom-call(s32[5]{0:T(128)S(1)} %stack.23.at_ref.spot_ref, bf16[1024,512]{1,0:T(8,128)(2,1)S(1)} %copy-done, bf16[1024,512]{1,0:T(8,128)(2,1)S(1)} %copy-done.1, bf16[1024,512]{1,0:T(8,128)(2,1)S(1)} %copy-done.2, bf16[1024,512]{1,0:T(8,128)(2,1)S(1)} %get-tuple-element.73.g_ref, ...), custom_call_target="tpu_custom_call" | custom-call | flops 8053063680 | bytes 18874368 | tf_op jit(solution)/shard_map/query_key/pallas_call | solution.py:52
  126.8 8.4 %collective-permute-done.15.x2 = bf16[512,128]{1,0:T(8,128)(2,1)S(1)} collective-permute-done((bf16[512,128]{1,0:T(8,128)(2,1)S(1)}, bf16[512,128]{1,0:T(8,128)(2,1)S(1)}, u32[]{:S(2)}, u32[]{:S(2)}) %collective-permute-start.15) | collective-permute-done | bytes 131104 | tf_op jit(solution)/shard_map/ppermute | solution.py:534
  135.5 2.9 %collective-permute-start.18 = (bf16[512,128]{1,0:T(8,128)(2,1)S(1)}, bf16[512,128]{1,0:T(8,128)(2,1)S(1)}, u32[]{:S(2)}, u32[]{:S(2)}) collective-permute-start(bf16[512,128]{1,0:T(8,128)(2,1)S(1)} %line.1), channel_id=1, source_target_pairs={{0,64},{4,68},{8,72},{12,76},{16,80},{20,84},{24,88},{28,92},{32,9... | collective-permute-start | bytes 393224 | tf_op jit(solution)/shard_map/ppermute | solution.py:538
  138.3 2.4 %collective-permute-start.19 = (bf16[512,128]{1,0:T(8,128)(2,1)S(1)}, bf16[512,128]{1,0:T(8,128)(2,1)S(1)}, u32[]{:S(2)}, u32[]{:S(2)}) collective-permute-start(bf16[512,128]{1,0:T(8,128)(2,1)S(1)} %line.1), channel_id=1, source_target_pairs={{0,96},{4,100},{8,104},{12,108},{16,112},{20,116},{24,120},{28,124... | collective-permute-start | bytes 393224 | tf_op jit(solution)/shard_map/ppermute | solution.py:538
  140.8 4.1 %value.1.value_ref = bf16[1024,512]{1,0:T(8,128)(2,1)S(1)} custom-call(s32[5]{0:T(128)S(1)} %stack.23.at_ref.spot_ref, bf16[1024,512]{1,0:T(8,128)(2,1)S(1)} %copy-done, bf16[1024,512]{1,0:T(8,128)(2,1)S(1)} %copy-done.1, bf16[1024,512]{1,0:T(8,128)(2,1)S(1)} %get-tuple-element.73.g_ref), custom_call_target="tpu_custom_call" | custom-call | flops 4026531840 | bytes 18874368 | tf_op jit(solution)/shard_map/value/pallas_call | solution.py:52
  144.9 2.7 %final.1 = (bf16[1024,512]{1,0:T(8,128)(2,1)}, bf16[1024,512]{1,0:T(8,128)(2,1)}) custom-call(s32[5]{0:T(128)S(1)} %stack.23.at_ref.spot_ref, f32[512,128]{1,0:T(8,128)S(1)} %collective-permute-done.13.other, bf16[512,128]{1,0:T(8,128)(2,1)S(1)} %collective-permute-done.14.x1, bf16[512,128]{1,0:T(8,128)(2,1)S(1)} %collective-permute-done.15.x2, ...), custom_call_target="tpu_custom_call" | custom-call | flops 1610612736 | bytes 25165824 | tf_op jit(solution)/shard_map/final/pallas_call | solution.py:52
  (47 shorter events, 19.8 us)
Async XLA Ops:
  7.2 77.0 %all-gather.3.cloned.1.call-start = ((), (), s32[]{:S(2)}) async-start(), calls=%async_computation.1 | async-start | bytes 6488064 | tf_op jit(solution)/shard_map/all_gather | solution.py:569
  8.1 9.9 %collective-permute-start = (bf16[16,2048]{1,0:T(8,128)(2,1)S(1)}, bf16[16,2048]{1,0:T(8,128)(2,1)S(1)}, u32[]{:S(2)}, u32[]{:S(2)}) collective-permute-start(bf16[16,2048]{1,0:T(8,128)(2,1)S(1)} %constant_dynamic-slice_fusion), channel_id=1, source_target_pairs={{0,1},{1,2},{2,3},{3,0},{4,5},{5,6},{6,7},{7,4},{8,9},{9,10},{10,1... | collective-permute-start | bytes 196616 | tf_op jit(solution)/shard_map/ppermute | solution.py:530
  9.7 8.2 %collective-permute-start.1 = (bf16[16,2048]{1,0:T(8,128)(2,1)S(1)}, bf16[16,2048]{1,0:T(8,128)(2,1)S(1)}, u32[]{:S(2)}, u32[]{:S(2)}) collective-permute-start(bf16[16,2048]{1,0:T(8,128)(2,1)S(1)} %constant_dynamic-slice_fusion), channel_id=1, source_target_pairs={{0,2},{1,3},{2,0},{3,1},{4,6},{5,7},{6,4},{7,5},{8,10},{9,11},{10,... | collective-permute-start | bytes 196616 | tf_op jit(solution)/shard_map/ppermute | solution.py:530
  12.6 5.3 %collective-permute-start.2 = (bf16[16,2048]{1,0:T(8,128)(2,1)S(1)}, bf16[16,2048]{1,0:T(8,128)(2,1)S(1)}, u32[]{:S(2)}, u32[]{:S(2)}) collective-permute-start(bf16[16,2048]{1,0:T(8,128)(2,1)S(1)} %constant_dynamic-slice_fusion), channel_id=1, source_target_pairs={{0,3},{1,0},{2,1},{3,2},{4,7},{5,4},{6,5},{7,6},{8,11},{9,8},{10,9... | collective-permute-start | bytes 196616 | tf_op jit(solution)/shard_map/ppermute | solution.py:530
  18.7 22.3 %collective-permute-start.4 = (bf16[2,96,2048]{2,1,0:T(8,128)(2,1)}, bf16[2,96,2048]{2,1,0:T(8,128)(2,1)S(1)}, u32[]{:S(2)}, u32[]{:S(2)}) collective-permute-start(bf16[2,96,2048]{2,1,0:T(8,128)(2,1)} %get-tuple-element.55), channel_id=1, source_target_pairs={{0,2},{1,3},{2,0},{3,1},{4,6},{5,7},{6,4},{7,5},{8,10},{9,11},{10,... | collective-permute-start | bytes 2359304 | tf_op jit(solution)/shard_map/ppermute | solution.py:530
  19.2 34.6 %collective-permute-start.5 = (bf16[2,96,2048]{2,1,0:T(8,128)(2,1)}, bf16[2,96,2048]{2,1,0:T(8,128)(2,1)S(1)}, u32[]{:S(2)}, u32[]{:S(2)}) collective-permute-start(bf16[2,96,2048]{2,1,0:T(8,128)(2,1)} %get-tuple-element.56), channel_id=1, source_target_pairs={{0,3},{1,0},{2,1},{3,2},{4,7},{5,4},{6,5},{7,6},{8,11},{9,8},{10,9... | collective-permute-start | bytes 2359304 | tf_op jit(solution)/shard_map/ppermute | solution.py:530
  22.1 33.7 %collective-permute-start.3 = (bf16[2,96,2048]{2,1,0:T(8,128)(2,1)}, bf16[2,96,2048]{2,1,0:T(8,128)(2,1)S(1)}, u32[]{:S(2)}, u32[]{:S(2)}) collective-permute-start(bf16[2,96,2048]{2,1,0:T(8,128)(2,1)} %get-tuple-element.54), channel_id=1, source_target_pairs={{0,1},{1,2},{2,3},{3,0},{4,5},{5,6},{6,7},{7,4},{8,9},{9,10},{10,1... | collective-permute-start | bytes 2359304 | tf_op jit(solution)/shard_map/ppermute | solution.py:530
  22.1 33.7 %copy-start.4 = (bf16[2,96,2048]{2,1,0:T(8,128)(2,1)S(1)}, bf16[2,96,2048]{2,1,0:T(8,128)(2,1)}, u32[]{:S(2)}) copy-start(bf16[2,96,2048]{2,1,0:T(8,128)(2,1)} %get-tuple-element.53.r0) | copy-start | bytes 2359300
  61.2 9.0 %collective-permute-start.7 = (bf16[384,5632]{1,0:T(8,128)(2,1)S(1)}, bf16[384,5632]{1,0:T(8,128)(2,1)S(1)}, u32[]{:S(2)}, u32[]{:S(2)}) collective-permute-start(bf16[384,5632]{1,0:T(8,128)(2,1)S(1)} %get-tuple-element.62.mine), channel_id=1, source_target_pairs={{0,4},{4,0},{8,12},{12,8},{16,20},{20,16},{24,28},{28,24},{32,36},... | collective-permute-start | bytes 12976136 | tf_op jit(solution)/shard_map/ppermute | solution.py:542
  61.4 20.2 %collective-permute-start.8 = (bf16[96,2176]{1,0:T(8,128)(2,1)}, bf16[96,2176]{1,0:T(8,128)(2,1)}, u32[]{:S(2)}, u32[]{:S(2)}) collective-permute-start(bf16[96,2176]{1,0:T(8,128)(2,1)} %get-tuple-element.65), channel_id=1, source_target_pairs={{0,2},{1,3},{2,0},{3,1},{4,6},{5,7},{6,4},{7,5},{8,10},{9,11},{10,... | collective-permute-start | bytes 1253384 | tf_op jit(solution)/shard_map/ppermute | solution.py:530
  62.7 21.4 %collective-permute-start.9 = (bf16[96,2176]{1,0:T(8,128)(2,1)}, bf16[96,2176]{1,0:T(8,128)(2,1)}, u32[]{:S(2)}, u32[]{:S(2)}) collective-permute-start(bf16[96,2176]{1,0:T(8,128)(2,1)} %get-tuple-element.66), channel_id=1, source_target_pairs={{0,1},{1,2},{2,3},{3,0},{4,5},{5,6},{6,7},{7,4},{8,9},{9,10},{10,1... | collective-permute-start | bytes 1253384 | tf_op jit(solution)/shard_map/ppermute | solution.py:530
  62.9 21.2 %collective-permute-start.6 = (bf16[96,2176]{1,0:T(8,128)(2,1)}, bf16[96,2176]{1,0:T(8,128)(2,1)}, u32[]{:S(2)}, u32[]{:S(2)}) collective-permute-start(bf16[96,2176]{1,0:T(8,128)(2,1)} %get-tuple-element.61), channel_id=1, source_target_pairs={{0,3},{1,0},{2,1},{3,2},{4,7},{5,4},{6,5},{7,6},{8,11},{9,8},{10,9... | collective-permute-start | bytes 1253384 | tf_op jit(solution)/shard_map/ppermute | solution.py:530
  74.6 73.0 %all-to-all-start = ((bf16[16,96,1024]{2,1,0:T(8,128)(2,1)}), bf16[16,96,1024]{2,1,0:T(8,128)(2,1)S(1)}, u32[]{:S(2)}, u32[]{:S(2)}) async-start(bf16[16,96,1024]{2,1,0:T(8,128)(2,1)} %weights.1), calls=%async_computation | async-start | bytes 6291456 | tf_op jit(solution)/shard_map/all_to_all | solution.py:583
  92.5 24.6 %copy-start.1 = (bf16[1024,512]{1,0:T(8,128)(2,1)S(1)}, bf16[1024,512]{1,0:T(8,128)(2,1)}, u32[]{:S(2)}) copy-start(bf16[1024,512]{1,0:T(8,128)(2,1)} %k_ref.5) | copy-start | bytes 3145732
  92.5 9.2 %collective-permute-start.10 = (bf16[256,512]{1,0:T(8,128)(2,1)S(1)}, bf16[256,512]{1,0:T(8,128)(2,1)S(1)}, u32[]{:S(2)}, u32[]{:S(2)}) collective-permute-start(bf16[256,512]{1,0:T(8,128)(2,1)S(1)} %get-tuple-element.70), channel_id=1, source_target_pairs={{0,3},{1,0},{2,1},{3,2},{4,7},{5,4},{6,5},{7,6},{8,11},{9,8},{10,9... | collective-permute-start | bytes 786440 | tf_op jit(solution)/shard_map/ppermute | solution.py:530
  93.3 10.8 %collective-permute-start.11 = (bf16[256,512]{1,0:T(8,128)(2,1)S(1)}, bf16[256,512]{1,0:T(8,128)(2,1)S(1)}, u32[]{:S(2)}, u32[]{:S(2)}) collective-permute-start(bf16[256,512]{1,0:T(8,128)(2,1)S(1)} %get-tuple-element.71), channel_id=1, source_target_pairs={{0,2},{1,3},{2,0},{3,1},{4,6},{5,7},{6,4},{7,5},{8,10},{9,11},{10,... | collective-permute-start | bytes 786440 | tf_op jit(solution)/shard_map/ppermute | solution.py:530
  94.7 13.7 %collective-permute-start.12 = (bf16[256,512]{1,0:T(8,128)(2,1)S(1)}, bf16[256,512]{1,0:T(8,128)(2,1)S(1)}, u32[]{:S(2)}, u32[]{:S(2)}) collective-permute-start(bf16[256,512]{1,0:T(8,128)(2,1)S(1)} %get-tuple-element.72), channel_id=1, source_target_pairs={{0,1},{1,2},{2,3},{3,0},{4,5},{5,6},{6,7},{7,4},{8,9},{9,10},{10,1... | collective-permute-start | bytes 786440 | tf_op jit(solution)/shard_map/ppermute | solution.py:530
  109.6 1.6 %collective-permute-start.13 = (f32[512,128]{1,0:T(8,128)S(1)}, f32[512,128]{1,0:T(8,128)S(1)}, u32[]{:S(2)}, u32[]{:S(2)}) collective-permute-start(f32[512,128]{1,0:T(8,128)S(1)} %get-tuple-element.75.state), channel_id=1, source_target_pairs={{0,4},{4,0},{8,12},{12,8},{16,20},{20,16},{24,28},{28,24},{32,36},... | collective-permute-start | bytes 786440 | tf_op jit(solution)/shard_map/ppermute | solution.py:542
  111.3 15.5 %collective-permute-start.14 = (bf16[512,128]{1,0:T(8,128)(2,1)S(1)}, bf16[512,128]{1,0:T(8,128)(2,1)S(1)}, u32[]{:S(2)}, u32[]{:S(2)}) collective-permute-start(bf16[512,128]{1,0:T(8,128)(2,1)S(1)} %get-tuple-element.76), channel_id=1, source_target_pairs={{0,8},{4,12},{8,16},{12,20},{16,24},{20,28},{24,0},{28,4},{32,40},... | collective-permute-start | bytes 393224 | tf_op jit(solution)/shard_map/ppermute | solution.py:534
  112.9 22.2 %collective-permute-start.15 = (bf16[512,128]{1,0:T(8,128)(2,1)S(1)}, bf16[512,128]{1,0:T(8,128)(2,1)S(1)}, u32[]{:S(2)}, u32[]{:S(2)}) collective-permute-start(bf16[512,128]{1,0:T(8,128)(2,1)S(1)} %get-tuple-element.76), channel_id=1, source_target_pairs={{0,16},{4,20},{8,24},{12,28},{16,0},{20,4},{24,8},{28,12},{32,48},... | collective-permute-start | bytes 393224 | tf_op jit(solution)/shard_map/ppermute | solution.py:534
  115.6 19.5 %collective-permute-start.16 = (bf16[512,128]{1,0:T(8,128)(2,1)S(1)}, bf16[512,128]{1,0:T(8,128)(2,1)S(1)}, u32[]{:S(2)}, u32[]{:S(2)}) collective-permute-start(bf16[512,128]{1,0:T(8,128)(2,1)S(1)} %get-tuple-element.76), channel_id=1, source_target_pairs={{0,24},{4,28},{8,0},{12,4},{16,8},{20,12},{24,16},{28,20},{32,56},... | collective-permute-start | bytes 393224 | tf_op jit(solution)/shard_map/ppermute | solution.py:534
  135.2 9.6 %collective-permute-start.17 = (bf16[512,128]{1,0:T(8,128)(2,1)S(1)}, bf16[512,128]{1,0:T(8,128)(2,1)S(1)}, u32[]{:S(2)}, u32[]{:S(2)}) collective-permute-start(bf16[512,128]{1,0:T(8,128)(2,1)S(1)} %line.1), channel_id=1, source_target_pairs={{0,32},{4,36},{8,40},{12,44},{16,48},{20,52},{24,56},{28,60},{32,6... | collective-permute-start | bytes 393224 | tf_op jit(solution)/shard_map/ppermute | solution.py:538
  135.5 9.4 %collective-permute-start.18 = (bf16[512,128]{1,0:T(8,128)(2,1)S(1)}, bf16[512,128]{1,0:T(8,128)(2,1)S(1)}, u32[]{:S(2)}, u32[]{:S(2)}) collective-permute-start(bf16[512,128]{1,0:T(8,128)(2,1)S(1)} %line.1), channel_id=1, source_target_pairs={{0,64},{4,68},{8,72},{12,76},{16,80},{20,84},{24,88},{28,92},{32,9... | collective-permute-start | bytes 393224 | tf_op jit(solution)/shard_map/ppermute | solution.py:538
  138.3 6.6 %collective-permute-start.19 = (bf16[512,128]{1,0:T(8,128)(2,1)S(1)}, bf16[512,128]{1,0:T(8,128)(2,1)S(1)}, u32[]{:S(2)}, u32[]{:S(2)}) collective-permute-start(bf16[512,128]{1,0:T(8,128)(2,1)S(1)} %line.1), channel_id=1, source_target_pairs={{0,96},{4,100},{8,104},{12,108},{16,112},{20,116},{24,120},{28,124... | collective-permute-start | bytes 393224 | tf_op jit(solution)/shard_map/ppermute | solution.py:538
  (3 other events, 73.3 us)
Sparse Core Ops, SparseCore 0:
  18.8 51.5 all-gather.2
